TPU v7x, 32 devices: a whole 2x2x4 slice. The times are simulated.
32 devices in a mesh: dp: 8 (over y, x, core), ctx: 4 (over z).
Axes of the slice: x: 2, y: 2, z: 4, core: 2. Of those that a mesh axis runs over, the one named last changes fastest.
Arguments:
- tokens_in: bfloat16 [2, 8, 1024, 1024], P(None, 'dp', 'ctx'), may hold values from -6 to 6
- seq_lengths: int32 [2, 8, 4], P(None, 'dp'), may hold values from 0 to 1024, as said below
- norm_linear: bfloat16 [1024], P(('dp', 'ctx')), may hold values from 0.25 to 1.75
- proj_qk: bfloat16 [1024, 512], P(('dp', 'ctx')), may hold values from -0.1875 to 0.1875
- proj_values: bfloat16 [1024, 1024], P(('dp', 'ctx')), may hold values from -0.1875 to 0.1875
- conv_taps: bfloat16 [1024, 3], P(('dp', 'ctx')), may hold values from -3.5 to 3.5
- out_linear: bfloat16 [1024, 1024], P(('dp', 'ctx')), may hold values from -3 to 3
- norm_ffn_one: bfloat16 [1024], P(('dp', 'ctx')), may hold values from 0.25 to 1.75
- gate_up_one: bfloat16 [1024, 5632], P(('dp', 'ctx')), may hold values from -0.1875 to 0.1875
- down_one: bfloat16 [2816, 1024], P(('dp', 'ctx')), may hold values from -0.109375 to 0.109375
- norm_window: bfloat16 [1024], P(('dp', 'ctx')), may hold values from 0.25 to 1.75
- proj_qkv: bfloat16 [1024, 3072], P(('dp', 'ctx')), may hold values from -0.1875 to 0.1875
- out_window: bfloat16 [1024, 1024], P(('dp', 'ctx')), may hold values from -1 to 1
- norm_ffn_two: bfloat16 [1024], P(('dp', 'ctx')), may hold values from 0.25 to 1.75
- gate_up_two: bfloat16 [1024, 5632], P(('dp', 'ctx')), may hold values from -0.1875 to 0.1875
- down_two: bfloat16 [2816, 1024], P(('dp', 'ctx')), may hold values from -0.109375 to 0.109375
- cotangent: bfloat16 [2, 8, 1024, 1024], P(None, 'dp', 'ctx'), may hold values from -6 to 6
Outputs:
- output: bfloat16 [2, 8, 1024, 1024], P(None, 'dp', 'ctx')
- tokens_grad: bfloat16 [2, 8, 1024, 1024], P(None, 'dp', 'ctx')
- grad_norm_linear: float32 [1024], P(('dp', 'ctx'))
- grad_proj_qk: float32 [1024, 512], P(('dp', 'ctx'))
- grad_proj_values: float32 [1024, 1024], P(('dp', 'ctx'))
- grad_conv_taps: float32 [1024, 3], P(('dp', 'ctx'))
- grad_out_linear: float32 [1024, 1024], P(('dp', 'ctx'))
- grad_norm_ffn_one: float32 [1024], P(('dp', 'ctx'))
- grad_gate_up_one: float32 [1024, 5632], P(('dp', 'ctx'))
- grad_down_one: float32 [2816, 1024], P(('dp', 'ctx'))
- grad_norm_window: float32 [1024], P(('dp', 'ctx'))
- grad_proj_qkv: float32 [1024, 3072], P(('dp', 'ctx'))
- grad_out_window: float32 [1024, 1024], P(('dp', 'ctx'))
- grad_norm_ffn_two: float32 [1024], P(('dp', 'ctx'))
- grad_gate_up_two: float32 [1024, 5632], P(('dp', 'ctx'))
- grad_down_two: float32 [2816, 1024], P(('dp', 'ctx'))
Inputs may be any that keep to these rules, and one draw needn't show every extreme that they name: `seq_lengths`: for each slot exactly one of the 2 micro-batches holds a single sequence of 1024 tokens there (its other entries zero); in the other micro-batches the first 3 entries lie between 128 and 307 and the last is zero. Tokens after the sum of a slot's lengths are padding.
All inputs are finite; a program needn't handle non-finite values.
Results may differ from a plain program's by a relative error of at most 0.014.
Values may be sent and summed in bfloat16 or wider, within the bound.
A program may use at most 384 MiB of HBM per device.

v0:
```python
from functools import partial
import math

import jax
import jax.numpy as jnp
from jax import lax
from jax.sharding import PartitionSpec as P

HEADS = 16
FEAT = 16
WINDOW = 64
CONV = 3


epsilon = 1e-05
masked_fill = -1e30
highest = lax.Precision.HIGHEST


def passed_along(value, axis, steps):
    count = lax.axis_size(axis)
    leading, last = (max(0, -steps), min(count, count - steps))
    return lax.ppermute(value, axis, [(source, source + steps) for source in range(leading, last)])


def carried_in(x, axis, join, neutral):
    place = lax.axis_index(axis)
    gathered = jax.tree.map(
        lambda a, kind: lax.all_gather(a.astype(kind), axis),
        x,
        (jnp.bfloat16, jnp.bfloat16, jnp.bfloat16),
    )
    state = jax.tree.map(lambda a, e: jnp.zeros_like(a) + jnp.asarray(e, a.dtype), x, neutral)

    def carried_one(hop, state):
        return join(
            state,
            jax.tree.map(
                lambda a, own: lax.dynamic_index_in_dim(a, hop, 0, False).astype(own.dtype),
                gathered,
                x,
            ),
        )

    return lax.fori_loop(0, place, carried_one, state)


def entering(x, axis, join, neutral):
    count = lax.axis_size(axis)
    place = lax.axis_index(axis)
    ahead = count - 1 - place
    gathered = jax.tree.map(
        lambda a, kind: lax.all_gather(a.astype(kind), axis),
        x,
        jax.tree.map(lambda a: jnp.bfloat16 if a.dtype == jnp.float32 else a.dtype, x),
    )
    state = jax.tree.map(lambda a, e: jnp.zeros_like(a) + jnp.asarray(e, a.dtype), x, neutral)

    def entering_one(hop, state):
        source = count - 1 - hop
        return join(
            state,
            jax.tree.map(
                lambda a, own: lax.dynamic_index_in_dim(a, source, 0, False).astype(own.dtype),
                gathered,
                x,
            ),
        )

    return lax.fori_loop(0, ahead, entering_one, state)


def normed(stream, scale_gain):
    return (
        stream * lax.rsqrt(jnp.mean(stream * stream, axis=-1, keepdims=True) + epsilon) * scale_gain
    )


def matmul(operand, weight):
    return jnp.einsum("mtd,de->mte", operand, weight, preferred_element_type=jnp.float32)


def matmul_back(operand, weight):
    return jnp.einsum("mte,de->mtd", operand, weight, preferred_element_type=jnp.float32)


def weight_grad(operand, gradient):
    return jnp.einsum("mtd,mte->de", operand, gradient, preferred_element_type=jnp.float32)


def feature_map(source):
    feat_width = source.shape[-1]
    outer_prod = (source[..., :, None] * source[..., None, :]).reshape(
        source.shape[:-1] + (feat_width * feat_width,)
    )
    ones_col = jnp.ones(source.shape[:-1] + (1,), source.dtype)
    return jnp.concatenate(
        [ones_col, source * feat_width ** (-0.25), outer_prod / math.sqrt(2.0 * feat_width)],
        axis=-1,
    )


def chain_states(earlier, later):
    keep_part = 1.0 - later[2]
    return (
        later[0] + keep_part[:, None, None, None] * earlier[0],
        later[1] + keep_part[:, None, None] * earlier[1],
        jnp.maximum(earlier[2], later[2]),
    )


def layout(seq_lengths, tok_count):
    seq_ends = jnp.cumsum(seq_lengths[:, 0, :], axis=-1, dtype=jnp.int32)
    first_pos = lax.axis_index("ctx") * tok_count

    def segment_of(positions):
        return jnp.sum(
            (positions[None, :, None] >= seq_ends[:, None, :]).astype(jnp.int32),
            axis=-1,
            dtype=jnp.int32,
        )

    own_pos = first_pos + jnp.arange(tok_count, dtype=jnp.int32)
    own_seg = segment_of(own_pos)
    before_seg = segment_of(own_pos - 1)
    starts = (own_seg != before_seg) | (own_pos == 0)[None, :]
    tap_masks = []
    for offset in range(CONV):
        source = own_pos - offset
        tap_masks.append(
            ((segment_of(source) == own_seg) & (source >= 0)[None, :]).astype(jnp.float32)
        )
    key_pos = first_pos - (WINDOW - 1) + jnp.arange(tok_count + WINDOW - 1, dtype=jnp.int32)
    visible = (key_pos[None, :] <= own_pos[:, None]) & (
        key_pos[None, :] > own_pos[:, None] - WINDOW
    )
    visible = visible & (key_pos >= 0)[None, :]
    window_mask = visible[None] & (segment_of(key_pos)[:, None, :] == own_seg[:, :, None])
    causal = (own_pos[:, None] >= own_pos[None, :])[None] & (
        own_seg[:, :, None] == own_seg[:, None, :]
    )
    return {
        "valid": (own_pos[None, :] < seq_ends[:, -1:]).astype(jnp.float32),
        "flag": jnp.max(starts.astype(jnp.float32), axis=1),
        "carried": ((own_seg == before_seg[:, :1]) & (first_pos > 0)).astype(jnp.float32),
        "last": (own_seg == own_seg[:, -1:]).astype(jnp.float32),
        "causal": causal,
        "taps": jnp.stack(tap_masks),
        "window": window_mask,
    }


def conv_gate(pre_values, rim_rows, tap_weights, tap_masks):
    tok_count = pre_values.shape[1]
    rim_width = rim_rows.shape[1]
    extended = jnp.concatenate([rim_rows, pre_values], axis=1)
    conv_sum = jnp.zeros_like(pre_values)
    for offset in range(rim_width + 1):
        shifted = extended[:, rim_width - offset : rim_width - offset + tok_count, :]
        conv_sum = conv_sum + tap_weights[:, offset] * shifted * tap_masks[offset][:, :, None]
    return conv_sum * jax.nn.silu(pre_values)


def end_state(key_rows, head_values, last_mask):
    features = feature_map(key_rows) * last_mask[:, :, None, None]
    return (
        jnp.einsum("mthr,mthe->mhre", features, head_values, precision=highest),
        jnp.sum(features, axis=1),
    )


def attend_linear(query_rows, key_rows, head_values, state_in, totals_in, causal, carried):
    micro_count, tok_count = (query_rows.shape[0], query_rows.shape[1])
    scores = jnp.einsum("mihf,mjhf->mhij", query_rows, key_rows, precision=highest) / math.sqrt(
        query_rows.shape[-1]
    )
    weights = (1.0 + scores + 0.5 * scores * scores) * causal[:, None].astype(jnp.float32)
    numerator = jnp.einsum("mhij,mjhe->mihe", weights, head_values, precision=highest)
    denominator = jnp.transpose(jnp.sum(weights, axis=-1), (0, 2, 1))
    features = feature_map(query_rows) * carried[:, :, None, None]
    numerator = numerator + jnp.einsum("mihr,mhre->mihe", features, state_in, precision=highest)
    denominator = denominator + jnp.einsum("mihr,mhr->mih", features, totals_in, precision=highest)
    return (numerator / denominator[..., None]).reshape(micro_count, tok_count, -1)


def linear_forward(stream, weights, layout_info):
    norm_gain, qk_weight, value_weight, tap_weights, out_weight = weights
    micro_count, tok_count, model_width = stream.shape
    normed_rows, norm_back = jax.vjp(normed, stream, norm_gain.astype(jnp.float32))
    normed_low = normed_rows.astype(jnp.bfloat16)
    qk_rows = matmul(normed_low, qk_weight).astype(jnp.bfloat16)
    pre_values = matmul(normed_low, value_weight)
    rim_rows = passed_along(pre_values[:, tok_count - CONV + 1 :, :], "ctx", 1)
    value_rows, conv_back = jax.vjp(
        partial(conv_gate, tap_masks=layout_info["taps"]),
        pre_values,
        rim_rows,
        tap_weights.astype(jnp.float32),
    )
    head_values = (
        value_rows.astype(jnp.bfloat16)
        .astype(jnp.float32)
        .reshape(micro_count, tok_count, HEADS, model_width // HEADS)
    )
    half_cols = qk_rows.shape[-1] // 2
    query_rows = (
        qk_rows[..., :half_cols].astype(jnp.float32).reshape(micro_count, tok_count, HEADS, FEAT)
    )
    key_rows = (
        qk_rows[..., half_cols:].astype(jnp.float32).reshape(micro_count, tok_count, HEADS, FEAT)
    )
    state_out, state_back = jax.vjp(
        partial(end_state, last_mask=layout_info["last"]), key_rows, head_values
    )
    incoming = carried_in(
        (state_out[0], state_out[1], layout_info["flag"]),
        "ctx",
        chain_states,
        (
            jnp.zeros_like(state_out[0]),
            jnp.zeros_like(state_out[1]),
            jnp.zeros_like(layout_info["flag"]),
        ),
    )
    attended, attend_back = jax.vjp(
        partial(attend_linear, causal=layout_info["causal"], carried=layout_info["carried"]),
        query_rows,
        key_rows,
        head_values,
        incoming[0],
        incoming[1],
    )
    attended_low = attended.astype(jnp.bfloat16)
    branch = matmul(attended_low, out_weight)
    return (
        stream + branch,
        (norm_back, normed_low, conv_back, state_back, attend_back, attended_low),
    )


def linear_backward(grad_stream, residuals, weights, layout_info):
    norm_back, normed_low, conv_back, state_back, attend_back, attended_low = residuals
    qk_weight, value_weight, out_weight = (weights[1], weights[2], weights[4])
    micro_count, tok_count, model_width = grad_stream.shape
    grad_branch = grad_stream.astype(jnp.bfloat16)
    grad_out = weight_grad(attended_low, grad_branch)
    grad_attended = matmul_back(grad_branch, out_weight)
    grad_query, grad_key, grad_value, grad_state, grad_totals = attend_back(grad_attended)
    later_grads = entering(
        (grad_state, grad_totals, layout_info["flag"]),
        "ctx",
        chain_states,
        (
            jnp.zeros_like(grad_state),
            jnp.zeros_like(grad_totals),
            jnp.zeros_like(layout_info["flag"]),
        ),
    )
    key_more, value_more = state_back((later_grads[0], later_grads[1]))
    grad_key = grad_key + key_more
    grad_value = grad_value + value_more
    grad_qk = jnp.concatenate(
        [
            grad_query.reshape(micro_count, tok_count, -1),
            grad_key.reshape(micro_count, tok_count, -1),
        ],
        axis=-1,
    ).astype(jnp.bfloat16)
    grad_pre, grad_rim, grad_taps = conv_back(
        grad_value.reshape(micro_count, tok_count, model_width)
    )
    returned = passed_along(grad_rim, "ctx", -1)
    grad_pre = grad_pre.at[:, tok_count - CONV + 1 :, :].add(returned)
    grad_pre_low = grad_pre.astype(jnp.bfloat16)
    grad_qk_weight = weight_grad(normed_low, grad_qk)
    grad_value_weight = weight_grad(normed_low, grad_pre_low)
    grad_normed = matmul_back(grad_qk, qk_weight) + matmul_back(grad_pre_low, value_weight)
    grad_input, grad_gain = norm_back(grad_normed)
    return (
        grad_stream + grad_input,
        (grad_gain, grad_qk_weight, grad_value_weight, grad_taps, grad_out),
    )


def window_scores(heads_query, key_ext, window_mask, head_size):
    raw_scores = jnp.einsum(
        "mihe,mjhe->mhij", heads_query, key_ext, preferred_element_type=jnp.float32
    ) * head_size ** (-0.5)
    return jnp.where(window_mask[:, None], raw_scores, masked_fill)


def window_forward(stream, weights, layout_info):
    norm_gain, qkv_weight, out_weight = weights
    micro_count, tok_count, model_width = stream.shape
    head_size = model_width // HEADS
    normed_rows, norm_back = jax.vjp(normed, stream, norm_gain.astype(jnp.float32))
    normed_low = normed_rows.astype(jnp.bfloat16)
    qkv_rows = matmul(normed_low, qkv_weight).astype(jnp.bfloat16)
    key_value = qkv_rows[..., model_width:]
    rim_rows = passed_along(key_value[:, tok_count - WINDOW + 1 :, :], "ctx", 1)
    extended = jnp.concatenate([rim_rows, key_value], axis=1)
    key_ext = extended[..., :model_width].reshape(micro_count, -1, HEADS, head_size)
    value_ext = extended[..., model_width:].reshape(micro_count, -1, HEADS, head_size)
    heads_query = qkv_rows[..., :model_width].reshape(micro_count, tok_count, HEADS, head_size)
    scores = window_scores(heads_query, key_ext, layout_info["window"], head_size)
    row_peak = jnp.max(scores, axis=-1, keepdims=True)
    exp_scores = jnp.exp(scores - row_peak)
    row_total = jnp.sum(exp_scores, axis=-1, keepdims=True)
    probabilities = (exp_scores / row_total).astype(jnp.bfloat16)
    attended = jnp.einsum(
        "mhij,mjhe->mihe", probabilities, value_ext, preferred_element_type=jnp.float32
    )
    attended = attended.astype(jnp.bfloat16).reshape(micro_count, tok_count, model_width)
    branch = matmul(attended, out_weight)
    return (
        stream + branch,
        (
            norm_back,
            normed_low,
            heads_query,
            key_ext,
            value_ext,
            row_peak + jnp.log(row_total),
            attended,
        ),
    )


def window_backward(grad_stream, residuals, weights, layout_info):
    norm_back, normed_low, heads_query, key_ext, value_ext, log_total, attended = residuals
    qkv_weight, out_weight = (weights[1], weights[2])
    micro_count, tok_count, model_width = grad_stream.shape
    head_size = model_width // HEADS
    grad_branch = grad_stream.astype(jnp.bfloat16)
    grad_out = weight_grad(attended, grad_branch)
    grad_attended = (
        matmul_back(grad_branch, out_weight)
        .astype(jnp.bfloat16)
        .reshape(micro_count, tok_count, HEADS, head_size)
    )
    scores = window_scores(heads_query, key_ext, layout_info["window"], head_size)
    probabilities = jnp.exp(scores - log_total)
    grad_probs = jnp.einsum(
        "mihe,mjhe->mhij", grad_attended, value_ext, preferred_element_type=jnp.float32
    )
    grad_value_ext = jnp.einsum(
        "mhij,mihe->mjhe",
        probabilities.astype(jnp.bfloat16),
        grad_attended,
        preferred_element_type=jnp.float32,
    )
    inner_sum = jnp.sum(grad_probs * probabilities, axis=-1, keepdims=True)
    grad_scores = (probabilities * (grad_probs - inner_sum)).astype(jnp.bfloat16)
    score_scale = head_size ** (-0.5)
    grad_query = (
        jnp.einsum("mhij,mjhe->mihe", grad_scores, key_ext, preferred_element_type=jnp.float32)
        * score_scale
    )
    grad_key_ext = (
        jnp.einsum("mhij,mihe->mjhe", grad_scores, heads_query, preferred_element_type=jnp.float32)
        * score_scale
    )
    rim_grads = jnp.concatenate(
        [
            grad_key_ext[:, : WINDOW - 1].reshape(micro_count, WINDOW - 1, model_width),
            grad_value_ext[:, : WINDOW - 1].reshape(micro_count, WINDOW - 1, model_width),
        ],
        axis=-1,
    )
    returned = passed_along(rim_grads.astype(jnp.bfloat16), "ctx", -1).astype(rim_grads.dtype)
    own_grads = jnp.concatenate(
        [
            grad_key_ext[:, WINDOW - 1 :].reshape(micro_count, tok_count, model_width),
            grad_value_ext[:, WINDOW - 1 :].reshape(micro_count, tok_count, model_width),
        ],
        axis=-1,
    )
    own_grads = own_grads.at[:, tok_count - WINDOW + 1 :, :].add(returned)
    grad_qkv = jnp.concatenate(
        [grad_query.reshape(micro_count, tok_count, model_width), own_grads], axis=-1
    ).astype(jnp.bfloat16)
    grad_qkv_weight = weight_grad(normed_low, grad_qkv)
    grad_input, grad_gain = norm_back(matmul_back(grad_qkv, qkv_weight))
    return (grad_stream + grad_input, (grad_gain, grad_qkv_weight, grad_out))


def ffn_forward(stream, weights):
    norm_gain, gate_up, down_weight = weights
    hidden_width = down_weight.shape[0]
    normed_rows, norm_back = jax.vjp(normed, stream, norm_gain.astype(jnp.float32))
    normed_low = normed_rows.astype(jnp.bfloat16)
    projected = matmul(normed_low, gate_up)
    hidden = (jax.nn.silu(projected[..., :hidden_width]) * projected[..., hidden_width:]).astype(
        jnp.bfloat16
    )
    branch = matmul(hidden, down_weight)
    return (stream + branch, (norm_back, normed_low, projected, hidden))


def ffn_backward(grad_stream, residuals, weights):
    norm_back, normed_low, projected, hidden = residuals
    gate_up, down_weight = (weights[1], weights[2])
    hidden_width = down_weight.shape[0]
    grad_branch = grad_stream.astype(jnp.bfloat16)
    grad_down = weight_grad(hidden, grad_branch)
    grad_hidden = matmul_back(grad_branch, down_weight)
    gate_part = projected[..., :hidden_width]
    up_part = projected[..., hidden_width:]
    sigmoid_gate = jax.nn.sigmoid(gate_part)
    grad_gate = grad_hidden * up_part * sigmoid_gate * (1.0 + gate_part * (1.0 - sigmoid_gate))
    grad_up = grad_hidden * gate_part * sigmoid_gate
    grad_projected = jnp.concatenate([grad_gate, grad_up], axis=-1).astype(jnp.bfloat16)
    grad_gate_up = weight_grad(normed_low, grad_projected)
    grad_input, grad_gain = norm_back(matmul_back(grad_projected, gate_up))
    return (grad_stream + grad_input, (grad_gain, grad_gate_up, grad_down))


def body(
    tokens_in,
    seq_lengths,
    norm_linear,
    proj_qk,
    proj_values,
    conv_taps,
    out_linear,
    norm_ffn_one,
    gate_up_one,
    down_one,
    norm_window,
    proj_qkv,
    out_window,
    norm_ffn_two,
    gate_up_two,
    down_two,
    cotangent,
):
    tok_count = tokens_in.shape[2]
    layout_info = layout(seq_lengths, tok_count)
    stream = tokens_in[:, 0].astype(jnp.float32)
    layer_one = (
        lax.all_gather(norm_linear, ("dp", "ctx"), axis=0, tiled=True),
        lax.all_gather(proj_qk, ("dp", "ctx"), axis=0, tiled=True),
        lax.all_gather(proj_values, ("dp", "ctx"), axis=0, tiled=True),
        lax.all_gather(conv_taps, ("dp", "ctx"), axis=0, tiled=True),
        lax.all_gather(out_linear, ("dp", "ctx"), axis=0, tiled=True),
        lax.all_gather(norm_ffn_one, ("dp", "ctx"), axis=0, tiled=True),
        lax.all_gather(gate_up_one, ("dp", "ctx"), axis=0, tiled=True),
        lax.all_gather(down_one, ("dp", "ctx"), axis=0, tiled=True),
    )
    middle, saved_linear = linear_forward(stream, layer_one[:5], layout_info)
    first_out, saved_ffn_one = ffn_forward(middle, layer_one[5:])
    layer_two = (
        lax.all_gather(norm_window, ("dp", "ctx"), axis=0, tiled=True),
        lax.all_gather(proj_qkv, ("dp", "ctx"), axis=0, tiled=True),
        lax.all_gather(out_window, ("dp", "ctx"), axis=0, tiled=True),
        lax.all_gather(norm_ffn_two, ("dp", "ctx"), axis=0, tiled=True),
        lax.all_gather(gate_up_two, ("dp", "ctx"), axis=0, tiled=True),
        lax.all_gather(down_two, ("dp", "ctx"), axis=0, tiled=True),
    )
    second_mid, saved_window = window_forward(first_out, layer_two[:3], layout_info)
    closing, saved_ffn_two = ffn_forward(second_mid, layer_two[3:])
    valid_rows = layout_info["valid"][:, :, None]
    output = (closing * valid_rows).astype(jnp.bfloat16)[:, None]
    grad_stream = cotangent[:, 0].astype(jnp.float32) * valid_rows
    again_two = (
        lax.all_gather(norm_window, ("dp", "ctx"), axis=0, tiled=True),
        lax.all_gather(proj_qkv, ("dp", "ctx"), axis=0, tiled=True),
        lax.all_gather(out_window, ("dp", "ctx"), axis=0, tiled=True),
        lax.all_gather(norm_ffn_two, ("dp", "ctx"), axis=0, tiled=True),
        lax.all_gather(gate_up_two, ("dp", "ctx"), axis=0, tiled=True),
        lax.all_gather(down_two, ("dp", "ctx"), axis=0, tiled=True),
    )
    grad_stream, grads_ffn_two = ffn_backward(grad_stream, saved_ffn_two, again_two[3:])
    grad_stream, grads_window = window_backward(
        grad_stream, saved_window, again_two[:3], layout_info
    )
    local_two = (
        grads_window[0],
        grads_window[1],
        grads_window[2],
        grads_ffn_two[0],
        grads_ffn_two[1],
        grads_ffn_two[2],
    )
    reduced_two = (
        lax.psum_scatter(local_two[0], ("dp", "ctx"), scatter_dimension=0, tiled=True),
        lax.psum_scatter(local_two[1], ("dp", "ctx"), scatter_dimension=0, tiled=True),
        lax.psum_scatter(local_two[2], ("dp", "ctx"), scatter_dimension=0, tiled=True),
        lax.psum_scatter(local_two[3], ("dp", "ctx"), scatter_dimension=0, tiled=True),
        lax.psum_scatter(local_two[4], ("dp", "ctx"), scatter_dimension=0, tiled=True),
        lax.psum_scatter(local_two[5], ("dp", "ctx"), scatter_dimension=0, tiled=True),
    )
    again_one = (
        lax.all_gather(norm_linear, ("dp", "ctx"), axis=0, tiled=True),
        lax.all_gather(proj_qk, ("dp", "ctx"), axis=0, tiled=True),
        lax.all_gather(proj_values, ("dp", "ctx"), axis=0, tiled=True),
        lax.all_gather(conv_taps, ("dp", "ctx"), axis=0, tiled=True),
        lax.all_gather(out_linear, ("dp", "ctx"), axis=0, tiled=True),
        lax.all_gather(norm_ffn_one, ("dp", "ctx"), axis=0, tiled=True),
        lax.all_gather(gate_up_one, ("dp", "ctx"), axis=0, tiled=True),
        lax.all_gather(down_one, ("dp", "ctx"), axis=0, tiled=True),
    )
    grad_stream, grads_ffn_one = ffn_backward(grad_stream, saved_ffn_one, again_one[5:])
    grad_stream, grads_linear = linear_backward(
        grad_stream, saved_linear, again_one[:5], layout_info
    )
    local_one = (
        grads_linear[0],
        grads_linear[1],
        grads_linear[2],
        grads_linear[3],
        grads_linear[4],
        grads_ffn_one[0],
        grads_ffn_one[1],
        grads_ffn_one[2],
    )
    reduced_one = (
        lax.psum_scatter(local_one[0], ("dp", "ctx"), scatter_dimension=0, tiled=True),
        lax.psum_scatter(local_one[1], ("dp", "ctx"), scatter_dimension=0, tiled=True),
        lax.psum_scatter(local_one[2], ("dp", "ctx"), scatter_dimension=0, tiled=True),
        lax.psum_scatter(local_one[3], ("dp", "ctx"), scatter_dimension=0, tiled=True),
        lax.psum_scatter(local_one[4], ("dp", "ctx"), scatter_dimension=0, tiled=True),
        lax.psum_scatter(local_one[5], ("dp", "ctx"), scatter_dimension=0, tiled=True),
        lax.psum_scatter(local_one[6], ("dp", "ctx"), scatter_dimension=0, tiled=True),
        lax.psum_scatter(local_one[7], ("dp", "ctx"), scatter_dimension=0, tiled=True),
    )
    tokens_grad = grad_stream.astype(jnp.bfloat16)[:, None]
    return (
        output,
        tokens_grad,
        reduced_one[0],
        reduced_one[1],
        reduced_one[2],
        reduced_one[3],
        reduced_one[4],
        reduced_one[5],
        reduced_one[6],
        reduced_one[7],
        reduced_two[0],
        reduced_two[1],
        reduced_two[2],
        reduced_two[3],
        reduced_two[4],
        reduced_two[5],
    )


def solution(mesh):
    placed = (
        P(None, "dp", "ctx", None),
        P(None, "dp", None),
        P(("dp", "ctx")),
        P(("dp", "ctx"), None),
        P(("dp", "ctx"), None),
        P(("dp", "ctx"), None),
        P(("dp", "ctx"), None),
        P(("dp", "ctx")),
        P(("dp", "ctx"), None),
        P(("dp", "ctx"), None),
        P(("dp", "ctx")),
        P(("dp", "ctx"), None),
        P(("dp", "ctx"), None),
        P(("dp", "ctx")),
        P(("dp", "ctx"), None),
        P(("dp", "ctx"), None),
        P(None, "dp", "ctx", None),
    )
    return jax.shard_map(
        body,
        mesh=mesh,
        in_specs=placed,
        out_specs=(
            P(None, "dp", "ctx", None),
            P(None, "dp", "ctx", None),
            P(("dp", "ctx")),
            P(("dp", "ctx"), None),
            P(("dp", "ctx"), None),
            P(("dp", "ctx"), None),
            P(("dp", "ctx"), None),
            P(("dp", "ctx")),
            P(("dp", "ctx"), None),
            P(("dp", "ctx"), None),
            P(("dp", "ctx")),
            P(("dp", "ctx"), None),
            P(("dp", "ctx"), None),
            P(("dp", "ctx")),
            P(("dp", "ctx"), None),
            P(("dp", "ctx"), None),
        ),
        check_vma=False,
    )
```

profile of v0, /device:TPU:0, one launch (start us, length us, event | category | flops | bytes accessed | tf_op | source)
XLA Modules:
  0.0 3490.7 jit_solution(1688724721440813147)
XLA Ops:
  12.1 42.2 %all-reduce.16 = (bf16[1024]{0:T(1024)(128)(2,1)S(1)}, bf16[1024]{0:T(1024)(128)(2,1)S(1)}, bf16[1024]{0:T(1024)(128)(2,1)S(1)}, bf16[1024]{0:T(1024)(128)(2,1)S(1)}) all-reduce(bf16[1024]{0:T(1024)(128)(2,1)S(1)} %dynamic-update-slice.6, bf16[1024]{0:T(1024)(128)(2,1)S(1)} %dynamic-update-slice.8, ...), channel_id=1, replica_groups=mesh['dp'=8,'ctx'=4] {'dp','ctx'}, use_global_device_ids=true, to_apply=%add.6 | all-reduce | flops 4096 | bytes 16384
  55.1 66.3 %all-gather.5 = bf16[32,32,3]{1,2,0:T(4,128)(2,1)S(1)} all-gather(bf16[1,32,3]{1,2,0:T(4,128)(2,1)} %bitcast.374), channel_id=1, replica_groups=mesh['dp'=8,'ctx'=4] {'dp','ctx'}, dimensions={0}, use_global_device_ids=true | all-gather | bytes 6336 | tf_op jit(solution)/shard_map/all_gather | solution.py:444
  142.8 10.8 convolution_convert_fusion
  160.4 11.0 all-reduce.7
  173.4 5.2 fusion.171
  179.9 16.9 all-gather.2
  196.8 4.7 multiply_multiply_fusion
  206.0 64.5 %all-gather.36.cloned.1.call-done = bf16[8,16,273,64]{2,3,1,0:T(8,128)(2,1)} async-done(((bf16[2,16,273,64]{2,3,1,0:T(8,128)(2,1)}), bf16[8,16,273,64]{2,3,1,0:T(8,128)(2,1)}) %all-gather.36.cloned.1.call-update) | async-done | bytes 4472848 | tf_op jit(solution)/shard_map/all_gather | solution.py:29
  273.2 8.5 fusion.137
  281.8 12.3 fusion.172
  294.8 6.2 fusion.68
  301.0 27.1 all-gather.22.cloned.1.call-done
  331.4 89.5 %all-gather.24.cloned.1.call-done = bf16[1024,5632]{1,0:T(8,128)(2,1)} async-done(((bf16[32,5632]{1,0:T(8,128)(2,1)}), bf16[1024,5632]{1,0:T(8,128)(2,1)}) %all-gather.24.cloned.1.call-update) | async-done | bytes 11534352 | tf_op jit(solution)/shard_map/all_gather | solution.py:447
  420.9 9.5 fusion.12
  437.5 51.8 %all-gather.26.cloned.1.call-done = bf16[2816,1024]{1,0:T(8,128)(2,1)} async-done(((bf16[88,1024]{1,0:T(8,128)(2,1)}), bf16[2816,1024]{1,0:T(8,128)(2,1)}) %all-gather.26.cloned.1.call-update) | async-done | bytes 5767184 | tf_op jit(solution)/shard_map/all_gather | solution.py:448
  489.4 8.0 multiply_reduce_fusion.15
  497.4 63.4 %all-gather.28.cloned.1.call-done = bf16[1024,3072]{1,0:T(8,128)(2,1)} async-done(((bf16[32,3072]{1,0:T(8,128)(2,1)}), bf16[1024,3072]{1,0:T(8,128)(2,1)}) %all-gather.28.cloned.1.call-update) | async-done | bytes 6291472 | tf_op jit(solution)/shard_map/all_gather | solution.py:454
  560.8 6.9 fusion.34
  577.4 7.5 collective-permute-done.1
  604.3 14.8 all-gather.30.cloned.1.call-done
  619.1 4.8 multiply_reduce_fusion.14
  623.9 88.2 %all-gather.32.cloned.1.call-done = bf16[1024,5632]{1,0:T(8,128)(2,1)} async-done(((bf16[32,5632]{1,0:T(8,128)(2,1)}), bf16[1024,5632]{1,0:T(8,128)(2,1)}) %all-gather.32.cloned.1.call-update) | async-done | bytes 11534352 | tf_op jit(solution)/shard_map/all_gather | solution.py:457
  712.1 12.3 fusion.8
  724.4 56.1 %all-gather.34.cloned.1.call-done = bf16[2816,1024]{1,0:T(8,128)(2,1)} async-done(((bf16[88,1024]{1,0:T(8,128)(2,1)}), bf16[2816,1024]{1,0:T(8,128)(2,1)}) %all-gather.34.cloned.1.call-update) | async-done | bytes 5767184 | tf_op jit(solution)/shard_map/all_gather | solution.py:458
  780.5 12.4 multiply_convert_fusion.4
  792.9 13.4 multiply_reduce_fusion.5
  813.8 8.3 fusion.77
  822.1 6.9 multiply_reduce_fusion
  849.8 5.1 multiply_convert_fusion.7
  870.9 8.5 multiply_reduce_fusion.6
  879.9 11.8 multiply_convert_fusion.2
  891.8 13.3 multiply_reduce_fusion.7
  912.0 11.8 fusion.80
  923.9 10.5 fusion.140
  934.5 14.2 all-gather.4
  948.6 90.9 %all-gather.38.cloned.1.call-done = bf16[8,16,273,64]{2,3,1,0:T(8,128)(2,1)} async-done(((bf16[2,16,273,64]{2,3,1,0:T(8,128)(2,1)}), bf16[8,16,273,64]{2,3,1,0:T(8,128)(2,1)}) %all-gather.38.cloned.1.call-update) | async-done | bytes 4472848 | tf_op jit(solution)/shard_map/all_gather | solution.py:53
  1041.9 32.4 while.33
  1047.8 4.9 convert_add_fusion.11
  1058.6 4.9 convert_add_fusion.11
  1069.4 4.9 convert_add_fusion.11
  1074.4 13.1 fusion.170
  1087.5 14.0 fusion.84
  1109.8 5.0 convolution_bitcast_fusion.5
  1116.0 4.8 convolution_bitcast_fusion.6
  1121.6 11.2 multiply_bitcast_fusion.1
  1138.6 9.1 fusion.16
  1152.4 6.2 multiply_bitcast_fusion
  1163.1 6.8 multiply_reduce_fusion.2
  1193.9 8.4 convolution_bitcast_fusion.3
  1203.6 7.9 convolution_bitcast_fusion.2
  1213.1 8.0 convolution_bitcast_fusion.4
  1222.7 13.6 convolution_bitcast_fusion
  1237.9 13.7 convolution_bitcast_fusion.1
  1253.2 7.8 fusion.104
  1265.7 40.8 %all-reduce.15 = (f32[1024]{0:T(1024)S(1)}, f32[1024]{0:T(1024)S(1)}, f32[1024]{0:T(1024)S(1)}, f32[1024]{0:T(1024)S(1)}) all-reduce(f32[1024]{0:T(1024)S(1)} %get-tuple-element.405, f32[1024]{0:T(1024)S(1)} %copy-done.107, f32[1024]{0:T(1024)S(1)} %copy-done.106, ...), channel_id=7, replica_groups=mesh['dp'=8,'ctx'=4] {'dp','ctx'}, use_global_device_ids=true, to_apply=%region_29.30.clone | all-reduce | flops 4096 | bytes 32768
  1313.4 77.2 %reduce-scatter.25.cloned.1.call-done = f32[32,1024]{1,0:T(8,128)} async-done(((f32[1024,1024]{1,0:T(8,128)}), f32[32,1024]{1,0:T(8,128)}) %reduce-scatter.25.cloned.1.call-update) | async-done | bytes 131088 | tf_op jit(solution)/shard_map/reduce_scatter | solution.py:488
  1390.5 149.4 %reduce-scatter.17.cloned.1.call-done = f32[32,1024]{1,0:T(8,128)} async-done(((f32[1024,1024]{1,0:T(8,128)}), f32[32,1024]{1,0:T(8,128)}) %reduce-scatter.17.cloned.1.call-update) | async-done | bytes 131088 | tf_op jit(solution)/shard_map/reduce_scatter | solution.py:522
  1539.9 139.8 %reduce-scatter.13.cloned.1.call-done = f32[32,512]{1,0:T(8,128)} async-done(((f32[1024,512]{1,0:T(8,128)}), f32[32,512]{1,0:T(8,128)}) %reduce-scatter.13.cloned.1.call-update) | async-done | bytes 65552 | tf_op jit(solution)/shard_map/reduce_scatter | solution.py:519
  1679.8 148.2 %reduce-scatter.15.cloned.1.call-done = f32[32,1024]{1,0:T(8,128)} async-done(((f32[1024,1024]{1,0:T(8,128)}), f32[32,1024]{1,0:T(8,128)}) %reduce-scatter.15.cloned.1.call-update) | async-done | bytes 131088 | tf_op jit(solution)/shard_map/reduce_scatter | solution.py:520
  1828.0 160.4 %reduce-scatter.23.cloned.1.call-done = f32[32,3072]{1,0:T(8,128)} async-done(((f32[1024,3072]{1,0:T(8,128)}), f32[32,3072]{1,0:T(8,128)}) %reduce-scatter.23.cloned.1.call-update) | async-done | bytes 393232 | tf_op jit(solution)/shard_map/reduce_scatter | solution.py:487
  1988.4 253.0 %reduce-scatter.29.cloned.1.call-done = f32[88,1024]{1,0:T(8,128)} async-done(((f32[2816,1024]{1,0:T(8,128)}), f32[88,1024]{1,0:T(8,128)}) %reduce-scatter.29.cloned.1.call-update) | async-done | bytes 360464 | tf_op jit(solution)/shard_map/reduce_scatter | solution.py:491
  2241.4 251.5 %reduce-scatter.21.cloned.1.call-done = f32[88,1024]{1,0:T(8,128)} async-done(((f32[2816,1024]{1,0:T(8,128)}), f32[88,1024]{1,0:T(8,128)}) %reduce-scatter.21.cloned.1.call-update) | async-done | bytes 360464 | tf_op jit(solution)/shard_map/reduce_scatter | solution.py:525
  2492.8 494.7 %reduce-scatter.27.cloned.1.call-done = f32[32,5632]{1,0:T(8,128)} async-done(((f32[1024,5632]{1,0:T(8,128)}), f32[32,5632]{1,0:T(8,128)}) %reduce-scatter.27.cloned.1.call-update) | async-done | bytes 720912 | tf_op jit(solution)/shard_map/reduce_scatter | solution.py:490
  2987.5 496.1 %reduce-scatter.19.cloned.1.call-done = f32[32,5632]{1,0:T(8,128)} async-done(((f32[1024,5632]{1,0:T(8,128)}), f32[32,5632]{1,0:T(8,128)}) %reduce-scatter.19.cloned.1.call-update) | async-done | bytes 720912 | tf_op jit(solution)/shard_map/reduce_scatter | solution.py:524
  (449 shorter events, 222.7 us)
Async XLA Ops:
  7.2 117.7 %all-gather.20.cloned.1.call-start = ((), (), s32[]{:S(2)}) async-start(), calls=%async_computation.11 | async-start | bytes 1081344 | tf_op jit(solution)/shard_map/all_gather | solution.py:442
  7.9 125.0 %all-gather.18.cloned.1.call-start = ((), (), s32[]{:S(2)}) async-start(), calls=%async_computation.10 | async-start | bytes 2162688 | tf_op jit(solution)/shard_map/all_gather | solution.py:443
  8.7 261.9 %all-gather.36.cloned.1.call-start = ((), (), s32[]{:S(2)}) async-start(), calls=%async_computation.28 | async-start | bytes 7864320 | tf_op jit(solution)/shard_map/all_gather | solution.py:29
  54.3 78.6 %copy-start.85 = (f32[1024]{0:T(1024)}, f32[1024]{0:T(1024)S(1)}, u32[]{:S(2)}) copy-start(f32[1024]{0:T(1024)S(1)} %convert_element_type.283) | copy-start | bytes 12292
  121.5 160.2 %copy-start.77 = (f32[273]{0:T(512)}, f32[273]{0:T(512)S(1)}, u32[]{:S(2)}) copy-start(f32[273]{0:T(512)S(1)} %pad.45.clone) | copy-start | bytes 3280
  121.6 17.3 copy-start.99
  124.7 14.1 copy-start.87
  124.7 14.1 copy-start.89
  124.8 48.6 %copy-start.75 = (f32[2,256]{1,0:T(2,128)}, f32[2,256]{1,0:T(2,128)S(1)}, u32[]{:S(2)}) copy-start(f32[2,256]{1,0:T(2,128)S(1)} %get-tuple-element.471) | copy-start | bytes 6148
  124.8 157.0 %copy-start.91 = (f32[2,256]{1,0:T(2,128)}, f32[2,256]{1,0:T(2,128)S(1)}, u32[]{:S(2)}) copy-start(f32[2,256]{1,0:T(2,128)S(1)} %get-tuple-element.470) | copy-start | bytes 6148
  124.8 14.1 copy-start.79
  124.8 14.1 copy-start.81
  124.8 14.1 copy-start.83
  127.3 74.2 %copy-start.39 = (bf16[2,256,256]{1,2,0:T(8,128)(2,1)}, bf16[2,256,256]{1,2,0:T(8,128)(2,1)S(1)}, u32[]{:S(2)}) copy-start(bf16[2,256,256]{1,2,0:T(8,128)(2,1)S(1)} %copy.283) | copy-start | bytes 786436
  135.8 3.1 collective-permute-start
  137.7 35.7 %copy-start.37 = (f32[2,256,16,16]{1,3,2,0:T(8,128)}, f32[2,256,16,16]{1,3,2,0:T(8,128)S(1)}, u32[]{:S(2)}) copy-start(f32[2,256,16,16]{1,3,2,0:T(8,128)S(1)} %broadcast_multiply_fusion.1) | copy-start | bytes 1572868
  138.9 14.7 copy-start.70
  153.6 174.4 %all-gather.22.cloned.1.call-start = ((), (), s32[]{:S(2)}) async-start(), calls=%async_computation.12 | async-start | bytes 2162688 | tf_op jit(solution)/shard_map/all_gather | solution.py:445
  154.2 266.7 %all-gather.24.cloned.1.call-start = ((), (), s32[]{:S(2)}) async-start(), calls=%async_computation.13 | async-start | bytes 11894784 | tf_op jit(solution)/shard_map/all_gather | solution.py:447
  154.8 334.5 %all-gather.26.cloned.1.call-start = ((), (), s32[]{:S(2)}) async-start(), calls=%async_computation.14 | async-start | bytes 5947392 | tf_op jit(solution)/shard_map/all_gather | solution.py:448
  155.4 405.4 %all-gather.28.cloned.1.call-start = ((), (), s32[]{:S(2)}) async-start(), calls=%async_computation.15 | async-start | bytes 6488064 | tf_op jit(solution)/shard_map/all_gather | solution.py:454
  156.1 462.9 %all-gather.30.cloned.1.call-start = ((), (), s32[]{:S(2)}) async-start(), calls=%async_computation.16 | async-start | bytes 2162688 | tf_op jit(solution)/shard_map/all_gather | solution.py:455
  156.9 555.2 %all-gather.32.cloned.1.call-start = ((), (), s32[]{:S(2)}) async-start(), calls=%async_computation.17 | async-start | bytes 11894784 | tf_op jit(solution)/shard_map/all_gather | solution.py:457
  157.6 622.9 %all-gather.34.cloned.1.call-start = ((), (), s32[]{:S(2)}) async-start(), calls=%async_computation.18 | async-start | bytes 5947392 | tf_op jit(solution)/shard_map/all_gather | solution.py:458
  158.2 881.3 %all-gather.38.cloned.1.call-start = ((), (), s32[]{:S(2)}) async-start(), calls=%async_computation.29 | async-start | bytes 7864320 | tf_op jit(solution)/shard_map/all_gather | solution.py:53
  158.7 42.8 %copy-start.58 = (f32[2,256,256]{1,2,0:T(8,128)}, f32[2,256,256]{1,2,0:T(8,128)S(1)}, u32[]{:S(2)}) copy-start(f32[2,256,256]{1,2,0:T(8,128)S(1)} %and_convert_fusion) | copy-start | bytes 1572868
  172.0 733.1 %copy-start.62 = (f32[1024]{0:T(1024)}, f32[1024]{0:T(1024)S(1)}, u32[]{:S(2)}) copy-start(f32[1024]{0:T(1024)S(1)} %convert_element_type.304) | copy-start | bytes 12292
  172.7 633.6 %copy-start.64 = (f32[1024]{0:T(1024)}, f32[1024]{0:T(1024)S(1)}, u32[]{:S(2)}) copy-start(f32[1024]{0:T(1024)S(1)} %convert_element_type.314) | copy-start | bytes 12292
  178.7 22.8 copy-start.41
  178.8 22.7 copy-start.18
  273.2 21.6 slice-start.9
  331.4 99.0 %copy-start.97 = (f32[2,256]{1,0:T(2,128)}, f32[2,256]{1,0:T(2,128)S(1)}, u32[]{:S(2)}) copy-start(f32[2,256]{1,0:T(2,128)S(1)} %get-tuple-element.478) | copy-start | bytes 6148
  331.4 573.8 %copy-start.5 = (f32[2,256,1024]{2,1,0:T(8,128)}, f32[2,256,1024]{2,1,0:T(8,128)S(1)}, u32[]{:S(2)}) copy-start(f32[2,256,1024]{2,1,0:T(8,128)S(1)} %get-tuple-element.479) | copy-start | bytes 6291460
  331.4 573.7 %copy-start.66 = (f32[2,256]{1,0:T(2,128)}, f32[2,256]{1,0:T(2,128)S(1)}, u32[]{:S(2)}) copy-start(f32[2,256]{1,0:T(2,128)S(1)} %fusion.145) | copy-start | bytes 6148
  568.7 16.2 collective-permute-start.1
  577.4 16.4 copy-start.21
  604.3 19.6 copy-start.109
  623.9 182.5 %copy-start.68 = (f32[2,256]{1,0:T(2,128)}, f32[2,256]{1,0:T(2,128)S(1)}, u32[]{:S(2)}) copy-start(f32[2,256]{1,0:T(2,128)S(1)} %fusion.147) | copy-start | bytes 6148
  712.1 68.4 %copy-start.54 = (bf16[2,1,256,1024]{3,2,1,0:T(8,128)(2,1)S(1)}, bf16[2,1,256,1024]{3,2,1,0:T(8,128)(2,1)}, u32[]{:S(2)}) copy-start(bf16[2,1,256,1024]{3,2,1,0:T(8,128)(2,1)} %param.41) | copy-start | bytes 3145732
  712.1 68.4 %copy-start.102 = (f32[2,256]{1,0:T(2,128)S(1)}, f32[2,256]{1,0:T(2,128)}, u32[]{:S(2)}) copy-start(f32[2,256]{1,0:T(2,128)} %compare_convert_fusion) | copy-start | bytes 6148
  813.8 20.3 slice-start.2
  813.8 20.3 slice-start.3
  848.5 16.6 collective-permute-start.2
  856.4 14.5 copy-start.46
  879.9 25.2 copy-start.12
  891.8 13.4 copy-start.98
  891.8 15.7 copy-start.74
  923.8 388.2 %reduce-scatter.31.cloned.1.call-start = ((), (), s32[]{:S(2)}) async-start(), calls=%async_computation.30 | async-start | bytes 540672
  934.4 107.4 %copy-start.111 = (bf16[4,2]{1,0:T(4,128)(2,1)S(1)}, bf16[4,2]{1,0:T(4,128)(2,1)}, u32[]{:S(2)}) copy-start(bf16[4,2]{1,0:T(4,128)(2,1)} %get-tuple-element.737) | copy-start | bytes 52
  1041.9 32.5 copy-start.38
  1041.9 32.5 copy-start.76
  1074.4 13.1 copy-start.34
  1109.7 280.8 %reduce-scatter.25.cloned.1.call-start = ((), (), s32[]{:S(2)}) async-start(), calls=%async_computation.25 | async-start | bytes 4325376 | tf_op jit(solution)/shard_map/reduce_scatter | solution.py:488
  1114.8 425.1 %reduce-scatter.17.cloned.1.call-start = ((), (), s32[]{:S(2)}) async-start(), calls=%async_computation.21 | async-start | bytes 4325376 | tf_op jit(solution)/shard_map/reduce_scatter | solution.py:522
  1120.9 558.9 %reduce-scatter.13.cloned.1.call-start = ((), (), s32[]{:S(2)}) async-start(), calls=%async_computation.19 | async-start | bytes 2162688 | tf_op jit(solution)/shard_map/reduce_scatter | solution.py:519
  1179.6 648.4 %reduce-scatter.15.cloned.1.call-start = ((), (), s32[]{:S(2)}) async-start(), calls=%async_computation.20 | async-start | bytes 4325376 | tf_op jit(solution)/shard_map/reduce_scatter | solution.py:520
  1181.9 5.8 collective-permute-start.3
  1192.4 796.0 %reduce-scatter.23.cloned.1.call-start = ((), (), s32[]{:S(2)}) async-start(), calls=%async_computation.24 | async-start | bytes 12976128 | tf_op jit(solution)/shard_map/reduce_scatter | solution.py:487
  1202.4 1039.0 %reduce-scatter.29.cloned.1.call-start = ((), (), s32[]{:S(2)}) async-start(), calls=%async_computation.27 | async-start | bytes 11894784 | tf_op jit(solution)/shard_map/reduce_scatter | solution.py:491
  1211.5 1281.3 %reduce-scatter.21.cloned.1.call-start = ((), (), s32[]{:S(2)}) async-start(), calls=%async_computation.23 | async-start | bytes 11894784 | tf_op jit(solution)/shard_map/reduce_scatter | solution.py:525
  1221.1 1766.4 %reduce-scatter.27.cloned.1.call-start = ((), (), s32[]{:S(2)}) async-start(), calls=%async_computation.26 | async-start | bytes 23789568 | tf_op jit(solution)/shard_map/reduce_scatter | solution.py:490
  1236.3 2247.3 %reduce-scatter.19.cloned.1.call-start = ((), (), s32[]{:S(2)}) async-start(), calls=%async_computation.22 | async-start | bytes 23789568 | tf_op jit(solution)/shard_map/reduce_scatter | solution.py:524
  1262.6 46.2 %copy-start.96 = (f32[2,256]{1,0:T(2,128)S(1)}, f32[2,256]{1,0:T(2,128)}, u32[]{:S(2)}) copy-start(f32[2,256]{1,0:T(2,128)} %copy-done.95) | copy-start | bytes 6148
  1262.6 46.2 %copy-start.11 = (f32[2,256,1024]{2,1,0:T(8,128)S(1)}, f32[2,256,1024]{2,1,0:T(8,128)}, u32[]{:S(2)}) copy-start(f32[2,256,1024]{2,1,0:T(8,128)} %copy-done.10) | copy-start | bytes 6291460
  (85 other events, 425.8 us)
Sparse Core Ops, SparseCore 0:
  11.0 56.4 all-gather.19
  70.4 55.5 all-gather.17
  153.8 116.7 all-gather.35
  273.3 54.7 all-gather.21
  330.8 90.1 all-gather.23
  423.6 65.6 all-gather.25
  492.2 68.5 all-gather.27
  563.7 55.2 all-gather.29
  621.9 90.1 all-gather.31
  714.7 65.6 all-gather.33
  924.0 115.5 all-gather.37
  1109.9 132.2 reduce-scatter.30
  1245.1 145.3 reduce-scatter.24
  1393.3 146.5 reduce-scatter.16
  1542.7 137.0 reduce-scatter.12
  1682.5 145.4 reduce-scatter.14
  1834.4 153.9 reduce-scatter.22
  1991.2 250.0 reduce-scatter.28
  2244.4 248.4 reduce-scatter.20
  2495.7 491.8 reduce-scatter.26
  2990.5 493.0 reduce-scatter.18
where the time goes:
time: 3500 us; the launch traced here: 3490 us
  waiting for transfers between devices  2740 us (78%)
  matrix products  347 us (10%)
  blocking collectives  191 us (5%)
  local copies, waits for them, and re-layouts  96.3 us (3%)
  other arithmetic  92.7 us (3%)
    reduce_scatter x1, waiting for transfers between devices, body(): lax.psum_scatter(local_one[6], ('dp', 'ctx'), scatter_dimension=0, tiled=...  496 us
    reduce_scatter x1, waiting for transfers between devices, body(): lax.psum_scatter(local_two[4], ('dp', 'ctx'), scatter_dimension=0, tiled=...  495 us
    reduce_scatter x1, waiting for transfers between devices, body(): lax.psum_scatter(local_two[5], ('dp', 'ctx'), scatter_dimension=0, tiled=...  253 us
    reduce_scatter x1, waiting for transfers between devices, body(): lax.psum_scatter(local_one[7], ('dp', 'ctx'), scatter_dimension=0, tiled=...  251 us
    reduce_scatter x1, waiting for transfers between devices, body(): lax.psum_scatter(local_two[1], ('dp', 'ctx'), scatter_dimension=0, tiled=...  160 us
    reduce_scatter x1, waiting for transfers between devices, body(): lax.psum_scatter(local_one[4], ('dp', 'ctx'), scatter_dimension=0, tiled=...  149 us
    reduce_scatter x1, waiting for transfers between devices, body(): lax.psum_scatter(local_one[2], ('dp', 'ctx'), scatter_dimension=0, tiled=...  148 us
    reduce_scatter x1, waiting for transfers between devices, body(): lax.psum_scatter(local_one[1], ('dp', 'ctx'), scatter_dimension=0, tiled=...  140 us
  transfers between devices with their start and end apart: 25, of which 22 were waited for; matrix products, arithmetic and copies ran while one was open for 9% of the time, Pallas kernels for 0%

commit v1 on v0

--- a/solution.py
+++ b/solution.py
@@ -4,6 +4,8 @@
 import jax
 import jax.numpy as jnp
 from jax import lax
+from jax.experimental import pallas as pl
+from jax.experimental.pallas import tpu as pltpu
 from jax.sharding import PartitionSpec as P
 
 HEADS = 16
@@ -17,57 +19,234 @@
 highest = lax.Precision.HIGHEST
 
 
+MESH = pl.DeviceIdType.MESH
+
+def gather_kernel(n_dp, n_ctx, chunks, lag, n_w, *refs):
+    ins, outs = refs[:n_w], refs[n_w:2 * n_w]
+    local_sem, send_sem, recv_sem = refs[2 * n_w:]
+    dp, ctx = lax.axis_index("dp"), lax.axis_index("ctx")
+    bits = [1 << i for i in range(n_dp.bit_length() - 1)]
+    low_bits, (bit_x, bit_y) = bits[:-2], bits[-2:]
+    barrier = pltpu.get_barrier_semaphore()
+    greeted = 0
+    for bit in bits:
+        pl.semaphore_signal(barrier, inc=1, device_id=(dp ^ bit, ctx), device_id_type=MESH)
+        greeted += 1
+    for hop in range(1, n_ctx):
+        pl.semaphore_signal(barrier, inc=1, device_id=(dp, lax.rem(ctx + hop, n_ctx)), device_id_type=MESH)
+        greeted += 1
+    pl.semaphore_wait(barrier, greeted)
+    sends = []
+
+    def piece(c, start, shards):
+        w, col, width = chunks[c]
+        return outs[w].at[pl.ds(start, shards), :, pl.ds(col, width)]
+
+    def send(c, slot, start, rows, target, src=None):
+        where = piece(c, start, rows)
+        copy = pltpu.make_async_remote_copy(
+            src_ref=where if src is None else src, dst_ref=where,
+            send_sem=send_sem.at[c, slot], recv_sem=recv_sem.at[c, slot],
+            device_id=target, device_id_type=MESH)
+        copy.start()
+        sends.append(copy)
+
+    def arrive(c, slot, start, rows):
+        where = piece(c, start, rows)
+        pltpu.make_async_remote_copy(
+            src_ref=where, dst_ref=where, send_sem=send_sem.at[c, slot], recv_sem=recv_sem.at[c, slot],
+            device_id=(dp ^ 1, ctx), device_id_type=MESH).wait_recv()
+
+    def stage_ctx(c):
+        w, col, width = chunks[c]
+        own = ins[w].at[:, :, pl.ds(col, width)]
+        start = dp * n_ctx + ctx
+        for hop in range(1, n_ctx):
+            send(c, hop - 1, start, 1, (dp, lax.rem(ctx + hop, n_ctx)), src=own)
+        pltpu.make_async_copy(own, piece(c, start, 1), local_sem.at[c]).start()
+
+    base = n_ctx - 1
+    SX, SY, SDX, SDY, SC = base, base + 1, base + 2, base + 3, base + 4
+
+    def stage_sides(c):
+        w, col, width = chunks[c]
+        for hop in range(1, n_ctx):
+            arrive(c, hop - 1, dp * n_ctx + lax.rem(ctx - hop + n_ctx, n_ctx), 1)
+        own = ins[w].at[:, :, pl.ds(col, width)]
+        pltpu.make_async_copy(own, piece(c, dp * n_ctx + ctx, 1), local_sem.at[c]).wait()
+        group = n_ctx
+        send(c, SX, dp * group, group, (dp ^ bit_x, ctx))
+        send(c, SY, dp * group, group, (dp ^ bit_y, ctx))
+
+    def stage_diag(c):
+        group = n_ctx
+        a0, an, b0, bn = 0, n_ctx // 2, n_ctx // 2, n_ctx - n_ctx // 2
+        arrive(c, SX, (dp ^ bit_x) * group, group)
+        send(c, SDY, (dp ^ bit_x) * group + a0, an, (dp ^ bit_y, ctx))
+        arrive(c, SY, (dp ^ bit_y) * group, group)
+        send(c, SDX, (dp ^ bit_y) * group + b0, bn, (dp ^ bit_x, ctx))
+
+    def low_slot(level, j):
+        return SC + 4 * ((1 << level) - 1) + j
+
+    def quads(base_dp, level):
+        out = []
+        for top in range(4):
+            for low in range(1 << level):
+                flip = (bit_x if top & 1 else 0) | (bit_y if top & 2 else 0)
+                for i in range(level):
+                    if low >> i & 1:
+                        flip |= low_bits[len(low_bits) - 1 - i]
+                out.append(base_dp ^ flip)
+        return out
+
+    def stage_low(c, level):
+        group = n_ctx
+        if level == 0:
+            a0, an, b0, bn = 0, n_ctx // 2, n_ctx // 2, n_ctx - n_ctx // 2
+            arrive(c, SDY, (dp ^ bit_x ^ bit_y) * group + a0, an)
+            arrive(c, SDX, (dp ^ bit_x ^ bit_y) * group + b0, bn)
+        else:
+            bit = low_bits[len(low_bits) - level]
+            for j, block in enumerate(quads(dp ^ bit, level - 1)):
+                arrive(c, low_slot(level - 1, j), block * group, group)
+        if level < len(low_bits):
+            bit = low_bits[len(low_bits) - 1 - level]
+            for j, block in enumerate(quads(dp, level)):
+                send(c, low_slot(level, j), block * group, group, (dp ^ bit, ctx))
+
+    stages = [stage_ctx, stage_sides, stage_diag] + [partial(stage_low, level=l) for l in range(len(low_bits) + 1)]
+    depth = len(stages)
+    for t in range(len(chunks) + (depth - 1) * lag):
+        for s in range(depth):
+            c = t - s * lag
+            if 0 <= c < len(chunks):
+                stages[s](c)
+    for copy in sends:
+        copy.wait_send()
+
+def gather_all(weights, n_dp, n_ctx, chunks, lag=1, cid=0):
+    n = len(weights)
+    places = n_dp * n_ctx
+    slots = n_ctx - 1 + 4 + 4 * (n_dp // 4 - 1)
+    full = pl.pallas_call(
+        partial(gather_kernel, n_dp, n_ctx, chunks, lag, n),
+        out_shape=[jax.ShapeDtypeStruct((places,) + w.shape, w.dtype) for w in weights],
+        in_specs=[pl.BlockSpec(memory_space=pltpu.HBM)] * n,
+        out_specs=[pl.BlockSpec(memory_space=pltpu.HBM)] * n,
+        scratch_shapes=[pltpu.SemaphoreType.DMA((len(chunks),)), pltpu.SemaphoreType.DMA((len(chunks), slots)), pltpu.SemaphoreType.DMA((len(chunks), slots))],
+        compiler_params=pltpu.CompilerParams(collective_id=cid, has_side_effects=True),
+        name="gather_weights")(*[w[None] for w in weights])
+    return [f.reshape(places * f.shape[1], f.shape[2]) for f in full]
+
+
 def passed_along(value, axis, steps):
     count = lax.axis_size(axis)
     leading, last = (max(0, -steps), min(count, count - steps))
     return lax.ppermute(value, axis, [(source, source + steps) for source in range(leading, last)])
 
 
-def carried_in(x, axis, join, neutral):
-    place = lax.axis_index(axis)
-    gathered = jax.tree.map(
-        lambda a, kind: lax.all_gather(a.astype(kind), axis),
-        x,
-        (jnp.bfloat16, jnp.bfloat16, jnp.bfloat16),
-    )
-    state = jax.tree.map(lambda a, e: jnp.zeros_like(a) + jnp.asarray(e, a.dtype), x, neutral)
-
-    def carried_one(hop, state):
-        return join(
-            state,
-            jax.tree.map(
-                lambda a, own: lax.dynamic_index_in_dim(a, hop, 0, False).astype(own.dtype),
-                gathered,
-                x,
-            ),
-        )
-
-    return lax.fori_loop(0, place, carried_one, state)
-
-
-def entering(x, axis, join, neutral):
+def carried_in(x, flags, axis, join):
     count = lax.axis_size(axis)
-    place = lax.axis_index(axis)
-    ahead = count - 1 - place
-    gathered = jax.tree.map(
-        lambda a, kind: lax.all_gather(a.astype(kind), axis),
-        x,
-        jax.tree.map(lambda a: jnp.bfloat16 if a.dtype == jnp.float32 else a.dtype, x),
-    )
-    state = jax.tree.map(lambda a, e: jnp.zeros_like(a) + jnp.asarray(e, a.dtype), x, neutral)
-
-    def entering_one(hop, state):
-        source = count - 1 - hop
-        return join(
-            state,
-            jax.tree.map(
-                lambda a, own: lax.dynamic_index_in_dim(a, source, 0, False).astype(own.dtype),
-                gathered,
-                x,
-            ),
-        )
-
-    return lax.fori_loop(0, ahead, entering_one, state)
+    low = jax.tree.map(lambda a: a.astype(jnp.bfloat16), x)
+    state = jax.tree.map(jnp.zeros_like, x) + (flags[0] * 0.0,)
+    for hop in range(count - 1, 0, -1):
+        pairs = [(source, source + hop) for source in range(count - hop)]
+        came = jax.tree.map(lambda a, own: lax.ppermute(a, axis, pairs).astype(own.dtype), low, x)
+        state = join(state, came + (flags[hop],))
+    return state
+
+
+def entering(x, flags, axis, join):
+    count = lax.axis_size(axis)
+    low = jax.tree.map(lambda a: a.astype(jnp.bfloat16), x)
+    state = jax.tree.map(jnp.zeros_like, x) + (flags[0] * 0.0,)
+    for hop in range(count - 1, 0, -1):
+        pairs = [(source + hop, source) for source in range(count - hop)]
+        came = jax.tree.map(lambda a, own: lax.ppermute(a, axis, pairs).astype(own.dtype), low, x)
+        state = join(state, came + (flags[hop],))
+    return state
+
+
+def chunks_of(shards):
+    out = []
+    for place, shard in enumerate(shards):
+        rows, columns = shard.shape
+        unit = max(128, 1408 * 32 // rows // 128 * 128)
+        width = -(-(columns // 128) // -(-columns // unit)) * 128
+        for first in range(0, columns, width):
+            out.append((place, first, min(width, columns - first)))
+    return out
+
+
+def bit_reversed(value, bits):
+    return sum(1 << (bits - 1 - i) for i in range(bits) if value >> i & 1)
+
+
+def swapped(value, bit):
+    count = lax.axis_size("dp")
+    return lax.ppermute(value, "dp", [(source, source ^ bit) for source in range(count)])
+
+
+def halving_order():
+    count = lax.axis_size("dp")
+    bits = count.bit_length() - 1
+    return sorted(range(count), key=lambda place: bit_reversed(place, bits))
+
+
+def by_place(operand):
+    tokens, rows = operand.shape
+    count = lax.axis_size("dp")
+    blocks = operand.reshape(tokens, count, rows // count)
+    me = lax.axis_index("dp")
+    return jnp.stack(
+        [lax.dynamic_index_in_dim(blocks, me ^ place, 1, False) for place in halving_order()],
+        axis=1,
+    )
+
+
+def token_dot(operand, gradient):
+    return jnp.einsum("tpr,te->pre", operand, gradient, preferred_element_type=jnp.float32)
+
+
+def summed_to_owner(operand, gradient, extra=None):
+    low = jnp.bfloat16
+    count, ctx_count = lax.axis_size("dp"), lax.axis_size("ctx")
+    bits = count.bit_length() - 1
+    operand = operand.reshape(-1, operand.shape[-1])
+    gradient = gradient.reshape(-1, gradient.shape[-1])
+    placed = by_place(operand)
+    half = count // 2
+    sent = token_dot(placed[:, half:], gradient)
+    kept = token_dot(placed[:, :half], gradient)
+    if extra is not None:
+        extra_placed = by_place(extra.T).transpose(1, 2, 0)
+        sent = jnp.concatenate([sent, extra_placed[half:]], axis=-1)
+        kept = jnp.concatenate([kept, extra_placed[:half]], axis=-1)
+    kept = (kept + swapped(sent.astype(low), 1).astype(jnp.float32)).astype(low)
+    for level in range(1, bits - 2):
+        half //= 2
+        came = swapped(kept[half:], 1 << level)
+        kept = (kept[:half].astype(jnp.float32) + came.astype(jnp.float32)).astype(low)
+    own, over_y, over_x, across = kept[0], kept[1], kept[2], kept[3]
+    bit_x, bit_y = count // 4, count // 2
+    rows, columns = own.shape
+    first = rows // 32 * 16
+    by_y = swapped(across[:first], bit_y)
+    by_x = swapped(across[first:], bit_x)
+    over_x = jnp.concatenate([over_x[:first] + by_y, over_x[first:]], axis=0)
+    over_y = jnp.concatenate([over_y[:first], over_y[first:] + by_x], axis=0)
+    came_x = swapped(over_x, bit_x)
+    came_y = swapped(over_y, bit_y)
+    total = own.astype(jnp.float32) + came_x.astype(jnp.float32) + came_y.astype(jnp.float32)
+    total = total.reshape(ctx_count, rows // ctx_count, columns)
+    me = lax.axis_index("ctx")
+    result = lax.dynamic_index_in_dim(total, me, 0, False)
+    for hop in range(1, ctx_count):
+        block = lax.dynamic_index_in_dim(total, lax.rem(me + hop, ctx_count), 0, False).astype(low)
+        came = lax.ppermute(block, "ctx", [(i, (i + hop) % ctx_count) for i in range(ctx_count)])
+        result = result + came.astype(jnp.float32)
+    return result
 
 
 def normed(stream, scale_gain):
@@ -123,7 +302,16 @@
     own_pos = first_pos + jnp.arange(tok_count, dtype=jnp.int32)
     own_seg = segment_of(own_pos)
     before_seg = segment_of(own_pos - 1)
-    starts = (own_seg != before_seg) | (own_pos == 0)[None, :]
+
+    def flags(direction):
+        out = []
+        for hop in range(lax.axis_size("ctx")):
+            first = first_pos + direction * hop * tok_count
+            held = (seq_ends >= first) & (seq_ends < first + tok_count) & (seq_ends < total_len)
+            out.append(jnp.any(held | (first == 0), axis=1).astype(jnp.float32))
+        return out
+
+    total_len = tok_count * lax.axis_size("ctx")
     tap_masks = []
     for offset in range(CONV):
         source = own_pos - offset
@@ -141,7 +329,8 @@
     )
     return {
         "valid": (own_pos[None, :] < seq_ends[:, -1:]).astype(jnp.float32),
-        "flag": jnp.max(starts.astype(jnp.float32), axis=1),
+        "flags_before": flags(-1),
+        "flags_after": flags(1),
         "carried": ((own_seg == before_seg[:, :1]) & (first_pos > 0)).astype(jnp.float32),
         "last": (own_seg == own_seg[:, -1:]).astype(jnp.float32),
         "causal": causal,
@@ -212,16 +401,7 @@
     state_out, state_back = jax.vjp(
         partial(end_state, last_mask=layout_info["last"]), key_rows, head_values
     )
-    incoming = carried_in(
-        (state_out[0], state_out[1], layout_info["flag"]),
-        "ctx",
-        chain_states,
-        (
-            jnp.zeros_like(state_out[0]),
-            jnp.zeros_like(state_out[1]),
-            jnp.zeros_like(layout_info["flag"]),
-        ),
-    )
+    incoming = carried_in(state_out, layout_info["flags_before"], "ctx", chain_states)
     attended, attend_back = jax.vjp(
         partial(attend_linear, causal=layout_info["causal"], carried=layout_info["carried"]),
         query_rows,
@@ -238,24 +418,15 @@
     )
 
 
-def linear_backward(grad_stream, residuals, weights, layout_info):
+def linear_backward(grad_stream, residuals, weights, layout_info, other_gains):
     norm_back, normed_low, conv_back, state_back, attend_back, attended_low = residuals
     qk_weight, value_weight, out_weight = (weights[1], weights[2], weights[4])
     micro_count, tok_count, model_width = grad_stream.shape
     grad_branch = grad_stream.astype(jnp.bfloat16)
-    grad_out = weight_grad(attended_low, grad_branch)
+    grad_out = summed_to_owner(attended_low, grad_branch)
     grad_attended = matmul_back(grad_branch, out_weight)
     grad_query, grad_key, grad_value, grad_state, grad_totals = attend_back(grad_attended)
-    later_grads = entering(
-        (grad_state, grad_totals, layout_info["flag"]),
-        "ctx",
-        chain_states,
-        (
-            jnp.zeros_like(grad_state),
-            jnp.zeros_like(grad_totals),
-            jnp.zeros_like(layout_info["flag"]),
-        ),
-    )
+    later_grads = entering((grad_state, grad_totals), layout_info["flags_after"], "ctx", chain_states)
     key_more, value_more = state_back((later_grads[0], later_grads[1]))
     grad_key = grad_key + key_more
     grad_value = grad_value + value_more
@@ -272,14 +443,13 @@
     returned = passed_along(grad_rim, "ctx", -1)
     grad_pre = grad_pre.at[:, tok_count - CONV + 1 :, :].add(returned)
     grad_pre_low = grad_pre.astype(jnp.bfloat16)
-    grad_qk_weight = weight_grad(normed_low, grad_qk)
-    grad_value_weight = weight_grad(normed_low, grad_pre_low)
     grad_normed = matmul_back(grad_qk, qk_weight) + matmul_back(grad_pre_low, value_weight)
     grad_input, grad_gain = norm_back(grad_normed)
-    return (
-        grad_stream + grad_input,
-        (grad_gain, grad_qk_weight, grad_value_weight, grad_taps, grad_out),
-    )
+    small = jnp.concatenate(
+        [other_gains, grad_gain[:, None], grad_taps, jnp.zeros((model_width, 121), jnp.float32)], axis=1
+    )
+    grad_both = summed_to_owner(normed_low, jnp.concatenate([grad_qk, grad_pre_low], axis=-1), small)
+    return (grad_stream + grad_input, grad_both, grad_out)
 
 
 def window_scores(heads_query, key_ext, window_mask, head_size):
@@ -332,7 +502,7 @@
     micro_count, tok_count, model_width = grad_stream.shape
     head_size = model_width // HEADS
     grad_branch = grad_stream.astype(jnp.bfloat16)
-    grad_out = weight_grad(attended, grad_branch)
+    grad_out = summed_to_owner(attended, grad_branch)
     grad_attended = (
         matmul_back(grad_branch, out_weight)
         .astype(jnp.bfloat16)
@@ -379,7 +549,7 @@
     grad_qkv = jnp.concatenate(
         [grad_query.reshape(micro_count, tok_count, model_width), own_grads], axis=-1
     ).astype(jnp.bfloat16)
-    grad_qkv_weight = weight_grad(normed_low, grad_qkv)
+    grad_qkv_weight = summed_to_owner(normed_low, grad_qkv)
     grad_input, grad_gain = norm_back(matmul_back(grad_qkv, qkv_weight))
     return (grad_stream + grad_input, (grad_gain, grad_qkv_weight, grad_out))
 
@@ -402,7 +572,7 @@
     gate_up, down_weight = (weights[1], weights[2])
     hidden_width = down_weight.shape[0]
     grad_branch = grad_stream.astype(jnp.bfloat16)
-    grad_down = weight_grad(hidden, grad_branch)
+    grad_down = summed_to_owner(hidden, grad_branch)
     grad_hidden = matmul_back(grad_branch, down_weight)
     gate_part = projected[..., :hidden_width]
     up_part = projected[..., hidden_width:]
@@ -410,7 +580,7 @@
     grad_gate = grad_hidden * up_part * sigmoid_gate * (1.0 + gate_part * (1.0 - sigmoid_gate))
     grad_up = grad_hidden * gate_part * sigmoid_gate
     grad_projected = jnp.concatenate([grad_gate, grad_up], axis=-1).astype(jnp.bfloat16)
-    grad_gate_up = weight_grad(normed_low, grad_projected)
+    grad_gate_up = summed_to_owner(normed_low, grad_projected)
     grad_input, grad_gain = norm_back(matmul_back(grad_projected, gate_up))
     return (grad_stream + grad_input, (grad_gain, grad_gate_up, grad_down))
 
@@ -437,111 +607,70 @@
     tok_count = tokens_in.shape[2]
     layout_info = layout(seq_lengths, tok_count)
     stream = tokens_in[:, 0].astype(jnp.float32)
-    layer_one = (
-        lax.all_gather(norm_linear, ("dp", "ctx"), axis=0, tiled=True),
-        lax.all_gather(proj_qk, ("dp", "ctx"), axis=0, tiled=True),
-        lax.all_gather(proj_values, ("dp", "ctx"), axis=0, tiled=True),
-        lax.all_gather(conv_taps, ("dp", "ctx"), axis=0, tiled=True),
-        lax.all_gather(out_linear, ("dp", "ctx"), axis=0, tiled=True),
-        lax.all_gather(norm_ffn_one, ("dp", "ctx"), axis=0, tiled=True),
-        lax.all_gather(gate_up_one, ("dp", "ctx"), axis=0, tiled=True),
-        lax.all_gather(down_one, ("dp", "ctx"), axis=0, tiled=True),
-    )
+    small = jnp.concatenate(
+        [
+            norm_linear[:, None],
+            norm_ffn_one[:, None],
+            norm_window[:, None],
+            norm_ffn_two[:, None],
+            conv_taps,
+            jnp.zeros((conv_taps.shape[0], 121), jnp.bfloat16),
+        ],
+        axis=1,
+    )
+    shards = [
+        small,
+        proj_qk,
+        proj_values,
+        out_linear,
+        gate_up_one,
+        down_one,
+        proj_qkv,
+        out_window,
+        gate_up_two,
+        down_two,
+    ]
+    small, w_qk, w_values, w_out_linear, w_gu_one, w_dn_one, w_qkv, w_out_window, w_gu_two, w_dn_two = (
+        gather_all(shards, lax.axis_size("dp"), lax.axis_size("ctx"), chunks_of(shards))
+    )
+    layer_one = (small[:, 0], w_qk, w_values, small[:, 4:7], w_out_linear, small[:, 1], w_gu_one, w_dn_one)
+    layer_two = (small[:, 2], w_qkv, w_out_window, small[:, 3], w_gu_two, w_dn_two)
     middle, saved_linear = linear_forward(stream, layer_one[:5], layout_info)
     first_out, saved_ffn_one = ffn_forward(middle, layer_one[5:])
-    layer_two = (
-        lax.all_gather(norm_window, ("dp", "ctx"), axis=0, tiled=True),
-        lax.all_gather(proj_qkv, ("dp", "ctx"), axis=0, tiled=True),
-        lax.all_gather(out_window, ("dp", "ctx"), axis=0, tiled=True),
-        lax.all_gather(norm_ffn_two, ("dp", "ctx"), axis=0, tiled=True),
-        lax.all_gather(gate_up_two, ("dp", "ctx"), axis=0, tiled=True),
-        lax.all_gather(down_two, ("dp", "ctx"), axis=0, tiled=True),
-    )
     second_mid, saved_window = window_forward(first_out, layer_two[:3], layout_info)
     closing, saved_ffn_two = ffn_forward(second_mid, layer_two[3:])
     valid_rows = layout_info["valid"][:, :, None]
     output = (closing * valid_rows).astype(jnp.bfloat16)[:, None]
     grad_stream = cotangent[:, 0].astype(jnp.float32) * valid_rows
-    again_two = (
-        lax.all_gather(norm_window, ("dp", "ctx"), axis=0, tiled=True),
-        lax.all_gather(proj_qkv, ("dp", "ctx"), axis=0, tiled=True),
-        lax.all_gather(out_window, ("dp", "ctx"), axis=0, tiled=True),
-        lax.all_gather(norm_ffn_two, ("dp", "ctx"), axis=0, tiled=True),
-        lax.all_gather(gate_up_two, ("dp", "ctx"), axis=0, tiled=True),
-        lax.all_gather(down_two, ("dp", "ctx"), axis=0, tiled=True),
-    )
-    grad_stream, grads_ffn_two = ffn_backward(grad_stream, saved_ffn_two, again_two[3:])
+    grad_stream, grads_ffn_two = ffn_backward(grad_stream, saved_ffn_two, layer_two[3:])
     grad_stream, grads_window = window_backward(
-        grad_stream, saved_window, again_two[:3], layout_info
-    )
-    local_two = (
-        grads_window[0],
-        grads_window[1],
-        grads_window[2],
-        grads_ffn_two[0],
-        grads_ffn_two[1],
-        grads_ffn_two[2],
-    )
-    reduced_two = (
-        lax.psum_scatter(local_two[0], ("dp", "ctx"), scatter_dimension=0, tiled=True),
-        lax.psum_scatter(local_two[1], ("dp", "ctx"), scatter_dimension=0, tiled=True),
-        lax.psum_scatter(local_two[2], ("dp", "ctx"), scatter_dimension=0, tiled=True),
-        lax.psum_scatter(local_two[3], ("dp", "ctx"), scatter_dimension=0, tiled=True),
-        lax.psum_scatter(local_two[4], ("dp", "ctx"), scatter_dimension=0, tiled=True),
-        lax.psum_scatter(local_two[5], ("dp", "ctx"), scatter_dimension=0, tiled=True),
-    )
-    again_one = (
-        lax.all_gather(norm_linear, ("dp", "ctx"), axis=0, tiled=True),
-        lax.all_gather(proj_qk, ("dp", "ctx"), axis=0, tiled=True),
-        lax.all_gather(proj_values, ("dp", "ctx"), axis=0, tiled=True),
-        lax.all_gather(conv_taps, ("dp", "ctx"), axis=0, tiled=True),
-        lax.all_gather(out_linear, ("dp", "ctx"), axis=0, tiled=True),
-        lax.all_gather(norm_ffn_one, ("dp", "ctx"), axis=0, tiled=True),
-        lax.all_gather(gate_up_one, ("dp", "ctx"), axis=0, tiled=True),
-        lax.all_gather(down_one, ("dp", "ctx"), axis=0, tiled=True),
-    )
-    grad_stream, grads_ffn_one = ffn_backward(grad_stream, saved_ffn_one, again_one[5:])
-    grad_stream, grads_linear = linear_backward(
-        grad_stream, saved_linear, again_one[:5], layout_info
-    )
-    local_one = (
-        grads_linear[0],
-        grads_linear[1],
-        grads_linear[2],
-        grads_linear[3],
-        grads_linear[4],
-        grads_ffn_one[0],
-        grads_ffn_one[1],
-        grads_ffn_one[2],
-    )
-    reduced_one = (
-        lax.psum_scatter(local_one[0], ("dp", "ctx"), scatter_dimension=0, tiled=True),
-        lax.psum_scatter(local_one[1], ("dp", "ctx"), scatter_dimension=0, tiled=True),
-        lax.psum_scatter(local_one[2], ("dp", "ctx"), scatter_dimension=0, tiled=True),
-        lax.psum_scatter(local_one[3], ("dp", "ctx"), scatter_dimension=0, tiled=True),
-        lax.psum_scatter(local_one[4], ("dp", "ctx"), scatter_dimension=0, tiled=True),
-        lax.psum_scatter(local_one[5], ("dp", "ctx"), scatter_dimension=0, tiled=True),
-        lax.psum_scatter(local_one[6], ("dp", "ctx"), scatter_dimension=0, tiled=True),
-        lax.psum_scatter(local_one[7], ("dp", "ctx"), scatter_dimension=0, tiled=True),
-    )
+        grad_stream, saved_window, layer_two[:3], layout_info
+    )
+    grad_stream, grads_ffn_one = ffn_backward(grad_stream, saved_ffn_one, layer_one[5:])
+    other_gains = jnp.stack([grads_ffn_one[0], grads_window[0], grads_ffn_two[0]], axis=1)
+    grad_stream, grad_both, grad_out = linear_backward(
+        grad_stream, saved_linear, layer_one[:5], layout_info, other_gains
+    )
+    qk_width, value_width = (proj_qk.shape[1], proj_values.shape[1])
+    grad_small = grad_both[:, qk_width + value_width :]
     tokens_grad = grad_stream.astype(jnp.bfloat16)[:, None]
     return (
         output,
         tokens_grad,
-        reduced_one[0],
-        reduced_one[1],
-        reduced_one[2],
-        reduced_one[3],
-        reduced_one[4],
-        reduced_one[5],
-        reduced_one[6],
-        reduced_one[7],
-        reduced_two[0],
-        reduced_two[1],
-        reduced_two[2],
-        reduced_two[3],
-        reduced_two[4],
-        reduced_two[5],
+        grad_small[:, 3],
+        grad_both[:, :qk_width],
+        grad_both[:, qk_width : qk_width + value_width],
+        grad_small[:, 4:7],
+        grad_out,
+        grad_small[:, 0],
+        grads_ffn_one[1],
+        grads_ffn_one[2],
+        grad_small[:, 1],
+        grads_window[1],
+        grads_window[2],
+        grad_small[:, 2],
+        grads_ffn_two[1],
+        grads_ffn_two[2],
     )
 
 

time: 3500 us -> 1510 us (0.43)
  waiting for transfers between devices: 2740 us -> 444 us
  Pallas kernels: 0 us -> 217 us
  blocking collectives: 191 us -> 0 us
  local copies, waits for them, and re-layouts: 96.3 us -> 239 us
  starting transfers between devices: 9.55 us -> 146 us
    reduce_scatter x9 -> x0, waiting for transfers between devices: 2170 us -> none  [the longest x1 496 us: body(): lax.psum_scatter(local_one[6], ('dp', 'ctx'), scatter_dimension=0, tiled=...]
    all_gather x11 -> x0, waiting for transfers between devices: 546 us -> none  [the longest x1 90.9 us: entering(): lax.all_gather(a.astype(kind), axis)]
    ppermute x0 -> x76, waiting for transfers between devices: none -> 444 us  [the longest x24 215 us: summed_to_owner(): lax.ppermute(block, 'ctx', [(i, (i + hop) % ctx_count) for i in range(ctx...]
    pallas_call x0 -> x1, Pallas kernels: none -> 217 us  [gather_all(): pl.pallas_call(partial(gather_kernel, n_dp, n_ctx, chunks, lag, n), out_s...]
    ppermute x0 -> x76, starting transfers between devices: none -> 103 us  [the longest x24 42.6 us: summed_to_owner(): lax.ppermute(block, 'ctx', [(i, (i + hop) % ctx_count) for i in range(ctx...]
    all_gather x3 -> x0, blocking collectives: 97.4 us -> none  [the longest x1 66.3 us: body(): lax.all_gather(conv_taps, ('dp', 'ctx'), axis=0, tiled=True)]
    unnamed x3 -> x0, blocking collectives: 94 us -> none
    unnamed x265 -> x539, local copies, waits for them, and re-layouts: 34.6 us -> 111 us
  transfers between devices with their start and end apart: 25 -> 80, of which waited for: 22 -> 33; matrix products, arithmetic and copies ran while one was open for 9% -> 33% of each run, Pallas kernels for 0% -> 0%
where the time goes in v1:
time: 1510 us; the launch traced here: 1490 us
  waiting for transfers between devices  444 us (29%)
  matrix products  329 us (22%)
  local copies, waits for them, and re-layouts  239 us (16%)
  Pallas kernels  217 us (14%)
  starting transfers between devices  146 us (10%)
  other arithmetic  116 us (8%)
    pallas_call x1, Pallas kernels, gather_all(): pl.pallas_call(partial(gather_kernel, n_dp, n_ctx, chunks, lag, n), out_s...  217 us
    ppermute x24, waiting for transfers between devices, summed_to_owner(): lax.ppermute(block, 'ctx', [(i, (i + hop) % ctx_count) for i in range(ctx...  215 us
    ppermute x40, waiting for transfers between devices, swapped(): lax.ppermute(value, 'dp', [(source, source ^ bit) for source in range(cou...  143 us
    unnamed x539, local copies, waits for them, and re-layouts  111 us
    ppermute x6, waiting for transfers between devices, carried_in(): lax.ppermute(a, axis, pairs).astype(own.dtype)  85.9 us
    dot_general x9, matrix products, matmul_back(): jnp.einsum('mte,de->mtd', operand, weight, preferred_element_type=jnp.flo...  67.9 us
    dot_general x16, matrix products, token_dot(): jnp.einsum('tpr,te->pre', operand, gradient, preferred_element_type=jnp.f...  59.4 us
    ppermute x4, starting transfers between devices, passed_along(): lax.ppermute(value, axis, [(source, source + steps) for source in range(l...  42.6 us
  transfers between devices with their start and end apart: 80, of which 33 were waited for; matrix products, arithmetic and copies ran while one was open for 33% of the time, Pallas kernels for 0%

profile of v1, /device:TPU:0, one launch (start us, length us, event | category | flops | bytes accessed | tf_op | source)
XLA Modules:
  0.0 1494.7 jit_solution(2326887001103310379)
XLA Ops:
  5.3 216.7 %gather_weights.1 = (bf16[32,32,128]{2,1,0:T(8,128)(2,1)}, bf16[32,32,512]{2,1,0:T(8,128)(2,1)}, bf16[32,32,1024]{2,1,0:T(8,128)(2,1)}, bf16[32,32,1024]{2,1,0:T...) custom-call(bf16[1,32,128]{2,1,0:T(8,128)(2,1)} %bitcast.760, ...), custom_call_target="tpu_custom_call" | custom-call | tf_op jit(solution)/shard_map/gather_weights/pallas_call | solution.py:132
  232.5 7.5 collective-permute-start.6
  255.6 6.0 multiply_multiply_fusion
  265.8 4.5 fusion.47
  275.0 10.9 convolution_convert_fusion.7
  303.8 85.9 %collective-permute-done.4 = bf16[2,16,273]{2,1,0:T(8,128)(2,1)S(1)} collective-permute-done((bf16[2,16,273]{2,1,0:T(8,128)(2,1)}, bf16[2,16,273]{2,1,0:T(8,128)(2,1)S(1)}, u32[]{:S(2)}, u32[]{:S(2)}) %collective-permute-start.4) | collective-permute-done | bytes 17504 | tf_op jit(solution)/shard_map/ppermute | solution.py:155
  390.5 8.4 fusion.267
  399.6 12.8 fusion.312
  412.5 10.4 fusion.36
  426.0 6.2 fusion.321
  439.5 6.9 reshape.941
  446.4 7.5 multiply_reduce_fusion.15
  460.1 37.9 %collective-permute-start.7 = (bf16[2,63,2048]{2,1,0:T(8,128)(2,1)}, bf16[2,63,2048]{2,1,0:T(8,128)(2,1)}, u32[]{:S(2)}, u32[]{:S(2)}) collective-permute-start(bf16[2,63,2048]{2,1,0:T(8,128)(2,1)} %slice.761), channel_id=1, source_target_pairs={{0,1},{1,2},{2,3},{4,5},{5,6},{6,7},{8,9},{9,10},{10,11},{12,13},{... | collective-permute-start | bytes 1548296 | tf_op jit(solution)/shard_map/ppermute | solution.py:146
  498.0 7.8 constant_dynamic-slice_fusion.39
  583.0 14.4 fusion.322
  597.5 10.4 multiply_convert_fusion.4
  607.9 11.8 multiply_reduce_fusion.8
  626.0 8.3 fusion.49
  634.3 7.0 multiply_reduce_fusion
  661.0 6.8 reshape.943
  703.8 7.8 constant_dynamic-slice_fusion.7
  752.3 8.4 convolution_convert_fusion
  765.5 8.8 multiply_reduce_fusion.9
  776.2 9.6 multiply_convert_fusion.2
  785.9 12.8 multiply_reduce_fusion.10
  805.8 8.1 fusion.269
  817.9 11.6 convolution_convert_fusion.8
  829.5 14.1 fusion.46
  843.7 8.7 fusion.2
  852.4 16.2 %multiply_bitcast_fusion.1 = f32[2,256,16,273]{1,3,2,0:T(8,128)} fusion(f32[2,256]{1,0:T(2,128)S(1)} %copy-done.206, f32[2,16,273]{2,1,0:T(8,128)S(1)} %copy-done.160, f32[2,16,256]{2,1,0:T(8,128)S(1)} %get-tuple-element.312, bf16[2,16,273,64]{2,3,1,0:T(8,128)(2,1)} %collective-permute-done.3, bf16[2,16,273,64]{2,3,1,0:T(8,128)(2,1)} %collective-permute-done.2, ...), kind=kOutput, calls=%fused_computation.13 | convolution fusion | flops 1729273856 | bytes 14499992 | tf_op jit(solution)/shard_map/transpose(jvp(mihr,mhre->mihe))/dot_general | solution.py:370
  868.6 4.7 slice_multiply_fusion.1
  873.4 8.4 convolution_convert_fusion.1
  881.8 7.0 multiply_reduce_fusion.4
  907.1 4.5 collective-permute-start.63
  918.9 5.3 collective-permute-start.62
  930.0 129.2 %collective-permute-done.62 = bf16[32,1024]{1,0:T(8,128)(2,1)} collective-permute-done((bf16[32,1024]{1,0:T(8,128)(2,1)}, bf16[32,1024]{1,0:T(8,128)(2,1)}, u32[]{:S(2)}, u32[]{:S(2)}) %collective-permute-start.62) | collective-permute-done | bytes 65568 | tf_op jit(solution)/shard_map/ppermute | solution.py:247
  1060.8 4.8 collective-permute-done.61
  1072.8 15.4 %convolution_add_fusion = f32[2,16,64,256]{3,2,1,0:T(8,128)} fusion(f32[2,16,64,256]{3,2,1,0:T(8,128)S(1)} %copy-done.217, f32[2,256,16,256]{1,3,2,0:T(8,128)} %bitcast.637, f32[2,256,16,16]{1,3,2,0:T(8,128)S(1)} %copy-done.65, f32[273]{0:T(512)S(1)} %copy-done.195, f32[2,256]{1,0:T(2,128)S(1)} %copy-done.170, ...), kind=kOutput, calls=%fused_computation.153 | convolution fusion | flops 1729273856 | bytes 16464988 | tf_op jit(solution)/shard_map/transpose(jvp(mthr,mthe->mhre))/dot_general | solution.py:356
  1099.1 7.9 multiply_bitcast_fusion
  1107.0 4.4 slice_multiply_fusion
  1111.4 6.7 multiply_reduce_fusion.2
  1127.0 4.6 fusion.32
  1136.0 5.5 fusion.43
  1160.7 4.9 collective-permute-done.28
  1178.1 4.8 collective-permute-done.73
  1191.3 14.9 collective-permute-done.17
  1217.5 13.7 collective-permute-done.43
  1238.3 5.6 collective-permute-done.18
  1258.5 8.0 collective-permute-done.23
  1266.5 10.3 collective-permute-start.78
  1276.8 8.0 collective-permute-done.22
  1285.8 11.3 collective-permute-done.21
  1299.8 8.1 collective-permute-done.77
  1321.3 5.7 collective-permute-done.52
  1327.4 5.4 collective-permute-done.50
  1344.9 12.6 collective-permute-done.54
  1358.5 5.5 add_convert_fusion
  1366.4 7.5 add_convert_fusion.1
  1376.3 7.1 collective-permute-done.65
  1387.7 11.1 collective-permute-done.33
  1403.1 26.6 %collective-permute-done.68 = bf16[128,5632]{1,0:T(8,128)(2,1)S(1)} collective-permute-done((bf16[128,5632]{1,0:T(8,128)(2,1)S(1)}, bf16[128,5632]{1,0:T(8,128)(2,1)S(1)}, u32[]{:S(2)}, u32[]{:S(2)}) %collective-permute-start.68) | collective-permute-done | bytes 1441824 | tf_op jit(solution)/shard_map/ppermute | solution.py:188
  1435.3 24.2 %collective-permute-done.36 = bf16[128,5632]{1,0:T(8,128)(2,1)S(1)} collective-permute-done((bf16[128,5632]{1,0:T(8,128)(2,1)S(1)}, bf16[128,5632]{1,0:T(8,128)(2,1)S(1)}, u32[]{:S(2)}, u32[]{:S(2)}) %collective-permute-start.36) | collective-permute-done | bytes 1441824 | tf_op jit(solution)/shard_map/ppermute | solution.py:188
  1465.9 5.7 collective-permute-done.39
  1471.6 21.9 %collective-permute-done.38 = bf16[32,5632]{1,0:T(8,128)(2,1)S(1)} collective-permute-done((bf16[32,5632]{1,0:T(8,128)(2,1)S(1)}, bf16[32,5632]{1,0:T(8,128)(2,1)S(1)}, u32[]{:S(2)}, u32[]{:S(2)}) %collective-permute-start.38) | collective-permute-done | bytes 360480 | tf_op jit(solution)/shard_map/ppermute | solution.py:247
  (904 shorter events, 464.6 us)
Async XLA Ops:
  232.5 60.8 %collective-permute-start.6 = (bf16[2,16,273]{2,1,0:T(8,128)(2,1)}, bf16[2,16,273]{2,1,0:T(8,128)(2,1)}, u32[]{:S(2)}, u32[]{:S(2)}) collective-permute-start(bf16[2,16,273]{2,1,0:T(8,128)(2,1)} %fusion.309), channel_id=1, source_target_pairs={{0,3},{4,7},{8,11},{12,15},{16,19},{20,23},{24,27},{28,31}} | collective-permute-start | bytes 52424 | tf_op jit(solution)/shard_map/ppermute | solution.py:155
  240.0 63.8 %collective-permute-start.5 = (bf16[2,16,273]{2,1,0:T(8,128)(2,1)}, bf16[2,16,273]{2,1,0:T(8,128)(2,1)}, u32[]{:S(2)}, u32[]{:S(2)}) collective-permute-start(bf16[2,16,273]{2,1,0:T(8,128)(2,1)} %fusion.309), channel_id=1, source_target_pairs={{0,2},{1,3},{4,6},{5,7},{8,10},{9,11},{12,14},{13,15},{16,18},{17,... | collective-permute-start | bytes 52424 | tf_op jit(solution)/shard_map/ppermute | solution.py:155
  243.8 26.5 %collective-permute-start = (f32[2,2,1024]{2,1,0:T(2,128)}, f32[2,2,1024]{2,1,0:T(2,128)S(1)}, u32[]{:S(2)}, u32[]{:S(2)}) collective-permute-start(f32[2,2,1024]{2,1,0:T(2,128)} %slice.749), channel_id=1, source_target_pairs={{0,1},{1,2},{2,3},{4,5},{5,6},{6,7},{8,9},{9,10},{10,11},{12,13},{... | collective-permute-start | bytes 49160 | tf_op jit(solution)/shard_map/ppermute | solution.py:146
  285.9 113.6 %collective-permute-start.3 = (bf16[2,16,273,64]{2,3,1,0:T(8,128)(2,1)}, bf16[2,16,273,64]{2,3,1,0:T(8,128)(2,1)}, u32[]{:S(2)}, u32[]{:S(2)}) collective-permute-start(bf16[2,16,273,64]{2,3,1,0:T(8,128)(2,1)} %convolution_convert_fusion.7), channel_id=1, source_target_pairs={{0,3},{4,7},{8,11},{12,15},{16,19},{20,23},{24,27},{28,31}} | collective-permute-start | bytes 3354632 | tf_op jit(solution)/shard_map/ppermute | solution.py:155
  288.3 111.2 %collective-permute-start.2 = (bf16[2,16,273,64]{2,3,1,0:T(8,128)(2,1)}, bf16[2,16,273,64]{2,3,1,0:T(8,128)(2,1)}, u32[]{:S(2)}, u32[]{:S(2)}) collective-permute-start(bf16[2,16,273,64]{2,3,1,0:T(8,128)(2,1)} %convolution_convert_fusion.7), channel_id=1, source_target_pairs={{0,2},{1,3},{4,6},{5,7},{8,10},{9,11},{12,14},{13,15},{16,18},{17,... | collective-permute-start | bytes 3354632 | tf_op jit(solution)/shard_map/ppermute | solution.py:155
  290.8 108.8 %collective-permute-start.1 = (bf16[2,16,273,64]{2,3,1,0:T(8,128)(2,1)}, bf16[2,16,273,64]{2,3,1,0:T(8,128)(2,1)}, u32[]{:S(2)}, u32[]{:S(2)}) collective-permute-start(bf16[2,16,273,64]{2,3,1,0:T(8,128)(2,1)} %convolution_convert_fusion.7), channel_id=1, source_target_pairs={{0,1},{1,2},{2,3},{4,5},{5,6},{6,7},{8,9},{9,10},{10,11},{12,13},{... | collective-permute-start | bytes 3354632 | tf_op jit(solution)/shard_map/ppermute | solution.py:155
  293.3 96.4 %collective-permute-start.4 = (bf16[2,16,273]{2,1,0:T(8,128)(2,1)}, bf16[2,16,273]{2,1,0:T(8,128)(2,1)S(1)}, u32[]{:S(2)}, u32[]{:S(2)}) collective-permute-start(bf16[2,16,273]{2,1,0:T(8,128)(2,1)} %fusion.309), channel_id=1, source_target_pairs={{0,1},{1,2},{2,3},{4,5},{5,6},{6,7},{8,9},{9,10},{10,11},{12,13},{... | collective-permute-start | bytes 52424 | tf_op jit(solution)/shard_map/ppermute | solution.py:155
  460.1 105.2 %collective-permute-start.7 = (bf16[2,63,2048]{2,1,0:T(8,128)(2,1)}, bf16[2,63,2048]{2,1,0:T(8,128)(2,1)}, u32[]{:S(2)}, u32[]{:S(2)}) collective-permute-start(bf16[2,63,2048]{2,1,0:T(8,128)(2,1)} %slice.761), channel_id=1, source_target_pairs={{0,1},{1,2},{2,3},{4,5},{5,6},{6,7},{8,9},{9,10},{10,11},{12,13},{... | collective-permute-start | bytes 1548296 | tf_op jit(solution)/shard_map/ppermute | solution.py:146
  678.7 82.0 %collective-permute-start.8 = (bf16[2,63,2048]{2,1,0:T(8,128)(2,1)}, bf16[2,63,2048]{2,1,0:T(8,128)(2,1)}, u32[]{:S(2)}, u32[]{:S(2)}) collective-permute-start(bf16[2,63,2048]{2,1,0:T(8,128)(2,1)} %pad_maximum_fusion.15), channel_id=1, source_target_pairs={{1,0},{2,1},{3,2},{5,4},{6,5},{7,6},{9,8},{10,9},{11,10},{13,12},{... | collective-permute-start | bytes 1548296 | tf_op jit(solution)/shard_map/ppermute | solution.py:146
  702.5 186.4 %collective-permute-start.56 = (bf16[4,128,1024]{2,1,0:T(8,128)(2,1)}, bf16[4,128,1024]{2,1,0:T(8,128)(2,1)}, u32[]{:S(2)}, u32[]{:S(2)}) collective-permute-start(bf16[4,128,1024]{2,1,0:T(8,128)(2,1)} %convolution_convert_fusion.10), channel_id=1, source_target_pairs={{0,4},{4,0},{8,12},{12,8},{16,20},{20,16},{24,28},{28,24},{1,5},{5... | collective-permute-start | bytes 3145736 | tf_op jit(solution)/shard_map/ppermute | solution.py:188
  814.0 100.9 %collective-permute-start.11 = (bf16[2,16,273]{2,1,0:T(8,128)(2,1)S(1)}, bf16[2,16,273]{2,1,0:T(8,128)(2,1)S(1)}, u32[]{:S(2)}, u32[]{:S(2)}) collective-permute-start(bf16[2,16,273]{2,1,0:T(8,128)(2,1)S(1)} %bitcast.763), channel_id=1, source_target_pairs={{3,0},{7,4},{11,8},{15,12},{19,16},{23,20},{27,24},{31,28}} | collective-permute-start | bytes 52424 | tf_op jit(solution)/shard_map/ppermute | solution.py:166
  815.3 100.9 %collective-permute-start.10 = (bf16[2,16,273]{2,1,0:T(8,128)(2,1)S(1)}, bf16[2,16,273]{2,1,0:T(8,128)(2,1)S(1)}, u32[]{:S(2)}, u32[]{:S(2)}) collective-permute-start(bf16[2,16,273]{2,1,0:T(8,128)(2,1)S(1)} %bitcast.764), channel_id=1, source_target_pairs={{2,0},{3,1},{6,4},{7,5},{10,8},{11,9},{14,12},{15,13},{18,16},{19,... | collective-permute-start | bytes 52424 | tf_op jit(solution)/shard_map/ppermute | solution.py:166
  816.6 100.9 %collective-permute-start.9 = (bf16[2,16,273]{2,1,0:T(8,128)(2,1)S(1)}, bf16[2,16,273]{2,1,0:T(8,128)(2,1)S(1)}, u32[]{:S(2)}, u32[]{:S(2)}) collective-permute-start(bf16[2,16,273]{2,1,0:T(8,128)(2,1)S(1)} %bitcast.765), channel_id=1, source_target_pairs={{1,0},{2,1},{3,2},{5,4},{6,5},{7,6},{9,8},{10,9},{11,10},{13,12},{... | collective-permute-start | bytes 52424 | tf_op jit(solution)/shard_map/ppermute | solution.py:166
  905.4 161.7 %collective-permute-start.24 = (bf16[4,128,1024]{2,1,0:T(8,128)(2,1)}, bf16[4,128,1024]{2,1,0:T(8,128)(2,1)}, u32[]{:S(2)}, u32[]{:S(2)}) collective-permute-start(bf16[4,128,1024]{2,1,0:T(8,128)(2,1)} %convolution_convert_fusion.11), channel_id=1, source_target_pairs={{0,4},{4,0},{8,12},{12,8},{16,20},{20,16},{24,28},{28,24},{1,5},{5... | collective-permute-start | bytes 3145736 | tf_op jit(solution)/shard_map/ppermute | solution.py:188
  907.1 11.8 collective-permute-start.63
  914.9 155.8 %collective-permute-start.14 = (bf16[2,16,273,64]{2,3,1,0:T(8,128)(2,1)}, bf16[2,16,273,64]{2,3,1,0:T(8,128)(2,1)}, u32[]{:S(2)}, u32[]{:S(2)}) collective-permute-start(bf16[2,16,273,64]{2,3,1,0:T(8,128)(2,1)} %convolution_convert_fusion.8), channel_id=1, source_target_pairs={{3,0},{7,4},{11,8},{15,12},{19,16},{23,20},{27,24},{31,28}} | collective-permute-start | bytes 3354632 | tf_op jit(solution)/shard_map/ppermute | solution.py:166
  916.2 154.9 %collective-permute-start.13 = (bf16[2,16,273,64]{2,3,1,0:T(8,128)(2,1)}, bf16[2,16,273,64]{2,3,1,0:T(8,128)(2,1)}, u32[]{:S(2)}, u32[]{:S(2)}) collective-permute-start(bf16[2,16,273,64]{2,3,1,0:T(8,128)(2,1)} %convolution_convert_fusion.8), channel_id=1, source_target_pairs={{2,0},{3,1},{6,4},{7,5},{10,8},{11,9},{14,12},{15,13},{18,16},{19,... | collective-permute-start | bytes 3354632 | tf_op jit(solution)/shard_map/ppermute | solution.py:166
  917.6 155.2 %collective-permute-start.12 = (bf16[2,16,273,64]{2,3,1,0:T(8,128)(2,1)}, bf16[2,16,273,64]{2,3,1,0:T(8,128)(2,1)}, u32[]{:S(2)}, u32[]{:S(2)}) collective-permute-start(bf16[2,16,273,64]{2,3,1,0:T(8,128)(2,1)} %convolution_convert_fusion.8), channel_id=1, source_target_pairs={{1,0},{2,1},{3,2},{5,4},{6,5},{7,6},{9,8},{10,9},{11,10},{13,12},{... | collective-permute-start | bytes 3354632 | tf_op jit(solution)/shard_map/ppermute | solution.py:166
  918.9 140.3 %collective-permute-start.62 = (bf16[32,1024]{1,0:T(8,128)(2,1)}, bf16[32,1024]{1,0:T(8,128)(2,1)}, u32[]{:S(2)}, u32[]{:S(2)}) collective-permute-start(bf16[32,1024]{1,0:T(8,128)(2,1)} %get-tuple-element.301), channel_id=1, source_target_pairs={{0,2},{1,3},{2,0},{3,1},{4,6},{5,7},{6,4},{7,5},{8,10},{9,11},{10,... | collective-permute-start | bytes 196616 | tf_op jit(solution)/shard_map/ppermute | solution.py:247
  1065.6 104.5 %collective-permute-start.72 = (bf16[4,352,1024]{2,1,0:T(8,128)(2,1)}, bf16[4,352,1024]{2,1,0:T(8,128)(2,1)}, u32[]{:S(2)}, u32[]{:S(2)}) collective-permute-start(bf16[4,352,1024]{2,1,0:T(8,128)(2,1)} %convolution_convert_fusion.5), channel_id=1, source_target_pairs={{0,4},{4,0},{8,12},{12,8},{16,20},{20,16},{24,28},{28,24},{1,5},{5... | collective-permute-start | bytes 8650760 | tf_op jit(solution)/shard_map/ppermute | solution.py:188
  1067.1 120.0 %collective-permute-start.40 = (bf16[4,352,1024]{2,1,0:T(8,128)(2,1)}, bf16[4,352,1024]{2,1,0:T(8,128)(2,1)}, u32[]{:S(2)}, u32[]{:S(2)}) collective-permute-start(bf16[4,352,1024]{2,1,0:T(8,128)(2,1)} %convolution_convert_fusion.6), channel_id=1, source_target_pairs={{0,4},{4,0},{8,12},{12,8},{16,20},{20,16},{24,28},{28,24},{1,5},{5... | collective-permute-start | bytes 8650760 | tf_op jit(solution)/shard_map/ppermute | solution.py:188
  1070.7 85.0 %collective-permute-start.25 = (bf16[64,1024]{1,0:T(8,128)(2,1)}, bf16[64,1024]{1,0:T(8,128)(2,1)}, u32[]{:S(2)}, u32[]{:S(2)}) collective-permute-start(bf16[64,1024]{1,0:T(8,128)(2,1)} %get-tuple-element.272), channel_id=1, source_target_pairs={{0,16},{4,20},{8,24},{12,28},{16,0},{20,4},{24,8},{28,12},{1,17},{... | collective-permute-start | bytes 393224 | tf_op jit(solution)/shard_map/ppermute | solution.py:188
  1071.2 84.5 %collective-permute-start.27 = (bf16[64,1024]{1,0:T(8,128)(2,1)}, bf16[64,1024]{1,0:T(8,128)(2,1)}, u32[]{:S(2)}, u32[]{:S(2)}) collective-permute-start(bf16[64,1024]{1,0:T(8,128)(2,1)} %get-tuple-element.273), channel_id=1, source_target_pairs={{0,8},{4,12},{8,0},{12,4},{16,24},{20,28},{24,16},{28,20},{1,9},{5... | collective-permute-start | bytes 393224 | tf_op jit(solution)/shard_map/ppermute | solution.py:188
  1122.2 10.5 collective-permute-start.15
  1155.6 29.3 %collective-permute-start.16 = (bf16[4,128,1664]{2,1,0:T(8,128)(2,1)S(1)}, bf16[4,128,1664]{2,1,0:T(8,128)(2,1)S(1)}, u32[]{:S(2)}, u32[]{:S(2)}) collective-permute-start(bf16[4,128,1664]{2,1,0:T(8,128)(2,1)S(1)} %pad_maximum_fusion.2), channel_id=1, source_target_pairs={{0,4},{4,0},{8,12},{12,8},{16,20},{20,16},{24,28},{28,24},{1,5},{5... | collective-permute-start | bytes 5111816 | tf_op jit(solution)/shard_map/ppermute | solution.py:188
  1177.3 181.1 %collective-permute-start.64 = (bf16[4,128,5632]{2,1,0:T(8,128)(2,1)}, bf16[4,128,5632]{2,1,0:T(8,128)(2,1)}, u32[]{:S(2)}, u32[]{:S(2)}) collective-permute-start(bf16[4,128,5632]{2,1,0:T(8,128)(2,1)} %convolution_convert_fusion), channel_id=1, source_target_pairs={{0,4},{4,0},{8,12},{12,8},{16,20},{20,16},{24,28},{28,24},{1,5},{5... | collective-permute-start | bytes 17301512 | tf_op jit(solution)/shard_map/ppermute | solution.py:188
  1182.9 25.5 %collective-permute-start.48 = (bf16[4,128,3072]{2,1,0:T(8,128)(2,1)S(1)}, bf16[4,128,3072]{2,1,0:T(8,128)(2,1)S(1)}, u32[]{:S(2)}, u32[]{:S(2)}) collective-permute-start(bf16[4,128,3072]{2,1,0:T(8,128)(2,1)S(1)} %copy-done.211), channel_id=1, source_target_pairs={{0,4},{4,0},{8,12},{12,8},{16,20},{20,16},{24,28},{28,24},{1,5},{5... | collective-permute-start | bytes 9437192 | tf_op jit(solution)/shard_map/ppermute | solution.py:188
  1184.2 50.5 %collective-permute-start.76 = (bf16[352,1024]{1,0:T(8,128)(2,1)S(1)}, bf16[352,1024]{1,0:T(8,128)(2,1)S(1)}, u32[]{:S(2)}, u32[]{:S(2)}) collective-permute-start(bf16[352,1024]{1,0:T(8,128)(2,1)S(1)} %pad_maximum_fusion.14), channel_id=1, source_target_pairs={{0,16},{4,20},{8,24},{12,28},{16,0},{20,4},{24,8},{28,12},{1,17},{... | collective-permute-start | bytes 2162696 | tf_op jit(solution)/shard_map/ppermute | solution.py:188
  1185.6 20.6 %collective-permute-start.17 = (bf16[64,1664]{1,0:T(8,128)(2,1)S(1)}, bf16[64,1664]{1,0:T(8,128)(2,1)S(1)}, u32[]{:S(2)}, u32[]{:S(2)}) collective-permute-start(bf16[64,1664]{1,0:T(8,128)(2,1)S(1)} %get-tuple-element.219), channel_id=1, source_target_pairs={{0,16},{4,20},{8,24},{12,28},{16,0},{20,4},{24,8},{28,12},{1,17},{... | collective-permute-start | bytes 638984 | tf_op jit(solution)/shard_map/ppermute | solution.py:188
  1187.1 20.5 %collective-permute-start.19 = (bf16[64,1664]{1,0:T(8,128)(2,1)S(1)}, bf16[64,1664]{1,0:T(8,128)(2,1)S(1)}, u32[]{:S(2)}, u32[]{:S(2)}) collective-permute-start(bf16[64,1664]{1,0:T(8,128)(2,1)S(1)} %get-tuple-element.220), channel_id=1, source_target_pairs={{0,8},{4,12},{8,0},{12,4},{16,24},{20,28},{24,16},{28,20},{1,9},{5... | collective-permute-start | bytes 638984 | tf_op jit(solution)/shard_map/ppermute | solution.py:188
  1206.2 28.9 %collective-permute-start.74 = (bf16[352,1024]{1,0:T(8,128)(2,1)S(1)}, bf16[352,1024]{1,0:T(8,128)(2,1)S(1)}, u32[]{:S(2)}, u32[]{:S(2)}) collective-permute-start(bf16[352,1024]{1,0:T(8,128)(2,1)S(1)} %pad_maximum_fusion.13), channel_id=1, source_target_pairs={{0,8},{4,12},{8,0},{12,4},{16,24},{20,28},{24,16},{28,20},{1,9},{5... | collective-permute-start | bytes 2162696 | tf_op jit(solution)/shard_map/ppermute | solution.py:188
  1208.4 22.8 %collective-permute-start.43 = (bf16[176,1024]{1,0:T(8,128)(2,1)S(1)}, bf16[176,1024]{1,0:T(8,128)(2,1)S(1)}, u32[]{:S(2)}, u32[]{:S(2)}) collective-permute-start(bf16[176,1024]{1,0:T(8,128)(2,1)S(1)} %get-tuple-element.206), channel_id=1, source_target_pairs={{0,8},{4,12},{8,0},{12,4},{16,24},{20,28},{24,16},{28,20},{1,9},{5... | collective-permute-start | bytes 1081352 | tf_op jit(solution)/shard_map/ppermute | solution.py:188
  1217.2 20.9 %collective-permute-start.20 = (bf16[128,1664]{1,0:T(8,128)(2,1)S(1)}, bf16[128,1664]{1,0:T(8,128)(2,1)S(1)}, u32[]{:S(2)}, u32[]{:S(2)}) collective-permute-start(bf16[128,1664]{1,0:T(8,128)(2,1)S(1)} %pad_maximum_fusion.17), channel_id=1, source_target_pairs={{0,16},{4,20},{8,24},{12,28},{16,0},{20,4},{24,8},{28,12},{1,17},{... | collective-permute-start | bytes 1277960 | tf_op jit(solution)/shard_map/ppermute | solution.py:188
  1231.1 12.8 collective-permute-start.18
  1234.8 21.1 %collective-permute-start.49 = (bf16[64,3072]{1,0:T(8,128)(2,1)}, bf16[64,3072]{1,0:T(8,128)(2,1)}, u32[]{:S(2)}, u32[]{:S(2)}) collective-permute-start(bf16[64,3072]{1,0:T(8,128)(2,1)} %get-tuple-element.182), channel_id=1, source_target_pairs={{0,16},{4,20},{8,24},{12,28},{16,0},{20,4},{24,8},{28,12},{1,17},{... | collective-permute-start | bytes 1179656 | tf_op jit(solution)/shard_map/ppermute | solution.py:188
  1235.1 20.8 %collective-permute-start.51 = (bf16[64,3072]{1,0:T(8,128)(2,1)}, bf16[64,3072]{1,0:T(8,128)(2,1)}, u32[]{:S(2)}, u32[]{:S(2)}) collective-permute-start(bf16[64,3072]{1,0:T(8,128)(2,1)} %get-tuple-element.183), channel_id=1, source_target_pairs={{0,8},{4,12},{8,0},{12,4},{16,24},{20,28},{24,16},{28,20},{1,9},{5... | collective-permute-start | bytes 1179656 | tf_op jit(solution)/shard_map/ppermute | solution.py:188
  1238.1 70.2 %collective-permute-start.44 = (bf16[352,1024]{1,0:T(8,128)(2,1)}, bf16[352,1024]{1,0:T(8,128)(2,1)}, u32[]{:S(2)}, u32[]{:S(2)}) collective-permute-start(bf16[352,1024]{1,0:T(8,128)(2,1)} %pad_maximum_fusion.12), channel_id=1, source_target_pairs={{0,16},{4,20},{8,24},{12,28},{16,0},{20,4},{24,8},{28,12},{1,17},{... | collective-permute-start | bytes 2162696 | tf_op jit(solution)/shard_map/ppermute | solution.py:188
  1243.9 53.1 %collective-permute-start.79 = (bf16[88,1024]{1,0:T(8,128)(2,1)}, bf16[88,1024]{1,0:T(8,128)(2,1)}, u32[]{:S(2)}, u32[]{:S(2)}) collective-permute-start(bf16[88,1024]{1,0:T(8,128)(2,1)} %get-tuple-element.227), channel_id=1, source_target_pairs={{0,3},{1,0},{2,1},{3,2},{4,7},{5,4},{6,5},{7,6},{8,11},{9,8},{10,9... | collective-permute-start | bytes 540680 | tf_op jit(solution)/shard_map/ppermute | solution.py:247
  1255.9 10.6 collective-permute-start.23
  1256.0 28.8 %collective-permute-start.22 = (bf16[32,1664]{0,1:T(8,128)(2,1)}, bf16[32,1664]{0,1:T(8,128)(2,1)S(1)}, u32[]{:S(2)}, u32[]{:S(2)}) collective-permute-start(bf16[32,1664]{0,1:T(8,128)(2,1)} %bitcast.563), channel_id=1, source_target_pairs={{0,2},{1,3},{2,0},{3,1},{4,6},{5,7},{6,4},{7,5},{8,10},{9,11},{10,... | collective-permute-start | bytes 319496 | tf_op jit(solution)/shard_map/ppermute | solution.py:247
  1266.5 32.2 %collective-permute-start.78 = (bf16[88,1024]{1,0:T(8,128)(2,1)}, bf16[88,1024]{1,0:T(8,128)(2,1)S(1)}, u32[]{:S(2)}, u32[]{:S(2)}) collective-permute-start(bf16[88,1024]{1,0:T(8,128)(2,1)} %get-tuple-element.228), channel_id=1, source_target_pairs={{0,2},{1,3},{2,0},{3,1},{4,6},{5,7},{6,4},{7,5},{8,10},{9,11},{10,... | collective-permute-start | bytes 540680 | tf_op jit(solution)/shard_map/ppermute | solution.py:247
  1284.8 12.2 collective-permute-start.21
  1297.0 69.4 %collective-permute-start.32 = (bf16[4,128,5632]{2,1,0:T(8,128)(2,1)}, bf16[4,128,5632]{2,1,0:T(8,128)(2,1)}, u32[]{:S(2)}, u32[]{:S(2)}) collective-permute-start(bf16[4,128,5632]{2,1,0:T(8,128)(2,1)} %convolution_convert_fusion.1), channel_id=1, source_target_pairs={{0,4},{4,0},{8,12},{12,8},{16,20},{20,16},{24,28},{28,24},{1,5},{5... | collective-permute-start | bytes 17301512 | tf_op jit(solution)/shard_map/ppermute | solution.py:188
  1297.0 19.2 %collective-permute-start.42 = (bf16[352,1024]{1,0:T(8,128)(2,1)}, bf16[352,1024]{1,0:T(8,128)(2,1)}, u32[]{:S(2)}, u32[]{:S(2)}) collective-permute-start(bf16[352,1024]{1,0:T(8,128)(2,1)} %pad_maximum_fusion.11), channel_id=1, source_target_pairs={{0,8},{4,12},{8,0},{12,4},{16,24},{20,28},{24,16},{28,20},{1,9},{5... | collective-permute-start | bytes 2162696 | tf_op jit(solution)/shard_map/ppermute | solution.py:188
  1307.9 19.1 %collective-permute-start.52 = (bf16[128,3072]{1,0:T(8,128)(2,1)}, bf16[128,3072]{1,0:T(8,128)(2,1)S(1)}, u32[]{:S(2)}, u32[]{:S(2)}) collective-permute-start(bf16[128,3072]{1,0:T(8,128)(2,1)} %pad_maximum_fusion.10), channel_id=1, source_target_pairs={{0,16},{4,20},{8,24},{12,28},{16,0},{20,4},{24,8},{28,12},{1,17},{... | collective-permute-start | bytes 2359304 | tf_op jit(solution)/shard_map/ppermute | solution.py:188
  1308.3 24.5 %collective-permute-start.50 = (bf16[128,3072]{1,0:T(8,128)(2,1)}, bf16[128,3072]{1,0:T(8,128)(2,1)}, u32[]{:S(2)}, u32[]{:S(2)}) collective-permute-start(bf16[128,3072]{1,0:T(8,128)(2,1)} %pad_maximum_fusion.9), channel_id=1, source_target_pairs={{0,8},{4,12},{8,0},{12,4},{16,24},{20,28},{24,16},{28,20},{1,9},{5... | collective-permute-start | bytes 2359304 | tf_op jit(solution)/shard_map/ppermute | solution.py:188
  1318.3 16.6 %collective-permute-start.47 = (bf16[88,1024]{1,0:T(8,128)(2,1)S(1)}, bf16[88,1024]{1,0:T(8,128)(2,1)S(1)}, u32[]{:S(2)}, u32[]{:S(2)}) collective-permute-start(bf16[88,1024]{1,0:T(8,128)(2,1)S(1)} %get-tuple-element.230), channel_id=1, source_target_pairs={{0,3},{1,0},{2,1},{3,2},{4,7},{5,4},{6,5},{7,6},{8,11},{9,8},{10,9... | collective-permute-start | bytes 540680 | tf_op jit(solution)/shard_map/ppermute | solution.py:247
  1327.0 11.8 collective-permute-start.46
  1334.9 10.0 collective-permute-start.55
  1338.8 18.8 %collective-permute-start.54 = (bf16[32,3072]{1,0:T(8,128)(2,1)S(1)}, bf16[32,3072]{1,0:T(8,128)(2,1)S(1)}, u32[]{:S(2)}, u32[]{:S(2)}) collective-permute-start(bf16[32,3072]{1,0:T(8,128)(2,1)S(1)} %get-tuple-element.225), channel_id=1, source_target_pairs={{0,2},{1,3},{2,0},{3,1},{4,6},{5,7},{6,4},{7,5},{8,10},{9,11},{10,... | collective-permute-start | bytes 589832 | tf_op jit(solution)/shard_map/ppermute | solution.py:247
  1341.4 16.2 %collective-permute-start.53 = (bf16[32,3072]{1,0:T(8,128)(2,1)S(1)}, bf16[32,3072]{1,0:T(8,128)(2,1)S(1)}, u32[]{:S(2)}, u32[]{:S(2)}) collective-permute-start(bf16[32,3072]{1,0:T(8,128)(2,1)S(1)} %get-tuple-element.223), channel_id=1, source_target_pairs={{0,1},{1,2},{2,3},{3,0},{4,5},{5,6},{6,7},{7,4},{8,9},{9,10},{10,1... | collective-permute-start | bytes 589832 | tf_op jit(solution)/shard_map/ppermute | solution.py:247
  1364.3 19.1 %collective-permute-start.65 = (bf16[64,5632]{1,0:T(8,128)(2,1)S(1)}, bf16[64,5632]{1,0:T(8,128)(2,1)S(1)}, u32[]{:S(2)}, u32[]{:S(2)}) collective-permute-start(bf16[64,5632]{1,0:T(8,128)(2,1)S(1)} %get-tuple-element.162), channel_id=1, source_target_pairs={{0,16},{4,20},{8,24},{12,28},{16,0},{20,4},{24,8},{28,12},{1,17},{... | collective-permute-start | bytes 2162696 | tf_op jit(solution)/shard_map/ppermute | solution.py:188
  1366.1 19.1 %collective-permute-start.67 = (bf16[64,5632]{1,0:T(8,128)(2,1)S(1)}, bf16[64,5632]{1,0:T(8,128)(2,1)S(1)}, u32[]{:S(2)}, u32[]{:S(2)}) collective-permute-start(bf16[64,5632]{1,0:T(8,128)(2,1)S(1)} %get-tuple-element.163), channel_id=1, source_target_pairs={{0,8},{4,12},{8,0},{12,4},{16,24},{20,28},{24,16},{28,20},{1,9},{5... | collective-permute-start | bytes 2162696 | tf_op jit(solution)/shard_map/ppermute | solution.py:188
  1374.2 24.6 %collective-permute-start.33 = (bf16[64,5632]{1,0:T(8,128)(2,1)S(1)}, bf16[64,5632]{1,0:T(8,128)(2,1)S(1)}, u32[]{:S(2)}, u32[]{:S(2)}) collective-permute-start(bf16[64,5632]{1,0:T(8,128)(2,1)S(1)} %get-tuple-element.168), channel_id=1, source_target_pairs={{0,16},{4,20},{8,24},{12,28},{16,0},{20,4},{24,8},{28,12},{1,17},{... | collective-permute-start | bytes 2162696 | tf_op jit(solution)/shard_map/ppermute | solution.py:188
  1376.0 24.7 %collective-permute-start.35 = (bf16[64,5632]{1,0:T(8,128)(2,1)S(1)}, bf16[64,5632]{1,0:T(8,128)(2,1)S(1)}, u32[]{:S(2)}, u32[]{:S(2)}) collective-permute-start(bf16[64,5632]{1,0:T(8,128)(2,1)S(1)} %get-tuple-element.169), channel_id=1, source_target_pairs={{0,8},{4,12},{8,0},{12,4},{16,24},{20,28},{24,16},{28,20},{1,9},{5... | collective-permute-start | bytes 2162696 | tf_op jit(solution)/shard_map/ppermute | solution.py:188
  1385.4 44.3 %collective-permute-start.68 = (bf16[128,5632]{1,0:T(8,128)(2,1)S(1)}, bf16[128,5632]{1,0:T(8,128)(2,1)S(1)}, u32[]{:S(2)}, u32[]{:S(2)}) collective-permute-start(bf16[128,5632]{1,0:T(8,128)(2,1)S(1)} %pad_maximum_fusion.7), channel_id=1, source_target_pairs={{0,16},{4,20},{8,24},{12,28},{16,0},{20,4},{24,8},{28,12},{1,17},{... | collective-permute-start | bytes 4325384 | tf_op jit(solution)/shard_map/ppermute | solution.py:188
  1385.8 45.7 %collective-permute-start.66 = (bf16[128,5632]{1,0:T(8,128)(2,1)S(1)}, bf16[128,5632]{1,0:T(8,128)(2,1)S(1)}, u32[]{:S(2)}, u32[]{:S(2)}) collective-permute-start(bf16[128,5632]{1,0:T(8,128)(2,1)S(1)} %pad_maximum_fusion.6), channel_id=1, source_target_pairs={{0,8},{4,12},{8,0},{12,4},{16,24},{20,28},{24,16},{28,20},{1,9},{5... | collective-permute-start | bytes 4325384 | tf_op jit(solution)/shard_map/ppermute | solution.py:188
  1400.9 58.6 %collective-permute-start.36 = (bf16[128,5632]{1,0:T(8,128)(2,1)S(1)}, bf16[128,5632]{1,0:T(8,128)(2,1)S(1)}, u32[]{:S(2)}, u32[]{:S(2)}) collective-permute-start(bf16[128,5632]{1,0:T(8,128)(2,1)S(1)} %pad_maximum_fusion.5), channel_id=1, source_target_pairs={{0,16},{4,20},{8,24},{12,28},{16,0},{20,4},{24,8},{28,12},{1,17},{... | collective-permute-start | bytes 4325384 | tf_op jit(solution)/shard_map/ppermute | solution.py:188
  1401.3 59.7 %collective-permute-start.34 = (bf16[128,5632]{1,0:T(8,128)(2,1)S(1)}, bf16[128,5632]{1,0:T(8,128)(2,1)S(1)}, u32[]{:S(2)}, u32[]{:S(2)}) collective-permute-start(bf16[128,5632]{1,0:T(8,128)(2,1)S(1)} %pad_maximum_fusion.4), channel_id=1, source_target_pairs={{0,8},{4,12},{8,0},{12,4},{16,24},{20,28},{24,16},{28,20},{1,9},{5... | collective-permute-start | bytes 4325384 | tf_op jit(solution)/shard_map/ppermute | solution.py:188
  1432.1 30.8 %collective-permute-start.71 = (bf16[32,5632]{1,0:T(8,128)(2,1)S(1)}, bf16[32,5632]{1,0:T(8,128)(2,1)S(1)}, u32[]{:S(2)}, u32[]{:S(2)}) collective-permute-start(bf16[32,5632]{1,0:T(8,128)(2,1)S(1)} %get-tuple-element.201), channel_id=1, source_target_pairs={{0,3},{1,0},{2,1},{3,2},{4,7},{5,4},{6,5},{7,6},{8,11},{9,8},{10,9... | collective-permute-start | bytes 1081352 | tf_op jit(solution)/shard_map/ppermute | solution.py:247
  1432.2 32.7 %collective-permute-start.70 = (bf16[32,5632]{1,0:T(8,128)(2,1)S(1)}, bf16[32,5632]{1,0:T(8,128)(2,1)S(1)}, u32[]{:S(2)}, u32[]{:S(2)}) collective-permute-start(bf16[32,5632]{1,0:T(8,128)(2,1)S(1)} %get-tuple-element.202), channel_id=1, source_target_pairs={{0,2},{1,3},{2,0},{3,1},{4,6},{5,7},{6,4},{7,5},{8,10},{9,11},{10,... | collective-permute-start | bytes 1081352 | tf_op jit(solution)/shard_map/ppermute | solution.py:247
  1433.3 31.6 %collective-permute-start.69 = (bf16[32,5632]{1,0:T(8,128)(2,1)S(1)}, bf16[32,5632]{1,0:T(8,128)(2,1)S(1)}, u32[]{:S(2)}, u32[]{:S(2)}) collective-permute-start(bf16[32,5632]{1,0:T(8,128)(2,1)S(1)} %get-tuple-element.200), channel_id=1, source_target_pairs={{0,1},{1,2},{2,3},{3,0},{4,5},{5,6},{6,7},{7,4},{8,9},{9,10},{10,1... | collective-permute-start | bytes 1081352 | tf_op jit(solution)/shard_map/ppermute | solution.py:247
  1461.6 31.8 %collective-permute-start.38 = (bf16[32,5632]{1,0:T(8,128)(2,1)S(1)}, bf16[32,5632]{1,0:T(8,128)(2,1)S(1)}, u32[]{:S(2)}, u32[]{:S(2)}) collective-permute-start(bf16[32,5632]{1,0:T(8,128)(2,1)S(1)} %get-tuple-element.211), channel_id=1, source_target_pairs={{0,2},{1,3},{2,0},{3,1},{4,6},{5,7},{6,4},{7,5},{8,10},{9,11},{10,... | collective-permute-start | bytes 1081352 | tf_op jit(solution)/shard_map/ppermute | solution.py:247
  1463.0 30.5 %collective-permute-start.37 = (bf16[32,5632]{1,0:T(8,128)(2,1)S(1)}, bf16[32,5632]{1,0:T(8,128)(2,1)S(1)}, u32[]{:S(2)}, u32[]{:S(2)}) collective-permute-start(bf16[32,5632]{1,0:T(8,128)(2,1)S(1)} %get-tuple-element.209), channel_id=1, source_target_pairs={{0,1},{1,2},{2,3},{3,0},{4,5},{5,6},{6,7},{7,4},{8,9},{9,10},{10,1... | collective-permute-start | bytes 1081352 | tf_op jit(solution)/shard_map/ppermute | solution.py:247
  (253 other events, 4206.7 us)

commit v2 on v1

--- a/solution.py
+++ b/solution.py
@@ -140,6 +140,285 @@
     return [f.reshape(places * f.shape[1], f.shape[2]) for f in full]
 
 
+WIDE = 512
+SLOTS_HELD = 8
+
+
+def scatter_kernel(n_dp, n_ctx, plan, lags, n_x, n_y, n_o, *refs):
+    xs, ys, outs = refs[:n_x], refs[n_x : n_x + n_y], refs[n_x + n_y : n_x + n_y + n_o]
+    refs = refs[n_x + n_y + n_o :]
+    bits = [1 << i for i in range(n_dp.bit_length() - 1)]
+    low_bits, (bit_x, bit_y) = bits[:-2], bits[-2:]
+    n_low = len(low_bits)
+    x_all, y_all = refs[0], refs[1]
+    low_out, low_in = refs[2 : 2 + n_low], refs[2 + n_low : 2 + 2 * n_low]
+    refs = refs[2 + 2 * n_low :]
+    cross, cross_y, cross_x, side_x, side_y, came_x, came_y, shards, came_ctx, result = refs[:10]
+    x_sem, y_sem, out_sem, sent, arrived, credit = refs[10:]
+    held = y_all.shape[0]
+    dp, ctx = lax.axis_index("dp"), lax.axis_index("ctx")
+    group = cross.shape[1]
+    half = group // 2
+    rows = group // n_ctx
+    f32, low = jnp.float32, jnp.bfloat16
+    A_CY, A_CX, A_X, A_Y, A_Z = n_low, n_low + 1, n_low + 2, n_low + 3, n_low + 4
+    C_X, C_Y, C_Z = n_low, n_low + 1, n_low + 2
+
+    def at_ctx(hop):
+        return (dp, lax.rem(ctx + hop, n_ctx))
+
+    barrier = pltpu.get_barrier_semaphore()
+    for bit in bits:
+        pl.semaphore_signal(barrier, inc=1, device_id=(dp ^ bit, ctx), device_id_type=MESH)
+    for hop in range(1, n_ctx):
+        pl.semaphore_signal(barrier, inc=1, device_id=at_ctx(hop), device_id_type=MESH)
+    pl.semaphore_wait(barrier, len(bits) + n_ctx - 1)
+
+    bounds, count = [], 0
+    for segment in plan:
+        bounds.append((count, count + segment[5]))
+        count += segment[5]
+    x_first = [None] * n_x
+    for segment, (first, _) in zip(plan, bounds):
+        if x_first[segment[0]] is None:
+            x_first[segment[0]] = first
+
+    def x_copy(i):
+        return pltpu.make_async_copy(xs[i], x_all.at[i], x_sem.at[i])
+
+    for i in range(n_x):
+        x_copy(i).start()
+
+    def y_start(c):
+        slot = lax.rem(c, held)
+        for segment, (first, last) in zip(plan, bounds):
+
+            @pl.when((c >= first) & (c < last))
+            def _():
+                where = pl.multiple_of((c - first) * WIDE, WIDE)
+                pltpu.make_async_copy(
+                    ys[segment[1]].at[:, pl.ds(where, WIDE)], y_all.at[slot], y_sem.at[slot]
+                ).start()
+
+    def x_place(c):
+        return sum((c >= first).astype(jnp.int32) for first in x_first[1:])
+
+    def partial_sum(c, flip):
+        return jnp.dot(
+            x_all[x_place(c), dp ^ flip], y_all[lax.rem(c, held)], preferred_element_type=f32
+        )
+
+    def rest(level):
+        free = low_bits[level + 1 :] + [bit_x, bit_y]
+        return [sum(b for i, b in enumerate(free) if n >> i & 1) for n in range(1 << len(free))]
+
+    def summed(c, flip, levels):
+        total = partial_sum(c, flip)
+        for level in range(levels):
+            total = total + low_in[level][lax.rem(c, held), rest(level).index(flip)].astype(f32)
+        return total
+
+    def remote(src, dst, slot, kind, target):
+        return pltpu.make_async_remote_copy(
+            src_ref=src,
+            dst_ref=dst,
+            send_sem=sent.at[slot, kind],
+            recv_sem=arrived.at[slot, kind],
+            device_id=target,
+            device_id_type=MESH,
+        )
+
+    def copy_of(slot, kind):
+        over_x, over_y = (dp ^ bit_x, ctx), (dp ^ bit_y, ctx)
+        if kind < n_low:
+            return remote(
+                low_out[kind].at[slot], low_in[kind].at[slot], slot, kind, (dp ^ low_bits[kind], ctx)
+            )
+        if kind == A_CY:
+            return remote(cross.at[slot, pl.ds(0, half)], cross_y.at[slot], slot, kind, over_y)
+        if kind == A_CX:
+            return remote(cross.at[slot, pl.ds(half, half)], cross_x.at[slot], slot, kind, over_x)
+        if kind == A_X:
+            return remote(side_x.at[slot], came_x.at[slot], slot, kind, over_x)
+        if kind == A_Y:
+            return remote(side_y.at[slot], came_y.at[slot], slot, kind, over_y)
+        hop = kind - A_Z + 1
+        there = lax.rem(ctx + hop, n_ctx)
+        return remote(shards.at[slot, there], came_ctx.at[slot, hop - 1], slot, kind, (dp, there))
+
+    def need_credit(c, kind):
+        @pl.when(c >= held)
+        def _():
+            pl.semaphore_wait(credit.at[kind], 1)
+
+    def step_low(level, c):
+        slot = lax.rem(c, held)
+        if level == 0:
+            for i, first in enumerate(x_first):
+
+                @pl.when(c == first)
+                def _():
+                    x_copy(i).wait()
+
+            pltpu.make_async_copy(ys[0].at[:, pl.ds(0, WIDE)], y_all.at[slot], y_sem.at[slot]).wait()
+        else:
+            copy_of(slot, level - 1).wait_recv()
+        need_credit(c, level)
+        for j, flip in enumerate(rest(level)):
+            low_out[level][slot, j] = summed(c, flip | low_bits[level], level).astype(low)
+        copy_of(slot, level).start()
+
+    def step_cross(c):
+        slot = lax.rem(c, held)
+        if n_low:
+            copy_of(slot, n_low - 1).wait_recv()
+        need_credit(c, C_X)
+        need_credit(c, C_Y)
+        cross[slot] = summed(c, bit_x | bit_y, n_low).astype(low)
+        copy_of(slot, A_CY).start()
+        copy_of(slot, A_CX).start()
+
+    def step_sides(c):
+        slot = lax.rem(c, held)
+        over_x = summed(c, bit_x, n_low)
+        over_y = summed(c, bit_y, n_low)
+        copy_of(slot, A_CY).wait_recv()
+        side_x[slot, :half] = (over_x[:half] + cross_y[slot].astype(f32)).astype(low)
+        side_x[slot, half:] = over_x[half:].astype(low)
+        copy_of(slot, A_X).start()
+        copy_of(slot, A_CX).wait_recv()
+        side_y[slot, :half] = over_y[:half].astype(low)
+        side_y[slot, half:] = (over_y[half:] + cross_x[slot].astype(f32)).astype(low)
+        copy_of(slot, A_Y).start()
+
+    def step_own(c):
+        slot = lax.rem(c, held)
+        total = summed(c, 0, n_low)
+        copy_of(slot, A_X).wait_recv()
+        copy_of(slot, A_Y).wait_recv()
+        total = total + came_x[slot].astype(f32) + came_y[slot].astype(f32)
+        for j in range(n_ctx):
+            shards[slot, j] = total[j * rows : (j + 1) * rows].astype(low)
+        for hop in range(1, n_ctx):
+            need_credit(c, C_Z + hop - 1)
+            copy_of(slot, A_Z + hop - 1).start()
+
+    def out_copy(c, slot, segment, first):
+        where = pl.multiple_of((c - first) * WIDE, WIDE)
+        _, _, o, row, n_rows, _ = segment
+        return pltpu.make_async_copy(
+            result.at[slot, pl.ds(0, n_rows)],
+            outs[o].at[pl.ds(row, n_rows), pl.ds(where, WIDE)],
+            out_sem.at[slot],
+        )
+
+    def each_segment(c, act):
+        for segment, (first, last) in zip(plan, bounds):
+
+            @pl.when((c >= first) & (c < last))
+            def _():
+                act(segment, first)
+
+    def out_wait(c):
+        slot = lax.rem(c, held)
+        each_segment(c, lambda segment, first: out_copy(c, slot, segment, first).wait())
+
+    def step_end(c):
+        slot = lax.rem(c, held)
+
+        @pl.when(c >= held)
+        def _():
+            out_wait(c - held)
+
+        total = shards[slot, ctx].astype(f32)
+        for hop in range(1, n_ctx):
+            copy_of(slot, A_Z + hop - 1).wait_recv()
+            total = total + came_ctx[slot, hop - 1].astype(f32)
+        result[slot] = total
+        each_segment(c, lambda segment, first: out_copy(c, slot, segment, first).start())
+        for kind in range(A_Z + n_ctx - 1):
+            copy_of(slot, kind).wait_send()
+
+        @pl.when(c + held < count)
+        def _():
+            for level, bit in enumerate(low_bits):
+                pl.semaphore_signal(credit.at[level], inc=1, device_id=(dp ^ bit, ctx), device_id_type=MESH)
+            pl.semaphore_signal(credit.at[C_X], inc=1, device_id=(dp ^ bit_x, ctx), device_id_type=MESH)
+            pl.semaphore_signal(credit.at[C_Y], inc=1, device_id=(dp ^ bit_y, ctx), device_id_type=MESH)
+            for hop in range(1, n_ctx):
+                pl.semaphore_signal(
+                    credit.at[C_Z + hop - 1], inc=1, device_id=at_ctx(n_ctx - hop), device_id_type=MESH
+                )
+
+    steps = [partial(step_low, level) for level in range(n_low)] + [step_cross, step_sides, step_own, step_end]
+    ahead = 2
+    for c in range(ahead):
+        y_start(jnp.int32(c))
+
+    def turn(t, carry):
+        @pl.when(t + ahead < count)
+        def _():
+            y_start(t + ahead)
+
+        for step, lag in zip(steps, lags):
+            c = t - lag
+
+            @pl.when((c >= 0) & (c < count))
+            def _():
+                step(c)
+
+        return carry
+
+    lax.fori_loop(0, count + lags[-1], turn, 0)
+    for c in range(max(0, count - held), count):
+        out_wait(jnp.int32(c))
+
+
+def scatter_sums(xs, ys, out_shapes, plan, n_dp, n_ctx, cid=1, lags=None, held=SLOTS_HELD):
+    group, tokens = xs[0].shape[1:]
+    n_low = n_dp.bit_length() - 3
+    rows = group // n_ctx
+    low, f32 = jnp.bfloat16, jnp.float32
+    lags = lags or list(range(n_low + 4))
+    low_shapes = [
+        pltpu.VMEM((held, n_dp >> (level + 1), group, WIDE), low) for level in range(n_low)
+    ]
+    half = group // 2
+    kinds = n_low + 4 + n_ctx - 1
+    return pl.pallas_call(
+        partial(scatter_kernel, n_dp, n_ctx, plan, lags, len(xs), len(ys), len(out_shapes)),
+        out_shape=[jax.ShapeDtypeStruct(shape, f32) for shape in out_shapes],
+        in_specs=[pl.BlockSpec(memory_space=pl.ANY)] * (len(xs) + len(ys)),
+        out_specs=[pl.BlockSpec(memory_space=pltpu.HBM)] * len(out_shapes),
+        scratch_shapes=[
+            pltpu.VMEM((len(xs),) + xs[0].shape, low),
+            pltpu.VMEM((held, tokens, WIDE), low),
+            *low_shapes,
+            *low_shapes,
+            pltpu.VMEM((held, group, WIDE), low),
+            pltpu.VMEM((held, half, WIDE), low),
+            pltpu.VMEM((held, half, WIDE), low),
+            pltpu.VMEM((held, group, WIDE), low),
+            pltpu.VMEM((held, group, WIDE), low),
+            pltpu.VMEM((held, group, WIDE), low),
+            pltpu.VMEM((held, group, WIDE), low),
+            pltpu.VMEM((held, n_ctx, rows, WIDE), low),
+            pltpu.VMEM((held, n_ctx - 1, rows, WIDE), low),
+            pltpu.VMEM((held, rows, WIDE), f32),
+            pltpu.SemaphoreType.DMA((len(xs),)),
+            pltpu.SemaphoreType.DMA((held,)),
+            pltpu.SemaphoreType.DMA((held,)),
+            pltpu.SemaphoreType.DMA((held, kinds)),
+            pltpu.SemaphoreType.DMA((held, kinds)),
+            pltpu.SemaphoreType.REGULAR((n_low + 2 + n_ctx - 1,)),
+        ],
+        compiler_params=pltpu.CompilerParams(
+            collective_id=cid, has_side_effects=True, vmem_limit_bytes=56 * 2**20
+        ),
+        name="scatter_sums",
+    )(*xs, *ys)
+
+
 def passed_along(value, axis, steps):
     count = lax.axis_size(axis)
     leading, last = (max(0, -steps), min(count, count - steps))
@@ -179,74 +458,63 @@
     return out
 
 
-def bit_reversed(value, bits):
-    return sum(1 << (bits - 1 - i) for i in range(bits) if value >> i & 1)
-
-
-def swapped(value, bit):
-    count = lax.axis_size("dp")
-    return lax.ppermute(value, "dp", [(source, source ^ bit) for source in range(count)])
-
-
-def halving_order():
-    count = lax.axis_size("dp")
-    bits = count.bit_length() - 1
-    return sorted(range(count), key=lambda place: bit_reversed(place, bits))
-
-
-def by_place(operand):
-    tokens, rows = operand.shape
-    count = lax.axis_size("dp")
-    blocks = operand.reshape(tokens, count, rows // count)
-    me = lax.axis_index("dp")
-    return jnp.stack(
-        [lax.dynamic_index_in_dim(blocks, me ^ place, 1, False) for place in halving_order()],
-        axis=1,
-    )
-
-
-def token_dot(operand, gradient):
-    return jnp.einsum("tpr,te->pre", operand, gradient, preferred_element_type=jnp.float32)
-
-
-def summed_to_owner(operand, gradient, extra=None):
-    low = jnp.bfloat16
-    count, ctx_count = lax.axis_size("dp"), lax.axis_size("ctx")
-    bits = count.bit_length() - 1
-    operand = operand.reshape(-1, operand.shape[-1])
-    gradient = gradient.reshape(-1, gradient.shape[-1])
-    placed = by_place(operand)
-    half = count // 2
-    sent = token_dot(placed[:, half:], gradient)
-    kept = token_dot(placed[:, :half], gradient)
-    if extra is not None:
-        extra_placed = by_place(extra.T).transpose(1, 2, 0)
-        sent = jnp.concatenate([sent, extra_placed[half:]], axis=-1)
-        kept = jnp.concatenate([kept, extra_placed[:half]], axis=-1)
-    kept = (kept + swapped(sent.astype(low), 1).astype(jnp.float32)).astype(low)
-    for level in range(1, bits - 2):
-        half //= 2
-        came = swapped(kept[half:], 1 << level)
-        kept = (kept[:half].astype(jnp.float32) + came.astype(jnp.float32)).astype(low)
-    own, over_y, over_x, across = kept[0], kept[1], kept[2], kept[3]
-    bit_x, bit_y = count // 4, count // 2
-    rows, columns = own.shape
-    first = rows // 32 * 16
-    by_y = swapped(across[:first], bit_y)
-    by_x = swapped(across[first:], bit_x)
-    over_x = jnp.concatenate([over_x[:first] + by_y, over_x[first:]], axis=0)
-    over_y = jnp.concatenate([over_y[:first], over_y[first:] + by_x], axis=0)
-    came_x = swapped(over_x, bit_x)
-    came_y = swapped(over_y, bit_y)
-    total = own.astype(jnp.float32) + came_x.astype(jnp.float32) + came_y.astype(jnp.float32)
-    total = total.reshape(ctx_count, rows // ctx_count, columns)
-    me = lax.axis_index("ctx")
-    result = lax.dynamic_index_in_dim(total, me, 0, False)
-    for hop in range(1, ctx_count):
-        block = lax.dynamic_index_in_dim(total, lax.rem(me + hop, ctx_count), 0, False).astype(low)
-        came = lax.ppermute(block, "ctx", [(i, (i + hop) % ctx_count) for i in range(ctx_count)])
-        result = result + came.astype(jnp.float32)
-    return result
+def chunk_plan(products, unit):
+    places, n_dp = lax.axis_size("dp") * lax.axis_size("ctx"), lax.axis_size("dp")
+    laid, first_laid, plan, shapes = [], {}, [], []
+    for number, (operand, gradient) in enumerate(products):
+        tokens, rows = operand.shape
+        shard = rows // places
+        shapes.append((shard, gradient.shape[1]))
+        if id(operand) not in first_laid:
+            first_laid[id(operand)] = len(laid)
+            turned = operand.T.reshape(places, shard, tokens)
+            for first in range(0, shard, unit):
+                piece = turned[:, first : first + unit]
+                piece = jnp.pad(piece, ((0, 0), (0, unit - piece.shape[1]), (0, 0)))
+                laid.append(piece.reshape(n_dp, -1, tokens))
+        for piece, first in enumerate(range(0, shard, unit)):
+            plan.append(
+                (
+                    first_laid[id(operand)] + piece,
+                    number,
+                    number,
+                    first,
+                    min(unit, shard - first),
+                    gradient.shape[1] // WIDE,
+                )
+            )
+    return laid, plan, shapes
+
+
+def summed_to_owners(products, small):
+    n_dp, n_ctx = lax.axis_size("dp"), lax.axis_size("ctx")
+    rows, few = small.shape
+    tokens = products[0][0].shape[0]
+    high = small.astype(jnp.bfloat16)
+    rest = (small - high.astype(jnp.float32)).astype(jnp.bfloat16)
+    both = jnp.zeros((tokens, rows), jnp.bfloat16).at[:few].set(high.T).at[few : 2 * few].set(rest.T)
+    pick = jnp.zeros((tokens, WIDE), jnp.bfloat16)
+    pick = pick.at[:few, :few].set(jnp.eye(few, dtype=jnp.bfloat16))
+    pick = pick.at[few : 2 * few, :few].set(jnp.eye(few, dtype=jnp.bfloat16))
+    products = [(both, pick)] + products
+    laid, plan, shapes = chunk_plan(products, rows // (n_dp * n_ctx))
+    sums = scatter_sums(laid, [gradient for _, gradient in products], shapes, plan, n_dp, n_ctx)
+    return sums[0][:, :few], sums[1:]
+
+
+def chunks_of(shards):
+    out = []
+    for place, shard in enumerate(shards):
+        rows, columns = shard.shape
+        unit = max(128, 1408 * 32 // rows // 128 * 128)
+        width = -(-(columns // 128) // -(-columns // unit)) * 128
+        for first in range(0, columns, width):
+            out.append((place, first, min(width, columns - first)))
+    return out
+
+
+def flat(value):
+    return value.reshape(-1, value.shape[-1])
 
 
 def normed(stream, scale_gain):
@@ -423,7 +691,7 @@
     qk_weight, value_weight, out_weight = (weights[1], weights[2], weights[4])
     micro_count, tok_count, model_width = grad_stream.shape
     grad_branch = grad_stream.astype(jnp.bfloat16)
-    grad_out = summed_to_owner(attended_low, grad_branch)
+    grad_out = (flat(attended_low), flat(grad_branch))
     grad_attended = matmul_back(grad_branch, out_weight)
     grad_query, grad_key, grad_value, grad_state, grad_totals = attend_back(grad_attended)
     later_grads = entering((grad_state, grad_totals), layout_info["flags_after"], "ctx", chain_states)
@@ -445,11 +713,15 @@
     grad_pre_low = grad_pre.astype(jnp.bfloat16)
     grad_normed = matmul_back(grad_qk, qk_weight) + matmul_back(grad_pre_low, value_weight)
     grad_input, grad_gain = norm_back(grad_normed)
-    small = jnp.concatenate(
-        [other_gains, grad_gain[:, None], grad_taps, jnp.zeros((model_width, 121), jnp.float32)], axis=1
-    )
-    grad_both = summed_to_owner(normed_low, jnp.concatenate([grad_qk, grad_pre_low], axis=-1), small)
-    return (grad_stream + grad_input, grad_both, grad_out)
+    small = jnp.concatenate([grad_gain[:, None], other_gains, grad_taps], axis=1)
+    operand = flat(normed_low)
+    return (
+        grad_stream + grad_input,
+        (operand, flat(grad_qk)),
+        (operand, flat(grad_pre_low)),
+        grad_out,
+        small,
+    )
 
 
 def window_scores(heads_query, key_ext, window_mask, head_size):
@@ -502,7 +774,7 @@
     micro_count, tok_count, model_width = grad_stream.shape
     head_size = model_width // HEADS
     grad_branch = grad_stream.astype(jnp.bfloat16)
-    grad_out = summed_to_owner(attended, grad_branch)
+    grad_out = (flat(attended), flat(grad_branch))
     grad_attended = (
         matmul_back(grad_branch, out_weight)
         .astype(jnp.bfloat16)
@@ -549,7 +821,7 @@
     grad_qkv = jnp.concatenate(
         [grad_query.reshape(micro_count, tok_count, model_width), own_grads], axis=-1
     ).astype(jnp.bfloat16)
-    grad_qkv_weight = summed_to_owner(normed_low, grad_qkv)
+    grad_qkv_weight = (flat(normed_low), flat(grad_qkv))
     grad_input, grad_gain = norm_back(matmul_back(grad_qkv, qkv_weight))
     return (grad_stream + grad_input, (grad_gain, grad_qkv_weight, grad_out))
 
@@ -572,7 +844,7 @@
     gate_up, down_weight = (weights[1], weights[2])
     hidden_width = down_weight.shape[0]
     grad_branch = grad_stream.astype(jnp.bfloat16)
-    grad_down = summed_to_owner(hidden, grad_branch)
+    grad_down = (flat(hidden), flat(grad_branch))
     grad_hidden = matmul_back(grad_branch, down_weight)
     gate_part = projected[..., :hidden_width]
     up_part = projected[..., hidden_width:]
@@ -580,7 +852,7 @@
     grad_gate = grad_hidden * up_part * sigmoid_gate * (1.0 + gate_part * (1.0 - sigmoid_gate))
     grad_up = grad_hidden * gate_part * sigmoid_gate
     grad_projected = jnp.concatenate([grad_gate, grad_up], axis=-1).astype(jnp.bfloat16)
-    grad_gate_up = summed_to_owner(normed_low, grad_projected)
+    grad_gate_up = (flat(normed_low), flat(grad_projected))
     grad_input, grad_gain = norm_back(matmul_back(grad_projected, gate_up))
     return (grad_stream + grad_input, (grad_gain, grad_gate_up, grad_down))
 
@@ -648,29 +920,41 @@
     )
     grad_stream, grads_ffn_one = ffn_backward(grad_stream, saved_ffn_one, layer_one[5:])
     other_gains = jnp.stack([grads_ffn_one[0], grads_window[0], grads_ffn_two[0]], axis=1)
-    grad_stream, grad_both, grad_out = linear_backward(
+    grad_stream, of_qk, of_values, of_out, small = linear_backward(
         grad_stream, saved_linear, layer_one[:5], layout_info, other_gains
     )
-    qk_width, value_width = (proj_qk.shape[1], proj_values.shape[1])
-    grad_small = grad_both[:, qk_width + value_width :]
+    small, sums = summed_to_owners(
+        [
+            of_qk,
+            of_values,
+            of_out,
+            grads_ffn_one[1],
+            grads_ffn_one[2],
+            grads_window[1],
+            grads_window[2],
+            grads_ffn_two[1],
+            grads_ffn_two[2],
+        ],
+        small,
+    )
     tokens_grad = grad_stream.astype(jnp.bfloat16)[:, None]
     return (
         output,
         tokens_grad,
-        grad_small[:, 3],
-        grad_both[:, :qk_width],
-        grad_both[:, qk_width : qk_width + value_width],
-        grad_small[:, 4:7],
-        grad_out,
-        grad_small[:, 0],
-        grads_ffn_one[1],
-        grads_ffn_one[2],
-        grad_small[:, 1],
-        grads_window[1],
-        grads_window[2],
-        grad_small[:, 2],
-        grads_ffn_two[1],
-        grads_ffn_two[2],
+        small[:, 0],
+        sums[0],
+        sums[1],
+        small[:, 4:7],
+        sums[2],
+        small[:, 1],
+        sums[3],
+        sums[4],
+        small[:, 2],
+        sums[5],
+        sums[6],
+        small[:, 3],
+        sums[7],
+        sums[8],
     )
 
 

time: 1510 us -> 1140 us (0.75)
  waiting for transfers between devices: 444 us -> 155 us
  Pallas kernels: 217 us -> 438 us
  local copies, waits for them, and re-layouts: 239 us -> 112 us
  starting transfers between devices: 146 us -> 58.6 us
  matrix products: 329 us -> 268 us
    ppermute x64 -> x0, waiting for transfers between devices: 358 us -> none  [the longest x24 215 us: summed_to_owner(): lax.ppermute(block, 'ctx', [(i, (i + hop) % ctx_count) for i in range(ctx...]
    pallas_call x0 -> x1, Pallas kernels: none -> 221 us  [scatter_sums(): pl.pallas_call(partial(scatter_kernel, n_dp, n_ctx, plan, lags, len(xs),...]
    unnamed x539 -> x343, local copies, waits for them, and re-layouts: 111 us -> 28.7 us
    ppermute x64 -> x0, starting transfers between devices: 77.1 us -> none  [the longest x24 42.6 us: summed_to_owner(): lax.ppermute(block, 'ctx', [(i, (i + hop) % ctx_count) for i in range(ctx...]
    ppermute x6, waiting for transfers between devices: 0.02 us -> 66.1 us  [entering(): lax.ppermute(a, axis, pairs).astype(own.dtype)]
    dot_general x16 -> x0, matrix products: 59.4 us -> none  [token_dot(): jnp.einsum('tpr,te->pre', operand, gradient, preferred_element_type=jnp.f...]
    dynamic_slice x11 -> x0, local copies, waits for them, and re-layouts: 30.7 us -> none  [the longest x8 28 us: by_place(): lax.dynamic_index_in_dim(blocks, me ^ place, 1, False)]
    another operation x7 -> x2, local copies, waits for them, and re-layouts: 20.1 us -> 0.54 us  [the longest x3 16.2 us: by_place(): blocks = operand.reshape(tokens, count, rows // count)]
  transfers between devices with their start and end apart: 80 -> 16, of which waited for: 33 -> 3; matrix products, arithmetic and copies ran while one was open for 33% -> 17% of each run, Pallas kernels for 0% -> 0%
where the time goes in v2:
time: 1140 us
  Pallas kernels  438 us (38%)
  matrix products  268 us (24%)
  waiting for transfers between devices  155 us (14%)
  local copies, waits for them, and re-layouts  112 us (10%)
  other arithmetic  101 us (9%)
  starting transfers between devices  58.6 us (5%)
    pallas_call x1, Pallas kernels, scatter_sums(): pl.pallas_call(partial(scatter_kernel, n_dp, n_ctx, plan, lags, len(xs),...  221 us
    pallas_call x1, Pallas kernels, gather_all(): pl.pallas_call(partial(gather_kernel, n_dp, n_ctx, chunks, lag, n), out_s...  217 us
    ppermute x6, waiting for transfers between devices, carried_in(): lax.ppermute(a, axis, pairs).astype(own.dtype)  88.5 us
    dot_general x9, matrix products, matmul_back(): jnp.einsum('mte,de->mtd', operand, weight, preferred_element_type=jnp.flo...  66.2 us
    ppermute x6, waiting for transfers between devices, entering(): lax.ppermute(a, axis, pairs).astype(own.dtype)  66.1 us
    dot_general x9, matrix products, matmul(): jnp.einsum('mtd,de->mte', operand, weight, preferred_element_type=jnp.flo...  43.3 us
    dot_general x3, matrix products, attend_linear(): jnp.einsum('mihr,mhre->mihe', features, state_in, precision=highest)  40 us
    dot_general x3, matrix products, end_state(): jnp.einsum('mthr,mthe->mhre', features, head_values, precision=highest)  34.6 us
  transfers between devices with their start and end apart: 16, of which 3 were waited for; matrix products, arithmetic and copies ran while one was open for 17% of the time, Pallas kernels for 0%

profile of v2, /device:TPU:0, one launch (start us, length us, event | category | flops | bytes accessed | tf_op | source)
XLA Modules:
  0.0 1135.0 jit_solution(5413305013623230174)
XLA Ops:
  5.7 216.7 %gather_weights.1 = (bf16[32,32,128]{2,1,0:T(8,128)(2,1)}, bf16[32,32,512]{2,1,0:T(8,128)(2,1)}, bf16[32,32,1024]{2,1,0:T(8,128)(2,1)}, bf16[32,32,1024]{2,1,0:T...) custom-call(bf16[1,32,128]{2,1,0:T(8,128)(2,1)} %bitcast.473, ...), custom_call_target="tpu_custom_call" | custom-call | tf_op jit(solution)/shard_map/gather_weights/pallas_call | solution.py:132
  222.5 2.8 slice_convert_fusion.2
  233.0 7.0 collective-permute-start.4
  240.0 3.0 collective-permute-start.5
  255.7 5.9 multiply_multiply_fusion
  264.5 4.5 fusion.41
  273.7 10.9 convolution_convert_fusion.1
  284.7 3.1 collective-permute-start.1
  287.8 2.4 collective-permute-start.2
  290.2 2.5 collective-permute-start.3
  300.5 88.5 %collective-permute-done.6 = bf16[2,16,273]{2,1,0:T(8,128)(2,1)S(1)} collective-permute-done((bf16[2,16,273]{2,1,0:T(8,128)(2,1)S(1)}, bf16[2,16,273]{2,1,0:T(8,128)(2,1)S(1)}, u32[]{:S(2)}, u32[]{:S(2)}) %collective-permute-start.6) | collective-permute-done | bytes 17504 | tf_op jit(solution)/shard_map/ppermute | solution.py:434
  389.9 9.3 fusion.75
  400.0 12.6 %fusion.107 = f32[2,16,64,256]{3,2,1,0:T(8,128)S(1)} fusion(bf16[2,16,273,64]{2,3,1,0:T(8,128)(2,1)} %collective-permute-done.3, bf16[2,16,273,64]{2,3,1,0:T(8,128)(2,1)} %collective-permute-done.2, bf16[2,16,273,64]{2,3,1,0:T(8,128)(2,1)} %collective-permute-done.1, f32[2]{0:T(128)S(1)} %get-tuple-element.288, f32[2]{0:T(128)S(1)} %get-tuple-element.289, ...), kind=kOutput, calls=%fused_computation.276 | convolution fusion | flops 1728749568 | bytes 14367836 | tf_op jit(solution)/shard_map/jvp(mihr,mhre->mihe)/dot_general | solution.py:638
  412.6 10.5 fusion.31
  424.8 6.2 fusion.118
  432.9 2.4 copy-done.16
  435.3 5.5 multiply_reduce_fusion.15
  442.1 4.1 convolution_convert_fusion
  447.3 25.8 %collective-permute-start.7 = (bf16[2,63,2048]{2,1,0:T(8,128)(2,1)}, bf16[2,63,2048]{2,1,0:T(8,128)(2,1)}, u32[]{:S(2)}, u32[]{:S(2)}) collective-permute-start(bf16[2,63,2048]{2,1,0:T(8,128)(2,1)} %slice.324), channel_id=1, source_target_pairs={{0,1},{1,2},{2,3},{4,5},{5,6},{6,7},{8,9},{9,10},{10,11},{12,13},{... | collective-permute-start | bytes 1548296 | tf_op jit(solution)/shard_map/ppermute | solution.py:425
  479.0 2.9 copy.248
  484.2 2.4 copy.249
  488.9 2.7 copy.282
  493.2 3.3 pad_maximum_fusion.5
  505.9 7.5 fusion.46
  515.1 14.5 %fusion.119 = f32[2,256,5632]{2,1,0:T(8,128)} fusion(bf16[2,256,1024]{2,1,0:T(8,128)(2,1)S(1)} %multiply_convert_fusion.11, bf16[1024,5632,1]{1,0,2:T(8,128)(2,1)} %bitcast.498), kind=kOutput, calls=%fused_computation.285 | convolution fusion | flops 5905580032 | bytes 24117248 | tf_op jit(solution)/shard_map/mtd,de->mte/dot_general | solution.py:527
  529.7 10.4 multiply_convert_fusion.4
  540.2 13.4 %multiply_reduce_fusion.8 = (f32[1024]{0:T(1024)}, f32[2,256]{1,0:T(2,128)S(1)}, f32[2,256,1024]{2,1,0:T(8,128)}) fusion(f32[2,256,1024]{2,1,0:T(8,128)S(1)} %get-tuple-element.271, f32[2,256]{1,0:T(2,128)S(1)} %fusion.85, f32[1024]{0:T(1024)S(1)} %bitcast.458, bf16[1024,5632,1]{1,0,2:T(8,128)(2,1)} %bitcast.499, ...), kind=kOutput, calls=%fused_computation.102 | convolution fusion | flops 5920258560 | bytes 21508096 | tf_op jit(solution)/shard_map/mte,de->mtd/dot_general | solution.py:531
  553.6 2.4 fusion.105
  560.8 6.9 multiply_reduce_fusion
  568.3 3.0 multiply_convert_fusion
  575.1 2.6 fusion.43
  592.4 2.3 copy.231
  594.7 2.9 copy.232
  599.0 8.2 fusion.47
  607.2 4.7 copy.252
  615.6 2.5 copy.250
  619.3 4.8 pad_maximum_fusion.1.refs_21_
  629.6 3.5 scatter-add.6
  633.1 8.2 multiply_reduce_fusion.9
  643.4 9.8 multiply_convert_fusion.2
  653.2 12.8 %multiply_reduce_fusion.10 = (f32[1024]{0:T(1024)S(1)}, f32[2,256]{1,0:T(2,128)S(1)}, f32[2,256,1024]{2,1,0:T(8,128)}) fusion(f32[2,256,1024]{2,1,0:T(8,128)S(1)} %copy-done.10, f32[2,256]{1,0:T(2,128)S(1)} %copy-done.111, f32[1024]{0:T(1024)S(1)} %bitcast.468, bf16[1024,5632,1]{1,0,2:T(8,128)(2,1)} %bitcast.494, ...), kind=kOutput, calls=%fused_computation.104 | convolution fusion | flops 5920258560 | bytes 21508096 | tf_op jit(solution)/shard_map/mte,de->mtd/dot_general | solution.py:531
  666.1 3.6 fusion.110
  669.8 3.7 fusion.32
  673.6 11.4 %convolution_convert_fusion.2 = bf16[2,16,273,64]{2,3,1,0:T(8,128)(2,1)} fusion(f32[2,256,16,64]{1,3,2,0:T(8,128)S(1)} %get-tuple-element.278, f32[2,16,256]{2,1,0:T(8,128)S(1)} %copy-done.101, f32[2,256,16,256]{1,3,2,0:T(8,128)S(1)} %bitcast.382, f32[2,256,16,16]{1,3,2,0:T(8,128)S(1)} %copy-done.71, f32[273]{0:T(512)S(1)} %copy-done.122, ...), kind=kOutput, calls=%fused_computation.129 | convolution fusion | flops 1725360128 | bytes 12164164 | tf_op jit(solution)/shard_map/transpose(jvp(mihr,mhre->mihe))/dot_general | solution.py:638
  689.3 8.1 fusion.77
  700.6 14.0 %fusion.40 = f32[2,16,64,256]{3,2,1,0:T(8,128)} fusion(f32[2,16,256,256]{2,3,1,0:T(8,128)} %get-tuple-element.261, f32[2,256,256]{1,2,0:T(8,128)S(1)} %copy-done.74, f32[2,256,16,64]{1,3,2,0:T(8,128)S(1)} %get-tuple-element.278, f32[2,16,256]{2,1,0:T(8,128)S(1)} %copy-done.101), kind=kOutput, calls=%fused_computation.124 | convolution fusion | flops 1623719936 | bytes 13139968 | tf_op jit(solution)/shard_map/transpose(jvp(mhij,mjhe->mihe))/dot_general | solution.py:635
  714.7 6.5 fusion.2
  721.3 16.0 %multiply_bitcast_fusion.1 = f32[2,256,16,273]{1,3,2,0:T(8,128)} fusion(f32[2,256]{1,0:T(2,128)S(1)} %copy-done.132, f32[2,16,273]{2,1,0:T(8,128)S(1)} %copy-done.95, f32[2,16,256]{2,1,0:T(8,128)S(1)} %get-tuple-element.250, bf16[2,16,273,64]{2,3,1,0:T(8,128)(2,1)} %collective-permute-done.3, bf16[2,16,273,64]{2,3,1,0:T(8,128)(2,1)} %collective-permute-done.2, ...), kind=kOutput, calls=%fused_computation.11 | convolution fusion | flops 1729273856 | bytes 14499992 | tf_op jit(solution)/shard_map/transpose(jvp(mihr,mhre->mihe))/dot_general | solution.py:638
  737.3 8.1 slice_multiply_fusion.1
  745.4 9.7 multiply_reduce_fusion.4
  755.1 3.0 pad_maximum_fusion.refs_17_
  758.1 4.4 fusion.51
  762.5 65.0 %collective-permute-done.10 = bf16[2,16,273]{2,1,0:T(8,128)(2,1)S(1)} collective-permute-done((bf16[2,16,273]{2,1,0:T(8,128)(2,1)S(1)}, bf16[2,16,273]{2,1,0:T(8,128)(2,1)S(1)}, u32[]{:S(2)}, u32[]{:S(2)}) %collective-permute-start.10) | collective-permute-done | bytes 17504 | tf_op jit(solution)/shard_map/ppermute | solution.py:445
  833.3 15.8 %convolution_add_fusion = f32[2,16,64,256]{3,2,1,0:T(8,128)} fusion(f32[2,16,64,256]{3,2,1,0:T(8,128)} %fusion.40, f32[2,256,16,256]{1,3,2,0:T(8,128)} %bitcast.356, f32[2,256,16,16]{1,3,2,0:T(8,128)S(1)} %copy-done.63, f32[273]{0:T(512)S(1)} %copy-done.122, f32[2,256]{1,0:T(2,128)S(1)} %copy-done.103, ...), kind=kOutput, calls=%fused_computation.130 | convolution fusion | flops 1729273856 | bytes 16464988 | tf_op jit(solution)/shard_map/transpose(jvp(mthr,mthe->mhre))/dot_general | solution.py:624
  849.1 3.6 copy.242
  852.8 2.9 multiply_reduce_fusion.7
  858.6 7.9 multiply_bitcast_fusion
  866.5 4.5 slice_multiply_fusion
  871.0 6.7 multiply_reduce_fusion.2
  877.7 3.8 fusion.52
  884.5 2.6 fusion.70
  891.4 3.0 fusion.38
  900.5 221.5 %scatter_sums.1 = (f32[32,512]{1,0:T(8,128)}, f32[32,512]{1,0:T(8,128)}, f32[32,1024]{1,0:T(8,128)}, f32[32,1024]{1,0:T(8,128)}, f32[32,5632]{1,0:T(8,128)}, /*i...) custom-call(bf16[8,128,512]{2,1,0:T(8,128)(2,1)} %bitcast.407, ...), custom_call_target="tpu_custom_call" | custom-call | tf_op jit(solution)/shard_map/scatter_sums/pallas_call | solution.py:388
  1125.0 3.2 fusion.57
  (507 shorter events, 147.4 us)
Async XLA Ops:
  0.6 224.8 %copy-start.11 = (bf16[2,1,256,1024]{3,2,1,0:T(8,128)(2,1)S(1)}, bf16[2,1,256,1024]{3,2,1,0:T(8,128)(2,1)}, u32[]{:S(2)}) copy-start(bf16[2,1,256,1024]{3,2,1,0:T(8,128)(2,1)} %param.29) | copy-start | bytes 3145732
  225.5 17.5 %copy-start.96 = (f32[1024,1]{0,1:T(1,128)}, f32[1024,1]{0,1:T(1,128)S(1)}, u32[]{:S(2)}) copy-start(f32[1024,1]{0,1:T(1,128)S(1)} %copy.287) | copy-start | bytes 12292
  225.8 17.2 %copy-start.118 = (f32[2,256]{1,0:T(2,128)}, f32[2,256]{1,0:T(2,128)S(1)}, u32[]{:S(2)}) copy-start(f32[2,256]{1,0:T(2,128)S(1)} %fusion.82) | copy-start | bytes 6148
  227.8 23.7 %copy-start.112 = (s32[2,4]{1,0:T(2,128)}, s32[2,4]{1,0:T(2,128)S(1)}, u32[]{:S(2)}) copy-start(s32[2,4]{1,0:T(2,128)S(1)} %reduce_window_sum.11) | copy-start | bytes 100
  230.2 38.8 %copy-start.90 = (f32[2,256]{1,0:T(2,128)}, f32[2,256]{1,0:T(2,128)S(1)}, u32[]{:S(2)}) copy-start(f32[2,256]{1,0:T(2,128)S(1)} %get-tuple-element.256) | copy-start | bytes 6148
  230.3 38.8 %copy-start.92 = (f32[2,256]{1,0:T(2,128)}, f32[2,256]{1,0:T(2,128)S(1)}, u32[]{:S(2)}) copy-start(f32[2,256]{1,0:T(2,128)S(1)} %get-tuple-element.259) | copy-start | bytes 6148
  230.3 43.5 %copy-start.102 = (f32[2,256]{1,0:T(2,128)}, f32[2,256]{1,0:T(2,128)S(1)}, u32[]{:S(2)}) copy-start(f32[2,256]{1,0:T(2,128)S(1)} %get-tuple-element.258) | copy-start | bytes 6148
  230.3 12.7 %copy-start.137 = (bf16[32,32,1024]{2,1,0:T(8,128)(2,1)S(1)}, bf16[32,32,1024]{2,1,0:T(8,128)(2,1)}, u32[]{:S(2)}) copy-start(bf16[32,32,1024]{2,1,0:T(8,128)(2,1)} %get-tuple-element.109) | copy-start | bytes 6291460
  233.0 59.7 %collective-permute-start.4 = (bf16[2,16,273]{2,1,0:T(8,128)(2,1)S(1)}, bf16[2,16,273]{2,1,0:T(8,128)(2,1)}, u32[]{:S(2)}, u32[]{:S(2)}) collective-permute-start(bf16[2,16,273]{2,1,0:T(8,128)(2,1)S(1)} %fusion.104), channel_id=1, source_target_pairs={{0,1},{1,2},{2,3},{4,5},{5,6},{6,7},{8,9},{9,10},{10,11},{12,13},{... | collective-permute-start | bytes 52424 | tf_op jit(solution)/shard_map/ppermute | solution.py:434
  240.0 60.5 %collective-permute-start.5 = (bf16[2,16,273]{2,1,0:T(8,128)(2,1)S(1)}, bf16[2,16,273]{2,1,0:T(8,128)(2,1)}, u32[]{:S(2)}, u32[]{:S(2)}) collective-permute-start(bf16[2,16,273]{2,1,0:T(8,128)(2,1)S(1)} %fusion.104), channel_id=1, source_target_pairs={{0,2},{1,3},{4,6},{5,7},{8,10},{9,11},{12,14},{13,15},{16,18},{17,... | collective-permute-start | bytes 52424 | tf_op jit(solution)/shard_map/ppermute | solution.py:434
  244.3 24.8 %copy-start.3 = (f32[2,256,1024]{2,1,0:T(8,128)}, f32[2,256,1024]{2,1,0:T(8,128)S(1)}, u32[]{:S(2)}) copy-start(f32[2,256,1024]{2,1,0:T(8,128)S(1)} %fusion.64) | copy-start | bytes 6291460
  244.9 24.1 %collective-permute-start = (f32[2,2,1024]{2,1,0:T(2,128)}, f32[2,2,1024]{2,1,0:T(2,128)S(1)}, u32[]{:S(2)}, u32[]{:S(2)}) collective-permute-start(f32[2,2,1024]{2,1,0:T(2,128)} %slice.312), channel_id=1, source_target_pairs={{0,1},{1,2},{2,3},{4,5},{5,6},{6,7},{8,9},{9,10},{10,11},{12,13},{... | collective-permute-start | bytes 49160 | tf_op jit(solution)/shard_map/ppermute | solution.py:425
  248.5 13.2 %copy-start.41 = (bf16[2,256,256]{1,2,0:T(8,128)(2,1)}, bf16[2,256,256]{1,2,0:T(8,128)(2,1)S(1)}, u32[]{:S(2)}) copy-start(bf16[2,256,256]{1,2,0:T(8,128)(2,1)S(1)} %copy.218) | copy-start | bytes 786436
  255.6 13.5 %copy-start.83 = (f32[1024,1]{0,1:T(1,128)}, f32[1024,1]{0,1:T(1,128)S(1)}, u32[]{:S(2)}) copy-start(f32[1024,1]{0,1:T(1,128)S(1)} %get-tuple-element.251) | copy-start | bytes 12292
  255.6 13.5 %copy-start.85 = (f32[1024,1]{0,1:T(1,128)}, f32[1024,1]{0,1:T(1,128)S(1)}, u32[]{:S(2)}) copy-start(f32[1024,1]{0,1:T(1,128)S(1)} %get-tuple-element.252) | copy-start | bytes 12292
  255.6 13.5 %copy-start.87 = (f32[1024,1]{0,1:T(1,128)}, f32[1024,1]{0,1:T(1,128)S(1)}, u32[]{:S(2)}) copy-start(f32[1024,1]{0,1:T(1,128)S(1)} %get-tuple-element.253) | copy-start | bytes 12292
  262.4 137.5 %copy-start.127 = (f32[2]{0:T(128)}, f32[2]{0:T(128)S(1)}, u32[]{:S(2)}) copy-start(f32[2]{0:T(128)S(1)} %get-tuple-element.288) | copy-start | bytes 28
  262.4 137.5 %copy-start.129 = (f32[2]{0:T(128)}, f32[2]{0:T(128)S(1)}, u32[]{:S(2)}) copy-start(f32[2]{0:T(128)S(1)} %get-tuple-element.289) | copy-start | bytes 28
  269.0 15.7 %copy-start.114 = (f32[256]{0:T(256)}, f32[256]{0:T(256)S(1)}, u32[]{:S(2)}) copy-start(f32[256]{0:T(256)S(1)} %compare_convert_fusion.3) | copy-start | bytes 3076
  269.0 15.7 %copy-start.78 = (f32[2,2,1024]{2,1,0:T(2,128)}, f32[2,2,1024]{2,1,0:T(2,128)S(1)}, u32[]{:S(2)}) copy-start(f32[2,2,1024]{2,1,0:T(2,128)S(1)} %collective-permute-done) | copy-start | bytes 49156
  273.7 24.5 %copy-start.31 = (f32[2,1,256,1024]{3,2,0,1:T(8,128)S(1)}, f32[2,1,256,1024]{3,2,0,1:T(8,128)}, u32[]{:S(2)}) copy-start(f32[2,1,256,1024]{3,2,0,1:T(8,128)} %bitcast_convert_fusion.2) | copy-start | bytes 6291460
  284.7 115.2 %collective-permute-start.1 = (bf16[2,16,273,64]{2,3,1,0:T(8,128)(2,1)}, bf16[2,16,273,64]{2,3,1,0:T(8,128)(2,1)}, u32[]{:S(2)}, u32[]{:S(2)}) collective-permute-start(bf16[2,16,273,64]{2,3,1,0:T(8,128)(2,1)} %convolution_convert_fusion.1), channel_id=1, source_target_pairs={{0,1},{1,2},{2,3},{4,5},{5,6},{6,7},{8,9},{9,10},{10,11},{12,13},{... | collective-permute-start | bytes 3354632 | tf_op jit(solution)/shard_map/ppermute | solution.py:434
  287.8 112.1 %collective-permute-start.2 = (bf16[2,16,273,64]{2,3,1,0:T(8,128)(2,1)}, bf16[2,16,273,64]{2,3,1,0:T(8,128)(2,1)}, u32[]{:S(2)}, u32[]{:S(2)}) collective-permute-start(bf16[2,16,273,64]{2,3,1,0:T(8,128)(2,1)} %convolution_convert_fusion.1), channel_id=1, source_target_pairs={{0,2},{1,3},{4,6},{5,7},{8,10},{9,11},{12,14},{13,15},{16,18},{17,... | collective-permute-start | bytes 3354632 | tf_op jit(solution)/shard_map/ppermute | solution.py:434
  290.2 109.7 %collective-permute-start.3 = (bf16[2,16,273,64]{2,3,1,0:T(8,128)(2,1)}, bf16[2,16,273,64]{2,3,1,0:T(8,128)(2,1)}, u32[]{:S(2)}, u32[]{:S(2)}) collective-permute-start(bf16[2,16,273,64]{2,3,1,0:T(8,128)(2,1)} %convolution_convert_fusion.1), channel_id=1, source_target_pairs={{0,3},{4,7},{8,11},{12,15},{16,19},{20,23},{24,27},{28,31}} | collective-permute-start | bytes 3354632 | tf_op jit(solution)/shard_map/ppermute | solution.py:434
  292.7 107.3 %copy-start.134 = (f32[2]{0:T(128)}, f32[2]{0:T(128)S(1)}, u32[]{:S(2)}) copy-start(f32[2]{0:T(128)S(1)} %convert_subtract_fusion.3) | copy-start | bytes 28
  292.7 96.3 %collective-permute-start.6 = (bf16[2,16,273]{2,1,0:T(8,128)(2,1)S(1)}, bf16[2,16,273]{2,1,0:T(8,128)(2,1)S(1)}, u32[]{:S(2)}, u32[]{:S(2)}) collective-permute-start(bf16[2,16,273]{2,1,0:T(8,128)(2,1)S(1)} %fusion.104), channel_id=1, source_target_pairs={{0,3},{4,7},{8,11},{12,15},{16,19},{20,23},{24,27},{28,31}} | collective-permute-start | bytes 52424 | tf_op jit(solution)/shard_map/ppermute | solution.py:434
  295.8 128.8 %copy-start.98 = (f32[1024,1]{0,1:T(1,128)}, f32[1024,1]{0,1:T(1,128)S(1)}, u32[]{:S(2)}) copy-start(f32[1024,1]{0,1:T(1,128)S(1)} %copy.288) | copy-start | bytes 12292
  295.8 94.1 %copy-start.131 = (f32[2,256]{1,0:T(2,128)S(1)}, f32[2,256]{1,0:T(2,128)}, u32[]{:S(2)}) copy-start(f32[2,256]{1,0:T(2,128)} %get-tuple-element.257) | copy-start | bytes 6148
  300.5 98.8 %copy-start.61 = (bf16[512,512]{1,0:T(8,128)(2,1)}, bf16[512,512]{1,0:T(8,128)(2,1)S(1)}, u32[]{:S(2)}) copy-start(bf16[512,512]{1,0:T(8,128)(2,1)S(1)} %scatter.19.refs_13_) | copy-start | bytes 1572868
  399.9 12.7 %copy-start.100 = (f32[2,16,256]{2,1,0:T(8,128)}, f32[2,16,256]{2,1,0:T(8,128)S(1)}, u32[]{:S(2)}) copy-start(f32[2,16,256]{2,1,0:T(8,128)S(1)} %get-tuple-element.222) | copy-start | bytes 98308
  399.9 12.7 %copy-start.47 = (bf16[2,256,1024]{1,2,0:T(8,128)(2,1)S(1)}, bf16[2,256,1024]{1,2,0:T(8,128)(2,1)}, u32[]{:S(2)}) copy-start(bf16[2,256,1024]{1,2,0:T(8,128)(2,1)} %copy.217) | copy-start | bytes 3145732
  399.9 12.7 %copy-start.73 = (f32[2,256,256]{1,2,0:T(8,128)S(1)}, f32[2,256,256]{1,2,0:T(8,128)}, u32[]{:S(2)}) copy-start(f32[2,256,256]{1,2,0:T(8,128)} %copy-done.72) | copy-start | bytes 1572868
  400.0 24.8 %slice-start.11 = ((s8[11534336]{0:T(1024)(128)(4,1)}), s8[4194304]{0:T(1024)(128)(4,1)S(1)}, s32[]{:S(2)}) async-start(s8[11534336]{0:T(1024)(128)(4,1)} %bitcast.495), calls=%async_computation.11 | async-start | bytes 8388608
  400.0 24.8 %slice-start.12 = ((s8[11534336]{0:T(1024)(128)(4,1)}), s8[4194304]{0:T(1024)(128)(4,1)S(1)}, s32[]{:S(2)}) async-start(s8[11534336]{0:T(1024)(128)(4,1)} %bitcast.495), calls=%async_computation.12 | async-start | bytes 8388608
  412.6 10.5 copy-start.56
  412.6 10.5 copy-start.19
  412.6 12.2 %slice-start.13 = ((s8[11534336]{0:T(1024)(128)(4,1)}), s8[3145728]{0:T(1024)(128)(4,1)S(1)}, s32[]{:S(2)}) async-start(s8[11534336]{0:T(1024)(128)(4,1)} %bitcast.495), calls=%async_computation.13 | async-start | bytes 6291456
  424.5 10.8 copy-start.9
  446.2 28.4 %copy-start.33 = (bf16[2,256,3072]{2,1,0:T(8,128)(2,1)}, bf16[2,256,3072]{2,1,0:T(8,128)(2,1)S(1)}, u32[]{:S(2)}) copy-start(bf16[2,256,3072]{2,1,0:T(8,128)(2,1)S(1)} %convolution_convert_fusion) | copy-start | bytes 9437188
  447.3 45.9 %collective-permute-start.7 = (bf16[2,63,2048]{2,1,0:T(8,128)(2,1)}, bf16[2,63,2048]{2,1,0:T(8,128)(2,1)}, u32[]{:S(2)}, u32[]{:S(2)}) collective-permute-start(bf16[2,63,2048]{2,1,0:T(8,128)(2,1)} %slice.324), channel_id=1, source_target_pairs={{0,1},{1,2},{2,3},{4,5},{5,6},{6,7},{8,9},{9,10},{10,11},{12,13},{... | collective-permute-start | bytes 1548296 | tf_op jit(solution)/shard_map/ppermute | solution.py:425
  513.5 16.2 %slice-start.16 = ((s8[5767168]{0:T(1024)(128)(4,1)}), s8[4194304]{0:T(1024)(128)(4,1)S(1)}, s32[]{:S(2)}) async-start(s8[5767168]{0:T(1024)(128)(4,1)} %bitcast.507), calls=%async_computation.16 | async-start | bytes 8388608
  514.8 38.8 %copy-start.7 = (f32[2,256,1024]{2,1,0:T(8,128)}, f32[2,256,1024]{2,1,0:T(8,128)S(1)}, u32[]{:S(2)}) copy-start(f32[2,256,1024]{2,1,0:T(8,128)S(1)} %get-tuple-element.271) | copy-start | bytes 6291460
  515.1 14.6 %copy-start.51 = (bf16[2,256,1024]{2,1,0:T(8,128)(2,1)}, bf16[2,256,1024]{2,1,0:T(8,128)(2,1)S(1)}, u32[]{:S(2)}) copy-start(bf16[2,256,1024]{2,1,0:T(8,128)(2,1)S(1)} %multiply_convert_fusion.11) | copy-start | bytes 3145732
  515.1 14.6 %copy-start.26 = (bf16[2,1,256,1024]{3,2,1,0:T(8,128)(2,1)S(1)}, bf16[2,1,256,1024]{3,2,1,0:T(8,128)(2,1)}, u32[]{:S(2)}) copy-start(bf16[2,1,256,1024]{3,2,1,0:T(8,128)(2,1)} %param.45) | copy-start | bytes 3145732
  515.1 14.6 %copy-start.109 = (f32[2,256]{1,0:T(2,128)S(1)}, f32[2,256]{1,0:T(2,128)}, u32[]{:S(2)}) copy-start(f32[2,256]{1,0:T(2,128)} %compare_convert_fusion) | copy-start | bytes 6148
  515.1 14.6 %slice-start.17 = ((s8[5767168]{0:T(1024)(128)(4,1)}), s8[1572864]{0:T(1024)(128)(4,1)S(1)}, s32[]{:S(2)}) async-start(s8[5767168]{0:T(1024)(128)(4,1)} %bitcast.507), calls=%async_computation.17 | async-start | bytes 3145728
  591.1 37.3 %collective-permute-start.8 = (bf16[2,63,2048]{2,1,0:T(8,128)(2,1)}, bf16[2,63,2048]{2,1,0:T(8,128)(2,1)}, u32[]{:S(2)}, u32[]{:S(2)}) collective-permute-start(bf16[2,63,2048]{2,1,0:T(8,128)(2,1)} %pad_maximum_fusion.6), channel_id=1, source_target_pairs={{1,0},{2,1},{3,2},{5,4},{6,5},{7,6},{9,8},{10,9},{11,10},{13,12},{... | collective-permute-start | bytes 1548296 | tf_op jit(solution)/shard_map/ppermute | solution.py:425
  642.6 10.6 copy-start.55
  653.2 12.8 %copy-start.105 = (f32[2,256]{1,0:T(2,128)S(1)}, f32[2,256]{1,0:T(2,128)}, u32[]{:S(2)}) copy-start(f32[2,256]{1,0:T(2,128)} %copy-done.104) | copy-start | bytes 6148
  685.0 148.3 %collective-permute-start.12 = (bf16[2,16,273,64]{2,3,1,0:T(8,128)(2,1)}, bf16[2,16,273,64]{2,3,1,0:T(8,128)(2,1)}, u32[]{:S(2)}, u32[]{:S(2)}) collective-permute-start(bf16[2,16,273,64]{2,3,1,0:T(8,128)(2,1)} %convolution_convert_fusion.2), channel_id=1, source_target_pairs={{1,0},{2,1},{3,2},{5,4},{6,5},{7,6},{9,8},{10,9},{11,10},{13,12},{... | collective-permute-start | bytes 3354632 | tf_op jit(solution)/shard_map/ppermute | solution.py:445
  686.3 147.0 %collective-permute-start.13 = (bf16[2,16,273,64]{2,3,1,0:T(8,128)(2,1)}, bf16[2,16,273,64]{2,3,1,0:T(8,128)(2,1)}, u32[]{:S(2)}, u32[]{:S(2)}) collective-permute-start(bf16[2,16,273,64]{2,3,1,0:T(8,128)(2,1)} %convolution_convert_fusion.2), channel_id=1, source_target_pairs={{2,0},{3,1},{6,4},{7,5},{10,8},{11,9},{14,12},{15,13},{18,16},{19,... | collective-permute-start | bytes 3354632 | tf_op jit(solution)/shard_map/ppermute | solution.py:445
  687.6 145.7 %collective-permute-start.14 = (bf16[2,16,273,64]{2,3,1,0:T(8,128)(2,1)}, bf16[2,16,273,64]{2,3,1,0:T(8,128)(2,1)}, u32[]{:S(2)}, u32[]{:S(2)}) collective-permute-start(bf16[2,16,273,64]{2,3,1,0:T(8,128)(2,1)} %convolution_convert_fusion.2), channel_id=1, source_target_pairs={{3,0},{7,4},{11,8},{15,12},{19,16},{23,20},{27,24},{31,28}} | collective-permute-start | bytes 3354632 | tf_op jit(solution)/shard_map/ppermute | solution.py:445
  689.3 11.3 copy-start.74
  697.5 17.2 %slice-start.18 = ((s8[8388608]{0:T(1024)(128)(4,1)}), s8[4194304]{0:T(1024)(128)(4,1)S(1)}, s32[]{:S(2)}) async-start(s8[8388608]{0:T(1024)(128)(4,1)} %bitcast.514), calls=%async_computation.18 | async-start | bytes 8388608
  697.5 17.2 %copy-start.48 = (bf16[2,256,1024]{1,2,0:T(8,128)(2,1)S(1)}, bf16[2,256,1024]{1,2,0:T(8,128)(2,1)}, u32[]{:S(2)}) copy-start(bf16[2,256,1024]{1,2,0:T(8,128)(2,1)} %copy.217) | copy-start | bytes 3145732
  697.5 17.2 %slice-start.19 = ((s8[8388608]{0:T(1024)(128)(4,1)}), s8[4194304]{0:T(1024)(128)(4,1)S(1)}, s32[]{:S(2)}) async-start(s8[8388608]{0:T(1024)(128)(4,1)} %bitcast.514), calls=%async_computation.19 | async-start | bytes 8388608
  697.5 130.0 %collective-permute-start.10 = (bf16[2,16,273]{2,1,0:T(8,128)(2,1)S(1)}, bf16[2,16,273]{2,1,0:T(8,128)(2,1)S(1)}, u32[]{:S(2)}, u32[]{:S(2)}) collective-permute-start(bf16[2,16,273]{2,1,0:T(8,128)(2,1)S(1)} %bitcast.476), channel_id=1, source_target_pairs={{2,0},{3,1},{6,4},{7,5},{10,8},{11,9},{14,12},{15,13},{18,16},{19,... | collective-permute-start | bytes 52424 | tf_op jit(solution)/shard_map/ppermute | solution.py:445
  699.1 133.0 %collective-permute-start.11 = (bf16[2,16,273]{2,1,0:T(8,128)(2,1)S(1)}, bf16[2,16,273]{2,1,0:T(8,128)(2,1)S(1)}, u32[]{:S(2)}, u32[]{:S(2)}) collective-permute-start(bf16[2,16,273]{2,1,0:T(8,128)(2,1)S(1)} %bitcast.477), channel_id=1, source_target_pairs={{3,0},{7,4},{11,8},{15,12},{19,16},{23,20},{27,24},{31,28}} | collective-permute-start | bytes 52424 | tf_op jit(solution)/shard_map/ppermute | solution.py:445
  721.3 36.8 %copy-start.1 = (f32[2,16,256,256]{2,3,1,0:T(8,128)}, f32[2,16,256,256]{2,3,1,0:T(8,128)S(1)}, u32[]{:S(2)}) copy-start(f32[2,16,256,256]{2,3,1,0:T(8,128)S(1)} %fusion.2) | copy-start | bytes 25165828
  758.1 70.7 %copy-start.29 = (bf16[2,256,2048]{2,1,0:T(8,128)(2,1)S(1)}, bf16[2,256,2048]{2,1,0:T(8,128)(2,1)}, u32[]{:S(2)}) copy-start(bf16[2,256,2048]{2,1,0:T(8,128)(2,1)} %scatter-add.6) | copy-start | bytes 6291460
  758.1 70.7 %copy-start.50 = (bf16[512,1024]{1,0:T(8,128)(2,1)S(1)}, bf16[512,1024]{1,0:T(8,128)(2,1)}, u32[]{:S(2)}) copy-start(bf16[512,1024]{1,0:T(8,128)(2,1)} %reshape.1002) | copy-start | bytes 3145732
  827.5 5.7 collective-permute-start.9
  882.0 7.4 collective-permute-start.15
  900.5 224.5 %copy-start.34 = (f32[2,256,1024]{2,1,0:T(8,128)S(1)}, f32[2,256,1024]{2,1,0:T(8,128)}, u32[]{:S(2)}) copy-start(f32[2,256,1024]{2,1,0:T(8,128)} %get-tuple-element.224) | copy-start | bytes 6291460
  (113 other events, 544.0 us)

commit v3 on v2

--- a/solution.py
+++ b/solution.py
@@ -3,6 +3,7 @@
 
 import jax
 import jax.numpy as jnp
+import numpy as np
 from jax import lax
 from jax.experimental import pallas as pl
 from jax.experimental.pallas import tpu as pltpu
@@ -21,9 +22,65 @@
 
 MESH = pl.DeviceIdType.MESH
 
-def gather_kernel(n_dp, n_ctx, chunks, lag, n_w, *refs):
-    ins, outs = refs[:n_w], refs[n_w:2 * n_w]
-    local_sem, send_sem, recv_sem = refs[2 * n_w:]
+def carried(sign, n_ctx, dp, ctx, own, keep, out, came, total, sent, arrived):
+    first, last = (0, n_ctx - 1) if sign > 0 else (n_ctx - 1, 0)
+    low, f32 = jnp.bfloat16, jnp.float32
+    planes, rows = own.shape[1:3]
+
+    def copy(m):
+        return pltpu.make_async_remote_copy(
+            src_ref=total.at[m],
+            dst_ref=came.at[m],
+            send_sem=sent.at[m],
+            recv_sem=arrived.at[m],
+            device_id=(dp, lax.rem(ctx + sign + n_ctx, n_ctx)),
+            device_id_type=MESH,
+        )
+
+    def act(m):
+        @pl.when(ctx != first)
+        def _():
+            copy(m).wait_recv()
+            for p in range(planes):
+                value = came[m, p]
+                out[m, p, :rows] = value
+                total[m, p] = (own[m, p].astype(f32) + keep[m, 0:1] * value.astype(f32)).astype(low)
+
+        @pl.when(ctx == first)
+        def _():
+            for p in range(planes):
+                out[m, p, :rows] = jnp.zeros((rows, 128), low)
+                total[m, p] = own[m, p]
+
+        @pl.when(ctx != last)
+        def _():
+            copy(m).start()
+
+    def finish():
+        for m in range(own.shape[0]):
+            for p in range(planes):
+                out[m, p, rows:] = jnp.zeros((out.shape[2] - rows, 128), low)
+
+        @pl.when(ctx != last)
+        def _():
+            for m in range(own.shape[0]):
+                copy(m).wait_send()
+
+    return act, finish
+
+
+def carry_specs(state):
+    whole = pl.BlockSpec(memory_space=pltpu.VMEM)
+    shape = state.shape[:2] + (TERMS,) + state.shape[3:]
+    held = pltpu.VMEM(state.shape, jnp.bfloat16)
+    sems = pltpu.SemaphoreType.DMA((state.shape[0],))
+    return [whole, whole], [whole], [jax.ShapeDtypeStruct(shape, jnp.bfloat16)], [held, held, sems, sems]
+
+
+def gather_kernel(n_dp, n_ctx, chunks, lag, n_w, carry, *refs):
+    n_c = 2 if carry else 0
+    ins, outs = refs[:n_w], refs[n_w + n_c:2 * n_w + n_c]
+    local_sem, send_sem, recv_sem = refs[2 * n_w + 3 * n_c // 2:][:3]
     dp, ctx = lax.axis_index("dp"), lax.axis_index("ctx")
     bits = [1 << i for i in range(n_dp.bit_length() - 1)]
     low_bits, (bit_x, bit_y) = bits[:-2], bits[-2:]
@@ -117,36 +174,54 @@
 
     stages = [stage_ctx, stage_sides, stage_diag] + [partial(stage_low, level=l) for l in range(len(low_bits) + 1)]
     depth = len(stages)
-    for t in range(len(chunks) + (depth - 1) * lag):
+    turns = len(chunks) + (depth - 1) * lag
+    due = {}
+    if carry:
+        own, keep = refs[n_w:n_w + 2]
+        act, finish = carried(carry, n_ctx, dp, ctx, own, keep, refs[2 * n_w + 2], *refs[2 * n_w + 6:])
+        micro = own.shape[0]
+        for n in range(n_ctx * micro):
+            due.setdefault(n * turns // (n_ctx * micro), []).append((n // micro, n % micro))
+    for t in range(turns):
+        for place, m in due.get(t, []):
+            @pl.when(ctx == (place if carry > 0 else n_ctx - 1 - place))
+            def _():
+                act(m)
         for s in range(depth):
             c = t - s * lag
             if 0 <= c < len(chunks):
                 stages[s](c)
+    if carry:
+        finish()
     for copy in sends:
         copy.wait_send()
 
-def gather_all(weights, n_dp, n_ctx, chunks, lag=1, cid=0):
+def gather_all(weights, n_dp, n_ctx, chunks, lag=1, cid=0, carry=0, state=()):
     n = len(weights)
     places = n_dp * n_ctx
     slots = n_ctx - 1 + 4 + 4 * (n_dp // 4 - 1)
+    more_in, more_out, more_shape, more_scratch = carry_specs(state[0]) if carry else ([], [], [], [])
     full = pl.pallas_call(
-        partial(gather_kernel, n_dp, n_ctx, chunks, lag, n),
-        out_shape=[jax.ShapeDtypeStruct((places,) + w.shape, w.dtype) for w in weights],
-        in_specs=[pl.BlockSpec(memory_space=pltpu.HBM)] * n,
-        out_specs=[pl.BlockSpec(memory_space=pltpu.HBM)] * n,
-        scratch_shapes=[pltpu.SemaphoreType.DMA((len(chunks),)), pltpu.SemaphoreType.DMA((len(chunks), slots)), pltpu.SemaphoreType.DMA((len(chunks), slots))],
+        partial(gather_kernel, n_dp, n_ctx, chunks, lag, n, carry),
+        out_shape=[jax.ShapeDtypeStruct((places,) + w.shape, w.dtype) for w in weights] + more_shape,
+        in_specs=[pl.BlockSpec(memory_space=pltpu.HBM)] * n + more_in,
+        out_specs=[pl.BlockSpec(memory_space=pltpu.HBM)] * n + more_out,
+        scratch_shapes=[pltpu.SemaphoreType.DMA((len(chunks),)), pltpu.SemaphoreType.DMA((len(chunks), slots)), pltpu.SemaphoreType.DMA((len(chunks), slots))]
+        + more_scratch,
         compiler_params=pltpu.CompilerParams(collective_id=cid, has_side_effects=True),
-        name="gather_weights")(*[w[None] for w in weights])
-    return [f.reshape(places * f.shape[1], f.shape[2]) for f in full]
+        name="gather_weights")(*[w[None] for w in weights], *state)
+    return [f.reshape(places * f.shape[1], f.shape[2]) for f in full[:n]] + list(full[n:])
 
 
 WIDE = 512
 SLOTS_HELD = 8
 
 
-def scatter_kernel(n_dp, n_ctx, plan, lags, n_x, n_y, n_o, *refs):
-    xs, ys, outs = refs[:n_x], refs[n_x : n_x + n_y], refs[n_x + n_y : n_x + n_y + n_o]
-    refs = refs[n_x + n_y + n_o :]
+def scatter_kernel(n_dp, n_ctx, plan, lags, n_x, n_y, n_o, carry, *refs):
+    xs, ys, refs = refs[:n_x], refs[n_x : n_x + n_y], refs[n_x + n_y :]
+    state, refs = (refs[:2], refs[2:]) if carry else ((), refs)
+    outs, refs = refs[:n_o], refs[n_o:]
+    state_out, refs = (refs[:1], refs[1:]) if carry else ((), refs)
     bits = [1 << i for i in range(n_dp.bit_length() - 1)]
     low_bits, (bit_x, bit_y) = bits[:-2], bits[-2:]
     n_low = len(low_bits)
@@ -154,7 +229,7 @@
     low_out, low_in = refs[2 : 2 + n_low], refs[2 + n_low : 2 + 2 * n_low]
     refs = refs[2 + 2 * n_low :]
     cross, cross_y, cross_x, side_x, side_y, came_x, came_y, shards, came_ctx, result = refs[:10]
-    x_sem, y_sem, out_sem, sent, arrived, credit = refs[10:]
+    x_sem, y_sem, out_sem, sent, arrived, credit = refs[10:16]
     held = y_all.shape[0]
     dp, ctx = lax.axis_index("dp"), lax.axis_index("ctx")
     group = cross.shape[1]
@@ -355,7 +430,21 @@
     for c in range(ahead):
         y_start(jnp.int32(c))
 
-    def turn(t, carry):
+    turns = count + lags[-1]
+    if carry:
+        act, finish = carried(carry, n_ctx, dp, ctx, *state, *state_out, *refs[16:])
+        micro = state[0].shape[0]
+        stride = turns // (n_ctx * micro)
+        place = ctx if carry > 0 else n_ctx - 1 - ctx
+
+    def turn(t, none):
+        if carry:
+            for m in range(micro):
+
+                @pl.when(t == (place * micro + m) * stride)
+                def _():
+                    act(m)
+
         @pl.when(t + ahead < count)
         def _():
             y_start(t + ahead)
@@ -367,14 +456,16 @@
             def _():
                 step(c)
 
-        return carry
-
-    lax.fori_loop(0, count + lags[-1], turn, 0)
+        return none
+
+    lax.fori_loop(0, turns, turn, 0)
+    if carry:
+        finish()
     for c in range(max(0, count - held), count):
         out_wait(jnp.int32(c))
 
 
-def scatter_sums(xs, ys, out_shapes, plan, n_dp, n_ctx, cid=1, lags=None, held=SLOTS_HELD):
+def scatter_sums(xs, ys, out_shapes, plan, n_dp, n_ctx, cid=1, carry=0, state=(), lags=None, held=SLOTS_HELD):
     group, tokens = xs[0].shape[1:]
     n_low = n_dp.bit_length() - 3
     rows = group // n_ctx
@@ -385,11 +476,12 @@
     ]
     half = group // 2
     kinds = n_low + 4 + n_ctx - 1
+    more_in, more_out, more_shape, more_scratch = carry_specs(state[0]) if carry else ([], [], [], [])
     return pl.pallas_call(
-        partial(scatter_kernel, n_dp, n_ctx, plan, lags, len(xs), len(ys), len(out_shapes)),
-        out_shape=[jax.ShapeDtypeStruct(shape, f32) for shape in out_shapes],
-        in_specs=[pl.BlockSpec(memory_space=pl.ANY)] * (len(xs) + len(ys)),
-        out_specs=[pl.BlockSpec(memory_space=pltpu.HBM)] * len(out_shapes),
+        partial(scatter_kernel, n_dp, n_ctx, plan, lags, len(xs), len(ys), len(out_shapes), carry),
+        out_shape=[jax.ShapeDtypeStruct(shape, f32) for shape in out_shapes] + more_shape,
+        in_specs=[pl.BlockSpec(memory_space=pl.ANY)] * (len(xs) + len(ys)) + more_in,
+        out_specs=[pl.BlockSpec(memory_space=pltpu.HBM)] * len(out_shapes) + more_out,
         scratch_shapes=[
             pltpu.VMEM((len(xs),) + xs[0].shape, low),
             pltpu.VMEM((held, tokens, WIDE), low),
@@ -411,12 +503,13 @@
             pltpu.SemaphoreType.DMA((held, kinds)),
             pltpu.SemaphoreType.DMA((held, kinds)),
             pltpu.SemaphoreType.REGULAR((n_low + 2 + n_ctx - 1,)),
+            *more_scratch,
         ],
         compiler_params=pltpu.CompilerParams(
             collective_id=cid, has_side_effects=True, vmem_limit_bytes=56 * 2**20
         ),
         name="scatter_sums",
-    )(*xs, *ys)
+    )(*xs, *ys, *state)
 
 
 def passed_along(value, axis, steps):
@@ -425,37 +518,235 @@
     return lax.ppermute(value, axis, [(source, source + steps) for source in range(leading, last)])
 
 
-def carried_in(x, flags, axis, join):
-    count = lax.axis_size(axis)
-    low = jax.tree.map(lambda a: a.astype(jnp.bfloat16), x)
-    state = jax.tree.map(jnp.zeros_like, x) + (flags[0] * 0.0,)
-    for hop in range(count - 1, 0, -1):
-        pairs = [(source, source + hop) for source in range(count - hop)]
-        came = jax.tree.map(lambda a, own: lax.ppermute(a, axis, pairs).astype(own.dtype), low, x)
-        state = join(state, came + (flags[hop],))
-    return state
-
-
-def entering(x, flags, axis, join):
-    count = lax.axis_size(axis)
-    low = jax.tree.map(lambda a: a.astype(jnp.bfloat16), x)
-    state = jax.tree.map(jnp.zeros_like, x) + (flags[0] * 0.0,)
-    for hop in range(count - 1, 0, -1):
-        pairs = [(source + hop, source) for source in range(count - hop)]
-        came = jax.tree.map(lambda a, own: lax.ppermute(a, axis, pairs).astype(own.dtype), low, x)
-        state = join(state, came + (flags[hop],))
-    return state
-
-
-def chunks_of(shards):
-    out = []
-    for place, shard in enumerate(shards):
-        rows, columns = shard.shape
-        unit = max(128, 1408 * 32 // rows // 128 * 128)
-        width = -(-(columns // 128) // -(-columns // unit)) * 128
-        for first in range(0, columns, width):
-            out.append((place, first, min(width, columns - first)))
-    return out
+TERMS = 256
+SENT = 160
+PER = 2
+
+
+def feature_tables():
+    first = np.zeros((FEAT, TERMS), np.float32)
+    second = np.zeros((FEAT, TERMS), np.float32)
+    base = np.zeros((8, TERMS), np.float32)
+    base[0, 0] = base[1, 0] = base[2, 0] = 1.0
+    column = 1
+    for f in range(FEAT):
+        first[f, column] = base[1, column] = 1.0
+        base[2, column] = 1.0 / math.sqrt(FEAT)
+        column += 1
+    for f in range(FEAT):
+        for g in range(f, FEAT):
+            first[f, column] = second[g, column] = 1.0
+            base[2, column] = (0.5 if f == g else 1.0) / FEAT
+            column += 1
+    tile = np.stack([np.tile(first, (HEADS, 1)), np.tile(second, (HEADS, 1))])
+    return jnp.asarray(tile, jnp.bfloat16), jnp.asarray(base)
+
+
+def dot_nn(a, b):
+    return jnp.dot(a, b, preferred_element_type=jnp.float32)
+
+
+def dot_nt(a, b):
+    return lax.dot_general(a, b, (((1,), (1,)), ((), ())), preferred_element_type=jnp.float32)
+
+
+def dot_tn(a, b):
+    return lax.dot_general(a, b, (((0,), (0,)), ((), ())), preferred_element_type=jnp.float32)
+
+
+def lanes_of(shape, size):
+    return lax.broadcasted_iota(jnp.int32, shape, len(shape) - 1) // size
+
+
+def only(mask, value):
+    return jnp.where(mask, value, jnp.zeros_like(value))
+
+
+def pairs_of(step):
+    return [(step * PER + n, slice(128 * n, 128 * (n + 1))) for n in range(PER)]
+
+
+def factors(rows, tables, base):
+    return (dot_nn(rows, tables[0]) + base[0:1], dot_nn(rows, tables[1]) + base[1:2])
+
+
+def states_kernel(key_ref, value_ref, last_ref, table_ref, base_ref, state_ref):
+    step = pl.program_id(1)
+    low, f32 = jnp.bfloat16, jnp.float32
+    keys = key_ref[0]
+    last = last_ref[0]
+    head_of = lanes_of(keys.shape, FEAT)
+    lane = lanes_of((SENT, 128), 1)
+    totals = state_ref[0, HEADS // 2]
+    totals = jnp.where(step == 0, jnp.zeros_like(totals), totals)
+    for pair, here in pairs_of(step):
+        values = value_ref[0, :, here].astype(f32)
+        held = jnp.concatenate([(values * last).astype(low), last.astype(low)], axis=1)
+        both = []
+        for side in range(2):
+            head = 2 * pair + side
+            one, two = factors(only(head_of == head, keys), table_ref, base_ref)
+            part = dot_tn((one * two).astype(low), held)[:SENT]
+            both.append(part[:, :128])
+            totals = jnp.where(lane == head, part[:, 128:].astype(low), totals)
+        state_ref[0, pair] = jnp.where(lane < 64, both[0], both[1]).astype(low)
+    state_ref[0, HEADS // 2] = totals
+
+
+def attend_kernel(
+    query_ref, key_ref, value_ref, state_ref, mask_ref, carried_ref, table_ref, base_ref, out_ref, den_ref
+):
+    step = pl.program_id(1)
+    low, f32 = jnp.bfloat16, jnp.float32
+    queries, keys = query_ref[0], key_ref[0]
+    mask, carried = mask_ref[0], carried_ref[0][:, :1]
+    totals = state_ref[0, HEADS // 2]
+    head_of = lanes_of(queries.shape, FEAT)
+    lane = lanes_of(totals.shape, 1)
+    for pair, here in pairs_of(step):
+        state = state_ref[0, pair]
+        values = value_ref[0, :, here]
+        held = jnp.concatenate([values, jnp.ones_like(values)], axis=1)
+        outs, dens = [], []
+        for side in range(2):
+            head = 2 * pair + side
+            own = only(head_of == head, queries)
+            score = dot_nt(own, keys) * (1.0 / math.sqrt(FEAT))
+            weight = ((1.0 + score + 0.5 * score * score) * mask).astype(low)
+            one, two = factors(own, table_ref, base_ref)
+            terms = (one * two * base_ref[2:3] * carried).astype(low)
+            total = jnp.sum(only(lane == head, totals.astype(f32)), axis=1, keepdims=True)
+            total = jnp.broadcast_to(total, totals.shape).astype(low)
+            result = dot_nn(weight, held) + dot_nn(terms, jnp.concatenate([state, total], axis=1))
+            outs.append(result[:, :128] / result[:, 128:])
+            dens.append(result[:, 128:])
+        first = lanes_of(outs[0].shape, 64) == 0
+        out_ref[0, :, here] = jnp.where(first, outs[0], outs[1]).astype(low)
+        den_ref[0, :, here] = jnp.where(first, dens[0], dens[1])
+
+
+def attend_back_kernel(
+    query_ref, key_ref, value_ref, state_ref, mask_ref, carried_ref, table_ref, base_ref, grad_ref, out_ref,
+    den_ref, dquery_ref, dkey_ref, dvalue_ref, dstate_ref,
+):
+    step = pl.program_id(1)
+    low, f32 = jnp.bfloat16, jnp.float32
+    queries, keys = query_ref[0], key_ref[0]
+    mask, carried = mask_ref[0], carried_ref[0][:, :1]
+    totals = state_ref[0, HEADS // 2]
+    head_of = lanes_of(queries.shape, FEAT)
+    lane = lanes_of(value_ref.shape[1:2] + (128,), 1)
+    dquery = jnp.zeros(queries.shape, f32)
+    dkey = jnp.zeros(queries.shape, f32)
+    dtotals = dstate_ref[0, HEADS // 2]
+    dtotals = jnp.where(step == 0, jnp.zeros_like(dtotals), dtotals)
+    inv_root = 1.0 / math.sqrt(FEAT)
+    for pair, here in pairs_of(step):
+        values = value_ref[0, :, here]
+        whole_state = jnp.concatenate([state_ref[0, pair], totals], axis=1)
+        dnum = grad_ref[0, :, here] / den_ref[0, :, here]
+        inner = dnum * out_ref[0, :, here].astype(f32)
+        dvalue = jnp.zeros(dnum.shape, f32)
+        dstate = jnp.zeros((SENT, 128), f32)
+        for side in range(2):
+            head = 2 * pair + side
+            own_lanes = (lane < 64) if side == 0 else (lane >= 64)
+            own, own_keys = only(head_of == head, queries), only(head_of == head, keys)
+            dnum_own = only(own_lanes, dnum).astype(low)
+            dden = -jnp.sum(only(own_lanes, inner), axis=1, keepdims=True)
+            score = dot_nt(own, keys) * inv_root
+            slope = (1.0 + score) * mask
+            weight = ((1.0 + score + 0.5 * score * score) * mask).astype(low)
+            dscore = ((dot_nt(dnum_own, values) + dden) * slope * inv_root).astype(low)
+            dvalue += dot_tn(weight, dnum_own)
+            dquery += dot_nn(dscore, own_keys)
+            dkey += dot_tn(dscore, own)
+            one, two = factors(own, table_ref, base_ref)
+            scale = base_ref[2:3] * carried
+            terms = (one * two * scale).astype(low)
+            dden_all = jnp.broadcast_to(dden, dnum.shape)
+            part = dot_tn(terms, jnp.concatenate([dnum_own, dden_all.astype(low)], axis=1))[:SENT]
+            dstate += part[:, :128]
+            dtotals = jnp.where(lanes_of(dtotals.shape, 1) == head, part[:, 128:].astype(low), dtotals)
+            both = jnp.concatenate([dnum_own, only(lane == head, dden_all).astype(low)], axis=1)
+            dterms = dot_nt(both, whole_state) * scale
+            through = dot_nt((dterms * two).astype(low), table_ref[0])
+            through += dot_nt((dterms * one).astype(low), table_ref[1])
+            dquery += only(head_of == head, through)
+        dvalue_ref[0, :, here] = dvalue
+        dstate_ref[0, pair] = dstate.astype(low)
+    dstate_ref[0, HEADS // 2] = dtotals
+
+    @pl.when(step == 0)
+    def _():
+        dquery_ref[0] = dquery
+        dkey_ref[0] = dkey
+
+    @pl.when(step != 0)
+    def _():
+        dquery_ref[0] += dquery
+        dkey_ref[0] += dkey
+
+
+def states_back_kernel(
+    key_ref, value_ref, last_ref, table_ref, base_ref, dstate_ref, dkey_in, dvalue_in, dkey_ref, dvalue_ref
+):
+    step = pl.program_id(1)
+    low, f32 = jnp.bfloat16, jnp.float32
+    keys = key_ref[0]
+    last = last_ref[0]
+    dtotals = dstate_ref[0, HEADS // 2]
+    head_of = lanes_of(keys.shape, FEAT)
+    lane = lanes_of(last.shape, 1)
+    dkey = jnp.zeros(keys.shape, f32)
+    for pair, here in pairs_of(step):
+        values = value_ref[0, :, here]
+        dstate = dstate_ref[0, pair]
+        whole = jnp.concatenate([dstate, dtotals], axis=1)
+        dvalue = dvalue_in[0, :, here]
+        for side in range(2):
+            head = 2 * pair + side
+            own_lanes = (lane < 64) if side == 0 else (lane >= 64)
+            one, two = factors(only(head_of == head, keys), table_ref, base_ref)
+            terms = (one * two).astype(low)
+            dvalue += only(own_lanes, dot_nn(terms, dstate)) * last
+            both = jnp.concatenate([only(own_lanes, values), (lane == head).astype(low)], axis=1)
+            dterms = dot_nt(both, whole) * last[:, :1]
+            through = dot_nt((dterms * two).astype(low), table_ref[0])
+            through += dot_nt((dterms * one).astype(low), table_ref[1])
+            dkey += only(head_of == head, through)
+        dvalue_ref[0, :, here] = dvalue
+
+    @pl.when(step == 0)
+    def _():
+        dkey_ref[0] = dkey_in[0] + dkey
+
+    @pl.when(step != 0)
+    def _():
+        dkey_ref[0] += dkey
+
+
+def by_pair(kernel, name, ins, outs):
+    def spec(kind, shape):
+        if kind == "query":
+            return pl.BlockSpec((1, shape[1], HEADS * FEAT), lambda m, p: (m, 0, 0))
+        if kind == "key":
+            return pl.BlockSpec((1, shape[1], HEADS * FEAT), lambda m, p: (m, 0, 1))
+        if kind == "pair":
+            return pl.BlockSpec((1, shape[1], PER * 128), lambda m, p: (m, 0, p))
+        if kind == "micro":
+            return pl.BlockSpec((1,) + shape[1:], lambda m, p: (m,) + (0,) * (len(shape) - 1))
+        return pl.BlockSpec(shape, lambda m, p: (0,) * len(shape))
+
+    return pl.pallas_call(
+        kernel,
+        grid=(ins[0][0].shape[0], HEADS // 2 // PER),
+        in_specs=[spec(kind, array.shape) for array, kind in ins],
+        out_specs=[spec(kind, shape) for shape, _, kind in outs],
+        out_shape=[jax.ShapeDtypeStruct(shape, dtype) for shape, dtype, _ in outs],
+        compiler_params=pltpu.CompilerParams(vmem_limit_bytes=48 * 2**20),
+        name=name,
+    )(*[array for array, _ in ins])
 
 
 def chunk_plan(products, unit):
@@ -486,20 +777,25 @@
     return laid, plan, shapes
 
 
-def summed_to_owners(products, small):
-    n_dp, n_ctx = lax.axis_size("dp"), lax.axis_size("ctx")
+def as_product(small):
     rows, few = small.shape
-    tokens = products[0][0].shape[0]
     high = small.astype(jnp.bfloat16)
     rest = (small - high.astype(jnp.float32)).astype(jnp.bfloat16)
-    both = jnp.zeros((tokens, rows), jnp.bfloat16).at[:few].set(high.T).at[few : 2 * few].set(rest.T)
-    pick = jnp.zeros((tokens, WIDE), jnp.bfloat16)
-    pick = pick.at[:few, :few].set(jnp.eye(few, dtype=jnp.bfloat16))
-    pick = pick.at[few : 2 * few, :few].set(jnp.eye(few, dtype=jnp.bfloat16))
-    products = [(both, pick)] + products
-    laid, plan, shapes = chunk_plan(products, rows // (n_dp * n_ctx))
-    sums = scatter_sums(laid, [gradient for _, gradient in products], shapes, plan, n_dp, n_ctx)
-    return sums[0][:, :few], sums[1:]
+
+    def product(tokens):
+        both = jnp.zeros((tokens, rows), jnp.bfloat16).at[:few].set(high.T).at[few : 2 * few].set(rest.T)
+        pick = np.zeros((tokens, WIDE), np.float32)
+        pick[:few, :few] = pick[few : 2 * few, :few] = np.eye(few)
+        return both, jnp.asarray(pick, jnp.bfloat16)
+
+    return product
+
+
+def summed_to_owners(products, cid, unit, carry=0, state=()):
+    n_dp, n_ctx = lax.axis_size("dp"), lax.axis_size("ctx")
+    laid, plan, shapes = chunk_plan(products, unit)
+    gradients = [gradient for _, gradient in products]
+    return scatter_sums(laid, gradients, shapes, plan, n_dp, n_ctx, cid, carry, state)
 
 
 def chunks_of(shards):
@@ -535,27 +831,6 @@
     return jnp.einsum("mtd,mte->de", operand, gradient, preferred_element_type=jnp.float32)
 
 
-def feature_map(source):
-    feat_width = source.shape[-1]
-    outer_prod = (source[..., :, None] * source[..., None, :]).reshape(
-        source.shape[:-1] + (feat_width * feat_width,)
-    )
-    ones_col = jnp.ones(source.shape[:-1] + (1,), source.dtype)
-    return jnp.concatenate(
-        [ones_col, source * feat_width ** (-0.25), outer_prod / math.sqrt(2.0 * feat_width)],
-        axis=-1,
-    )
-
-
-def chain_states(earlier, later):
-    keep_part = 1.0 - later[2]
-    return (
-        later[0] + keep_part[:, None, None, None] * earlier[0],
-        later[1] + keep_part[:, None, None] * earlier[1],
-        jnp.maximum(earlier[2], later[2]),
-    )
-
-
 def layout(seq_lengths, tok_count):
     seq_ends = jnp.cumsum(seq_lengths[:, 0, :], axis=-1, dtype=jnp.int32)
     first_pos = lax.axis_index("ctx") * tok_count
@@ -571,37 +846,35 @@
     own_seg = segment_of(own_pos)
     before_seg = segment_of(own_pos - 1)
 
-    def flags(direction):
-        out = []
-        for hop in range(lax.axis_size("ctx")):
-            first = first_pos + direction * hop * tok_count
-            held = (seq_ends >= first) & (seq_ends < first + tok_count) & (seq_ends < total_len)
-            out.append(jnp.any(held | (first == 0), axis=1).astype(jnp.float32))
-        return out
-
-    total_len = tok_count * lax.axis_size("ctx")
+    def in_lanes(flag):
+        return jnp.broadcast_to(flag[:, :, None].astype(jnp.float32), flag.shape + (128,))
+
+    starts = (own_seg != before_seg) | (own_pos == 0)[None, :]
+    keep = 1.0 - jnp.max(starts.astype(jnp.float32), axis=1)
     tap_masks = []
     for offset in range(CONV):
         source = own_pos - offset
         tap_masks.append(
             ((segment_of(source) == own_seg) & (source >= 0)[None, :]).astype(jnp.float32)
         )
-    key_pos = first_pos - (WINDOW - 1) + jnp.arange(tok_count + WINDOW - 1, dtype=jnp.int32)
-    visible = (key_pos[None, :] <= own_pos[:, None]) & (
-        key_pos[None, :] > own_pos[:, None] - WINDOW
-    )
-    visible = visible & (key_pos >= 0)[None, :]
-    window_mask = visible[None] & (segment_of(key_pos)[:, None, :] == own_seg[:, :, None])
+    key_pos = first_pos - BAND + jnp.arange(tok_count + BAND, dtype=jnp.int32)
+    key_seg = jnp.where(key_pos >= 0, segment_of(key_pos), -1)
+    window_mask = []
+    for first in range(0, tok_count, BAND):
+        queries, keys = slice(first, first + BAND), slice(first, first + 2 * BAND)
+        ahead = own_pos[queries][:, None] - key_pos[keys][None, :]
+        same = own_seg[:, queries][:, :, None] == key_seg[:, keys][:, None, :]
+        window_mask.append(((ahead >= 0) & (ahead < WINDOW))[None] & same)
+    window_mask = jnp.concatenate(window_mask, axis=1).astype(jnp.float32)
     causal = (own_pos[:, None] >= own_pos[None, :])[None] & (
         own_seg[:, :, None] == own_seg[:, None, :]
     )
     return {
         "valid": (own_pos[None, :] < seq_ends[:, -1:]).astype(jnp.float32),
-        "flags_before": flags(-1),
-        "flags_after": flags(1),
-        "carried": ((own_seg == before_seg[:, :1]) & (first_pos > 0)).astype(jnp.float32),
-        "last": (own_seg == own_seg[:, -1:]).astype(jnp.float32),
-        "causal": causal,
+        "keep": jnp.broadcast_to(keep[:, None, None], keep.shape + (8, 128)),
+        "carried": in_lanes((own_seg == before_seg[:, :1]) & (first_pos > 0)),
+        "last": in_lanes(own_seg == own_seg[:, -1:]),
+        "causal": causal.astype(jnp.float32),
         "taps": jnp.stack(tap_masks),
         "window": window_mask,
     }
@@ -618,30 +891,8 @@
     return conv_sum * jax.nn.silu(pre_values)
 
 
-def end_state(key_rows, head_values, last_mask):
-    features = feature_map(key_rows) * last_mask[:, :, None, None]
-    return (
-        jnp.einsum("mthr,mthe->mhre", features, head_values, precision=highest),
-        jnp.sum(features, axis=1),
-    )
-
-
-def attend_linear(query_rows, key_rows, head_values, state_in, totals_in, causal, carried):
-    micro_count, tok_count = (query_rows.shape[0], query_rows.shape[1])
-    scores = jnp.einsum("mihf,mjhf->mhij", query_rows, key_rows, precision=highest) / math.sqrt(
-        query_rows.shape[-1]
-    )
-    weights = (1.0 + scores + 0.5 * scores * scores) * causal[:, None].astype(jnp.float32)
-    numerator = jnp.einsum("mhij,mjhe->mihe", weights, head_values, precision=highest)
-    denominator = jnp.transpose(jnp.sum(weights, axis=-1), (0, 2, 1))
-    features = feature_map(query_rows) * carried[:, :, None, None]
-    numerator = numerator + jnp.einsum("mihr,mhre->mihe", features, state_in, precision=highest)
-    denominator = denominator + jnp.einsum("mihr,mhr->mih", features, totals_in, precision=highest)
-    return (numerator / denominator[..., None]).reshape(micro_count, tok_count, -1)
-
-
-def linear_forward(stream, weights, layout_info):
-    norm_gain, qk_weight, value_weight, tap_weights, out_weight = weights
+def linear_forward(stream, weights, layout_info, gather_more):
+    norm_gain, qk_weight, value_weight, tap_weights = weights
     micro_count, tok_count, model_width = stream.shape
     normed_rows, norm_back = jax.vjp(normed, stream, norm_gain.astype(jnp.float32))
     normed_low = normed_rows.astype(jnp.bfloat16)
@@ -654,60 +905,72 @@
         rim_rows,
         tap_weights.astype(jnp.float32),
     )
-    head_values = (
-        value_rows.astype(jnp.bfloat16)
-        .astype(jnp.float32)
-        .reshape(micro_count, tok_count, HEADS, model_width // HEADS)
-    )
-    half_cols = qk_rows.shape[-1] // 2
-    query_rows = (
-        qk_rows[..., :half_cols].astype(jnp.float32).reshape(micro_count, tok_count, HEADS, FEAT)
-    )
-    key_rows = (
-        qk_rows[..., half_cols:].astype(jnp.float32).reshape(micro_count, tok_count, HEADS, FEAT)
-    )
-    state_out, state_back = jax.vjp(
-        partial(end_state, last_mask=layout_info["last"]), key_rows, head_values
-    )
-    incoming = carried_in(state_out, layout_info["flags_before"], "ctx", chain_states)
-    attended, attend_back = jax.vjp(
-        partial(attend_linear, causal=layout_info["causal"], carried=layout_info["carried"]),
-        query_rows,
-        key_rows,
-        head_values,
-        incoming[0],
-        incoming[1],
-    )
-    attended_low = attended.astype(jnp.bfloat16)
+    values = value_rows.astype(jnp.bfloat16)
+    tables, base = feature_tables()
+    state_shape = (micro_count, HEADS // 2 + 1, SENT, 128)
+    (state,) = by_pair(
+        states_kernel,
+        "states",
+        [(qk_rows, "key"), (values, "pair"), (layout_info["last"], "micro"), (tables, "whole"), (base, "whole")],
+        [(state_shape, jnp.bfloat16, "micro")],
+    )
+    *more, state_in = gather_more((state, layout_info["keep"]))
+    out_weight = more[0]
+    shared = [
+        (qk_rows, "query"),
+        (qk_rows, "key"),
+        (values, "pair"),
+        (state_in, "micro"),
+        (layout_info["causal"], "micro"),
+        (layout_info["carried"], "micro"),
+        (tables, "whole"),
+        (base, "whole"),
+    ]
+    attended_low, den = by_pair(
+        attend_kernel,
+        "linear_attend",
+        shared,
+        [(values.shape, jnp.bfloat16, "pair"), (values.shape, jnp.float32, "pair")],
+    )
     branch = matmul(attended_low, out_weight)
     return (
         stream + branch,
-        (norm_back, normed_low, conv_back, state_back, attend_back, attended_low),
-    )
-
-
-def linear_backward(grad_stream, residuals, weights, layout_info, other_gains):
-    norm_back, normed_low, conv_back, state_back, attend_back, attended_low = residuals
+        (norm_back, normed_low, conv_back, shared, attended_low, den),
+        more,
+    )
+
+
+def linear_backward(grad_stream, residuals, weights, layout_info, other_gains, sum_others):
+    norm_back, normed_low, conv_back, shared, attended_low, den = residuals
     qk_weight, value_weight, out_weight = (weights[1], weights[2], weights[4])
     micro_count, tok_count, model_width = grad_stream.shape
     grad_branch = grad_stream.astype(jnp.bfloat16)
     grad_out = (flat(attended_low), flat(grad_branch))
     grad_attended = matmul_back(grad_branch, out_weight)
-    grad_query, grad_key, grad_value, grad_state, grad_totals = attend_back(grad_attended)
-    later_grads = entering((grad_state, grad_totals), layout_info["flags_after"], "ctx", chain_states)
-    key_more, value_more = state_back((later_grads[0], later_grads[1]))
-    grad_key = grad_key + key_more
-    grad_value = grad_value + value_more
-    grad_qk = jnp.concatenate(
+    f32, low = jnp.float32, jnp.bfloat16
+    feat_shape = (micro_count, tok_count, HEADS * FEAT)
+    state_shape = (micro_count, HEADS // 2 + 1, SENT, 128)
+    grad_query, grad_key, grad_value, grad_state = by_pair(
+        attend_back_kernel,
+        "linear_attend_back",
+        shared + [(grad_attended, "pair"), (attended_low, "pair"), (den, "pair")],
         [
-            grad_query.reshape(micro_count, tok_count, -1),
-            grad_key.reshape(micro_count, tok_count, -1),
+            (feat_shape, f32, "micro"),
+            (feat_shape, f32, "micro"),
+            (grad_stream.shape, f32, "pair"),
+            (state_shape, low, "micro"),
         ],
-        axis=-1,
-    ).astype(jnp.bfloat16)
-    grad_pre, grad_rim, grad_taps = conv_back(
-        grad_value.reshape(micro_count, tok_count, model_width)
-    )
+    )
+    *sums, later = sum_others(grad_out, (grad_state, layout_info["keep"]))
+    grad_key, grad_value = by_pair(
+        states_back_kernel,
+        "states_back",
+        [shared[1], shared[2], (layout_info["last"], "micro"), shared[6], shared[7], (later, "micro")]
+        + [(grad_key, "micro"), (grad_value, "pair")],
+        [(feat_shape, f32, "micro"), (grad_stream.shape, f32, "pair")],
+    )
+    grad_qk = jnp.concatenate([grad_query, grad_key], axis=-1).astype(low)
+    grad_pre, grad_rim, grad_taps = conv_back(grad_value)
     returned = passed_along(grad_rim, "ctx", -1)
     grad_pre = grad_pre.at[:, tok_count - CONV + 1 :, :].add(returned)
     grad_pre_low = grad_pre.astype(jnp.bfloat16)
@@ -715,112 +978,201 @@
     grad_input, grad_gain = norm_back(grad_normed)
     small = jnp.concatenate([grad_gain[:, None], other_gains, grad_taps], axis=1)
     operand = flat(normed_low)
-    return (
-        grad_stream + grad_input,
-        (operand, flat(grad_qk)),
-        (operand, flat(grad_pre_low)),
-        grad_out,
-        small,
-    )
-
-
-def window_scores(heads_query, key_ext, window_mask, head_size):
-    raw_scores = jnp.einsum(
-        "mihe,mjhe->mhij", heads_query, key_ext, preferred_element_type=jnp.float32
-    ) * head_size ** (-0.5)
-    return jnp.where(window_mask[:, None], raw_scores, masked_fill)
+    own = summed_to_owners(
+        [
+            as_product(small)(operand.shape[0]),
+            (operand, flat(grad_qk)),
+            (operand, flat(grad_pre_low)),
+        ],
+        3,
+        model_width // (lax.axis_size("dp") * lax.axis_size("ctx")),
+    )
+    return (grad_stream + grad_input, own, sums)
+
+
+BAND = 128
+RIM = 64
+
+
+def band_probabilities(queries, keys, mask):
+    score = jnp.where(mask > 0, dot_nt(queries, keys) * 0.125, masked_fill)
+    power = jnp.exp(score - jnp.max(score, axis=1, keepdims=True))
+    return power / jnp.sum(power, axis=1, keepdims=True)
+
+
+def band_attend(queries, keys, values, mask):
+    lane = lanes_of(queries.shape, 1)
+    outs = []
+    for own in (lane < 64, lane >= 64):
+        chance = band_probabilities(only(own, queries), keys, mask)
+        outs.append(dot_nn(chance.astype(jnp.bfloat16), values))
+    return jnp.where(lane < 64, outs[0], outs[1]).astype(jnp.bfloat16)
+
+
+def band_back(queries, grads, keys, values, mask):
+    low = jnp.bfloat16
+    lane = lanes_of(queries.shape, 1)
+    dqueries, dkeys, dvalues = [], 0.0, 0.0
+    for own in (lane < 64, lane >= 64):
+        own_queries, own_grads = only(own, queries), only(own, grads)
+        chance = band_probabilities(own_queries, keys, mask)
+        dchance = dot_nt(own_grads, values)
+        inner = jnp.sum(dchance * chance, axis=1, keepdims=True)
+        dscore = (chance * (dchance - inner)).astype(low)
+        dqueries.append(dot_nn(dscore, keys) * 0.125)
+        dkeys += dot_tn(dscore, own_queries) * 0.125
+        dvalues += dot_tn(chance.astype(low), own_grads)
+    return jnp.where(lane < 64, dqueries[0], dqueries[1]).astype(low), dkeys, dvalues
+
+
+def with_rim(own_ref, rim_ref, here):
+    own, rim = own_ref[0, :, here], rim_ref[0, :, here]
+    return jnp.concatenate([jnp.zeros((BAND - RIM, 128), own.dtype), rim, own], axis=0)
+
+
+def first_band_kernel(query_ref, key_ref, value_ref, rim_key_ref, rim_value_ref, mask_ref, out_ref):
+    for _, here in pairs_of(0):
+        keys, values = with_rim(key_ref, rim_key_ref, here), with_rim(value_ref, rim_value_ref, here)
+        out_ref[0, :, here] = band_attend(query_ref[0, :, here], keys, values, mask_ref[0])
+
+
+def later_bands_kernel(query_ref, key_ref, value_ref, mask_ref, out_ref):
+    for _, here in pairs_of(0):
+        for first in range(BAND, query_ref.shape[1], BAND):
+            rows, near = slice(first, first + BAND), slice(first - BAND, first + BAND)
+            out_ref[0, first - BAND : first, here] = band_attend(
+                query_ref[0, rows, here], key_ref[0, near, here], value_ref[0, near, here], mask_ref[0, rows]
+            )
+
+
+def first_band_back_kernel(
+    query_ref, key_ref, value_ref, rim_key_ref, rim_value_ref, mask_ref, grad_ref, dquery_ref, dkey_ref,
+    dvalue_ref, drim_key_ref, drim_value_ref,
+):
+    for _, here in pairs_of(0):
+        keys, values = with_rim(key_ref, rim_key_ref, here), with_rim(value_ref, rim_value_ref, here)
+        dquery, dkey, dvalue = band_back(
+            query_ref[0, :, here], grad_ref[0, :, here], keys, values, mask_ref[0]
+        )
+        dquery_ref[0, :, here] = dquery
+        dkey_ref[0, :, here] = dkey[BAND:]
+        dvalue_ref[0, :, here] = dvalue[BAND:]
+        drim_key_ref[0, :, here] = dkey[BAND - RIM : BAND].astype(jnp.bfloat16)
+        drim_value_ref[0, :, here] = dvalue[BAND - RIM : BAND].astype(jnp.bfloat16)
+
+
+def later_bands_back_kernel(
+    query_ref, key_ref, value_ref, mask_ref, grad_ref, first_dkey_ref, first_dvalue_ref, dquery_ref, dkey_ref,
+    dvalue_ref,
+):
+    for _, here in pairs_of(0):
+        dkey_ref[0, :BAND, here] = first_dkey_ref[0, :, here]
+        dvalue_ref[0, :BAND, here] = first_dvalue_ref[0, :, here]
+        for first in range(BAND, query_ref.shape[1], BAND):
+            rows, before, near = (
+                slice(first, first + BAND),
+                slice(first - BAND, first),
+                slice(first - BAND, first + BAND),
+            )
+            dquery, dkey, dvalue = band_back(
+                query_ref[0, rows, here],
+                grad_ref[0, rows, here],
+                key_ref[0, near, here],
+                value_ref[0, near, here],
+                mask_ref[0, rows],
+            )
+            dquery_ref[0, before, here] = dquery
+            dkey_ref[0, before, here] += dkey[:BAND]
+            dvalue_ref[0, before, here] += dvalue[:BAND]
+            dkey_ref[0, rows, here] = dkey[BAND:]
+            dvalue_ref[0, rows, here] = dvalue[BAND:]
+
+
+def by_window(kernel, name, ins, outs):
+    micro, steps = ins[0][0].shape[0], HEADS // 2 // PER
+
+    def spec(rows, place, width):
+        if place is None:
+            return pl.BlockSpec((1, rows, width), lambda m, p: (m, 0, 0))
+        return pl.BlockSpec((1, rows, PER * 128), lambda m, p: (m, 0, p + place * steps))
+
+    return pl.pallas_call(
+        kernel,
+        grid=(micro, steps),
+        in_specs=[spec(rows, place, array.shape[2]) for array, rows, place in ins],
+        out_specs=[spec(rows, 0, 0) for rows, _ in outs],
+        out_shape=[jax.ShapeDtypeStruct((micro, rows, HEADS * 64), dtype) for rows, dtype in outs],
+        compiler_params=pltpu.CompilerParams(vmem_limit_bytes=48 * 2**20),
+        name=name,
+    )(*[array for array, _, _ in ins])
 
 
 def window_forward(stream, weights, layout_info):
     norm_gain, qkv_weight, out_weight = weights
     micro_count, tok_count, model_width = stream.shape
-    head_size = model_width // HEADS
     normed_rows, norm_back = jax.vjp(normed, stream, norm_gain.astype(jnp.float32))
     normed_low = normed_rows.astype(jnp.bfloat16)
     qkv_rows = matmul(normed_low, qkv_weight).astype(jnp.bfloat16)
-    key_value = qkv_rows[..., model_width:]
-    rim_rows = passed_along(key_value[:, tok_count - WINDOW + 1 :, :], "ctx", 1)
-    extended = jnp.concatenate([rim_rows, key_value], axis=1)
-    key_ext = extended[..., :model_width].reshape(micro_count, -1, HEADS, head_size)
-    value_ext = extended[..., model_width:].reshape(micro_count, -1, HEADS, head_size)
-    heads_query = qkv_rows[..., :model_width].reshape(micro_count, tok_count, HEADS, head_size)
-    scores = window_scores(heads_query, key_ext, layout_info["window"], head_size)
-    row_peak = jnp.max(scores, axis=-1, keepdims=True)
-    exp_scores = jnp.exp(scores - row_peak)
-    row_total = jnp.sum(exp_scores, axis=-1, keepdims=True)
-    probabilities = (exp_scores / row_total).astype(jnp.bfloat16)
-    attended = jnp.einsum(
-        "mhij,mjhe->mihe", probabilities, value_ext, preferred_element_type=jnp.float32
-    )
-    attended = attended.astype(jnp.bfloat16).reshape(micro_count, tok_count, model_width)
+    rim_rows = passed_along(qkv_rows[:, tok_count - RIM :, model_width:], "ctx", 1)
+    mask = layout_info["window"]
+    parts = []
+    if tok_count > BAND:
+        parts = by_window(
+            later_bands_kernel,
+            "window_later",
+            [(qkv_rows, tok_count, 0), (qkv_rows, tok_count, 1), (qkv_rows, tok_count, 2), (mask, tok_count, None)],
+            [(tok_count - BAND, jnp.bfloat16)],
+        )
+        rim_rows, parts = lax.optimization_barrier((rim_rows, parts))
+    (start,) = by_window(
+        first_band_kernel,
+        "window_first",
+        [(qkv_rows, BAND, 0), (qkv_rows, BAND, 1), (qkv_rows, BAND, 2), (rim_rows, RIM, 0), (rim_rows, RIM, 1)]
+        + [(mask, BAND, None)],
+        [(BAND, jnp.bfloat16)],
+    )
+    attended = jnp.concatenate([start] + list(parts), axis=1)
     branch = matmul(attended, out_weight)
-    return (
-        stream + branch,
-        (
-            norm_back,
-            normed_low,
-            heads_query,
-            key_ext,
-            value_ext,
-            row_peak + jnp.log(row_total),
-            attended,
-        ),
-    )
+    return (stream + branch, (norm_back, normed_low, qkv_rows, rim_rows, attended))
 
 
 def window_backward(grad_stream, residuals, weights, layout_info):
-    norm_back, normed_low, heads_query, key_ext, value_ext, log_total, attended = residuals
+    norm_back, normed_low, qkv_rows, rim_rows, attended = residuals
     qkv_weight, out_weight = (weights[1], weights[2])
     micro_count, tok_count, model_width = grad_stream.shape
-    head_size = model_width // HEADS
-    grad_branch = grad_stream.astype(jnp.bfloat16)
+    f32, low = jnp.float32, jnp.bfloat16
+    grad_branch = grad_stream.astype(low)
     grad_out = (flat(attended), flat(grad_branch))
-    grad_attended = (
-        matmul_back(grad_branch, out_weight)
-        .astype(jnp.bfloat16)
-        .reshape(micro_count, tok_count, HEADS, head_size)
-    )
-    scores = window_scores(heads_query, key_ext, layout_info["window"], head_size)
-    probabilities = jnp.exp(scores - log_total)
-    grad_probs = jnp.einsum(
-        "mihe,mjhe->mhij", grad_attended, value_ext, preferred_element_type=jnp.float32
-    )
-    grad_value_ext = jnp.einsum(
-        "mhij,mihe->mjhe",
-        probabilities.astype(jnp.bfloat16),
-        grad_attended,
-        preferred_element_type=jnp.float32,
-    )
-    inner_sum = jnp.sum(grad_probs * probabilities, axis=-1, keepdims=True)
-    grad_scores = (probabilities * (grad_probs - inner_sum)).astype(jnp.bfloat16)
-    score_scale = head_size ** (-0.5)
-    grad_query = (
-        jnp.einsum("mhij,mjhe->mihe", grad_scores, key_ext, preferred_element_type=jnp.float32)
-        * score_scale
-    )
-    grad_key_ext = (
-        jnp.einsum("mhij,mihe->mjhe", grad_scores, heads_query, preferred_element_type=jnp.float32)
-        * score_scale
-    )
-    rim_grads = jnp.concatenate(
+    grad_attended = matmul_back(grad_branch, out_weight).astype(low)
+    mask = layout_info["window"]
+    grad_query, grad_key, grad_value, rim_key, rim_value = by_window(
+        first_band_back_kernel,
+        "window_first_back",
+        [(qkv_rows, BAND, 0), (qkv_rows, BAND, 1), (qkv_rows, BAND, 2), (rim_rows, RIM, 0), (rim_rows, RIM, 1)]
+        + [(mask, BAND, None), (grad_attended, BAND, 0)],
+        [(BAND, low), (BAND, f32), (BAND, f32), (RIM, low), (RIM, low)],
+    )
+    returned = passed_along(jnp.concatenate([rim_key, rim_value], axis=-1), "ctx", -1)
+    if tok_count > BAND:
+        more_query, grad_key, grad_value = by_window(
+            later_bands_back_kernel,
+            "window_later_back",
+            [(qkv_rows, tok_count, 0), (qkv_rows, tok_count, 1), (qkv_rows, tok_count, 2), (mask, tok_count, None)]
+            + [(grad_attended, tok_count, 0), (grad_key, BAND, 0), (grad_value, BAND, 0)],
+            [(tok_count - BAND, low), (tok_count, f32), (tok_count, f32)],
+        )
+        grad_query = jnp.concatenate([grad_query, more_query], axis=1)
+        returned, grad_key = lax.optimization_barrier((returned, grad_key))
+    returned = returned.astype(f32)
+    returned = jnp.pad(returned, ((0, 0), (tok_count - RIM, 0), (0, 0)))
+    grad_qkv = jnp.concatenate(
         [
-            grad_key_ext[:, : WINDOW - 1].reshape(micro_count, WINDOW - 1, model_width),
-            grad_value_ext[:, : WINDOW - 1].reshape(micro_count, WINDOW - 1, model_width),
+            grad_query,
+            (grad_key + returned[..., :model_width]).astype(low),
+            (grad_value + returned[..., model_width:]).astype(low),
         ],
         axis=-1,
     )
-    returned = passed_along(rim_grads.astype(jnp.bfloat16), "ctx", -1).astype(rim_grads.dtype)
-    own_grads = jnp.concatenate(
-        [
-            grad_key_ext[:, WINDOW - 1 :].reshape(micro_count, tok_count, model_width),
-            grad_value_ext[:, WINDOW - 1 :].reshape(micro_count, tok_count, model_width),
-        ],
-        axis=-1,
-    )
-    own_grads = own_grads.at[:, tok_count - WINDOW + 1 :, :].add(returned)
-    grad_qkv = jnp.concatenate(
-        [grad_query.reshape(micro_count, tok_count, model_width), own_grads], axis=-1
-    ).astype(jnp.bfloat16)
     grad_qkv_weight = (flat(normed_low), flat(grad_qkv))
     grad_input, grad_gain = norm_back(matmul_back(grad_qkv, qkv_weight))
     return (grad_stream + grad_input, (grad_gain, grad_qkv_weight, grad_out))
@@ -890,24 +1242,22 @@
         ],
         axis=1,
     )
-    shards = [
-        small,
-        proj_qk,
-        proj_values,
-        out_linear,
-        gate_up_one,
-        down_one,
-        proj_qkv,
-        out_window,
-        gate_up_two,
-        down_two,
-    ]
-    small, w_qk, w_values, w_out_linear, w_gu_one, w_dn_one, w_qkv, w_out_window, w_gu_two, w_dn_two = (
-        gather_all(shards, lax.axis_size("dp"), lax.axis_size("ctx"), chunks_of(shards))
-    )
+    n_dp, n_ctx = lax.axis_size("dp"), lax.axis_size("ctx")
+    first_shards = [small, proj_qk, proj_values]
+    small, w_qk, w_values = gather_all(first_shards, n_dp, n_ctx, chunks_of(first_shards), cid=0)
+
+    def gather_more(state):
+        shards = [out_linear, gate_up_one, down_one, proj_qkv, out_window, down_two]
+        return gather_all(shards, n_dp, n_ctx, chunks_of(shards), cid=2, carry=1, state=state)
+
+    middle, saved_linear, more = linear_forward(
+        stream, (small[:, 0], w_qk, w_values, small[:, 4:7]), layout_info, gather_more
+    )
+    w_out_linear, w_gu_one, w_dn_one, w_qkv, w_out_window, w_dn_two = more
+    w_out_linear, late = lax.optimization_barrier((w_out_linear, gate_up_two))
+    w_gu_two = lax.all_gather(late, ("dp", "ctx"), axis=0, tiled=True)
     layer_one = (small[:, 0], w_qk, w_values, small[:, 4:7], w_out_linear, small[:, 1], w_gu_one, w_dn_one)
     layer_two = (small[:, 2], w_qkv, w_out_window, small[:, 3], w_gu_two, w_dn_two)
-    middle, saved_linear = linear_forward(stream, layer_one[:5], layout_info)
     first_out, saved_ffn_one = ffn_forward(middle, layer_one[5:])
     second_mid, saved_window = window_forward(first_out, layer_two[:3], layout_info)
     closing, saved_ffn_two = ffn_forward(second_mid, layer_two[3:])
@@ -920,13 +1270,9 @@
     )
     grad_stream, grads_ffn_one = ffn_backward(grad_stream, saved_ffn_one, layer_one[5:])
     other_gains = jnp.stack([grads_ffn_one[0], grads_window[0], grads_ffn_two[0]], axis=1)
-    grad_stream, of_qk, of_values, of_out, small = linear_backward(
-        grad_stream, saved_linear, layer_one[:5], layout_info, other_gains
-    )
-    small, sums = summed_to_owners(
-        [
-            of_qk,
-            of_values,
+
+    def sum_others(of_out, state):
+        products = [
             of_out,
             grads_ffn_one[1],
             grads_ffn_one[2],
@@ -934,27 +1280,31 @@
             grads_window[2],
             grads_ffn_two[1],
             grads_ffn_two[2],
-        ],
-        small,
-    )
+        ]
+        return summed_to_owners(products, 1, out_linear.shape[0], -1, state)
+
+    grad_stream, own_sums, sums = linear_backward(
+        grad_stream, saved_linear, layer_one[:5], layout_info, other_gains, sum_others
+    )
+    small, grad_qk, grad_values = own_sums
     tokens_grad = grad_stream.astype(jnp.bfloat16)[:, None]
     return (
         output,
         tokens_grad,
         small[:, 0],
+        grad_qk,
+        grad_values,
+        small[:, 4:7],
         sums[0],
+        small[:, 1],
         sums[1],
-        small[:, 4:7],
         sums[2],
-        small[:, 1],
+        small[:, 2],
         sums[3],
         sums[4],
-        small[:, 2],
+        small[:, 3],
         sums[5],
         sums[6],
-        small[:, 3],
-        sums[7],
-        sums[8],
     )
 
 

time: 1140 us -> 829 us (0.73)
  matrix products: 268 us -> 103 us
  waiting for transfers between devices: 155 us -> 3.57 us
  Pallas kernels: 438 us -> 571 us
  other arithmetic: 101 us -> 41 us
  starting transfers between devices: 58.6 us -> 13.5 us
  local copies, waits for them, and re-layouts: 112 us -> 72.1 us
  between operations: 3.22 us -> 16 us
    dot_general x20 -> x0, matrix products: 159 us -> none  [the longest x3 40 us: attend_linear(): jnp.einsum('mihr,mhre->mihe', features, state_in, precision=highest)]
    ppermute x12 -> x0, waiting for transfers between devices: 155 us -> none  [the longest x6 88.5 us: carried_in(): lax.ppermute(a, axis, pairs).astype(own.dtype)]
    pallas_call x1 -> x10, Pallas kernels: 217 us -> 300 us  [the longest x2 188 us: gather_all(): pl.pallas_call(partial(gather_kernel, n_dp, n_ctx, chunks, lag, n, carry)...]
    pallas_call x1 -> x2, Pallas kernels: 221 us -> 271 us  [scatter_sums(): pl.pallas_call(partial(scatter_kernel, n_dp, n_ctx, plan, lags, len(xs),...]
    ppermute x12 -> x0, starting transfers between devices: 28.4 us -> none  [the longest x6 19.8 us: carried_in(): lax.ppermute(a, axis, pairs).astype(own.dtype)]
    reduce_sum x4 -> x0, other arithmetic: 20.7 us -> none  [the longest x2 16.3 us: feature_map(): source[..., :, None] * source[..., None, :]]
    div x5 -> x0, other arithmetic: 20.4 us -> none  [the longest x4 19.8 us: feature_map(): outer_prod / math.sqrt(2.0 * feat_width)]
    ppermute x4, starting transfers between devices: 30.1 us -> 13.5 us  [passed_along(): lax.ppermute(value, axis, [(source, source + steps) for source in range(l...]
  transfers between devices with their start and end apart: 16 -> 5, of which waited for: 3 -> 2; matrix products, arithmetic and copies ran while one was open for 17% -> 10% of each run, Pallas kernels for 0% -> 6%
where the time goes in v3:
time: 829 us; the launch traced here: 820 us
  Pallas kernels  571 us (69%)
  matrix products  103 us (12%)
  local copies, waits for them, and re-layouts  72.1 us (9%)
  other arithmetic  41 us (5%)
  between operations  16 us (2%)
  starting transfers between devices  13.5 us (2%)
    pallas_call x2, Pallas kernels, scatter_sums(): pl.pallas_call(partial(scatter_kernel, n_dp, n_ctx, plan, lags, len(xs),...  271 us
    pallas_call x2, Pallas kernels, gather_all(): pl.pallas_call(partial(gather_kernel, n_dp, n_ctx, chunks, lag, n, carry)...  188 us
    dot_general x9, matrix products, matmul_back(): jnp.einsum('mte,de->mtd', operand, weight, preferred_element_type=jnp.flo...  61 us
    pallas_call x4, Pallas kernels, by_pair(): pl.pallas_call(kernel, grid=(ins[0][0].shape[0], HEADS // 2 // PER), in_s...  58.9 us
    pallas_call x4, Pallas kernels, by_window(): pl.pallas_call(kernel, grid=(micro, steps), in_specs=[spec(rows, place, a...  53 us
    dot_general x9, matrix products, matmul(): jnp.einsum('mtd,de->mte', operand, weight, preferred_element_type=jnp.flo...  42 us
    unnamed x237, local copies, waits for them, and re-layouts  27.2 us
  transfers between devices with their start and end apart: 5, of which 2 were waited for; matrix products, arithmetic and copies ran while one was open for 10% of the time, Pallas kernels for 6%

profile of v3, /device:TPU:0, one launch (start us, length us, event | category | flops | bytes accessed | tf_op | source)
XLA Modules:
  0.0 820.2 jit_solution(14479375914057990619)
XLA Ops:
  11.8 30.4 %gather_weights.2 = (bf16[32,32,128]{2,1,0:T(8,128)(2,1)}, bf16[32,32,512]{2,1,0:T(8,128)(2,1)}, bf16[32,32,1024]{2,1,0:T(8,128)(2,1)}) custom-call(bf16[1,32,128]{2,1,0:T(8,128)(2,1)} %bitcast.295, bf16[1,32,512]{2,1,0:T(8,128)(2,1)} %bitcast.294, bf16[1,32,1024]{2,1,0:T(8,128)(2,1)} %bitcast.278), custom_call_target="tpu_custom_call" | custom-call | tf_op jit(solution)/shard_map/gather_weights/pallas_call | solution.py:204
  42.2 2.8 slice_convert_fusion
  45.5 3.0 fusion.39
  48.6 1.4 copy-done.31
  49.9 3.6 collective-permute-start
  56.1 1.6 multiply_convert_fusion.12.value_ref
  57.9 11.2 %states.1.refs_6_ = bf16[2,9,160,128]{3,2,1,0:T(8,128)(2,1)S(1)} custom-call(bf16[2,256,512]{2,1,0:T(8,128)(2,1)S(1)} %convolution_convert_fusion.2.key_ref.query_ref, bf16[2,256,1024]{2,1,0:T(8,128)(2,1)S(1)} %multiply_convert_fusion.12.value_ref, f32[2,256,128]{2,1,0:T(8,128)S(1)} %broadcast_in_dim.76.last_ref, bf16[2,256,256]{2,1,0:T(8,128)(2,1)S(1)} %copy-done.11, ...), custom_call_target="tpu_custom_call" | custom-call | tf_op jit(solution)/shard_map/states/pallas_call | solution.py:741
  70.7 157.8 %gather_weights.3 = (bf16[32,32,1024]{2,1,0:T(8,128)(2,1)}, bf16[32,32,5632]{2,1,0:T(8,128)(2,1)}, bf16[32,88,1024]{2,1,0:T(8,128)(2,1)}, bf16[32,32,3072]{2,1,0...) custom-call(bf16[1,32,1024]{2,1,0:T(8,128)(2,1)} %bitcast.276, ...), custom_call_target="tpu_custom_call" | custom-call | tf_op jit(solution)/shard_map/gather_weights/pallas_call | solution.py:204
  229.7 1.2 copy.151
  231.4 1.6 bitcast_convert_fusion.2
  233.0 3.1 copy.138
  239.3 11.7 %linear_attend.1 = (bf16[2,256,1024]{2,1,0:T(8,128)(2,1)S(1)}, f32[2,256,1024]{2,1,0:T(8,128)}) custom-call(bf16[2,256,512]{2,1,0:T(8,128)(2,1)S(1)} %convolution_convert_fusion.2.key_ref.query_ref, bf16[2,256,512]{2,1,0:T(8,128)(2,1)S(1)} %convolution_convert_fusion.2.key_ref.query_ref, bf16[2,256,1024]{2,1,0:T(8,128)(2,1)S(1)} %multiply_convert_fusion.12.value_ref, ...), custom_call_target="tpu_custom_call" | custom-call | tf_op jit(solution)/shard_map/linear_attend/pallas_call | solution.py:741
  251.0 1.4 multiply_reduce_fusion.11
  252.6 10.3 %fusion.77 = f32[2,256,5632]{2,1,0:T(8,128)S(1)} fusion(bf16[2,256,1024]{2,1,0:T(8,128)(2,1)S(1)} %multiply_convert_fusion.11, bf16[1024,5632,1]{1,0,2:T(8,128)(2,1)} %bitcast.311), kind=kOutput, calls=%fused_computation.190 | convolution fusion | flops 5905580032 | bytes 24117248 | tf_op jit(solution)/shard_map/mtd,de->mte/dot_general | solution.py:823
  262.9 1.9 multiply_convert_fusion.5
  264.8 2.3 copy-done.38
  267.1 3.3 multiply_reduce_fusion.10
  271.0 3.6 convolution_convert_fusion.query_ref.key_ref.value_ref
  275.6 7.1 collective-permute-start.1
  282.8 8.3 %window_later.1 = bf16[2,128,1024]{2,1,0:T(8,128)(2,1)S(1)} custom-call(bf16[2,256,3072]{2,1,0:T(8,128)(2,1)S(1)} %convolution_convert_fusion.query_ref.key_ref.value_ref, bf16[2,256,3072]{2,1,0:T(8,128)(2,1)S(1)} %convolution_convert_fusion.query_ref.key_ref.value_ref, bf16[2,256,3072]{2,1,0:T(8,128)(2,1)S(1)} %convolution_convert_fusion.query_ref.key_ref.value_ref, ...), custom_call_target="tpu_custom_call" | custom-call | tf_op jit(solution)/shard_map/window_later/pallas_call | solution.py:1099
  291.9 4.6 copy.132
  298.8 2.3 copy.133
  301.1 2.3 copy.131
  303.4 2.3 copy.130
  305.7 3.2 fusion.71
  308.9 8.6 %window_first.1 = bf16[2,128,1024]{2,1,0:T(8,128)(2,1)S(1)} custom-call(bf16[2,256,3072]{2,1,0:T(8,128)(2,1)S(1)} %convolution_convert_fusion.query_ref.key_ref.value_ref, bf16[2,256,3072]{2,1,0:T(8,128)(2,1)S(1)} %convolution_convert_fusion.query_ref.key_ref.value_ref, bf16[2,256,3072]{2,1,0:T(8,128)(2,1)S(1)} %convolution_convert_fusion.query_ref.key_ref.value_ref, ...), custom_call_target="tpu_custom_call" | custom-call | tf_op jit(solution)/shard_map/window_first/pallas_call | solution.py:1099
  318.3 1.3 copy.134
  319.7 3.6 multiply_reduce_fusion.9
  324.7 1.4 copy.135
  326.0 3.1 all-gather.2.cloned.1.call-done
  329.1 9.2 %fusion.2 = f32[2,256,5632]{2,1,0:T(8,128)S(1)} fusion(bf16[2,256,1024]{2,1,0:T(8,128)(2,1)} %copy-done.59, bf16[1024,5632]{1,0:T(8,128)(2,1)} %all-gather.2.cloned.1.call-done), kind=kOutput, calls=%fused_computation.2 | convolution fusion | flops 5905580032 | bytes 24117248 | tf_op jit(solution)/shard_map/mtd,de->mte/dot_general | solution.py:823
  338.4 10.3 %multiply_convert_fusion.3 = (bf16[2,256,2816]{2,1,0:T(8,128)(2,1)}, bf16[2,256,2816]{2,1,0:T(8,128)(2,1)}, bf16[2,256,2816]{2,1,0:T(8,128)(2,1)}) fusion(f32[2,256,5632]{2,1,0:T(8,128)S(1)} %fusion.2, bf16[2816,1024,1]{1,0,2:T(8,128)(2,1)} %bitcast.321, bf16[2,1,256,1024]{3,2,1,0:T(8,128)(2,1)S(1)} %copy-done.43, f32[2,256]{1,0:T(2,128)S(1)} %compare_convert_fusion), kind=kOutput, calls=%fused_computation.16 | convolution fusion | flops 2977431552 | bytes 27002880 | tf_op jit(solution)/shard_map/mte,de->mtd/dot_general | solution.py:827
  348.7 12.0 %multiply_reduce_fusion.3 = (f32[1024]{0:T(1024)S(1)}, f32[2,256]{1,0:T(2,128)S(1)}, f32[2,256,1024]{2,1,0:T(8,128)S(1)}) fusion(f32[2,256,1024]{2,1,0:T(8,128)S(1)} %get-tuple-element.267, f32[2,256]{1,0:T(2,128)S(1)} %fusion.55, f32[1024]{0:T(1024)S(1)} %bitcast.280, bf16[1024,5632]{1,0:T(8,128)(2,1)} %all-gather.2.cloned.1.call-done, ...), kind=kOutput, calls=%fused_computation.66 | convolution fusion | flops 5920258560 | bytes 21508096 | tf_op jit(solution)/shard_map/mte,de->mtd/dot_general | solution.py:827
  363.0 1.3 convolution_convert_fusion.1.grad_ref
  364.4 17.6 %window_first_back.1 = (bf16[2,128,1024]{2,1,0:T(8,128)(2,1)S(1)}, f32[2,128,1024]{2,1,0:T(8,128)S(1)}, f32[2,128,1024]{2,1,0:T(8,128)S(1)}, bf16[2,64,1024]{2,1,0:T(8,128)(2,1)S(1)}, bf16[2,64,1024]{2,1,0:T(8,128)(2,1)S(1)}) custom-call(bf16[2,256,3072]{2,1,0:T(8,128)(2,1)} %copy-done, bf16[2,256,3072]{2,1,0:T(8,128)(2,1)} %copy-done, ...), custom_call_target="tpu_custom_call" | custom-call | tf_op jit(solution)/shard_map/window_first_back/pallas_call | solution.py:1099
  382.9 1.3 collective-permute-start.2
  384.3 6.9 fusion.32
  391.2 2.9 pad_maximum_fusion.1.refs_16_
  394.1 4.6 copy.136
  398.7 1.3 slice.260
  401.1 18.4 %window_later_back.1 = (bf16[2,128,1024]{2,1,0:T(8,128)(2,1)S(1)}, f32[2,256,1024]{2,1,0:T(8,128)}, f32[2,256,1024]{2,1,0:T(8,128)}) custom-call(bf16[2,256,3072]{2,1,0:T(8,128)(2,1)} %copy-done, bf16[2,256,3072]{2,1,0:T(8,128)(2,1)} %copy-done, bf16[2,256,3072]{2,1,0:T(8,128)(2,1)} %copy-done, f32[2,256,256]{2,1,0:T(8,128)S(1)} %copy-done.7, ...), custom_call_target="tpu_custom_call" | custom-call | tf_op jit(solution)/shard_map/window_later_back/pallas_call | solution.py:1099
  419.5 1.6 fusion.70
  421.2 1.7 pad_convert_fusion
  425.1 6.7 multiply_reduce_fusion.4
  431.8 1.8 pad_maximum_fusion.2
  436.7 11.4 %multiply_convert_fusion.1 = (bf16[2,256,2816]{2,1,0:T(8,128)(2,1)}, bf16[2,256,2816]{2,1,0:T(8,128)(2,1)}) fusion(f32[2,256,5632]{2,1,0:T(8,128)} %copy-done.38, bf16[2,256,1024]{2,1,0:T(8,128)(2,1)S(1)} %get-tuple-element.223, bf16[2816,1024,1]{1,0,2:T(8,128)(2,1)} %bitcast.317), kind=kOutput, calls=%fused_computation.14 | convolution fusion | flops 2971533312 | bytes 24117248 | tf_op jit(solution)/shard_map/mte,de->mtd/dot_general | solution.py:827
  448.1 13.0 %multiply_reduce_fusion.5 = (f32[1024]{0:T(1024)S(1)}, f32[2,256]{1,0:T(2,128)S(1)}, f32[2,256,1024]{2,1,0:T(8,128)}) fusion(f32[2,256,1024]{2,1,0:T(8,128)S(1)} %copy-done.51, f32[2,256]{1,0:T(2,128)S(1)} %fusion.53, f32[1024]{0:T(1024)S(1)} %bitcast.289, bf16[1024,5632,1]{1,0,2:T(8,128)(2,1)} %bitcast.312, bf16[2,256,2816]{2,1,0:T(8,128)(2,1)} %get-tuple-element.226, ...), kind=kOutput, calls=%fused_computation.68 | convolution fusion | flops 5920258560 | bytes 21508096 | tf_op jit(solution)/shard_map/mte,de->mtd/dot_general | solution.py:827
  461.2 3.7 fusion.66
  465.0 2.6 fusion.23.grad_ref
  467.7 24.1 %linear_attend_back.1 = (f32[2,256,256]{2,1,0:T(8,128)S(1)}, f32[2,256,256]{2,1,0:T(8,128)S(1)}, f32[2,256,1024]{2,1,0:T(8,128)}, bf16[2,9,160,128]{3,2,1,0:T(8,128)(2,1)S(1)}) custom-call(bf16[2,256,512]{2,1,0:T(8,128)(2,1)S(1)} %copy-done.4, bf16[2,256,512]{2,1,0:T(8,128)(2,1)S(1)} %copy-done.4, bf16[2,256,1024]{2,1,0:T(8,128)(2,1)S(1)} %copy-done.2, ...), custom_call_target="tpu_custom_call" | custom-call | tf_op jit(solution)/shard_map/linear_attend_back/pallas_call | solution.py:741
  491.8 2.9 pad_maximum_fusion.refs_12_
  494.7 238.1 %scatter_sums.2 = (f32[32,1024]{1,0:T(8,128)}, f32[32,5632]{1,0:T(8,128)}, f32[88,1024]{1,0:T(8,128)}, f32[32,3072]{1,0:T(8,128)}, f32[32,1024]{1,0:T(8,128)}, /...) custom-call(bf16[8,128,512]{2,1,0:T(8,128)(2,1)} %bitcast.235, ...), custom_call_target="tpu_custom_call" | custom-call | tf_op jit(solution)/shard_map/scatter_sums/pallas_call | solution.py:480
  732.8 1.3 copy-done.25
  734.1 11.8 %states_back.1 = (f32[2,256,256]{2,1,0:T(8,128)S(1)}, f32[2,256,1024]{2,1,0:T(8,128)}) custom-call(bf16[2,256,512]{2,1,0:T(8,128)(2,1)S(1)} %copy-done.4, bf16[2,256,1024]{2,1,0:T(8,128)(2,1)S(1)} %copy-done.2, f32[2,256,128]{2,1,0:T(8,128)S(1)} %copy-done.19, bf16[2,256,256]{2,1,0:T(8,128)(2,1)S(1)} %copy-done.12, f32[8,256]{1,0:T(8,128)S(1)} %copy-done.30, ...), custom_call_target="tpu_custom_call" | custom-call | tf_op jit(solution)/shard_map/states_back/pallas_call | solution.py:741
  746.0 3.1 multiply_reduce_fusion.2
  750.9 1.6 collective-permute-start.3
  754.0 2.2 fusion.17
  758.2 3.0 fusion.30
  762.4 1.4 scatter.9
  763.7 2.3 copy.137
  766.0 1.2 multiply_convert_fusion.6
  767.2 32.8 %scatter_sums.3 = (f32[32,512]{1,0:T(8,128)}, f32[32,512]{1,0:T(8,128)}, f32[32,1024]{1,0:T(8,128)}) custom-call(bf16[8,128,512]{2,1,0:T(8,128)(2,1)} %bitcast.250, bf16[8,128,512]{2,1,0:T(8,128)(2,1)} %bitcast.251, bf16[512,512]{1,0:T(8,128)(2,1)} %constant.149.clone.refs_2_, bf16[512,512]{1,0:T(8,128)(2,1)} %pad_maximum_fusion.6.refs_3_, ...), custom_call_target="tpu_custom_call" | custom-call | tf_op jit(solution)/shard_map/scatter_sums/pallas_call | solution.py:480
  800.8 1.6 slice_reduce_fusion
  803.1 3.2 fusion.37
  (322 shorter events, 45.2 us)
Async XLA Ops:
  7.2 38.0 %copy-start.40 = (bf16[2,1,256,1024]{3,2,1,0:T(8,128)(2,1)S(1)}, bf16[2,1,256,1024]{3,2,1,0:T(8,128)(2,1)}, u32[]{:S(2)}) copy-start(bf16[2,1,256,1024]{3,2,1,0:T(8,128)(2,1)} %param.26) | copy-start | bytes 3145732
  7.2 321.9 %all-gather.2.cloned.1.call-start = ((), (), s32[]{:S(2)}) async-start(), calls=%async_computation | async-start | bytes 11894784 | tf_op jit(solution)/shard_map/all_gather | solution.py:1258
  45.2 9.3 %copy-start.92 = (f32[1024,1]{0,1:T(1,128)}, f32[1024,1]{0,1:T(1,128)S(1)}, u32[]{:S(2)}) copy-start(f32[1024,1]{0,1:T(1,128)S(1)} %copy.149) | copy-start | bytes 12292
  45.5 9.0 %copy-start.98 = (f32[2,256]{1,0:T(2,128)}, f32[2,256]{1,0:T(2,128)S(1)}, u32[]{:S(2)}) copy-start(f32[2,256]{1,0:T(2,128)S(1)} %fusion.52) | copy-start | bytes 6148
  45.5 8.1 copy-start.54
  45.5 8.2 copy-start.100
  45.5 9.0 %copy-start.69 = (bf16[32,32,512]{2,1,0:T(8,128)(2,1)S(1)}, bf16[32,32,512]{2,1,0:T(8,128)(2,1)}, u32[]{:S(2)}) copy-start(bf16[32,32,512]{2,1,0:T(8,128)(2,1)} %get-tuple-element.96) | copy-start | bytes 3145732
  49.9 5.6 collective-permute-start
  55.3 183.6 %copy-start.3 = (bf16[2,256,512]{2,1,0:T(8,128)(2,1)}, bf16[2,256,512]{2,1,0:T(8,128)(2,1)S(1)}, u32[]{:S(2)}) copy-start(bf16[2,256,512]{2,1,0:T(8,128)(2,1)S(1)} %convolution_convert_fusion.2.key_ref.query_ref) | copy-start | bytes 1572868
  55.6 13.5 %copy-start.76 = (f32[2,2,1024]{2,1,0:T(2,128)}, f32[2,2,1024]{2,1,0:T(2,128)S(1)}, u32[]{:S(2)}) copy-start(f32[2,2,1024]{2,1,0:T(2,128)S(1)} %collective-permute-done) | copy-start | bytes 49156
  57.7 181.2 %copy-start.1 = (bf16[2,256,1024]{2,1,0:T(8,128)(2,1)}, bf16[2,256,1024]{2,1,0:T(8,128)(2,1)S(1)}, u32[]{:S(2)}) copy-start(bf16[2,256,1024]{2,1,0:T(8,128)(2,1)S(1)} %multiply_convert_fusion.12.value_ref) | copy-start | bytes 3145732
  57.8 11.3 %copy-start.18 = (f32[2,256,128]{2,1,0:T(8,128)}, f32[2,256,128]{2,1,0:T(8,128)S(1)}, u32[]{:S(2)}) copy-start(f32[2,256,128]{2,1,0:T(8,128)S(1)} %broadcast_in_dim.76.last_ref) | copy-start | bytes 786436
  236.8 46.0 %copy-start.5 = (f32[2,256,256]{2,1,0:T(8,128)}, f32[2,256,256]{2,1,0:T(8,128)S(1)}, u32[]{:S(2)}) copy-start(f32[2,256,256]{2,1,0:T(8,128)S(1)} %add_convert_fusion.mask_ref) | copy-start | bytes 1572868
  239.3 11.7 %copy-start.16 = (f32[2,256,128]{2,1,0:T(8,128)}, f32[2,256,128]{2,1,0:T(8,128)S(1)}, u32[]{:S(2)}) copy-start(f32[2,256,128]{2,1,0:T(8,128)S(1)} %broadcast_in_dim.78.carried_ref) | copy-start | bytes 786436
  239.3 11.7 %copy-start.102 = (bf16[32,32,1024]{2,1,0:T(8,128)(2,1)S(1)}, bf16[32,32,1024]{2,1,0:T(8,128)(2,1)}, u32[]{:S(2)}) copy-start(bf16[32,32,1024]{2,1,0:T(8,128)(2,1)} %get-tuple-element.100) | copy-start | bytes 6291460
  252.3 14.8 %copy-start.50 = (f32[2,256,1024]{2,1,0:T(8,128)}, f32[2,256,1024]{2,1,0:T(8,128)S(1)}, u32[]{:S(2)}) copy-start(f32[2,256,1024]{2,1,0:T(8,128)S(1)} %get-tuple-element.263) | copy-start | bytes 6291460
  252.4 14.8 %slice-start.2 = ((s8[5767168]{0:T(1024)(128)(4,1)}), s8[4194304]{0:T(1024)(128)(4,1)S(1)}, s32[]{:S(2)}) async-start(s8[5767168]{0:T(1024)(128)(4,1)} %bitcast.318), calls=%async_computation.3 | async-start | bytes 8388608
  252.6 10.3 %copy-start.57 = (bf16[2,256,1024]{2,1,0:T(8,128)(2,1)}, bf16[2,256,1024]{2,1,0:T(8,128)(2,1)S(1)}, u32[]{:S(2)}) copy-start(bf16[2,256,1024]{2,1,0:T(8,128)(2,1)S(1)} %multiply_convert_fusion.11) | copy-start | bytes 3145732
  252.6 14.5 %slice-start.3 = ((s8[5767168]{0:T(1024)(128)(4,1)}), s8[1572864]{0:T(1024)(128)(4,1)S(1)}, s32[]{:S(2)}) async-start(s8[5767168]{0:T(1024)(128)(4,1)} %bitcast.318), calls=%async_computation.4 | async-start | bytes 3145728
  262.9 4.2 copy-start.38
  267.1 3.3 copy-start.37
  267.1 3.6 slice-start
  267.1 3.9 slice-start.1
  270.4 4.3 copy-start.52
  270.7 4.0 copy-start.58
  274.7 34.2 %copy-start = (bf16[2,256,3072]{2,1,0:T(8,128)(2,1)}, bf16[2,256,3072]{2,1,0:T(8,128)(2,1)S(1)}, u32[]{:S(2)}) copy-start(bf16[2,256,3072]{2,1,0:T(8,128)(2,1)S(1)} %convolution_convert_fusion.query_ref.key_ref.value_ref) | copy-start | bytes 9437188
  275.6 33.3 %collective-permute-start.1 = (bf16[2,64,2048]{2,1,0:T(8,128)(2,1)}, bf16[2,64,2048]{2,1,0:T(8,128)(2,1)}, u32[]{:S(2)}, u32[]{:S(2)}) collective-permute-start(bf16[2,64,2048]{2,1,0:T(8,128)(2,1)} %slice.245), channel_id=1, source_target_pairs={{0,1},{1,2},{2,3},{4,5},{5,6},{6,7},{8,9},{9,10},{10,11},{12,13},{... | collective-permute-start | bytes 1572872 | tf_op jit(solution)/shard_map/ppermute | solution.py:518
  305.7 3.2 copy-start.6
  308.9 8.6 %copy-start.21 = (bf16[2,128,1024]{2,1,0:T(8,128)(2,1)S(1)}, bf16[2,128,1024]{2,1,0:T(8,128)(2,1)}, u32[]{:S(2)}) copy-start(bf16[2,128,1024]{2,1,0:T(8,128)(2,1)} %copy-done.20) | copy-start | bytes 1572868
  323.2 37.5 %copy-start.34 = (f32[2,256,1024]{2,1,0:T(8,128)}, f32[2,256,1024]{2,1,0:T(8,128)S(1)}, u32[]{:S(2)}) copy-start(f32[2,256,1024]{2,1,0:T(8,128)S(1)} %get-tuple-element.267) | copy-start | bytes 6291460
  326.0 12.3 %copy-start.43 = (bf16[2,1,256,1024]{3,2,1,0:T(8,128)(2,1)S(1)}, bf16[2,1,256,1024]{3,2,1,0:T(8,128)(2,1)}, u32[]{:S(2)}) copy-start(bf16[2,1,256,1024]{3,2,1,0:T(8,128)(2,1)} %param.42) | copy-start | bytes 3145732
  364.4 19.8 %copy-start.35 = (f32[2,256,1024]{2,1,0:T(8,128)S(1)}, f32[2,256,1024]{2,1,0:T(8,128)}, u32[]{:S(2)}) copy-start(f32[2,256,1024]{2,1,0:T(8,128)} %copy-done.34) | copy-start | bytes 6291460
  364.4 19.8 %copy-start.62 = (bf16[2,256,2816]{2,1,0:T(8,128)(2,1)S(1)}, bf16[2,256,2816]{2,1,0:T(8,128)(2,1)}, u32[]{:S(2)}) copy-start(bf16[2,256,2816]{2,1,0:T(8,128)(2,1)} %get-tuple-element.229) | copy-start | bytes 8650756
  382.1 9.1 %copy-start.26 = (f32[2,128,1024]{2,1,0:T(8,128)}, f32[2,128,1024]{2,1,0:T(8,128)S(1)}, u32[]{:S(2)}) copy-start(f32[2,128,1024]{2,1,0:T(8,128)S(1)} %get-tuple-element.111.first_dvalue_ref) | copy-start | bytes 3145732
  382.9 38.2 %collective-permute-start.2 = (bf16[2,64,2048]{2,1,0:T(8,128)(2,1)}, bf16[2,64,2048]{2,1,0:T(8,128)(2,1)}, u32[]{:S(2)}, u32[]{:S(2)}) collective-permute-start(bf16[2,64,2048]{2,1,0:T(8,128)(2,1)} %pad_maximum_fusion.5), channel_id=1, source_target_pairs={{1,0},{2,1},{3,2},{5,4},{6,5},{7,6},{9,8},{10,9},{11,10},{13,12},{... | collective-permute-start | bytes 1572872 | tf_op jit(solution)/shard_map/ppermute | solution.py:518
  384.2 6.9 copy-start.65
  384.3 6.9 copy-start.66
  401.1 18.4 %copy-start.39 = (bf16[2816,512]{1,0:T(8,128)(2,1)S(1)}, bf16[2816,512]{1,0:T(8,128)(2,1)}, u32[]{:S(2)}) copy-start(bf16[2816,512]{1,0:T(8,128)(2,1)} %copy.136) | copy-start | bytes 8650756
  431.8 3.7 copy-start.48
  436.7 11.4 %copy-start.60 = (bf16[2,256,1024]{2,1,0:T(8,128)(2,1)}, bf16[2,256,1024]{2,1,0:T(8,128)(2,1)S(1)}, u32[]{:S(2)}) copy-start(bf16[2,256,1024]{2,1,0:T(8,128)(2,1)S(1)} %get-tuple-element.223) | copy-start | bytes 3145732
  436.7 11.4 %copy-start.51 = (f32[2,256,1024]{2,1,0:T(8,128)S(1)}, f32[2,256,1024]{2,1,0:T(8,128)}, u32[]{:S(2)}) copy-start(f32[2,256,1024]{2,1,0:T(8,128)} %copy-done.50) | copy-start | bytes 6291460
  461.2 3.7 copy-start.103
  467.6 24.1 %copy-start.63 = (bf16[2,256,2816]{2,1,0:T(8,128)(2,1)S(1)}, bf16[2,256,2816]{2,1,0:T(8,128)(2,1)}, u32[]{:S(2)}) copy-start(bf16[2,256,2816]{2,1,0:T(8,128)(2,1)} %get-tuple-element.225) | copy-start | bytes 8650756
  467.7 24.1 %copy-start.64 = (bf16[2,256,2816]{2,1,0:T(8,128)(2,1)S(1)}, bf16[2,256,2816]{2,1,0:T(8,128)(2,1)}, u32[]{:S(2)}) copy-start(bf16[2,256,2816]{2,1,0:T(8,128)(2,1)} %get-tuple-element.226) | copy-start | bytes 8650756
  494.7 238.1 %copy-start.19 = (f32[2,256,128]{2,1,0:T(8,128)S(1)}, f32[2,256,128]{2,1,0:T(8,128)}, u32[]{:S(2)}) copy-start(f32[2,256,128]{2,1,0:T(8,128)} %copy-done.18) | copy-start | bytes 786436
  734.1 11.9 %copy-start.33 = (f32[2,256,1024]{2,1,0:T(8,128)S(1)}, f32[2,256,1024]{2,1,0:T(8,128)}, u32[]{:S(2)}) copy-start(f32[2,256,1024]{2,1,0:T(8,128)} %copy-done.31) | copy-start | bytes 6291460
  734.1 11.9 %copy-start.77 = (f32[2,2,1024]{2,1,0:T(2,128)S(1)}, f32[2,2,1024]{2,1,0:T(2,128)}, u32[]{:S(2)}) copy-start(f32[2,2,1024]{2,1,0:T(2,128)} %copy-done.76) | copy-start | bytes 49156
  734.1 11.9 %copy-start.89 = (f32[2,256]{1,0:T(2,128)S(1)}, f32[2,256]{1,0:T(2,128)}, u32[]{:S(2)}) copy-start(f32[2,256]{1,0:T(2,128)} %copy-done.88) | copy-start | bytes 6148
  734.1 11.9 %copy-start.91 = (f32[2,256]{1,0:T(2,128)S(1)}, f32[2,256]{1,0:T(2,128)}, u32[]{:S(2)}) copy-start(f32[2,256]{1,0:T(2,128)} %copy-done.90) | copy-start | bytes 6148
  734.1 11.9 %copy-start.97 = (f32[256]{0:T(256)S(1)}, f32[256]{0:T(256)}, u32[]{:S(2)}) copy-start(f32[256]{0:T(256)} %copy-done.96) | copy-start | bytes 3076
  746.0 3.2 copy-start.82
  746.0 3.2 copy-start.84
  750.8 3.2 copy-start.45
  750.9 5.9 collective-permute-start.3
  761.2 4.8 copy-start.46
  767.2 35.8 %copy-start.49 = (f32[2,256,1024]{2,1,0:T(8,128)S(1)}, f32[2,256,1024]{2,1,0:T(8,128)}, u32[]{:S(2)}) copy-start(f32[2,256,1024]{2,1,0:T(8,128)} %get-tuple-element.222) | copy-start | bytes 6291460
  803.1 3.3 copy-start.87
  803.1 3.9 copy-start.80
  803.1 4.5 copy-start.79
  803.1 5.2 copy-start.72
  806.3 3.6 copy-start.73
  806.3 4.3 copy-start.78
  806.3 5.0 copy-start.71
  808.3 3.9 copy-start.74
  (50 other events, 105.0 us)
Sparse Core Ops, SparseCore 0:
  228.6 100.4 all-gather.1

commit v4 on v3

--- a/solution.py
+++ b/solution.py
@@ -25,55 +25,56 @@
 def carried(sign, n_ctx, dp, ctx, own, keep, out, came, total, sent, arrived):
     first, last = (0, n_ctx - 1) if sign > 0 else (n_ctx - 1, 0)
     low, f32 = jnp.bfloat16, jnp.float32
-    planes, rows = own.shape[1:3]
-
-    def copy(m):
+    micro, planes, rows = own.shape[:3]
+
+    def copy(m, p):
         return pltpu.make_async_remote_copy(
-            src_ref=total.at[m],
-            dst_ref=came.at[m],
-            send_sem=sent.at[m],
-            recv_sem=arrived.at[m],
+            src_ref=total.at[m, p],
+            dst_ref=came.at[m, p],
+            send_sem=sent.at[m, p],
+            recv_sem=arrived.at[m, p],
             device_id=(dp, lax.rem(ctx + sign + n_ctx, n_ctx)),
             device_id_type=MESH,
         )
 
-    def act(m):
+    def act(i):
+        m, p = i // planes, i % planes
+
         @pl.when(ctx != first)
         def _():
-            copy(m).wait_recv()
-            for p in range(planes):
-                value = came[m, p]
-                out[m, p, :rows] = value
-                total[m, p] = (own[m, p].astype(f32) + keep[m, 0:1] * value.astype(f32)).astype(low)
+            copy(m, p).wait_recv()
+            value = came[m, p]
+            out[m, p, :rows] = value
+            total[m, p] = (own[m, p].astype(f32) + keep[m, 0:1] * value.astype(f32)).astype(low)
 
         @pl.when(ctx == first)
         def _():
-            for p in range(planes):
-                out[m, p, :rows] = jnp.zeros((rows, 128), low)
-                total[m, p] = own[m, p]
+            out[m, p, :rows] = jnp.zeros((rows, 128), low)
+            total[m, p] = own[m, p]
 
         @pl.when(ctx != last)
         def _():
-            copy(m).start()
+            copy(m, p).start()
 
     def finish():
-        for m in range(own.shape[0]):
+        for m in range(micro):
             for p in range(planes):
                 out[m, p, rows:] = jnp.zeros((out.shape[2] - rows, 128), low)
 
         @pl.when(ctx != last)
         def _():
-            for m in range(own.shape[0]):
-                copy(m).wait_send()
-
-    return act, finish
+            for m in range(micro):
+                for p in range(planes):
+                    copy(m, p).wait_send()
+
+    return micro * planes, act, finish
 
 
 def carry_specs(state):
     whole = pl.BlockSpec(memory_space=pltpu.VMEM)
     shape = state.shape[:2] + (TERMS,) + state.shape[3:]
     held = pltpu.VMEM(state.shape, jnp.bfloat16)
-    sems = pltpu.SemaphoreType.DMA((state.shape[0],))
+    sems = pltpu.SemaphoreType.DMA(state.shape[:2])
     return [whole, whole], [whole], [jax.ShapeDtypeStruct(shape, jnp.bfloat16)], [held, held, sems, sems]
 
 
@@ -178,15 +179,16 @@
     due = {}
     if carry:
         own, keep = refs[n_w:n_w + 2]
-        act, finish = carried(carry, n_ctx, dp, ctx, own, keep, refs[2 * n_w + 2], *refs[2 * n_w + 6:])
-        micro = own.shape[0]
-        for n in range(n_ctx * micro):
-            due.setdefault(n * turns // (n_ctx * micro), []).append((n // micro, n % micro))
+        n_pieces, act, finish = carried(carry, n_ctx, dp, ctx, own, keep, refs[2 * n_w + 2], *refs[2 * n_w + 6:])
+        for place in range(n_ctx):
+            for i in range(n_pieces):
+                due.setdefault(place + i // 2, []).append((place, i))
+        turns = max(turns, max(due) + 1)
     for t in range(turns):
-        for place, m in due.get(t, []):
+        for place, i in due.get(t, []):
             @pl.when(ctx == (place if carry > 0 else n_ctx - 1 - place))
             def _():
-                act(m)
+                act(i)
         for s in range(depth):
             c = t - s * lag
             if 0 <= c < len(chunks):
@@ -215,9 +217,11 @@
 
 WIDE = 512
 SLOTS_HELD = 8
-
-
-def scatter_kernel(n_dp, n_ctx, plan, lags, n_x, n_y, n_o, carry, *refs):
+APART = 4
+
+
+def scatter_kernel(n_dp, n_ctx, plan, lags, pieces, n_y, n_o, carry, *refs):
+    n_x = len(pieces)
     xs, ys, refs = refs[:n_x], refs[n_x : n_x + n_y], refs[n_x + n_y :]
     state, refs = (refs[:2], refs[2:]) if carry else ((), refs)
     outs, refs = refs[:n_o], refs[n_o:]
@@ -225,7 +229,7 @@
     bits = [1 << i for i in range(n_dp.bit_length() - 1)]
     low_bits, (bit_x, bit_y) = bits[:-2], bits[-2:]
     n_low = len(low_bits)
-    x_all, y_all = refs[0], refs[1]
+    x_all, y_all, natural = refs[0], refs[1], refs[-1]
     low_out, low_in = refs[2 : 2 + n_low], refs[2 + n_low : 2 + 2 * n_low]
     refs = refs[2 + 2 * n_low :]
     cross, cross_y, cross_x, side_x, side_y, came_x, came_y, shards, came_ctx, result = refs[:10]
@@ -253,13 +257,22 @@
     for segment in plan:
         bounds.append((count, count + segment[5]))
         count += segment[5]
-    x_first = [None] * n_x
+    laid_at = [sum(max(1, n) for n in pieces[:i]) for i in range(n_x)]
+    x_first = {}
     for segment, (first, _) in zip(plan, bounds):
-        if x_first[segment[0]] is None:
-            x_first[segment[0]] = first
+        x_first.setdefault(segment[0], first)
 
     def x_copy(i):
-        return pltpu.make_async_copy(xs[i], x_all.at[i], x_sem.at[i])
+        if pieces[i]:
+            return pltpu.make_async_copy(xs[i], x_all.at[pl.ds(laid_at[i], pieces[i])], x_sem.at[i])
+        return pltpu.make_async_copy(xs[i], natural.at[pieces[:i].count(0)], x_sem.at[i])
+
+    def x_ready(i):
+        x_copy(i).wait()
+        if not pieces[i]:
+            for place in range(n_dp):
+                value = natural[pieces[:i].count(0), :, place * group : (place + 1) * group]
+                x_all[laid_at[i], place] = value.T
 
     for i in range(n_x):
         x_copy(i).start()
@@ -276,7 +289,7 @@
                 ).start()
 
     def x_place(c):
-        return sum((c >= first).astype(jnp.int32) for first in x_first[1:])
+        return sum((c >= first).astype(jnp.int32) for first in sorted(x_first.values())[1:])
 
     def partial_sum(c, flip):
         return jnp.dot(
@@ -329,11 +342,11 @@
     def step_low(level, c):
         slot = lax.rem(c, held)
         if level == 0:
-            for i, first in enumerate(x_first):
-
-                @pl.when(c == first)
+            for i in range(n_x):
+
+                @pl.when(c == x_first[laid_at[i]])
                 def _():
-                    x_copy(i).wait()
+                    x_ready(i)
 
             pltpu.make_async_copy(ys[0].at[:, pl.ds(0, WIDE)], y_all.at[slot], y_sem.at[slot]).wait()
         else:
@@ -432,18 +445,17 @@
 
     turns = count + lags[-1]
     if carry:
-        act, finish = carried(carry, n_ctx, dp, ctx, *state, *state_out, *refs[16:])
-        micro = state[0].shape[0]
-        stride = turns // (n_ctx * micro)
+        n_pieces, act, finish = carried(carry, n_ctx, dp, ctx, *state, *state_out, *refs[16:-1])
         place = ctx if carry > 0 else n_ctx - 1 - ctx
+        turns = max(turns, n_pieces + APART * (n_ctx - 1))
 
     def turn(t, none):
         if carry:
-            for m in range(micro):
-
-                @pl.when(t == (place * micro + m) * stride)
-                def _():
-                    act(m)
+            i = t - APART * place
+
+            @pl.when((i >= 0) & (i < n_pieces))
+            def _():
+                act(i)
 
         @pl.when(t + ahead < count)
         def _():
@@ -466,7 +478,9 @@
 
 
 def scatter_sums(xs, ys, out_shapes, plan, n_dp, n_ctx, cid=1, carry=0, state=(), lags=None, held=SLOTS_HELD):
-    group, tokens = xs[0].shape[1:]
+    pieces = [n for _, n in xs]
+    tokens = ys[0].shape[0]
+    group = [x.shape[1] // n_dp for x, n in xs if not n][0]
     n_low = n_dp.bit_length() - 3
     rows = group // n_ctx
     low, f32 = jnp.bfloat16, jnp.float32
@@ -478,12 +492,12 @@
     kinds = n_low + 4 + n_ctx - 1
     more_in, more_out, more_shape, more_scratch = carry_specs(state[0]) if carry else ([], [], [], [])
     return pl.pallas_call(
-        partial(scatter_kernel, n_dp, n_ctx, plan, lags, len(xs), len(ys), len(out_shapes), carry),
+        partial(scatter_kernel, n_dp, n_ctx, plan, lags, pieces, len(ys), len(out_shapes), carry),
         out_shape=[jax.ShapeDtypeStruct(shape, f32) for shape in out_shapes] + more_shape,
         in_specs=[pl.BlockSpec(memory_space=pl.ANY)] * (len(xs) + len(ys)) + more_in,
         out_specs=[pl.BlockSpec(memory_space=pltpu.HBM)] * len(out_shapes) + more_out,
         scratch_shapes=[
-            pltpu.VMEM((len(xs),) + xs[0].shape, low),
+            pltpu.VMEM((sum(max(1, n) for n in pieces), n_dp, group, tokens), low),
             pltpu.VMEM((held, tokens, WIDE), low),
             *low_shapes,
             *low_shapes,
@@ -504,12 +518,13 @@
             pltpu.SemaphoreType.DMA((held, kinds)),
             pltpu.SemaphoreType.REGULAR((n_low + 2 + n_ctx - 1,)),
             *more_scratch,
+            pltpu.VMEM((pieces.count(0), tokens, n_dp * group), low),
         ],
         compiler_params=pltpu.CompilerParams(
             collective_id=cid, has_side_effects=True, vmem_limit_bytes=56 * 2**20
         ),
         name="scatter_sums",
-    )(*xs, *ys, *state)
+    )(*[x for x, _ in xs], *ys, *state)
 
 
 def passed_along(value, axis, steps):
@@ -749,21 +764,53 @@
     )(*[array for array, _ in ins])
 
 
+def turn_kernel(places, unit, value_ref, out_ref, turned):
+    tokens, rows = value_ref.shape
+    for first in range(0, rows, 128):
+        turned[first : first + 128] = value_ref[:, first : first + 128].T.astype(jnp.float32)
+    pieces, n_dp = out_ref.shape[:2]
+    n_ctx, shard = places // n_dp, rows // places
+    for place in range(places):
+        for piece in range(pieces):
+            start, count = piece * unit, min(unit, shard - piece * unit)
+            value = turned[place * shard + start : place * shard + start + count]
+            if count < unit:
+                value = jnp.concatenate([value, jnp.zeros((unit - count, tokens), jnp.float32)], axis=0)
+            where = place % n_ctx * unit
+            out_ref[piece, place // n_ctx, where : where + unit] = value.astype(jnp.bfloat16)
+
+
+def turned_pieces(value, places, n_dp, unit):
+    tokens, rows = value.shape
+    pieces = -(-(rows // places) // unit)
+    return pl.pallas_call(
+        partial(turn_kernel, places, unit),
+        out_shape=jax.ShapeDtypeStruct((pieces, n_dp, places // n_dp * unit, tokens), jnp.bfloat16),
+        in_specs=[pl.BlockSpec(memory_space=pltpu.VMEM)],
+        out_specs=pl.BlockSpec(memory_space=pltpu.VMEM),
+        scratch_shapes=[pltpu.VMEM((rows, tokens), jnp.float32)],
+        compiler_params=pltpu.CompilerParams(vmem_limit_bytes=48 * 2**20),
+        name="turn",
+    )(value)
+
+
 def chunk_plan(products, unit):
-    places, n_dp = lax.axis_size("dp") * lax.axis_size("ctx"), lax.axis_size("dp")
-    laid, first_laid, plan, shapes = [], {}, [], []
+    n_dp = lax.axis_size("dp")
+    places = n_dp * lax.axis_size("ctx")
+    operands, first_laid, plan, shapes, count = [], {}, [], [], 0
     for number, (operand, gradient) in enumerate(products):
-        tokens, rows = operand.shape
-        shard = rows // places
+        shard = operand.shape[1] // places
+        pieces = -(-shard // unit)
         shapes.append((shard, gradient.shape[1]))
         if id(operand) not in first_laid:
-            first_laid[id(operand)] = len(laid)
-            turned = operand.T.reshape(places, shard, tokens)
-            for first in range(0, shard, unit):
-                piece = turned[:, first : first + unit]
-                piece = jnp.pad(piece, ((0, 0), (0, unit - piece.shape[1]), (0, 0)))
-                laid.append(piece.reshape(n_dp, -1, tokens))
-        for piece, first in enumerate(range(0, shard, unit)):
+            first_laid[id(operand)] = count
+            count += pieces
+            if pieces > 1:
+                operands.append((turned_pieces(operand, places, n_dp, unit), pieces))
+            else:
+                operands.append((operand, 0))
+        for piece in range(pieces):
+            first = piece * unit
             plan.append(
                 (
                     first_laid[id(operand)] + piece,
@@ -774,7 +821,7 @@
                     gradient.shape[1] // WIDE,
                 )
             )
-    return laid, plan, shapes
+    return operands, plan, shapes
 
 
 def as_product(small):
@@ -1174,7 +1221,7 @@
         axis=-1,
     )
     grad_qkv_weight = (flat(normed_low), flat(grad_qkv))
-    grad_input, grad_gain = norm_back(matmul_back(grad_qkv, qkv_weight))
+    grad_input, grad_gain = norm_back(lax.optimization_barrier(matmul_back(grad_qkv, qkv_weight)))
     return (grad_stream + grad_input, (grad_gain, grad_qkv_weight, grad_out))
 
 
@@ -1187,6 +1234,7 @@
     hidden = (jax.nn.silu(projected[..., :hidden_width]) * projected[..., hidden_width:]).astype(
         jnp.bfloat16
     )
+    hidden, projected = lax.optimization_barrier((hidden, projected.astype(jnp.bfloat16)))
     branch = matmul(hidden, down_weight)
     return (stream + branch, (norm_back, normed_low, projected, hidden))
 
@@ -1198,14 +1246,14 @@
     grad_branch = grad_stream.astype(jnp.bfloat16)
     grad_down = (flat(hidden), flat(grad_branch))
     grad_hidden = matmul_back(grad_branch, down_weight)
-    gate_part = projected[..., :hidden_width]
-    up_part = projected[..., hidden_width:]
+    gate_part = projected[..., :hidden_width].astype(jnp.float32)
+    up_part = projected[..., hidden_width:].astype(jnp.float32)
     sigmoid_gate = jax.nn.sigmoid(gate_part)
     grad_gate = grad_hidden * up_part * sigmoid_gate * (1.0 + gate_part * (1.0 - sigmoid_gate))
     grad_up = grad_hidden * gate_part * sigmoid_gate
     grad_projected = jnp.concatenate([grad_gate, grad_up], axis=-1).astype(jnp.bfloat16)
     grad_gate_up = (flat(normed_low), flat(grad_projected))
-    grad_input, grad_gain = norm_back(matmul_back(grad_projected, gate_up))
+    grad_input, grad_gain = norm_back(lax.optimization_barrier(matmul_back(grad_projected, gate_up)))
     return (grad_stream + grad_input, (grad_gain, grad_gate_up, grad_down))
 
 
@@ -1254,8 +1302,7 @@
         stream, (small[:, 0], w_qk, w_values, small[:, 4:7]), layout_info, gather_more
     )
     w_out_linear, w_gu_one, w_dn_one, w_qkv, w_out_window, w_dn_two = more
-    w_out_linear, late = lax.optimization_barrier((w_out_linear, gate_up_two))
-    w_gu_two = lax.all_gather(late, ("dp", "ctx"), axis=0, tiled=True)
+    w_gu_two = lax.all_gather(gate_up_two, ("dp", "ctx"), axis=0, tiled=True)
     layer_one = (small[:, 0], w_qk, w_values, small[:, 4:7], w_out_linear, small[:, 1], w_gu_one, w_dn_one)
     layer_two = (small[:, 2], w_qkv, w_out_window, small[:, 3], w_gu_two, w_dn_two)
     first_out, saved_ffn_one = ffn_forward(middle, layer_one[5:])
@@ -1265,6 +1312,12 @@
     output = (closing * valid_rows).astype(jnp.bfloat16)[:, None]
     grad_stream = cotangent[:, 0].astype(jnp.float32) * valid_rows
     grad_stream, grads_ffn_two = ffn_backward(grad_stream, saved_ffn_two, layer_two[3:])
+    operand, gradient = grads_ffn_two[1]
+    partial_sums = jnp.einsum("tr,te->re", operand, gradient, preferred_element_type=jnp.float32)
+    partial_sums = partial_sums.astype(jnp.bfloat16)
+    for axis in ("dp", "ctx"):
+        partial_sums = lax.psum_scatter(partial_sums, axis, scatter_dimension=0, tiled=True)
+    sum_gate_up_two = partial_sums.astype(jnp.float32)
     grad_stream, grads_window = window_backward(
         grad_stream, saved_window, layer_two[:3], layout_info
     )
@@ -1278,7 +1331,6 @@
             grads_ffn_one[2],
             grads_window[1],
             grads_window[2],
-            grads_ffn_two[1],
             grads_ffn_two[2],
         ]
         return summed_to_owners(products, 1, out_linear.shape[0], -1, state)
@@ -1303,8 +1355,8 @@
         sums[3],
         sums[4],
         small[:, 3],
+        sum_gate_up_two,
         sums[5],
-        sums[6],
     )
 
 

time: 829 us -> 757 us (0.913)
  Pallas kernels: 571 us -> 512 us
  local copies, waits for them, and re-layouts: 72.1 us -> 37.3 us
  matrix products: 103 us -> 115 us
  other arithmetic: 41 us -> 49.8 us
    pallas_call x2 -> x4, Pallas kernels: 271 us -> 199 us  [the longest x2 197 us: scatter_sums(): pl.pallas_call(partial(scatter_kernel, n_dp, n_ctx, plan, lags, pieces, l...]
    pallas_call x2, Pallas kernels: 188 us -> 203 us  [gather_all(): pl.pallas_call(partial(gather_kernel, n_dp, n_ctx, chunks, lag, n, carry)...]
    transpose x3 -> x0, local copies, waits for them, and re-layouts: 11.5 us -> none  [chunk_plan(): turned = operand.T.reshape(places, shard, tokens)]
    dot_general x0 -> x1, matrix products: none -> 10.9 us  [body(): jnp.einsum('tr,te->re', operand, gradient, preferred_element_type=jnp.flo...]
    reshape x5 -> x0, local copies, waits for them, and re-layouts: 9.54 us -> none  [flat(): return value.reshape(-1, value.shape[-1])]
    unnamed x237 -> x240, local copies, waits for them, and re-layouts: 27.2 us -> 26.2 us
  transfers between devices with their start and end apart: 5 -> 7, of which waited for: 2 -> 1; matrix products, arithmetic and copies ran while one was open for 10% -> 19% of each run, Pallas kernels for 6% -> 68%
where the time goes in v4:
time: 757 us; the launch traced here: 748 us
  Pallas kernels  512 us (68%)
  matrix products  115 us (15%)
  other arithmetic  49.8 us (7%)
  local copies, waits for them, and re-layouts  37.3 us (5%)
  between operations  15.8 us (2%)
  starting transfers between devices  14.4 us (2%)
    pallas_call x2, Pallas kernels, gather_all(): pl.pallas_call(partial(gather_kernel, n_dp, n_ctx, chunks, lag, n, carry)...  203 us
    pallas_call x2, Pallas kernels, scatter_sums(): pl.pallas_call(partial(scatter_kernel, n_dp, n_ctx, plan, lags, pieces, l...  197 us
    pallas_call x4, Pallas kernels, by_pair(): pl.pallas_call(kernel, grid=(ins[0][0].shape[0], HEADS // 2 // PER), in_s...  58.2 us
    dot_general x9, matrix products, matmul_back(): jnp.einsum('mte,de->mtd', operand, weight, preferred_element_type=jnp.flo...  58 us
    pallas_call x4, Pallas kernels, by_window(): pl.pallas_call(kernel, grid=(micro, steps), in_specs=[spec(rows, place, a...  51.6 us
    dot_general x9, matrix products, matmul(): jnp.einsum('mtd,de->mte', operand, weight, preferred_element_type=jnp.flo...  46 us
    unnamed x240, local copies, waits for them, and re-layouts  26.2 us
  transfers between devices with their start and end apart: 7, of which 1 were waited for; matrix products, arithmetic and copies ran while one was open for 19% of the time, Pallas kernels for 68%

profile of v4, /device:TPU:0, one launch (start us, length us, event | category | flops | bytes accessed | tf_op | source)
XLA Modules:
  0.0 748.2 jit_solution(317850651351628230)
XLA Ops:
  12.4 32.6 %gather_weights.2 = (bf16[32,32,128]{2,1,0:T(8,128)(2,1)}, bf16[32,32,512]{2,1,0:T(8,128)(2,1)}, bf16[32,32,1024]{2,1,0:T(8,128)(2,1)}) custom-call(bf16[1,32,128]{2,1,0:T(8,128)(2,1)} %bitcast.247, bf16[1,32,512]{2,1,0:T(8,128)(2,1)} %bitcast.246, bf16[1,32,1024]{2,1,0:T(8,128)(2,1)} %bitcast.240), custom_call_target="tpu_custom_call" | custom-call | tf_op jit(solution)/shard_map/gather_weights/pallas_call | solution.py:206
  45.1 2.4 slice_convert_fusion
  48.1 2.9 fusion.54
  51.0 1.3 copy-done.36
  53.0 4.2 collective-permute-start
  62.0 2.2 convolution_convert_fusion.2.key_ref.query_ref
  64.8 1.2 copy.120
  66.5 4.4 multiply_convert_fusion.5.value_ref
  71.8 11.2 %states.1.refs_6_ = bf16[2,9,160,128]{3,2,1,0:T(8,128)(2,1)S(1)} custom-call(bf16[2,256,512]{2,1,0:T(8,128)(2,1)S(1)} %convolution_convert_fusion.2.key_ref.query_ref, bf16[2,256,1024]{2,1,0:T(8,128)(2,1)S(1)} %multiply_convert_fusion.5.value_ref, f32[2,256,128]{2,1,0:T(8,128)S(1)} %broadcast_in_dim.76.last_ref, bf16[2,256,256]{2,1,0:T(8,128)(2,1)S(1)} %copy-done.16, ...), custom_call_target="tpu_custom_call" | custom-call | tf_op jit(solution)/shard_map/states/pallas_call | solution.py:756
  84.6 170.6 %gather_weights.3 = (bf16[32,32,1024]{2,1,0:T(8,128)(2,1)}, bf16[32,32,5632]{2,1,0:T(8,128)(2,1)}, bf16[32,88,1024]{2,1,0:T(8,128)(2,1)}, bf16[32,32,3072]{2,1,0...) custom-call(bf16[1,32,1024]{2,1,0:T(8,128)(2,1)} %bitcast.238, ...), custom_call_target="tpu_custom_call" | custom-call | tf_op jit(solution)/shard_map/gather_weights/pallas_call | solution.py:206
  255.4 1.3 copy-done.13
  256.6 11.7 %linear_attend.1 = (bf16[2,256,1024]{2,1,0:T(8,128)(2,1)S(1)}, f32[2,256,1024]{2,1,0:T(8,128)}) custom-call(bf16[2,256,512]{2,1,0:T(8,128)(2,1)S(1)} %convolution_convert_fusion.2.key_ref.query_ref, bf16[2,256,512]{2,1,0:T(8,128)(2,1)S(1)} %convolution_convert_fusion.2.key_ref.query_ref, bf16[2,256,1024]{2,1,0:T(8,128)(2,1)S(1)} %multiply_convert_fusion.5.value_ref, ...), custom_call_target="tpu_custom_call" | custom-call | tf_op jit(solution)/shard_map/linear_attend/pallas_call | solution.py:756
  268.3 1.4 multiply_reduce_fusion.11
  270.0 11.4 %fusion.91 = (bf16[2,256,5632]{2,1,0:T(8,128)(2,1)}, f32[2,256,5632]{2,1,0:T(8,128)S(1)}) fusion(bf16[2,256,1024]{2,1,0:T(8,128)(2,1)S(1)} %multiply_convert_fusion.4, bf16[1024,5632,1]{1,0,2:T(8,128)(2,1)} %bitcast.195), kind=kOutput, calls=%fused_computation.204 | convolution fusion | flops 5908463616 | bytes 29884416 | tf_op jit(solution)/shard_map/mtd,de->mte/dot_general | solution.py:870
  281.4 1.8 fusion.21
  283.3 6.4 multiply_reduce_fusion.10
  290.0 3.7 convolution_convert_fusion.query_ref.key_ref.value_ref
  293.7 7.1 collective-permute-start.1
  301.2 7.9 %window_later.1 = bf16[2,128,1024]{2,1,0:T(8,128)(2,1)S(1)} custom-call(bf16[2,256,3072]{2,1,0:T(8,128)(2,1)S(1)} %convolution_convert_fusion.query_ref.key_ref.value_ref, bf16[2,256,3072]{2,1,0:T(8,128)(2,1)S(1)} %convolution_convert_fusion.query_ref.key_ref.value_ref, bf16[2,256,3072]{2,1,0:T(8,128)(2,1)S(1)} %convolution_convert_fusion.query_ref.key_ref.value_ref, ...), custom_call_target="tpu_custom_call" | custom-call | tf_op jit(solution)/shard_map/window_later/pallas_call | solution.py:1146
  309.1 3.6 collective-permute-done.1.rim_key_ref.rim_value_ref
  312.6 7.8 %window_first.1 = bf16[2,128,1024]{2,1,0:T(8,128)(2,1)S(1)} custom-call(bf16[2,256,3072]{2,1,0:T(8,128)(2,1)S(1)} %convolution_convert_fusion.query_ref.key_ref.value_ref, bf16[2,256,3072]{2,1,0:T(8,128)(2,1)S(1)} %convolution_convert_fusion.query_ref.key_ref.value_ref, bf16[2,256,3072]{2,1,0:T(8,128)(2,1)S(1)} %convolution_convert_fusion.query_ref.key_ref.value_ref, ...), custom_call_target="tpu_custom_call" | custom-call | tf_op jit(solution)/shard_map/window_first/pallas_call | solution.py:1146
  320.5 1.3 multiply_reduce_fusion.9
  321.9 9.8 %fusion.92 = (bf16[2,256,5632]{2,1,0:T(8,128)(2,1)S(1)}, f32[2,256,5632]{2,1,0:T(8,128)S(1)}) fusion(bf16[1024,5632]{1,0:T(8,128)(2,1)} %all-gather.2.cloned.1.call-done, f32[2,256,1024]{2,1,0:T(8,128)S(1)} %get-tuple-element.266, f32[1024]{0:T(1024)S(1)} %bitcast.214, f32[2,256]{1,0:T(2,128)S(1)} %fusion.70), kind=kOutput, calls=%fused_computation.205 | convolution fusion | flops 5910036480 | bytes 30939136 | tf_op jit(solution)/shard_map/mtd,de->mte/dot_general | solution.py:870
  331.8 1.8 fusion.20
  333.6 9.4 %fusion.9 = (bf16[2,256,2816]{2,1,0:T(8,128)(2,1)S(1)}, bf16[2,256,2816]{2,1,0:T(8,128)(2,1)}) fusion(bf16[2,256,5632]{2,1,0:T(8,128)(2,1)S(1)} %get-tuple-element.111, bf16[2816,1024,1]{1,0,2:T(8,128)(2,1)} %bitcast.269, bf16[2,1,256,1024]{3,2,1,0:T(8,128)(2,1)S(1)} %copy-done.45, f32[2,256]{1,0:T(2,128)S(1)} %compare_convert_fusion), kind=kOutput, calls=%fused_computation.16 | convolution fusion | flops 2975989760 | bytes 18352128 | tf_op jit(solution)/shard_map/mte,de->mtd/dot_general | solution.py:874
  343.0 1.6 copy-done.105
  344.6 10.9 %bitcast_convert_fusion = bf16[1024,5632]{1,0:T(8,128)(2,1)} fusion(bf16[2,256,2816]{2,1,0:T(8,128)(2,1)} %get-tuple-element.230, bf16[2,256,2816]{2,1,0:T(8,128)(2,1)S(1)} %get-tuple-element.229, f32[2,256,1024]{2,1,0:T(8,128)S(1)} %copy-done.34, f32[1024]{0:T(1024)S(1)} %bitcast.215, f32[2,256]{1,0:T(2,128)S(1)} %fusion.70), kind=kOutput, calls=%fused_computation | convolution fusion | flops 5924454400 | bytes 19404800 | tf_op jit(solution)/shard_map/tr,te->re/dot_general | solution.py:1316
  356.0 1.5 bitcast_convert_fusion.1
  357.5 1.2 fusion.39.refs_11_
  358.7 1.0 copy-done.10
  361.2 1.1 pad_maximum_fusion.6
  362.7 12.5 %fusion = f32[2,256,1024]{2,1,0:T(8,128)S(1)} fusion(bf16[1024,5632]{1,0:T(8,128)(2,1)} %all-gather.2.cloned.1.call-done, bf16[2,256,2816]{2,1,0:T(8,128)(2,1)} %get-tuple-element.230, bf16[2,256,2816]{2,1,0:T(8,128)(2,1)S(1)} %copy-done.106), kind=kOutput, calls=%fused_computation.1 | convolution fusion | flops 5917114368 | bytes 19398656 | tf_op jit(solution)/shard_map/mte,de->mtd/dot_general | solution.py:874
  378.1 1.3 convolution_convert_fusion.1.grad_ref
  379.4 17.5 %window_first_back.1 = (bf16[2,128,1024]{2,1,0:T(8,128)(2,1)S(1)}, f32[2,128,1024]{2,1,0:T(8,128)S(1)}, f32[2,128,1024]{2,1,0:T(8,128)S(1)}, bf16[2,64,1024]{2,1,0:T(8,128)(2,1)S(1)}, bf16[2,64,1024]{2,1,0:T(8,128)(2,1)S(1)}) custom-call(bf16[2,256,3072]{2,1,0:T(8,128)(2,1)} %copy-done, bf16[2,256,3072]{2,1,0:T(8,128)(2,1)} %copy-done, ...), custom_call_target="tpu_custom_call" | custom-call | tf_op jit(solution)/shard_map/window_first_back/pallas_call | solution.py:1146
  397.7 1.3 collective-permute-start.2
  399.8 1.6 copy-done.8
  401.5 18.4 %window_later_back.1 = (bf16[2,128,1024]{2,1,0:T(8,128)(2,1)S(1)}, f32[2,256,1024]{2,1,0:T(8,128)}, f32[2,256,1024]{2,1,0:T(8,128)}) custom-call(bf16[2,256,3072]{2,1,0:T(8,128)(2,1)} %copy-done, bf16[2,256,3072]{2,1,0:T(8,128)(2,1)} %copy-done, bf16[2,256,3072]{2,1,0:T(8,128)(2,1)} %copy-done, f32[2,256,256]{2,1,0:T(8,128)S(1)} %copy-done.6, ...), custom_call_target="tpu_custom_call" | custom-call | tf_op jit(solution)/shard_map/window_later_back/pallas_call | solution.py:1146
  419.9 7.0 fusion.47
  427.3 1.1 copy-done.57
  429.1 1.1 fusion.36
  430.2 6.6 fusion.80
  437.3 1.2 fusion.84
  438.6 9.4 %fusion.17 = (bf16[2,256,2816]{2,1,0:T(8,128)(2,1)S(1)}, bf16[2,256,2816]{2,1,0:T(8,128)(2,1)}) fusion(bf16[2,256,5632]{2,1,0:T(8,128)(2,1)S(1)} %bitcast.201, bf16[2,256,1024]{2,1,0:T(8,128)(2,1)S(1)} %get-tuple-element.225, bf16[2816,1024,1]{1,0,2:T(8,128)(2,1)} %bitcast.268), kind=kOutput, calls=%fused_computation.24 | convolution fusion | flops 2974416896 | bytes 18350080 | tf_op jit(solution)/shard_map/mte,de->mtd/dot_general | solution.py:874
  448.0 11.3 %fusion.22 = f32[2,256,1024]{2,1,0:T(8,128)S(1)} fusion(bf16[1024,5632,1]{1,0,2:T(8,128)(2,1)} %bitcast.196, bf16[2,256,2816]{2,1,0:T(8,128)(2,1)} %get-tuple-element.228, bf16[2,256,2816]{2,1,0:T(8,128)(2,1)S(1)} %get-tuple-element.227), kind=kOutput, calls=%fused_computation.32 | convolution fusion | flops 5917114368 | bytes 19398656 | tf_op jit(solution)/shard_map/mte,de->mtd/dot_general | solution.py:874
  460.0 1.9 fusion.82
  462.0 2.6 fusion.93.grad_ref
  464.7 23.4 %linear_attend_back.1 = (f32[2,256,256]{2,1,0:T(8,128)S(1)}, f32[2,256,256]{2,1,0:T(8,128)S(1)}, f32[2,256,1024]{2,1,0:T(8,128)}, bf16[2,9,160,128]{3,2,1,0:T(8,128)(2,1)S(1)}) custom-call(bf16[2,256,512]{2,1,0:T(8,128)(2,1)S(1)} %copy-done.4, bf16[2,256,512]{2,1,0:T(8,128)(2,1)S(1)} %copy-done.4, bf16[2,256,1024]{2,1,0:T(8,128)(2,1)S(1)} %copy-done.2, ...), custom_call_target="tpu_custom_call" | custom-call | tf_op jit(solution)/shard_map/linear_attend_back/pallas_call | solution.py:756
  488.1 1.8 pad_maximum_fusion.4
  490.1 1.2 copy-done.56
  491.3 4.6 pad_maximum_fusion.1.refs_7_
  496.0 161.4 %scatter_sums.2 = (f32[32,1024]{1,0:T(8,128)}, f32[32,5632]{1,0:T(8,128)}, f32[88,1024]{1,0:T(8,128)}, f32[32,3072]{1,0:T(8,128)}, f32[32,1024]{1,0:T(8,128)}, /...) custom-call(bf16[512,1024]{1,0:T(8,128)(2,1)} %bitcast.193, bf16[512,1024]{1,0:T(8,128)(2,1)} %bitcast.197, ...), custom_call_target="tpu_custom_call" | custom-call | tf_op jit(solution)/shard_map/scatter_sums/pallas_call | solution.py:494
  657.4 1.3 copy-done.29
  658.7 11.8 %states_back.1 = (f32[2,256,256]{2,1,0:T(8,128)S(1)}, f32[2,256,1024]{2,1,0:T(8,128)}) custom-call(bf16[2,256,512]{2,1,0:T(8,128)(2,1)S(1)} %copy-done.4, bf16[2,256,1024]{2,1,0:T(8,128)(2,1)S(1)} %copy-done.2, f32[2,256,128]{2,1,0:T(8,128)S(1)} %copy-done.24, bf16[2,256,256]{2,1,0:T(8,128)(2,1)S(1)} %copy-done.17, f32[8,256]{1,0:T(8,128)S(1)} %copy-done.32, ...), custom_call_target="tpu_custom_call" | custom-call | tf_op jit(solution)/shard_map/states_back/pallas_call | solution.py:756
  670.7 3.1 multiply_reduce_fusion.2
  674.5 1.3 collective-permute-start.3
  676.6 2.3 pad_add_fusion
  678.9 2.0 fusion.57
  681.0 3.8 fusion.32
  686.8 3.0 fusion.45
  690.2 1.3 fusion.38.refs_1_
  691.6 35.7 %scatter_sums.3 = (f32[32,512]{1,0:T(8,128)}, f32[32,512]{1,0:T(8,128)}, f32[32,1024]{1,0:T(8,128)}) custom-call(bf16[512,1024]{1,0:T(8,128)(2,1)} %copy-done.52, bf16[512,1024]{1,0:T(8,128)(2,1)} %fusion.38.refs_1_, bf16[512,512]{1,0:T(8,128)(2,1)} %constant.148.clone.refs_2_, bf16[512,512]{1,0:T(8,128)(2,1)} %pad_maximum_fusion.8.refs_3_, ...), custom_call_target="tpu_custom_call" | custom-call | tf_op jit(solution)/shard_map/scatter_sums/pallas_call | solution.py:494
  728.7 1.6 slice_reduce_fusion
  730.4 3.2 fusion.52
  733.6 2.0 convert_element_type.322
  (320 shorter events, 36.1 us)
Async XLA Ops:
  7.2 40.5 %copy-start.43 = (bf16[2,1,256,1024]{3,2,1,0:T(8,128)(2,1)S(1)}, bf16[2,1,256,1024]{3,2,1,0:T(8,128)(2,1)}, u32[]{:S(2)}) copy-start(bf16[2,1,256,1024]{3,2,1,0:T(8,128)(2,1)} %param.26) | copy-start | bytes 3145732
  7.2 314.7 %all-gather.2.cloned.1.call-start = ((), (), s32[]{:S(2)}) async-start(), calls=%async_computation.2 | async-start | bytes 11894784 | tf_op jit(solution)/shard_map/all_gather | solution.py:1305
  7.9 673.1 %reduce-scatter.3.cloned.1.call-start = ((), (), s32[]{:S(2)}) async-start(), calls=%async_computation.3 | async-start | bytes 12976128 | tf_op jit(solution)/shard_map/reduce_scatter | solution.py:1319
  47.7 14.3 %copy-start.81 = (f32[1024,1]{0,1:T(1,128)}, f32[1024,1]{0,1:T(1,128)S(1)}, u32[]{:S(2)}) copy-start(f32[1024,1]{0,1:T(1,128)S(1)} %copy.119) | copy-start | bytes 12292
  48.0 14.0 %copy-start.91 = (f32[2,256]{1,0:T(2,128)}, f32[2,256]{1,0:T(2,128)S(1)}, u32[]{:S(2)}) copy-start(f32[2,256]{1,0:T(2,128)S(1)} %fusion.67) | copy-start | bytes 6148
  48.0 9.1 %copy-start.48 = (bf16[32,32,128]{2,1,0:T(8,128)(2,1)S(1)}, bf16[32,32,128]{2,1,0:T(8,128)(2,1)}, u32[]{:S(2)}) copy-start(bf16[32,32,128]{2,1,0:T(8,128)(2,1)} %get-tuple-element.96) | copy-start | bytes 786436
  48.0 9.3 %copy-start.98 = (s32[2,1,4]{2,1,0:T(1,128)S(1)}, s32[2,1,4]{2,1,0:T(1,128)}, u32[]{:S(2)}) copy-start(s32[2,1,4]{2,1,0:T(1,128)} %param.27) | copy-start | bytes 100
  53.0 13.5 %collective-permute-start = (f32[2,2,1024]{2,1,0:T(2,128)}, f32[2,2,1024]{2,1,0:T(2,128)S(1)}, u32[]{:S(2)}, u32[]{:S(2)}) collective-permute-start(f32[2,2,1024]{2,1,0:T(2,128)} %slice.223), channel_id=1, source_target_pairs={{0,1},{1,2},{2,3},{4,5},{5,6},{6,7},{8,9},{9,10},{10,11},{12,13},{... | collective-permute-start | bytes 49160 | tf_op jit(solution)/shard_map/ppermute | solution.py:533
  57.7 6.5 copy-start.83
  62.0 193.4 %copy-start.14 = (f32[2,256,256]{2,1,0:T(8,128)}, f32[2,256,256]{2,1,0:T(8,128)S(1)}, u32[]{:S(2)}) copy-start(f32[2,256,256]{2,1,0:T(8,128)S(1)} %and_convert_fusion.mask_ref) | copy-start | bytes 1572868
  64.2 191.2 %copy-start.3 = (bf16[2,256,512]{2,1,0:T(8,128)(2,1)}, bf16[2,256,512]{2,1,0:T(8,128)(2,1)S(1)}, u32[]{:S(2)}) copy-start(bf16[2,256,512]{2,1,0:T(8,128)(2,1)S(1)} %convolution_convert_fusion.2.key_ref.query_ref) | copy-start | bytes 1572868
  66.0 203.7 %copy-start.70 = (f32[1024,1]{0,1:T(1,128)}, f32[1024,1]{0,1:T(1,128)S(1)}, u32[]{:S(2)}) copy-start(f32[1024,1]{0,1:T(1,128)S(1)} %copy.120) | copy-start | bytes 12292
  66.2 5.5 copy-start.31
  66.4 16.6 %copy-start.65 = (f32[2,2,1024]{2,1,0:T(2,128)}, f32[2,2,1024]{2,1,0:T(2,128)S(1)}, u32[]{:S(2)}) copy-start(f32[2,2,1024]{2,1,0:T(2,128)S(1)} %collective-permute-done) | copy-start | bytes 49156
  70.8 184.5 %copy-start.1 = (bf16[2,256,1024]{2,1,0:T(8,128)(2,1)}, bf16[2,256,1024]{2,1,0:T(8,128)(2,1)S(1)}, u32[]{:S(2)}) copy-start(bf16[2,256,1024]{2,1,0:T(8,128)(2,1)S(1)} %multiply_convert_fusion.5.value_ref) | copy-start | bytes 3145732
  70.8 13.1 %copy-start.99 = (f32[2]{0:T(128)S(1)}, f32[2]{0:T(128)}, u32[]{:S(2)}) copy-start(f32[2]{0:T(128)} %broadcast_subtract_fusion) | copy-start | bytes 28
  71.8 11.3 %copy-start.23 = (f32[2,256,128]{2,1,0:T(8,128)}, f32[2,256,128]{2,1,0:T(8,128)S(1)}, u32[]{:S(2)}) copy-start(f32[2,256,128]{2,1,0:T(8,128)S(1)} %broadcast_in_dim.76.last_ref) | copy-start | bytes 786436
  71.8 183.4 %copy-start.90 = (f32[2,256]{1,0:T(2,128)S(1)}, f32[2,256]{1,0:T(2,128)}, u32[]{:S(2)}) copy-start(f32[2,256]{1,0:T(2,128)} %get-tuple-element.253) | copy-start | bytes 6148
  256.6 11.7 %copy-start.21 = (f32[2,256,128]{2,1,0:T(8,128)}, f32[2,256,128]{2,1,0:T(8,128)S(1)}, u32[]{:S(2)}) copy-start(f32[2,256,128]{2,1,0:T(8,128)S(1)} %broadcast_in_dim.78.carried_ref) | copy-start | bytes 786436
  256.6 11.7 %copy-start.101 = (bf16[32,32,1024]{2,1,0:T(8,128)(2,1)S(1)}, bf16[32,32,1024]{2,1,0:T(8,128)(2,1)}, u32[]{:S(2)}) copy-start(bf16[32,32,1024]{2,1,0:T(8,128)(2,1)} %get-tuple-element.101) | copy-start | bytes 6291460
  269.7 11.7 %copy-start.93 = (f32[2,256]{1,0:T(2,128)}, f32[2,256]{1,0:T(2,128)S(1)}, u32[]{:S(2)}) copy-start(f32[2,256]{1,0:T(2,128)S(1)} %get-tuple-element.259) | copy-start | bytes 6148
  269.7 13.5 %copy-start.38 = (f32[2,256,1024]{2,1,0:T(8,128)}, f32[2,256,1024]{2,1,0:T(8,128)S(1)}, u32[]{:S(2)}) copy-start(f32[2,256,1024]{2,1,0:T(8,128)S(1)} %get-tuple-element.260) | copy-start | bytes 6291460
  269.7 11.6 %copy-start.85 = (f32[2,256]{1,0:T(2,128)}, f32[2,256]{1,0:T(2,128)S(1)}, u32[]{:S(2)}) copy-start(f32[2,256]{1,0:T(2,128)S(1)} %fusion.68) | copy-start | bytes 6148
  270.0 11.4 %copy-start.42 = (bf16[2,256,1024]{2,1,0:T(8,128)(2,1)}, bf16[2,256,1024]{2,1,0:T(8,128)(2,1)S(1)}, u32[]{:S(2)}) copy-start(bf16[2,256,1024]{2,1,0:T(8,128)(2,1)S(1)} %multiply_convert_fusion.4) | copy-start | bytes 3145732
  283.2 6.4 copy-start.9
  283.2 6.7 slice-start.2
  283.3 6.7 slice-start.3
  289.7 30.8 %copy-start.40 = (f32[2,256,1024]{2,1,0:T(8,128)}, f32[2,256,1024]{2,1,0:T(8,128)S(1)}, u32[]{:S(2)}) copy-start(f32[2,256,1024]{2,1,0:T(8,128)S(1)} %get-tuple-element.264) | copy-start | bytes 6291460
  290.0 10.9 %copy-start.95 = (s32[2,256]{1,0:T(2,128)S(1)}, s32[2,256]{1,0:T(2,128)}, u32[]{:S(2)}) copy-start(s32[2,256]{1,0:T(2,128)} %get-tuple-element.245) | copy-start | bytes 6148
  290.0 10.9 %copy-start.96 = (s32[2,128]{1,0:T(2,128)S(1)}, s32[2,128]{1,0:T(2,128)}, u32[]{:S(2)}) copy-start(s32[2,128]{1,0:T(2,128)} %get-tuple-element.251) | copy-start | bytes 3076
  290.0 11.1 %copy-start.84 = (s32[256]{0:T(256)S(1)}, s32[256]{0:T(256)}, u32[]{:S(2)}) copy-start(s32[256]{0:T(256)} %copy-done.83) | copy-start | bytes 3076
  290.0 11.1 %copy-start.97 = (s32[2]{0:T(128)S(1)}, s32[2]{0:T(128)}, u32[]{:S(2)}) copy-start(s32[2]{0:T(128)} %slice_reduce_fusion.6) | copy-start | bytes 28
  293.7 19.0 %copy-start = (bf16[2,256,3072]{2,1,0:T(8,128)(2,1)}, bf16[2,256,3072]{2,1,0:T(8,128)(2,1)S(1)}, u32[]{:S(2)}) copy-start(bf16[2,256,3072]{2,1,0:T(8,128)(2,1)S(1)} %convolution_convert_fusion.query_ref.key_ref.value_ref) | copy-start | bytes 9437188
  293.7 18.9 %collective-permute-start.1 = (bf16[2,64,2048]{2,1,0:T(8,128)(2,1)S(1)}, bf16[2,64,2048]{2,1,0:T(8,128)(2,1)S(1)}, u32[]{:S(2)}, u32[]{:S(2)}) collective-permute-start(bf16[2,64,2048]{2,1,0:T(8,128)(2,1)S(1)} %slice.233), channel_id=1, source_target_pairs={{0,1},{1,2},{2,3},{4,5},{5,6},{6,7},{8,9},{9,10},{10,11},{12,13},{... | collective-permute-start | bytes 1572872 | tf_op jit(solution)/shard_map/ppermute | solution.py:533
  301.1 11.6 %copy-start.5 = (f32[2,256,256]{2,1,0:T(8,128)}, f32[2,256,256]{2,1,0:T(8,128)S(1)}, u32[]{:S(2)}) copy-start(f32[2,256,256]{2,1,0:T(8,128)S(1)} %add_convert_fusion.mask_ref) | copy-start | bytes 1572868
  309.1 11.4 %copy-start.25 = (bf16[2,128,1024]{2,1,0:T(8,128)(2,1)}, bf16[2,128,1024]{2,1,0:T(8,128)(2,1)S(1)}, u32[]{:S(2)}) copy-start(bf16[2,128,1024]{2,1,0:T(8,128)(2,1)S(1)} %window_later.1) | copy-start | bytes 1572868
  309.1 11.4 %copy-start.103 = (bf16[32,32,1024]{2,1,0:T(8,128)(2,1)S(1)}, bf16[32,32,1024]{2,1,0:T(8,128)(2,1)}, u32[]{:S(2)}) copy-start(bf16[32,32,1024]{2,1,0:T(8,128)(2,1)} %get-tuple-element.108) | copy-start | bytes 6291460
  312.6 7.8 %copy-start.11 = (bf16[2,64,2048]{2,1,0:T(8,128)(2,1)}, bf16[2,64,2048]{2,1,0:T(8,128)(2,1)S(1)}, u32[]{:S(2)}) copy-start(bf16[2,64,2048]{2,1,0:T(8,128)(2,1)S(1)} %collective-permute-done.1.rim_key_ref.rim_value_ref) | copy-start | bytes 1572868
  321.9 9.9 %copy-start.33 = (f32[2,256,1024]{2,1,0:T(8,128)}, f32[2,256,1024]{2,1,0:T(8,128)S(1)}, u32[]{:S(2)}) copy-start(f32[2,256,1024]{2,1,0:T(8,128)S(1)} %get-tuple-element.266) | copy-start | bytes 6291460
  333.6 11.0 %copy-start.34 = (f32[2,256,1024]{2,1,0:T(8,128)S(1)}, f32[2,256,1024]{2,1,0:T(8,128)}, u32[]{:S(2)}) copy-start(f32[2,256,1024]{2,1,0:T(8,128)} %copy-done.33) | copy-start | bytes 6291460
  355.5 378.1 %reduce-scatter.5.cloned.1.call-start = ((), (), s32[]{:S(2)}) async-start(), calls=%async_computation.4 | async-start | bytes 1802240 | tf_op jit(solution)/shard_map/reduce_scatter | solution.py:1319
  361.2 14.0 %copy-start.7 = (bf16[3,8,128,512]{3,2,1,0:T(8,128)(2,1)}, bf16[3,8,128,512]{3,2,1,0:T(8,128)(2,1)S(1)}, u32[]{:S(2)}) copy-start(bf16[3,8,128,512]{3,2,1,0:T(8,128)(2,1)S(1)} %turn.2.refs_2_) | copy-start | bytes 9437188
  362.7 12.5 %copy-start.35 = (f32[2,256,1024]{2,1,0:T(8,128)S(1)}, f32[2,256,1024]{2,1,0:T(8,128)}, u32[]{:S(2)}) copy-start(f32[2,256,1024]{2,1,0:T(8,128)} %copy-done.33) | copy-start | bytes 6291460
  397.7 29.1 %collective-permute-start.2 = (bf16[2,64,2048]{2,1,0:T(8,128)(2,1)}, bf16[2,64,2048]{2,1,0:T(8,128)(2,1)S(1)}, u32[]{:S(2)}, u32[]{:S(2)}) collective-permute-start(bf16[2,64,2048]{2,1,0:T(8,128)(2,1)} %pad_maximum_fusion.7), channel_id=1, source_target_pairs={{1,0},{2,1},{3,2},{5,4},{6,5},{7,6},{9,8},{10,9},{11,10},{13,12},{... | collective-permute-start | bytes 1572872 | tf_op jit(solution)/shard_map/ppermute | solution.py:533
  429.1 9.5 %slice-start = ((s8[5767168]{0:T(1024)(128)(4,1)}), s8[4194304]{0:T(1024)(128)(4,1)S(1)}, s32[]{:S(2)}) async-start(s8[5767168]{0:T(1024)(128)(4,1)} %bitcast.200), calls=%async_computation.5 | async-start | bytes 8388608
  430.2 6.6 copy-start.41
  430.2 8.4 %slice-start.1 = ((s8[5767168]{0:T(1024)(128)(4,1)}), s8[1572864]{0:T(1024)(128)(4,1)S(1)}, s32[]{:S(2)}) async-start(s8[5767168]{0:T(1024)(128)(4,1)} %bitcast.200), calls=%async_computation.6 | async-start | bytes 3145728
  438.5 9.5 %copy-start.53 = (bf16[2,256,1024]{2,1,0:T(8,128)(2,1)}, bf16[2,256,1024]{2,1,0:T(8,128)(2,1)S(1)}, u32[]{:S(2)}) copy-start(bf16[2,256,1024]{2,1,0:T(8,128)(2,1)S(1)} %get-tuple-element.225) | copy-start | bytes 3145732
  448.0 11.3 %copy-start.55 = (bf16[2,256,2816]{2,1,0:T(8,128)(2,1)}, bf16[2,256,2816]{2,1,0:T(8,128)(2,1)S(1)}, u32[]{:S(2)}) copy-start(bf16[2,256,2816]{2,1,0:T(8,128)(2,1)S(1)} %get-tuple-element.227) | copy-start | bytes 8650756
  448.0 11.3 %copy-start.39 = (f32[2,256,1024]{2,1,0:T(8,128)S(1)}, f32[2,256,1024]{2,1,0:T(8,128)}, u32[]{:S(2)}) copy-start(f32[2,256,1024]{2,1,0:T(8,128)} %copy-done.38) | copy-start | bytes 6291460
  448.0 11.3 %copy-start.71 = (f32[1024,1]{0,1:T(1,128)S(1)}, f32[1024,1]{0,1:T(1,128)}, u32[]{:S(2)}) copy-start(f32[1024,1]{0,1:T(1,128)} %copy-done.70) | copy-start | bytes 12292
  448.0 11.3 %copy-start.86 = (f32[2,256]{1,0:T(2,128)S(1)}, f32[2,256]{1,0:T(2,128)}, u32[]{:S(2)}) copy-start(f32[2,256]{1,0:T(2,128)} %copy-done.85) | copy-start | bytes 6148
  496.0 161.4 %copy-start.24 = (f32[2,256,128]{2,1,0:T(8,128)S(1)}, f32[2,256,128]{2,1,0:T(8,128)}, u32[]{:S(2)}) copy-start(f32[2,256,128]{2,1,0:T(8,128)} %copy-done.23) | copy-start | bytes 786436
  658.7 11.9 %copy-start.37 = (f32[2,256,1024]{2,1,0:T(8,128)S(1)}, f32[2,256,1024]{2,1,0:T(8,128)}, u32[]{:S(2)}) copy-start(f32[2,256,1024]{2,1,0:T(8,128)} %copy-done.36) | copy-start | bytes 6291460
  658.7 11.9 %copy-start.66 = (f32[2,2,1024]{2,1,0:T(2,128)S(1)}, f32[2,2,1024]{2,1,0:T(2,128)}, u32[]{:S(2)}) copy-start(f32[2,2,1024]{2,1,0:T(2,128)} %copy-done.65) | copy-start | bytes 49156
  658.7 11.9 %copy-start.79 = (f32[2,256]{1,0:T(2,128)S(1)}, f32[2,256]{1,0:T(2,128)}, u32[]{:S(2)}) copy-start(f32[2,256]{1,0:T(2,128)} %get-tuple-element.255) | copy-start | bytes 6148
  658.7 11.9 %copy-start.80 = (f32[2,256]{1,0:T(2,128)S(1)}, f32[2,256]{1,0:T(2,128)}, u32[]{:S(2)}) copy-start(f32[2,256]{1,0:T(2,128)} %get-tuple-element.256) | copy-start | bytes 6148
  658.7 12.0 %copy-start.89 = (f32[256]{0:T(256)S(1)}, f32[256]{0:T(256)}, u32[]{:S(2)}) copy-start(f32[256]{0:T(256)} %compare_convert_fusion.3) | copy-start | bytes 3076
  674.5 10.4 %collective-permute-start.3 = (f32[2,2,1024]{2,1,0:T(2,128)S(1)}, f32[2,2,1024]{2,1,0:T(2,128)S(1)}, u32[]{:S(2)}, u32[]{:S(2)}) collective-permute-start(f32[2,2,1024]{2,1,0:T(2,128)S(1)} %pad_add_fusion.1), channel_id=1, source_target_pairs={{1,0},{2,1},{3,2},{5,4},{6,5},{7,6},{9,8},{10,9},{11,10},{13,12},{... | collective-permute-start | bytes 49160 | tf_op jit(solution)/shard_map/ppermute | solution.py:533
  691.6 38.8 %copy-start.47 = (f32[2,256,1024]{2,1,0:T(8,128)S(1)}, f32[2,256,1024]{2,1,0:T(8,128)}, u32[]{:S(2)}) copy-start(f32[2,256,1024]{2,1,0:T(8,128)} %get-tuple-element.224) | copy-start | bytes 6291460
  730.4 5.9 copy-start.69
  730.4 6.5 copy-start.68
  733.5 5.6 copy-start.62
  733.5 6.3 copy-start.67
  (54 other events, 136.7 us)
Sparse Core Ops, SparseCore 0:
  10.9 111.6 all-gather.1
  355.6 85.9 reduce-scatter.2
  681.1 37.6 reduce-scatter.4

commit v5 on v4

--- a/solution.py
+++ b/solution.py
@@ -277,16 +277,40 @@
     for i in range(n_x):
         x_copy(i).start()
 
+    def y_part(slot, number, where, to, width):
+        pltpu.make_async_copy(
+            ys[number].at[:, pl.ds(where, width)], y_all.at[slot, :, pl.ds(to, width)], y_sem.at[slot]
+        ).start()
+
+    def y_fetch(k, slot, numbers):
+        if len(numbers) == 1:
+            y_part(slot, numbers[0], pl.multiple_of(k * WIDE, WIDE), 0, WIDE)
+            return
+        width = ys[numbers[0]].shape[1]
+        whole, left = width // WIDE, width % WIDE
+
+        @pl.when(k < whole)
+        def _():
+            y_part(slot, numbers[0], pl.multiple_of(k * WIDE, WIDE), 0, WIDE)
+
+        if left:
+
+            @pl.when(k == whole)
+            def _():
+                y_part(slot, numbers[0], whole * WIDE, 0, left)
+                y_part(slot, numbers[1], 0, left, WIDE - left)
+
+        @pl.when(k >= whole + (1 if left else 0))
+        def _():
+            y_part(slot, numbers[1], pl.multiple_of(k * WIDE - width, 128), 0, WIDE)
+
     def y_start(c):
         slot = lax.rem(c, held)
         for segment, (first, last) in zip(plan, bounds):
 
             @pl.when((c >= first) & (c < last))
             def _():
-                where = pl.multiple_of((c - first) * WIDE, WIDE)
-                pltpu.make_async_copy(
-                    ys[segment[1]].at[:, pl.ds(where, WIDE)], y_all.at[slot], y_sem.at[slot]
-                ).start()
+                y_fetch(c - first, slot, segment[1])
 
     def x_place(c):
         return sum((c >= first).astype(jnp.int32) for first in sorted(x_first.values())[1:])
@@ -348,7 +372,7 @@
                 def _():
                     x_ready(i)
 
-            pltpu.make_async_copy(ys[0].at[:, pl.ds(0, WIDE)], y_all.at[slot], y_sem.at[slot]).wait()
+            pltpu.make_async_copy(y_all.at[slot], y_all.at[slot], y_sem.at[slot]).wait()
         else:
             copy_of(slot, level - 1).wait_recv()
         need_credit(c, level)
@@ -581,6 +605,43 @@
     return [(step * PER + n, slice(128 * n, 128 * (n + 1))) for n in range(PER)]
 
 
+def twice(value):
+    return jnp.concatenate([value, value], axis=0)
+
+
+def features_apart(value, pair):
+    head = lanes_of(value.shape, FEAT)
+    return jnp.concatenate([only(head == 2 * pair, value), only(head == 2 * pair + 1, value)], axis=0)
+
+
+def features_joined(value, pair):
+    rows = value.shape[0] // 2
+    head = lanes_of((rows, value.shape[1]), FEAT)
+    return only(head == 2 * pair, value[:rows]) + only(head == 2 * pair + 1, value[rows:])
+
+
+def heads_apart(value):
+    lane = lanes_of(value.shape, 64)
+    return jnp.concatenate([only(lane == 0, value), only(lane == 1, value)], axis=0)
+
+
+def heads_joined(value):
+    rows = value.shape[0] // 2
+    return jnp.where(lanes_of((rows, value.shape[1]), 64) == 0, value[:rows], value[rows:])
+
+
+def at_head(value, pair):
+    rows = value.shape[0] // 2
+    lane = lanes_of((rows, 128), 1)
+    return jnp.concatenate(
+        [
+            only(lane == 2 * pair, jnp.broadcast_to(value[:rows], (rows, 128))),
+            only(lane == 2 * pair + 1, jnp.broadcast_to(value[rows:], (rows, 128))),
+        ],
+        axis=0,
+    )
+
+
 def factors(rows, tables, base):
     return (dot_nn(rows, tables[0]) + base[0:1], dot_nn(rows, tables[1]) + base[1:2])
 
@@ -588,23 +649,20 @@
 def states_kernel(key_ref, value_ref, last_ref, table_ref, base_ref, state_ref):
     step = pl.program_id(1)
     low, f32 = jnp.bfloat16, jnp.float32
-    keys = key_ref[0]
-    last = last_ref[0]
-    head_of = lanes_of(keys.shape, FEAT)
+    keys, last = key_ref[0], last_ref[0]
+    rows = keys.shape[0]
     lane = lanes_of((SENT, 128), 1)
     totals = state_ref[0, HEADS // 2]
     totals = jnp.where(step == 0, jnp.zeros_like(totals), totals)
     for pair, here in pairs_of(step):
         values = value_ref[0, :, here].astype(f32)
         held = jnp.concatenate([(values * last).astype(low), last.astype(low)], axis=1)
-        both = []
+        one, two = factors(features_apart(keys, pair), table_ref, base_ref)
+        terms = (one * two).astype(low)
+        parts = [dot_tn(terms[:rows], held)[:SENT], dot_tn(terms[rows:], held)[:SENT]]
+        state_ref[0, pair] = jnp.where(lane < 64, parts[0][:, :128], parts[1][:, :128]).astype(low)
         for side in range(2):
-            head = 2 * pair + side
-            one, two = factors(only(head_of == head, keys), table_ref, base_ref)
-            part = dot_tn((one * two).astype(low), held)[:SENT]
-            both.append(part[:, :128])
-            totals = jnp.where(lane == head, part[:, 128:].astype(low), totals)
-        state_ref[0, pair] = jnp.where(lane < 64, both[0], both[1]).astype(low)
+            totals = jnp.where(lane == 2 * pair + side, parts[side][:, 128:].astype(low), totals)
     state_ref[0, HEADS // 2] = totals
 
 
@@ -612,32 +670,25 @@
     query_ref, key_ref, value_ref, state_ref, mask_ref, carried_ref, table_ref, base_ref, out_ref, den_ref
 ):
     step = pl.program_id(1)
-    low, f32 = jnp.bfloat16, jnp.float32
+    low = jnp.bfloat16
     queries, keys = query_ref[0], key_ref[0]
-    mask, carried = mask_ref[0], carried_ref[0][:, :1]
+    mask, carried = twice(mask_ref[0]), twice(carried_ref[0][:, :1])
     totals = state_ref[0, HEADS // 2]
-    head_of = lanes_of(queries.shape, FEAT)
-    lane = lanes_of(totals.shape, 1)
+    inv_root = 1.0 / math.sqrt(FEAT)
     for pair, here in pairs_of(step):
-        state = state_ref[0, pair]
         values = value_ref[0, :, here]
         held = jnp.concatenate([values, jnp.ones_like(values)], axis=1)
-        outs, dens = [], []
-        for side in range(2):
-            head = 2 * pair + side
-            own = only(head_of == head, queries)
-            score = dot_nt(own, keys) * (1.0 / math.sqrt(FEAT))
-            weight = ((1.0 + score + 0.5 * score * score) * mask).astype(low)
-            one, two = factors(own, table_ref, base_ref)
-            terms = (one * two * base_ref[2:3] * carried).astype(low)
-            total = jnp.sum(only(lane == head, totals.astype(f32)), axis=1, keepdims=True)
-            total = jnp.broadcast_to(total, totals.shape).astype(low)
-            result = dot_nn(weight, held) + dot_nn(terms, jnp.concatenate([state, total], axis=1))
-            outs.append(result[:, :128] / result[:, 128:])
-            dens.append(result[:, 128:])
-        first = lanes_of(outs[0].shape, 64) == 0
-        out_ref[0, :, here] = jnp.where(first, outs[0], outs[1]).astype(low)
-        den_ref[0, :, here] = jnp.where(first, dens[0], dens[1])
+        own = features_apart(queries, pair)
+        slope = dot_nt(own * inv_root, keys) + 1.0
+        weight = ((0.5 * slope * slope + 0.5) * mask).astype(low)
+        one, two = factors(own, table_ref, base_ref)
+        terms = (one * two * base_ref[2:3] * carried).astype(low)
+        near = dot_nn(weight, held)
+        far = dot_nn(terms, jnp.concatenate([state_ref[0, pair], totals], axis=1))
+        picked = far[:, 128:] * at_head(jnp.ones((far.shape[0], 1), jnp.float32), pair)
+        den = near[:, 128:] + jnp.sum(picked, axis=1, keepdims=True)
+        out_ref[0, :, here] = heads_joined((near[:, :128] + far[:, :128]) / den).astype(low)
+        den_ref[0, :, here] = heads_joined(den)
 
 
 def attend_back_kernel(
@@ -647,50 +698,39 @@
     step = pl.program_id(1)
     low, f32 = jnp.bfloat16, jnp.float32
     queries, keys = query_ref[0], key_ref[0]
-    mask, carried = mask_ref[0], carried_ref[0][:, :1]
+    mask, carried = twice(mask_ref[0]), twice(carried_ref[0][:, :1])
     totals = state_ref[0, HEADS // 2]
-    head_of = lanes_of(queries.shape, FEAT)
-    lane = lanes_of(value_ref.shape[1:2] + (128,), 1)
     dquery = jnp.zeros(queries.shape, f32)
     dkey = jnp.zeros(queries.shape, f32)
-    dtotals = dstate_ref[0, HEADS // 2]
+    keys_small = keys * (1.0 / math.sqrt(FEAT))
+    dtotals = dstate_ref[0, HEADS // 2].astype(f32)
     dtotals = jnp.where(step == 0, jnp.zeros_like(dtotals), dtotals)
     inv_root = 1.0 / math.sqrt(FEAT)
     for pair, here in pairs_of(step):
         values = value_ref[0, :, here]
         whole_state = jnp.concatenate([state_ref[0, pair], totals], axis=1)
         dnum = grad_ref[0, :, here] / den_ref[0, :, here]
-        inner = dnum * out_ref[0, :, here].astype(f32)
-        dvalue = jnp.zeros(dnum.shape, f32)
-        dstate = jnp.zeros((SENT, 128), f32)
-        for side in range(2):
-            head = 2 * pair + side
-            own_lanes = (lane < 64) if side == 0 else (lane >= 64)
-            own, own_keys = only(head_of == head, queries), only(head_of == head, keys)
-            dnum_own = only(own_lanes, dnum).astype(low)
-            dden = -jnp.sum(only(own_lanes, inner), axis=1, keepdims=True)
-            score = dot_nt(own, keys) * inv_root
-            slope = (1.0 + score) * mask
-            weight = ((1.0 + score + 0.5 * score * score) * mask).astype(low)
-            dscore = ((dot_nt(dnum_own, values) + dden) * slope * inv_root).astype(low)
-            dvalue += dot_tn(weight, dnum_own)
-            dquery += dot_nn(dscore, own_keys)
-            dkey += dot_tn(dscore, own)
-            one, two = factors(own, table_ref, base_ref)
-            scale = base_ref[2:3] * carried
-            terms = (one * two * scale).astype(low)
-            dden_all = jnp.broadcast_to(dden, dnum.shape)
-            part = dot_tn(terms, jnp.concatenate([dnum_own, dden_all.astype(low)], axis=1))[:SENT]
-            dstate += part[:, :128]
-            dtotals = jnp.where(lanes_of(dtotals.shape, 1) == head, part[:, 128:].astype(low), dtotals)
-            both = jnp.concatenate([dnum_own, only(lane == head, dden_all).astype(low)], axis=1)
-            dterms = dot_nt(both, whole_state) * scale
-            through = dot_nt((dterms * two).astype(low), table_ref[0])
-            through += dot_nt((dterms * one).astype(low), table_ref[1])
-            dquery += only(head_of == head, through)
-        dvalue_ref[0, :, here] = dvalue
-        dstate_ref[0, pair] = dstate.astype(low)
-    dstate_ref[0, HEADS // 2] = dtotals
+        dden = -jnp.sum(heads_apart(dnum * out_ref[0, :, here].astype(f32)), axis=1, keepdims=True)
+        dnum = heads_apart(dnum).astype(low)
+        both = jnp.concatenate([dnum, at_head(dden, pair).astype(low)], axis=1)
+        own = features_apart(queries, pair)
+        own_small = own * inv_root
+        slope = dot_nt(own_small, keys) + 1.0
+        weight = ((0.5 * slope * slope + 0.5) * mask).astype(low)
+        dscore = ((dot_nt(dnum, values) + dden) * (slope * mask)).astype(low)
+        dvalue_ref[0, :, here] = dot_tn(weight, dnum)
+        dkey += dot_tn(dscore, own_small)
+        one, two = factors(own, table_ref, base_ref)
+        scale = base_ref[2:3] * carried
+        terms = (one * two * scale).astype(low)
+        part = dot_tn(terms, both)[:SENT]
+        dstate_ref[0, pair] = part[:, :128].astype(low)
+        dtotals += part[:, 128:]
+        dterms = dot_nt(both, whole_state) * scale
+        through = dot_nt((dterms * two).astype(low), table_ref[0])
+        through += dot_nt((dterms * one).astype(low), table_ref[1])
+        dquery += features_joined(dot_nn(dscore, keys_small) + through, pair)
+    dstate_ref[0, HEADS // 2] = dtotals.astype(low)
 
     @pl.when(step == 0)
     def _():
@@ -708,29 +748,22 @@
 ):
     step = pl.program_id(1)
     low, f32 = jnp.bfloat16, jnp.float32
-    keys = key_ref[0]
-    last = last_ref[0]
+    keys, last = key_ref[0], last_ref[0]
+    last_twice = twice(last[:, :1])
     dtotals = dstate_ref[0, HEADS // 2]
-    head_of = lanes_of(keys.shape, FEAT)
-    lane = lanes_of(last.shape, 1)
     dkey = jnp.zeros(keys.shape, f32)
     for pair, here in pairs_of(step):
-        values = value_ref[0, :, here]
         dstate = dstate_ref[0, pair]
         whole = jnp.concatenate([dstate, dtotals], axis=1)
-        dvalue = dvalue_in[0, :, here]
-        for side in range(2):
-            head = 2 * pair + side
-            own_lanes = (lane < 64) if side == 0 else (lane >= 64)
-            one, two = factors(only(head_of == head, keys), table_ref, base_ref)
-            terms = (one * two).astype(low)
-            dvalue += only(own_lanes, dot_nn(terms, dstate)) * last
-            both = jnp.concatenate([only(own_lanes, values), (lane == head).astype(low)], axis=1)
-            dterms = dot_nt(both, whole) * last[:, :1]
-            through = dot_nt((dterms * two).astype(low), table_ref[0])
-            through += dot_nt((dterms * one).astype(low), table_ref[1])
-            dkey += only(head_of == head, through)
-        dvalue_ref[0, :, here] = dvalue
+        one, two = factors(features_apart(keys, pair), table_ref, base_ref)
+        terms = (one * two).astype(low)
+        dvalue_ref[0, :, here] = dvalue_in[0, :, here] + heads_joined(dot_nn(terms, dstate)) * last
+        ones = at_head(jnp.ones((terms.shape[0], 1), f32), pair).astype(low)
+        both = jnp.concatenate([heads_apart(value_ref[0, :, here]), ones], axis=1)
+        dterms = dot_nt(both, whole) * last_twice
+        through = dot_nt((dterms * two).astype(low), table_ref[0])
+        through += dot_nt((dterms * one).astype(low), table_ref[1])
+        dkey += features_joined(through, pair)
 
     @pl.when(step == 0)
     def _():
@@ -797,11 +830,15 @@
 def chunk_plan(products, unit):
     n_dp = lax.axis_size("dp")
     places = n_dp * lax.axis_size("ctx")
-    operands, first_laid, plan, shapes, count = [], {}, [], [], 0
+    operands, first_laid, plan, shapes, count, taken = [], {}, [], [], 0, 0
     for number, (operand, gradient) in enumerate(products):
+        parts = gradient if isinstance(gradient, tuple) else (gradient,)
+        columns = sum(part.shape[1] for part in parts)
+        places_of = tuple(range(taken, taken + len(parts)))
+        taken += len(parts)
         shard = operand.shape[1] // places
         pieces = -(-shard // unit)
-        shapes.append((shard, gradient.shape[1]))
+        shapes.append((shard, columns))
         if id(operand) not in first_laid:
             first_laid[id(operand)] = count
             count += pieces
@@ -814,11 +851,11 @@
             plan.append(
                 (
                     first_laid[id(operand)] + piece,
-                    number,
+                    places_of,
                     number,
                     first,
                     min(unit, shard - first),
-                    gradient.shape[1] // WIDE,
+                    columns // WIDE,
                 )
             )
     return operands, plan, shapes
@@ -841,7 +878,9 @@
 def summed_to_owners(products, cid, unit, carry=0, state=()):
     n_dp, n_ctx = lax.axis_size("dp"), lax.axis_size("ctx")
     laid, plan, shapes = chunk_plan(products, unit)
-    gradients = [gradient for _, gradient in products]
+    gradients = []
+    for _, gradient in products:
+        gradients += gradient if isinstance(gradient, tuple) else (gradient,)
     return scatter_sums(laid, gradients, shapes, plan, n_dp, n_ctx, cid, carry, state)
 
 
@@ -912,7 +951,7 @@
         ahead = own_pos[queries][:, None] - key_pos[keys][None, :]
         same = own_seg[:, queries][:, :, None] == key_seg[:, keys][:, None, :]
         window_mask.append(((ahead >= 0) & (ahead < WINDOW))[None] & same)
-    window_mask = jnp.concatenate(window_mask, axis=1).astype(jnp.float32)
+    window_mask = jnp.where(jnp.concatenate(window_mask, axis=1), 0.0, masked_fill)
     causal = (own_pos[:, None] >= own_pos[None, :])[None] & (
         own_seg[:, :, None] == own_seg[:, None, :]
     )
@@ -938,14 +977,15 @@
     return conv_sum * jax.nn.silu(pre_values)
 
 
-def linear_forward(stream, weights, layout_info, gather_more):
+def linear_forward(stream, rim_stream, weights, layout_info, gather_more):
     norm_gain, qk_weight, value_weight, tap_weights = weights
     micro_count, tok_count, model_width = stream.shape
     normed_rows, norm_back = jax.vjp(normed, stream, norm_gain.astype(jnp.float32))
     normed_low = normed_rows.astype(jnp.bfloat16)
     qk_rows = matmul(normed_low, qk_weight).astype(jnp.bfloat16)
     pre_values = matmul(normed_low, value_weight)
-    rim_rows = passed_along(pre_values[:, tok_count - CONV + 1 :, :], "ctx", 1)
+    rim_normed = normed(rim_stream.astype(jnp.float32), norm_gain.astype(jnp.float32))
+    rim_rows = matmul(rim_normed.astype(jnp.bfloat16), value_weight)
     value_rows, conv_back = jax.vjp(
         partial(conv_gate, tap_masks=layout_info["taps"]),
         pre_values,
@@ -1039,68 +1079,77 @@
 
 BAND = 128
 RIM = 64
-
-
-def band_probabilities(queries, keys, mask):
-    score = jnp.where(mask > 0, dot_nt(queries, keys) * 0.125, masked_fill)
-    power = jnp.exp(score - jnp.max(score, axis=1, keepdims=True))
-    return power / jnp.sum(power, axis=1, keepdims=True)
-
-
-def band_attend(queries, keys, values, mask):
-    lane = lanes_of(queries.shape, 1)
-    outs = []
-    for own in (lane < 64, lane >= 64):
-        chance = band_probabilities(only(own, queries), keys, mask)
-        outs.append(dot_nn(chance.astype(jnp.bfloat16), values))
-    return jnp.where(lane < 64, outs[0], outs[1]).astype(jnp.bfloat16)
-
-
-def band_back(queries, grads, keys, values, mask):
+WIDE_PER = 4
+
+
+def band_probabilities(queries, keys, bias):
+    scores = [dot_nt(q, k) + bias for q, k in zip(queries, keys)]
+    tops = [jnp.max(score, axis=1, keepdims=True) for score in scores]
+    powers = [jnp.exp(score - top) for score, top in zip(scores, tops)]
+    totals = [1.0 / jnp.sum(power, axis=1, keepdims=True) for power in powers]
+    return [power * total for power, total in zip(powers, totals)]
+
+
+def band_attend(queries, keys, values, bias):
     low = jnp.bfloat16
-    lane = lanes_of(queries.shape, 1)
-    dqueries, dkeys, dvalues = [], 0.0, 0.0
-    for own in (lane < 64, lane >= 64):
-        own_queries, own_grads = only(own, queries), only(own, grads)
-        chance = band_probabilities(own_queries, keys, mask)
-        dchance = dot_nt(own_grads, values)
-        inner = jnp.sum(dchance * chance, axis=1, keepdims=True)
-        dscore = (chance * (dchance - inner)).astype(low)
-        dqueries.append(dot_nn(dscore, keys) * 0.125)
-        dkeys += dot_tn(dscore, own_queries) * 0.125
-        dvalues += dot_tn(chance.astype(low), own_grads)
-    return jnp.where(lane < 64, dqueries[0], dqueries[1]).astype(low), dkeys, dvalues
-
-
-def with_rim(own_ref, rim_ref, here):
-    own, rim = own_ref[0, :, here], rim_ref[0, :, here]
-    return jnp.concatenate([jnp.zeros((BAND - RIM, 128), own.dtype), rim, own], axis=0)
-
-
-def first_band_kernel(query_ref, key_ref, value_ref, rim_key_ref, rim_value_ref, mask_ref, out_ref):
-    for _, here in pairs_of(0):
-        keys, values = with_rim(key_ref, rim_key_ref, here), with_rim(value_ref, rim_value_ref, here)
-        out_ref[0, :, here] = band_attend(query_ref[0, :, here], keys, values, mask_ref[0])
-
-
-def later_bands_kernel(query_ref, key_ref, value_ref, mask_ref, out_ref):
-    for _, here in pairs_of(0):
-        for first in range(BAND, query_ref.shape[1], BAND):
-            rows, near = slice(first, first + BAND), slice(first - BAND, first + BAND)
-            out_ref[0, first - BAND : first, here] = band_attend(
-                query_ref[0, rows, here], key_ref[0, near, here], value_ref[0, near, here], mask_ref[0, rows]
-            )
+    chances = band_probabilities([heads_apart(q * 0.125) for q in queries], keys, twice(bias))
+    outs = [dot_nn(chance.astype(low), v) for chance, v in zip(chances, values)]
+    return [heads_joined(out).astype(low) for out in outs]
+
+
+def band_back(queries, grads, keys, values, bias):
+    low = jnp.bfloat16
+    queries = [heads_apart(q * 0.125) for q in queries]
+    grads = [heads_apart(g) for g in grads]
+    dchances = [dot_nt(g, v) for g, v in zip(grads, values)]
+    chances = band_probabilities(queries, keys, twice(bias))
+    inners = [jnp.sum(d * c, axis=1, keepdims=True) for d, c in zip(dchances, chances)]
+    dscores = [(c * (d - inner)).astype(low) for c, d, inner in zip(chances, dchances, inners)]
+    dqueries = [dot_nn(d, k) for d, k in zip(dscores, keys)]
+    dkeys = [dot_tn(d, q) for d, q in zip(dscores, queries)]
+    dvalues = [dot_tn(c.astype(low), g) for c, g in zip(chances, grads)]
+    return [(heads_joined(d) * 0.125).astype(low) for d in dqueries], dkeys, dvalues
+
+
+LANES = [slice(128 * n, 128 * (n + 1)) for n in range(WIDE_PER)]
+
+
+def by_pairs(ref, rows):
+    return [ref[0, rows, here] for here in LANES]
+
+
+def with_rim(own_ref, rim_ref):
+    out = []
+    for own, rim in zip(by_pairs(own_ref, slice(None)), by_pairs(rim_ref, slice(None))):
+        out.append(jnp.concatenate([jnp.zeros((BAND - RIM, 128), own.dtype), rim, own], axis=0))
+    return out
+
+
+def first_band_kernel(query_ref, key_ref, value_ref, rim_key_ref, rim_value_ref, bias_ref, out_ref):
+    keys, values = with_rim(key_ref, rim_key_ref), with_rim(value_ref, rim_value_ref)
+    outs = band_attend(by_pairs(query_ref, slice(None)), keys, values, bias_ref[0])
+    for here, out in zip(LANES, outs):
+        out_ref[0, :, here] = out
+
+
+def later_bands_kernel(query_ref, key_ref, value_ref, bias_ref, out_ref):
+    for first in range(BAND, query_ref.shape[1], BAND):
+        rows, near = slice(first, first + BAND), slice(first - BAND, first + BAND)
+        outs = band_attend(
+            by_pairs(query_ref, rows), by_pairs(key_ref, near), by_pairs(value_ref, near), bias_ref[0, rows]
+        )
+        for here, out in zip(LANES, outs):
+            out_ref[0, first - BAND : first, here] = out
 
 
 def first_band_back_kernel(
-    query_ref, key_ref, value_ref, rim_key_ref, rim_value_ref, mask_ref, grad_ref, dquery_ref, dkey_ref,
+    query_ref, key_ref, value_ref, rim_key_ref, rim_value_ref, bias_ref, grad_ref, dquery_ref, dkey_ref,
     dvalue_ref, drim_key_ref, drim_value_ref,
 ):
-    for _, here in pairs_of(0):
-        keys, values = with_rim(key_ref, rim_key_ref, here), with_rim(value_ref, rim_value_ref, here)
-        dquery, dkey, dvalue = band_back(
-            query_ref[0, :, here], grad_ref[0, :, here], keys, values, mask_ref[0]
-        )
+    keys, values = with_rim(key_ref, rim_key_ref), with_rim(value_ref, rim_value_ref)
+    whole = slice(None)
+    all_back = band_back(by_pairs(query_ref, whole), by_pairs(grad_ref, whole), keys, values, bias_ref[0])
+    for here, dquery, dkey, dvalue in zip(LANES, *all_back):
         dquery_ref[0, :, here] = dquery
         dkey_ref[0, :, here] = dkey[BAND:]
         dvalue_ref[0, :, here] = dvalue[BAND:]
@@ -1109,25 +1158,25 @@
 
 
 def later_bands_back_kernel(
-    query_ref, key_ref, value_ref, mask_ref, grad_ref, first_dkey_ref, first_dvalue_ref, dquery_ref, dkey_ref,
+    query_ref, key_ref, value_ref, bias_ref, grad_ref, first_dkey_ref, first_dvalue_ref, dquery_ref, dkey_ref,
     dvalue_ref,
 ):
-    for _, here in pairs_of(0):
-        dkey_ref[0, :BAND, here] = first_dkey_ref[0, :, here]
-        dvalue_ref[0, :BAND, here] = first_dvalue_ref[0, :, here]
-        for first in range(BAND, query_ref.shape[1], BAND):
-            rows, before, near = (
-                slice(first, first + BAND),
-                slice(first - BAND, first),
-                slice(first - BAND, first + BAND),
-            )
-            dquery, dkey, dvalue = band_back(
-                query_ref[0, rows, here],
-                grad_ref[0, rows, here],
-                key_ref[0, near, here],
-                value_ref[0, near, here],
-                mask_ref[0, rows],
-            )
+    dkey_ref[0, :BAND] = first_dkey_ref[0]
+    dvalue_ref[0, :BAND] = first_dvalue_ref[0]
+    for first in range(BAND, query_ref.shape[1], BAND):
+        rows, before, near = (
+            slice(first, first + BAND),
+            slice(first - BAND, first),
+            slice(first - BAND, first + BAND),
+        )
+        all_back = band_back(
+            by_pairs(query_ref, rows),
+            by_pairs(grad_ref, rows),
+            by_pairs(key_ref, near),
+            by_pairs(value_ref, near),
+            bias_ref[0, rows],
+        )
+        for here, dquery, dkey, dvalue in zip(LANES, *all_back):
             dquery_ref[0, before, here] = dquery
             dkey_ref[0, before, here] += dkey[:BAND]
             dvalue_ref[0, before, here] += dvalue[:BAND]
@@ -1136,12 +1185,12 @@
 
 
 def by_window(kernel, name, ins, outs):
-    micro, steps = ins[0][0].shape[0], HEADS // 2 // PER
+    micro, steps = ins[0][0].shape[0], HEADS // 2 // WIDE_PER
 
     def spec(rows, place, width):
         if place is None:
             return pl.BlockSpec((1, rows, width), lambda m, p: (m, 0, 0))
-        return pl.BlockSpec((1, rows, PER * 128), lambda m, p: (m, 0, p + place * steps))
+        return pl.BlockSpec((1, rows, WIDE_PER * 128), lambda m, p: (m, 0, p + place * steps))
 
     return pl.pallas_call(
         kernel,
@@ -1252,7 +1301,8 @@
     grad_gate = grad_hidden * up_part * sigmoid_gate * (1.0 + gate_part * (1.0 - sigmoid_gate))
     grad_up = grad_hidden * gate_part * sigmoid_gate
     grad_projected = jnp.concatenate([grad_gate, grad_up], axis=-1).astype(jnp.bfloat16)
-    grad_gate_up = (flat(normed_low), flat(grad_projected))
+    low = jnp.bfloat16
+    grad_gate_up = (flat(normed_low), (flat(grad_gate.astype(low)), flat(grad_up.astype(low))))
     grad_input, grad_gain = norm_back(lax.optimization_barrier(matmul_back(grad_projected, gate_up)))
     return (grad_stream + grad_input, (grad_gain, grad_gate_up, grad_down))
 
@@ -1292,14 +1342,16 @@
     )
     n_dp, n_ctx = lax.axis_size("dp"), lax.axis_size("ctx")
     first_shards = [small, proj_qk, proj_values]
+    rim_stream = passed_along(tokens_in[:, 0, tok_count - CONV + 1 :], "ctx", 1)
     small, w_qk, w_values = gather_all(first_shards, n_dp, n_ctx, chunks_of(first_shards), cid=0)
+    small, rim_stream = lax.optimization_barrier((small, rim_stream))
 
     def gather_more(state):
         shards = [out_linear, gate_up_one, down_one, proj_qkv, out_window, down_two]
         return gather_all(shards, n_dp, n_ctx, chunks_of(shards), cid=2, carry=1, state=state)
 
     middle, saved_linear, more = linear_forward(
-        stream, (small[:, 0], w_qk, w_values, small[:, 4:7]), layout_info, gather_more
+        stream, rim_stream, (small[:, 0], w_qk, w_values, small[:, 4:7]), layout_info, gather_more
     )
     w_out_linear, w_gu_one, w_dn_one, w_qkv, w_out_window, w_dn_two = more
     w_gu_two = lax.all_gather(gate_up_two, ("dp", "ctx"), axis=0, tiled=True)
@@ -1313,6 +1365,7 @@
     grad_stream = cotangent[:, 0].astype(jnp.float32) * valid_rows
     grad_stream, grads_ffn_two = ffn_backward(grad_stream, saved_ffn_two, layer_two[3:])
     operand, gradient = grads_ffn_two[1]
+    gradient = jnp.concatenate(gradient, axis=-1)
     partial_sums = jnp.einsum("tr,te->re", operand, gradient, preferred_element_type=jnp.float32)
     partial_sums = partial_sums.astype(jnp.bfloat16)
     for axis in ("dp", "ctx"):

time: 757 us -> 725 us (0.958)
  Pallas kernels: 512 us -> 490 us
  other arithmetic: 49.8 us -> 41.1 us
    pallas_call x4, Pallas kernels: 51.6 us -> 20.3 us  [by_window(): pl.pallas_call(kernel, grid=(micro, steps), in_specs=[spec(rows, place, a...]
    pallas_call x2, Pallas kernels: 203 us -> 218 us  [gather_all(): pl.pallas_call(partial(gather_kernel, n_dp, n_ctx, chunks, lag, n, carry)...]
    unnamed x240 -> x239, local copies, waits for them, and re-layouts: 26.2 us -> 22.7 us
    dot_general x9 -> x10, matrix products: 46 us -> 44.3 us  [matmul(): jnp.einsum('mtd,de->mte', operand, weight, preferred_element_type=jnp.flo...]
  transfers between devices with their start and end apart: 7 -> 7, of which waited for: 1 -> 1; matrix products, arithmetic and copies ran while one was open for 19% -> 18% of each run, Pallas kernels for 68% -> 68%
where the time goes in v5:
time: 725 us; the launch traced here: 717 us
  Pallas kernels  490 us (68%)
  matrix products  114 us (16%)
  other arithmetic  41.1 us (6%)
  local copies, waits for them, and re-layouts  31.1 us (4%)
  between operations  15.9 us (2%)
  starting transfers between devices  15.8 us (2%)
  waiting for transfers between devices  9.15 us (1%)
    pallas_call x2, Pallas kernels, gather_all(): pl.pallas_call(partial(gather_kernel, n_dp, n_ctx, chunks, lag, n, carry)...  218 us
    pallas_call x2, Pallas kernels, scatter_sums(): pl.pallas_call(partial(scatter_kernel, n_dp, n_ctx, plan, lags, pieces, l...  199 us
    dot_general x9, matrix products, matmul_back(): jnp.einsum('mte,de->mtd', operand, weight, preferred_element_type=jnp.flo...  58.9 us
    pallas_call x4, Pallas kernels, by_pair(): pl.pallas_call(kernel, grid=(ins[0][0].shape[0], HEADS // 2 // PER), in_s...  50.9 us
    dot_general x10, matrix products, matmul(): jnp.einsum('mtd,de->mte', operand, weight, preferred_element_type=jnp.flo...  44.3 us
    unnamed x239, local copies, waits for them, and re-layouts  22.7 us
    pallas_call x4, Pallas kernels, by_window(): pl.pallas_call(kernel, grid=(micro, steps), in_specs=[spec(rows, place, a...  20.3 us
    ppermute x4, starting transfers between devices, passed_along(): lax.ppermute(value, axis, [(source, source + steps) for source in range(l...  15.3 us
  transfers between devices with their start and end apart: 7, of which 1 were waited for; matrix products, arithmetic and copies ran while one was open for 18% of the time, Pallas kernels for 68%

profile of v5, /device:TPU:0, one launch (start us, length us, event | category | flops | bytes accessed | tf_op | source)
XLA Modules:
  0.0 716.6 jit_solution(3491598107445524731)
XLA Ops:
  8.8 4.9 collective-permute-start
  15.3 1.5 fusion.48
  20.4 38.6 %gather_weights.2 = (bf16[32,32,128]{2,1,0:T(8,128)(2,1)}, bf16[32,32,512]{2,1,0:T(8,128)(2,1)}, bf16[32,32,1024]{2,1,0:T(8,128)(2,1)}) custom-call(bf16[1,32,128]{2,1,0:T(8,128)(2,1)} %bitcast.256, bf16[1,32,512]{2,1,0:T(8,128)(2,1)} %bitcast.255, bf16[1,32,1024]{2,1,0:T(8,128)(2,1)} %bitcast.254), custom_call_target="tpu_custom_call" | custom-call | tf_op jit(solution)/shard_map/gather_weights/pallas_call | solution.py:206
  59.1 1.2 copy.98
  60.5 2.0 fusion.75
  64.1 1.3 fusion.60
  65.5 1.6 multiply_convert_fusion.5.value_ref
  67.3 7.6 %states.1.refs_6_ = bf16[2,9,160,128]{3,2,1,0:T(8,128)(2,1)S(1)} custom-call(bf16[2,256,512]{2,1,0:T(8,128)(2,1)S(1)} %convolution_convert_fusion.3.key_ref.query_ref, bf16[2,256,1024]{2,1,0:T(8,128)(2,1)S(1)} %multiply_convert_fusion.5.value_ref, f32[2,256,128]{2,1,0:T(8,128)S(1)} %broadcast_in_dim.84.last_ref, bf16[2,256,256]{2,1,0:T(8,128)(2,1)S(1)} %copy-done.16, ...), custom_call_target="tpu_custom_call" | custom-call | tf_op jit(solution)/shard_map/states/pallas_call | solution.py:789
  76.5 179.7 %gather_weights.3 = (bf16[32,32,1024]{2,1,0:T(8,128)(2,1)}, bf16[32,32,5632]{2,1,0:T(8,128)(2,1)}, bf16[32,88,1024]{2,1,0:T(8,128)(2,1)}, bf16[32,32,3072]{2,1,0...) custom-call(bf16[1,32,1024]{2,1,0:T(8,128)(2,1)} %bitcast.252, ...), custom_call_target="tpu_custom_call" | custom-call | tf_op jit(solution)/shard_map/gather_weights/pallas_call | solution.py:206
  256.4 1.3 copy-done.13
  257.6 9.0 %linear_attend.1 = (bf16[2,256,1024]{2,1,0:T(8,128)(2,1)S(1)}, f32[2,256,1024]{2,1,0:T(8,128)}) custom-call(bf16[2,256,512]{2,1,0:T(8,128)(2,1)S(1)} %convolution_convert_fusion.3.key_ref.query_ref, bf16[2,256,512]{2,1,0:T(8,128)(2,1)S(1)} %convolution_convert_fusion.3.key_ref.query_ref, bf16[2,256,1024]{2,1,0:T(8,128)(2,1)S(1)} %multiply_convert_fusion.5.value_ref, ...), custom_call_target="tpu_custom_call" | custom-call | tf_op jit(solution)/shard_map/linear_attend/pallas_call | solution.py:789
  266.7 1.4 multiply_reduce_fusion.11
  268.3 11.4 %fusion.104 = (bf16[2,256,5632]{2,1,0:T(8,128)(2,1)}, f32[2,256,5632]{2,1,0:T(8,128)S(1)}) fusion(bf16[2,256,1024]{2,1,0:T(8,128)(2,1)S(1)} %multiply_convert_fusion.4, bf16[1024,5632,1]{1,0,2:T(8,128)(2,1)} %bitcast.201), kind=kOutput, calls=%fused_computation.219 | convolution fusion | flops 5908463616 | bytes 29884416 | tf_op jit(solution)/shard_map/mtd,de->mte/dot_general | solution.py:909
  279.7 1.8 fusion.21
  281.6 6.4 multiply_reduce_fusion.10
  288.3 3.7 convolution_convert_fusion.1.query_ref.key_ref.value_ref
  292.0 7.8 %collective-permute-start.1 = (bf16[2,64,2048]{2,1,0:T(8,128)(2,1)S(1)}, bf16[2,64,2048]{2,1,0:T(8,128)(2,1)S(1)}, u32[]{:S(2)}, u32[]{:S(2)}) collective-permute-start(bf16[2,64,2048]{2,1,0:T(8,128)(2,1)S(1)} %slice.232), channel_id=1, source_target_pairs={{0,1},{1,2},{2,3},{4,5},{5,6},{6,7},{8,9},{9,10},{10,11},{12,13},{... | collective-permute-start | bytes 1572872 | tf_op jit(solution)/shard_map/ppermute | solution.py:557
  300.1 3.1 window_later.1
  303.2 8.4 %collective-permute-done.1.rim_key_ref.rim_value_ref = bf16[2,64,2048]{2,1,0:T(8,128)(2,1)S(1)} collective-permute-done((bf16[2,64,2048]{2,1,0:T(8,128)(2,1)S(1)}, bf16[2,64,2048]{2,1,0:T(8,128)(2,1)S(1)}, u32[]{:S(2)}, u32[]{:S(2)}) %collective-permute-start.1) | collective-permute-done | bytes 524320 | tf_op jit(solution)/shard_map/ppermute | solution.py:557
  311.6 3.0 window_first.1
  314.6 1.3 multiply_reduce_fusion.9
  316.0 1.3 copy-done.33
  317.6 9.3 %fusion.105 = (bf16[2,256,5632]{2,1,0:T(8,128)(2,1)S(1)}, f32[2,256,5632]{2,1,0:T(8,128)S(1)}) fusion(bf16[2,256,1024]{2,1,0:T(8,128)(2,1)S(1)} %multiply_convert_fusion.2, bf16[1024,5632]{1,0:T(8,128)(2,1)} %all-gather.2.cloned.1.call-done), kind=kOutput, calls=%fused_computation.220 | convolution fusion | flops 5908463616 | bytes 29884416 | tf_op jit(solution)/shard_map/mtd,de->mte/dot_general | solution.py:909
  327.0 1.8 fusion.20
  328.8 9.2 %fusion.9 = (bf16[2,256,2816]{2,1,0:T(8,128)(2,1)S(1)}, bf16[2,256,2816]{2,1,0:T(8,128)(2,1)}) fusion(bf16[2,256,5632]{2,1,0:T(8,128)(2,1)S(1)} %get-tuple-element.115, bf16[2816,1024,1]{1,0,2:T(8,128)(2,1)} %bitcast.278, bf16[2,1,256,1024]{3,2,1,0:T(8,128)(2,1)S(1)} %copy-done.44, f32[2,256]{1,0:T(2,128)S(1)} %compare_convert_fusion), kind=kOutput, calls=%fused_computation.16 | convolution fusion | flops 2975989760 | bytes 18352128 | tf_op jit(solution)/shard_map/mte,de->mtd/dot_general | solution.py:913
  338.1 1.6 copy-done.108
  339.7 10.7 %convolution_convert_fusion = bf16[1024,5632]{1,0:T(8,128)(2,1)} fusion(bf16[512,1024]{1,0:T(8,128)(2,1)S(1)} %bitcast.208, bf16[512,2816]{1,0:T(8,128)(2,1)} %bitcast.285, bf16[512,2816]{1,0:T(8,128)(2,1)S(1)} %bitcast.284), kind=kOutput, calls=%fused_computation.4 | convolution fusion | flops 5922881536 | bytes 18350080 | tf_op jit(solution)/shard_map/tr,te->re/dot_general | solution.py:1369
  350.9 1.5 bitcast_convert_fusion
  352.4 1.2 fusion.45.refs_12_
  353.6 1.0 copy-done.10
  355.8 1.2 pad_maximum_fusion.2
  357.0 13.1 %fusion = f32[2,256,1024]{2,1,0:T(8,128)S(1)} fusion(bf16[1024,5632]{1,0:T(8,128)(2,1)} %all-gather.2.cloned.1.call-done, bf16[2,256,2816]{2,1,0:T(8,128)(2,1)} %get-tuple-element.234, bf16[2,256,2816]{2,1,0:T(8,128)(2,1)} %copy-done.108), kind=kOutput, calls=%fused_computation | convolution fusion | flops 5917114368 | bytes 19398656 | tf_op jit(solution)/shard_map/mte,de->mtd/dot_general | solution.py:913
  372.0 1.0 copy-done.50
  373.2 1.3 convolution_convert_fusion.2.grad_ref
  374.5 6.5 window_first_back.1
  381.8 1.3 collective-permute-start.2
  383.9 1.7 copy-done.8
  385.6 7.7 %window_later_back.1 = (bf16[2,128,1024]{2,1,0:T(8,128)(2,1)S(1)}, f32[2,256,1024]{2,1,0:T(8,128)}, f32[2,256,1024]{2,1,0:T(8,128)}) custom-call(bf16[2,256,3072]{2,1,0:T(8,128)(2,1)} %copy-done, bf16[2,256,3072]{2,1,0:T(8,128)(2,1)} %copy-done, bf16[2,256,3072]{2,1,0:T(8,128)(2,1)} %copy-done, f32[2,256,256]{2,1,0:T(8,128)S(1)} %copy-done.6, ...), custom_call_target="tpu_custom_call" | custom-call | tf_op jit(solution)/shard_map/window_later_back/pallas_call | solution.py:1195
  393.3 6.7 fusion.53
  400.6 1.2 copy-done.55
  402.4 1.1 fusion.42
  403.5 6.6 fusion.93
  410.6 1.2 fusion.97
  411.9 9.9 %fusion.17 = (bf16[2,256,2816]{2,1,0:T(8,128)(2,1)}, bf16[2,256,2816]{2,1,0:T(8,128)(2,1)}) fusion(bf16[2,256,5632]{2,1,0:T(8,128)(2,1)S(1)} %bitcast.205, bf16[2,256,1024]{2,1,0:T(8,128)(2,1)S(1)} %get-tuple-element.229, bf16[2816,1024,1]{1,0,2:T(8,128)(2,1)} %bitcast.277), kind=kOutput, calls=%fused_computation.24 | convolution fusion | flops 2974416896 | bytes 18350080 | tf_op jit(solution)/shard_map/mte,de->mtd/dot_general | solution.py:913
  421.9 11.0 %fusion.25 = f32[2,256,1024]{2,1,0:T(8,128)S(1)} fusion(bf16[1024,5632,1]{1,0,2:T(8,128)(2,1)} %bitcast.202, bf16[2,256,2816]{2,1,0:T(8,128)(2,1)} %get-tuple-element.232, bf16[2,256,2816]{2,1,0:T(8,128)(2,1)} %get-tuple-element.231), kind=kOutput, calls=%fused_computation.34 | convolution fusion | flops 5917114368 | bytes 19398656 | tf_op jit(solution)/shard_map/mte,de->mtd/dot_general | solution.py:913
  433.6 1.9 fusion.95
  435.6 2.6 fusion.106.grad_ref
  438.3 21.8 %linear_attend_back.1 = (f32[2,256,256]{2,1,0:T(8,128)S(1)}, f32[2,256,256]{2,1,0:T(8,128)S(1)}, f32[2,256,1024]{2,1,0:T(8,128)}, bf16[2,9,160,128]{3,2,1,0:T(8,128)(2,1)S(1)}) custom-call(bf16[2,256,512]{2,1,0:T(8,128)(2,1)S(1)} %copy-done.4, bf16[2,256,512]{2,1,0:T(8,128)(2,1)S(1)} %copy-done.4, bf16[2,256,1024]{2,1,0:T(8,128)(2,1)S(1)} %copy-done.2, ...), custom_call_target="tpu_custom_call" | custom-call | tf_op jit(solution)/shard_map/linear_attend_back/pallas_call | solution.py:789
  460.1 1.8 pad_maximum_fusion
  462.0 162.8 %scatter_sums.2 = (f32[32,1024]{1,0:T(8,128)}, f32[32,5632]{1,0:T(8,128)}, f32[88,1024]{1,0:T(8,128)}, f32[32,3072]{1,0:T(8,128)}, f32[32,1024]{1,0:T(8,128)}, /...) custom-call(bf16[512,1024]{1,0:T(8,128)(2,1)} %bitcast.199, bf16[512,1024]{1,0:T(8,128)(2,1)} %bitcast.203, ...), custom_call_target="tpu_custom_call" | custom-call | tf_op jit(solution)/shard_map/scatter_sums/pallas_call | solution.py:518
  624.8 1.3 copy-done.29
  626.1 12.4 %states_back.1 = (f32[2,256,256]{2,1,0:T(8,128)S(1)}, f32[2,256,1024]{2,1,0:T(8,128)}) custom-call(bf16[2,256,512]{2,1,0:T(8,128)(2,1)S(1)} %copy-done.4, bf16[2,256,1024]{2,1,0:T(8,128)(2,1)S(1)} %copy-done.2, f32[2,256,128]{2,1,0:T(8,128)S(1)} %copy-done.24, bf16[2,256,256]{2,1,0:T(8,128)(2,1)S(1)} %copy-done.17, f32[8,256]{1,0:T(8,128)S(1)} %copy-done.32, ...), custom_call_target="tpu_custom_call" | custom-call | tf_op jit(solution)/shard_map/states_back/pallas_call | solution.py:789
  638.7 3.1 multiply_reduce_fusion.2
  642.4 1.3 collective-permute-start.3
  644.6 2.3 pad_add_fusion
  646.9 2.1 fusion.63
  649.0 3.8 fusion.38
  653.1 1.0 copy-done.42
  654.7 3.0 fusion.51
  658.2 1.3 fusion.44.refs_1_
  659.5 36.1 %scatter_sums.3 = (f32[32,512]{1,0:T(8,128)}, f32[32,512]{1,0:T(8,128)}, f32[32,1024]{1,0:T(8,128)}) custom-call(bf16[512,1024]{1,0:T(8,128)(2,1)} %copy-done.52, bf16[512,1024]{1,0:T(8,128)(2,1)} %fusion.44.refs_1_, bf16[512,512]{1,0:T(8,128)(2,1)} %constant.153.clone.refs_2_, bf16[512,512]{1,0:T(8,128)(2,1)} %pad_maximum_fusion.4.refs_3_, ...), custom_call_target="tpu_custom_call" | custom-call | tf_op jit(solution)/shard_map/scatter_sums/pallas_call | solution.py:518
  697.1 1.7 slice_reduce_fusion
  698.7 3.2 fusion.58
  702.0 2.0 convert_element_type.330
  (322 shorter events, 29.3 us)
Async XLA Ops:
  7.2 12.0 %copy-start.99 = (bf16[32]{0:T(256)(128)(2,1)S(1)}, bf16[32]{0:T(256)(128)(2,1)}, u32[]{:S(2)}) copy-start(bf16[32]{0:T(256)(128)(2,1)} %param.28) | copy-start | bytes 196
  7.2 12.1 %copy-start.100 = (bf16[32]{0:T(256)(128)(2,1)S(1)}, bf16[32]{0:T(256)(128)(2,1)}, u32[]{:S(2)}) copy-start(bf16[32]{0:T(256)(128)(2,1)} %param.33) | copy-start | bytes 196
  7.2 12.2 %copy-start.101 = (bf16[32]{0:T(256)(128)(2,1)S(1)}, bf16[32]{0:T(256)(128)(2,1)}, u32[]{:S(2)}) copy-start(bf16[32]{0:T(256)(128)(2,1)} %param.36) | copy-start | bytes 196
  7.2 12.3 %copy-start.102 = (bf16[32]{0:T(256)(128)(2,1)S(1)}, bf16[32]{0:T(256)(128)(2,1)}, u32[]{:S(2)}) copy-start(bf16[32]{0:T(256)(128)(2,1)} %param.39) | copy-start | bytes 196
  7.2 12.4 %copy-start.98 = (bf16[32,3]{0,1:T(4,128)(2,1)S(1)}, bf16[32,3]{0,1:T(4,128)(2,1)}, u32[]{:S(2)}) copy-start(bf16[32,3]{0,1:T(4,128)(2,1)} %param.31) | copy-start | bytes 580
  7.2 310.4 %all-gather.2.cloned.1.call-start = ((), (), s32[]{:S(2)}) async-start(), calls=%async_computation.2 | async-start | bytes 11894784 | tf_op jit(solution)/shard_map/all_gather | solution.py:1357
  8.0 641.0 %reduce-scatter.3.cloned.1.call-start = ((), (), s32[]{:S(2)}) async-start(), calls=%async_computation.3 | async-start | bytes 12976128 | tf_op jit(solution)/shard_map/reduce_scatter | solution.py:1372
  8.8 50.3 %collective-permute-start = (bf16[2,2,1024]{2,1,0:T(2,128)(2,1)S(1)}, bf16[2,2,1024]{2,1,0:T(2,128)(2,1)S(1)}, u32[]{:S(2)}, u32[]{:S(2)}) collective-permute-start(bf16[2,2,1024]{2,1,0:T(2,128)(2,1)S(1)} %slice_bitcast_fusion), channel_id=1, source_target_pairs={{0,1},{1,2},{2,3},{4,5},{5,6},{6,7},{8,9},{9,10},{10,11},{12,13},{... | collective-permute-start | bytes 24584 | tf_op jit(solution)/shard_map/ppermute | solution.py:557
  14.6 50.8 %copy-start.88 = (f32[256]{0:T(256)}, f32[256]{0:T(256)S(1)}, u32[]{:S(2)}) copy-start(f32[256]{0:T(256)S(1)} %get-tuple-element.274) | copy-start | bytes 3076
  16.8 42.3 %copy-start.90 = (f32[2,256]{1,0:T(2,128)}, f32[2,256]{1,0:T(2,128)S(1)}, u32[]{:S(2)}) copy-start(f32[2,256]{1,0:T(2,128)S(1)} %fusion.48) | copy-start | bytes 6148
  16.8 45.7 %copy-start.41 = (bf16[2,1,256,1024]{3,2,1,0:T(8,128)(2,1)S(1)}, bf16[2,1,256,1024]{3,2,1,0:T(8,128)(2,1)}, u32[]{:S(2)}) copy-start(bf16[2,1,256,1024]{3,2,1,0:T(8,128)(2,1)} %param.26) | copy-start | bytes 3145732
  17.9 45.4 %copy-start.92 = (f32[2,256]{1,0:T(2,128)}, f32[2,256]{1,0:T(2,128)S(1)}, u32[]{:S(2)}) copy-start(f32[2,256]{1,0:T(2,128)S(1)} %fusion.80) | copy-start | bytes 6148
  18.0 47.5 %copy-start.82 = (f32[2,256]{1,0:T(2,128)}, f32[2,256]{1,0:T(2,128)S(1)}, u32[]{:S(2)}) copy-start(f32[2,256]{1,0:T(2,128)S(1)} %get-tuple-element.259) | copy-start | bytes 6148
  18.0 47.5 %copy-start.84 = (f32[2,256]{1,0:T(2,128)}, f32[2,256]{1,0:T(2,128)S(1)}, u32[]{:S(2)}) copy-start(f32[2,256]{1,0:T(2,128)S(1)} %get-tuple-element.260) | copy-start | bytes 6148
  18.5 237.8 %copy-start.14 = (f32[2,256,256]{2,1,0:T(8,128)}, f32[2,256,256]{2,1,0:T(8,128)S(1)}, u32[]{:S(2)}) copy-start(f32[2,256,256]{2,1,0:T(8,128)S(1)} %and_convert_fusion.mask_ref) | copy-start | bytes 1572868
  60.4 5.1 copy-start.71
  60.5 207.6 %copy-start.79 = (f32[1024,1]{0,1:T(1,128)}, f32[1024,1]{0,1:T(1,128)S(1)}, u32[]{:S(2)}) copy-start(f32[1024,1]{0,1:T(1,128)S(1)} %get-tuple-element.242) | copy-start | bytes 12292
  64.1 192.2 %copy-start.3 = (bf16[2,256,512]{2,1,0:T(8,128)(2,1)}, bf16[2,256,512]{2,1,0:T(8,128)(2,1)S(1)}, u32[]{:S(2)}) copy-start(bf16[2,256,512]{2,1,0:T(8,128)(2,1)S(1)} %convolution_convert_fusion.3.key_ref.query_ref) | copy-start | bytes 1572868
  67.1 189.2 %copy-start.1 = (bf16[2,256,1024]{2,1,0:T(8,128)(2,1)}, bf16[2,256,1024]{2,1,0:T(8,128)(2,1)S(1)}, u32[]{:S(2)}) copy-start(bf16[2,256,1024]{2,1,0:T(8,128)(2,1)S(1)} %multiply_convert_fusion.5.value_ref) | copy-start | bytes 3145732
  67.1 8.7 %copy-start.103 = (f32[2]{0:T(128)S(1)}, f32[2]{0:T(128)}, u32[]{:S(2)}) copy-start(f32[2]{0:T(128)} %broadcast_subtract_fusion) | copy-start | bytes 28
  67.3 7.7 %copy-start.23 = (f32[2,256,128]{2,1,0:T(8,128)}, f32[2,256,128]{2,1,0:T(8,128)S(1)}, u32[]{:S(2)}) copy-start(f32[2,256,128]{2,1,0:T(8,128)S(1)} %broadcast_in_dim.84.last_ref) | copy-start | bytes 786436
  257.6 9.0 %copy-start.21 = (f32[2,256,128]{2,1,0:T(8,128)}, f32[2,256,128]{2,1,0:T(8,128)S(1)}, u32[]{:S(2)}) copy-start(f32[2,256,128]{2,1,0:T(8,128)S(1)} %broadcast_in_dim.86.carried_ref) | copy-start | bytes 786436
  257.6 9.0 %copy-start.104 = (bf16[32,32,1024]{2,1,0:T(8,128)(2,1)S(1)}, bf16[32,32,1024]{2,1,0:T(8,128)(2,1)}, u32[]{:S(2)}) copy-start(bf16[32,32,1024]{2,1,0:T(8,128)(2,1)} %get-tuple-element.105) | copy-start | bytes 6291460
  268.0 11.7 %copy-start.94 = (f32[2,256]{1,0:T(2,128)}, f32[2,256]{1,0:T(2,128)S(1)}, u32[]{:S(2)}) copy-start(f32[2,256]{1,0:T(2,128)S(1)} %get-tuple-element.263) | copy-start | bytes 6148
  268.0 13.5 %copy-start.37 = (f32[2,256,1024]{2,1,0:T(8,128)}, f32[2,256,1024]{2,1,0:T(8,128)S(1)}, u32[]{:S(2)}) copy-start(f32[2,256,1024]{2,1,0:T(8,128)S(1)} %get-tuple-element.264) | copy-start | bytes 6291460
  268.0 11.7 %copy-start.86 = (f32[2,256]{1,0:T(2,128)}, f32[2,256]{1,0:T(2,128)S(1)}, u32[]{:S(2)}) copy-start(f32[2,256]{1,0:T(2,128)S(1)} %fusion.81) | copy-start | bytes 6148
  268.3 11.4 %copy-start.43 = (bf16[2,256,1024]{2,1,0:T(8,128)(2,1)}, bf16[2,256,1024]{2,1,0:T(8,128)(2,1)S(1)}, u32[]{:S(2)}) copy-start(bf16[2,256,1024]{2,1,0:T(8,128)(2,1)S(1)} %multiply_convert_fusion.4) | copy-start | bytes 3145732
  281.5 6.4 copy-start.9
  281.5 6.7 slice-start.2
  281.6 6.7 slice-start.3
  288.0 26.6 %copy-start.39 = (f32[2,256,1024]{2,1,0:T(8,128)}, f32[2,256,1024]{2,1,0:T(8,128)S(1)}, u32[]{:S(2)}) copy-start(f32[2,256,1024]{2,1,0:T(8,128)S(1)} %get-tuple-element.268) | copy-start | bytes 6291460
  288.3 11.5 %copy-start.96 = (s32[2,128]{1,0:T(2,128)S(1)}, s32[2,128]{1,0:T(2,128)}, u32[]{:S(2)}) copy-start(s32[2,128]{1,0:T(2,128)} %get-tuple-element.255) | copy-start | bytes 3076
  288.3 11.7 %copy-start.97 = (s32[2]{0:T(128)S(1)}, s32[2]{0:T(128)}, u32[]{:S(2)}) copy-start(s32[2]{0:T(128)} %slice_reduce_fusion.6) | copy-start | bytes 28
  292.0 19.6 %copy-start = (bf16[2,256,3072]{2,1,0:T(8,128)(2,1)}, bf16[2,256,3072]{2,1,0:T(8,128)(2,1)S(1)}, u32[]{:S(2)}) copy-start(bf16[2,256,3072]{2,1,0:T(8,128)(2,1)S(1)} %convolution_convert_fusion.1.query_ref.key_ref.value_ref) | copy-start | bytes 9437188
  292.0 19.5 %collective-permute-start.1 = (bf16[2,64,2048]{2,1,0:T(8,128)(2,1)S(1)}, bf16[2,64,2048]{2,1,0:T(8,128)(2,1)S(1)}, u32[]{:S(2)}, u32[]{:S(2)}) collective-permute-start(bf16[2,64,2048]{2,1,0:T(8,128)(2,1)S(1)} %slice.232), channel_id=1, source_target_pairs={{0,1},{1,2},{2,3},{4,5},{5,6},{6,7},{8,9},{9,10},{10,11},{12,13},{... | collective-permute-start | bytes 1572872 | tf_op jit(solution)/shard_map/ppermute | solution.py:557
  300.0 11.6 %copy-start.5 = (f32[2,256,256]{2,1,0:T(8,128)}, f32[2,256,256]{2,1,0:T(8,128)S(1)}, u32[]{:S(2)}) copy-start(f32[2,256,256]{2,1,0:T(8,128)S(1)} %add_select_fusion.bias_ref) | copy-start | bytes 1572868
  303.1 11.5 %copy-start.25 = (bf16[2,128,1024]{2,1,0:T(8,128)(2,1)}, bf16[2,128,1024]{2,1,0:T(8,128)(2,1)S(1)}, u32[]{:S(2)}) copy-start(bf16[2,128,1024]{2,1,0:T(8,128)(2,1)S(1)} %window_later.1) | copy-start | bytes 1572868
  303.2 11.5 %copy-start.106 = (bf16[32,32,1024]{2,1,0:T(8,128)(2,1)S(1)}, bf16[32,32,1024]{2,1,0:T(8,128)(2,1)}, u32[]{:S(2)}) copy-start(bf16[32,32,1024]{2,1,0:T(8,128)(2,1)} %get-tuple-element.112) | copy-start | bytes 6291460
  317.6 9.4 %copy-start.48 = (bf16[2,256,1024]{2,1,0:T(8,128)(2,1)}, bf16[2,256,1024]{2,1,0:T(8,128)(2,1)S(1)}, u32[]{:S(2)}) copy-start(bf16[2,256,1024]{2,1,0:T(8,128)(2,1)S(1)} %multiply_convert_fusion.2) | copy-start | bytes 3145732
  328.8 10.9 %copy-start.49 = (bf16[2,256,1024]{2,1,0:T(8,128)(2,1)S(1)}, bf16[2,256,1024]{2,1,0:T(8,128)(2,1)}, u32[]{:S(2)}) copy-start(bf16[2,256,1024]{2,1,0:T(8,128)(2,1)} %copy-done.48) | copy-start | bytes 3145732
  350.4 351.6 %reduce-scatter.5.cloned.1.call-start = ((), (), s32[]{:S(2)}) async-start(), calls=%async_computation.4 | async-start | bytes 1802240 | tf_op jit(solution)/shard_map/reduce_scatter | solution.py:1372
  355.8 14.3 %copy-start.7 = (bf16[3,8,128,512]{3,2,1,0:T(8,128)(2,1)}, bf16[3,8,128,512]{3,2,1,0:T(8,128)(2,1)S(1)}, u32[]{:S(2)}) copy-start(bf16[3,8,128,512]{3,2,1,0:T(8,128)(2,1)S(1)} %turn.2.refs_2_) | copy-start | bytes 9437188
  357.0 13.1 %copy-start.34 = (f32[2,256,1024]{2,1,0:T(8,128)S(1)}, f32[2,256,1024]{2,1,0:T(8,128)}, u32[]{:S(2)}) copy-start(f32[2,256,1024]{2,1,0:T(8,128)} %copy-done.33) | copy-start | bytes 6291460
  381.8 18.3 %collective-permute-start.2 = (bf16[2,64,2048]{2,1,0:T(8,128)(2,1)}, bf16[2,64,2048]{2,1,0:T(8,128)(2,1)S(1)}, u32[]{:S(2)}, u32[]{:S(2)}) collective-permute-start(bf16[2,64,2048]{2,1,0:T(8,128)(2,1)} %pad_maximum_fusion.3), channel_id=1, source_target_pairs={{1,0},{2,1},{3,2},{5,4},{6,5},{7,6},{9,8},{10,9},{11,10},{13,12},{... | collective-permute-start | bytes 1572872 | tf_op jit(solution)/shard_map/ppermute | solution.py:557
  402.4 9.5 %slice-start = ((s8[5767168]{0:T(1024)(128)(4,1)}), s8[4194304]{0:T(1024)(128)(4,1)S(1)}, s32[]{:S(2)}) async-start(s8[5767168]{0:T(1024)(128)(4,1)} %bitcast.204), calls=%async_computation.5 | async-start | bytes 8388608
  403.5 6.6 copy-start.40
  403.5 8.4 %slice-start.1 = ((s8[5767168]{0:T(1024)(128)(4,1)}), s8[1572864]{0:T(1024)(128)(4,1)S(1)}, s32[]{:S(2)}) async-start(s8[5767168]{0:T(1024)(128)(4,1)} %bitcast.204), calls=%async_computation.6 | async-start | bytes 3145728
  411.9 10.0 %copy-start.53 = (bf16[2,256,1024]{2,1,0:T(8,128)(2,1)}, bf16[2,256,1024]{2,1,0:T(8,128)(2,1)S(1)}, u32[]{:S(2)}) copy-start(bf16[2,256,1024]{2,1,0:T(8,128)(2,1)S(1)} %get-tuple-element.229) | copy-start | bytes 3145732
  421.8 11.1 %copy-start.38 = (f32[2,256,1024]{2,1,0:T(8,128)S(1)}, f32[2,256,1024]{2,1,0:T(8,128)}, u32[]{:S(2)}) copy-start(f32[2,256,1024]{2,1,0:T(8,128)} %copy-done.37) | copy-start | bytes 6291460
  421.8 11.1 %copy-start.80 = (f32[1024,1]{0,1:T(1,128)S(1)}, f32[1024,1]{0,1:T(1,128)}, u32[]{:S(2)}) copy-start(f32[1024,1]{0,1:T(1,128)} %copy-done.79) | copy-start | bytes 12292
  421.9 11.1 %copy-start.87 = (f32[2,256]{1,0:T(2,128)S(1)}, f32[2,256]{1,0:T(2,128)}, u32[]{:S(2)}) copy-start(f32[2,256]{1,0:T(2,128)} %copy-done.86) | copy-start | bytes 6148
  462.0 162.8 %copy-start.24 = (f32[2,256,128]{2,1,0:T(8,128)S(1)}, f32[2,256,128]{2,1,0:T(8,128)}, u32[]{:S(2)}) copy-start(f32[2,256,128]{2,1,0:T(8,128)} %copy-done.23) | copy-start | bytes 786436
  626.1 12.5 %copy-start.36 = (f32[2,256,1024]{2,1,0:T(8,128)S(1)}, f32[2,256,1024]{2,1,0:T(8,128)}, u32[]{:S(2)}) copy-start(f32[2,256,1024]{2,1,0:T(8,128)} %copy-done.35) | copy-start | bytes 6291460
  626.1 12.5 %copy-start.67 = (f32[2,2,1024]{2,1,0:T(2,128)S(1)}, f32[2,2,1024]{2,1,0:T(2,128)}, u32[]{:S(2)}) copy-start(f32[2,2,1024]{2,1,0:T(2,128)} %copy-done.66) | copy-start | bytes 49156
  626.1 12.5 %copy-start.83 = (f32[2,256]{1,0:T(2,128)S(1)}, f32[2,256]{1,0:T(2,128)}, u32[]{:S(2)}) copy-start(f32[2,256]{1,0:T(2,128)} %copy-done.82) | copy-start | bytes 6148
  626.1 12.5 %copy-start.85 = (f32[2,256]{1,0:T(2,128)S(1)}, f32[2,256]{1,0:T(2,128)}, u32[]{:S(2)}) copy-start(f32[2,256]{1,0:T(2,128)} %copy-done.84) | copy-start | bytes 6148
  626.1 12.5 %copy-start.89 = (f32[256]{0:T(256)S(1)}, f32[256]{0:T(256)}, u32[]{:S(2)}) copy-start(f32[256]{0:T(256)} %copy-done.88) | copy-start | bytes 3076
  642.4 10.4 %collective-permute-start.3 = (f32[2,2,1024]{2,1,0:T(2,128)S(1)}, f32[2,2,1024]{2,1,0:T(2,128)S(1)}, u32[]{:S(2)}, u32[]{:S(2)}) collective-permute-start(f32[2,2,1024]{2,1,0:T(2,128)S(1)} %pad_add_fusion.1), channel_id=1, source_target_pairs={{1,0},{2,1},{3,2},{5,4},{6,5},{7,6},{9,8},{10,9},{11,10},{13,12},{... | collective-permute-start | bytes 49160 | tf_op jit(solution)/shard_map/ppermute | solution.py:557
  659.5 39.2 %copy-start.46 = (f32[2,256,1024]{2,1,0:T(8,128)S(1)}, f32[2,256,1024]{2,1,0:T(8,128)}, u32[]{:S(2)}) copy-start(f32[2,256,1024]{2,1,0:T(8,128)} %get-tuple-element.228) | copy-start | bytes 6291460
  698.7 5.2 copy-start.81
  698.7 5.9 copy-start.70
  698.7 6.5 copy-start.69
  701.9 5.6 copy-start.63
  701.9 6.3 copy-start.68
  (56 other events, 131.5 us)
Sparse Core Ops, SparseCore 0:
  10.9 126.7 all-gather.1
  350.5 89.4 reduce-scatter.2
  649.1 36.9 reduce-scatter.4

commit v6 on v5

--- a/solution.py
+++ b/solution.py
@@ -559,7 +559,7 @@
 
 TERMS = 256
 SENT = 160
-PER = 2
+PER = 4
 
 
 def feature_tables():
@@ -642,8 +642,10 @@
     )
 
 
-def factors(rows, tables, base):
-    return (dot_nn(rows, tables[0]) + base[0:1], dot_nn(rows, tables[1]) + base[1:2])
+def factors(all_rows, tables, base):
+    one = [dot_nn(rows, tables[0]) + base[0:1] for rows in all_rows]
+    two = [dot_nn(rows, tables[1]) + base[1:2] for rows in all_rows]
+    return one, two
 
 
 def states_kernel(key_ref, value_ref, last_ref, table_ref, base_ref, state_ref):
@@ -654,15 +656,19 @@
     lane = lanes_of((SENT, 128), 1)
     totals = state_ref[0, HEADS // 2]
     totals = jnp.where(step == 0, jnp.zeros_like(totals), totals)
-    for pair, here in pairs_of(step):
-        values = value_ref[0, :, here].astype(f32)
-        held = jnp.concatenate([(values * last).astype(low), last.astype(low)], axis=1)
-        one, two = factors(features_apart(keys, pair), table_ref, base_ref)
-        terms = (one * two).astype(low)
-        parts = [dot_tn(terms[:rows], held)[:SENT], dot_tn(terms[rows:], held)[:SENT]]
-        state_ref[0, pair] = jnp.where(lane < 64, parts[0][:, :128], parts[1][:, :128]).astype(low)
-        for side in range(2):
-            totals = jnp.where(lane == 2 * pair + side, parts[side][:, 128:].astype(low), totals)
+    pairs = pairs_of(step)
+    held = [
+        jnp.concatenate([(value_ref[0, :, here].astype(f32) * last).astype(low), last.astype(low)], axis=1)
+        for _, here in pairs
+    ]
+    ones, twos = factors([features_apart(keys, pair) for pair, _ in pairs], table_ref, base_ref)
+    terms = [(one * two).astype(low) for one, two in zip(ones, twos)]
+    first = [dot_tn(t[:rows], h)[:SENT] for t, h in zip(terms, held)]
+    second = [dot_tn(t[rows:], h)[:SENT] for t, h in zip(terms, held)]
+    for (pair, _), one, two in zip(pairs, first, second):
+        state_ref[0, pair] = jnp.where(lane < 64, one[:, :128], two[:, :128]).astype(low)
+        totals = jnp.where(lane == 2 * pair, one[:, 128:].astype(low), totals)
+        totals = jnp.where(lane == 2 * pair + 1, two[:, 128:].astype(low), totals)
     state_ref[0, HEADS // 2] = totals
 
 
@@ -670,24 +676,29 @@
     query_ref, key_ref, value_ref, state_ref, mask_ref, carried_ref, table_ref, base_ref, out_ref, den_ref
 ):
     step = pl.program_id(1)
-    low = jnp.bfloat16
+    low, f32 = jnp.bfloat16, jnp.float32
     queries, keys = query_ref[0], key_ref[0]
     mask, carried = twice(mask_ref[0]), twice(carried_ref[0][:, :1])
+    scale = base_ref[2:3] * carried
     totals = state_ref[0, HEADS // 2]
     inv_root = 1.0 / math.sqrt(FEAT)
-    for pair, here in pairs_of(step):
-        values = value_ref[0, :, here]
-        held = jnp.concatenate([values, jnp.ones_like(values)], axis=1)
-        own = features_apart(queries, pair)
-        slope = dot_nt(own * inv_root, keys) + 1.0
-        weight = ((0.5 * slope * slope + 0.5) * mask).astype(low)
-        one, two = factors(own, table_ref, base_ref)
-        terms = (one * two * base_ref[2:3] * carried).astype(low)
-        near = dot_nn(weight, held)
-        far = dot_nn(terms, jnp.concatenate([state_ref[0, pair], totals], axis=1))
-        picked = far[:, 128:] * at_head(jnp.ones((far.shape[0], 1), jnp.float32), pair)
-        den = near[:, 128:] + jnp.sum(picked, axis=1, keepdims=True)
-        out_ref[0, :, here] = heads_joined((near[:, :128] + far[:, :128]) / den).astype(low)
+    pairs = pairs_of(step)
+    values = [value_ref[0, :, here] for _, here in pairs]
+    held = [jnp.concatenate([v, jnp.ones_like(v)], axis=1) for v in values]
+    states = [jnp.concatenate([state_ref[0, pair], totals], axis=1) for pair, _ in pairs]
+    own = [features_apart(queries, pair) for pair, _ in pairs]
+    slopes = [dot_nt(o * inv_root, keys) + 1.0 for o in own]
+    ones, twos = factors(own, table_ref, base_ref)
+    weights = [((0.5 * slope * slope + 0.5) * mask).astype(low) for slope in slopes]
+    terms = [(one * two * scale).astype(low) for one, two in zip(ones, twos)]
+    near = [dot_nn(w, h) for w, h in zip(weights, held)]
+    far = [dot_nn(t, s) for t, s in zip(terms, states)]
+    picks = [at_head(jnp.ones((2 * queries.shape[0], 1), f32), pair) for pair, _ in pairs]
+    dens = [
+        n[:, 128:] + jnp.sum(f[:, 128:] * pick, axis=1, keepdims=True) for n, f, pick in zip(near, far, picks)
+    ]
+    for (_, here), n, f, den in zip(pairs, near, far, dens):
+        out_ref[0, :, here] = heads_joined((n[:, :128] + f[:, :128]) / den).astype(low)
         den_ref[0, :, here] = heads_joined(den)
 
 
@@ -699,37 +710,47 @@
     low, f32 = jnp.bfloat16, jnp.float32
     queries, keys = query_ref[0], key_ref[0]
     mask, carried = twice(mask_ref[0]), twice(carried_ref[0][:, :1])
+    scale = base_ref[2:3] * carried
     totals = state_ref[0, HEADS // 2]
-    dquery = jnp.zeros(queries.shape, f32)
-    dkey = jnp.zeros(queries.shape, f32)
-    keys_small = keys * (1.0 / math.sqrt(FEAT))
+    inv_root = 1.0 / math.sqrt(FEAT)
+    keys_small = keys * inv_root
     dtotals = dstate_ref[0, HEADS // 2].astype(f32)
     dtotals = jnp.where(step == 0, jnp.zeros_like(dtotals), dtotals)
-    inv_root = 1.0 / math.sqrt(FEAT)
-    for pair, here in pairs_of(step):
-        values = value_ref[0, :, here]
-        whole_state = jnp.concatenate([state_ref[0, pair], totals], axis=1)
-        dnum = grad_ref[0, :, here] / den_ref[0, :, here]
-        dden = -jnp.sum(heads_apart(dnum * out_ref[0, :, here].astype(f32)), axis=1, keepdims=True)
-        dnum = heads_apart(dnum).astype(low)
-        both = jnp.concatenate([dnum, at_head(dden, pair).astype(low)], axis=1)
-        own = features_apart(queries, pair)
-        own_small = own * inv_root
-        slope = dot_nt(own_small, keys) + 1.0
-        weight = ((0.5 * slope * slope + 0.5) * mask).astype(low)
-        dscore = ((dot_nt(dnum, values) + dden) * (slope * mask)).astype(low)
-        dvalue_ref[0, :, here] = dot_tn(weight, dnum)
-        dkey += dot_tn(dscore, own_small)
-        one, two = factors(own, table_ref, base_ref)
-        scale = base_ref[2:3] * carried
-        terms = (one * two * scale).astype(low)
-        part = dot_tn(terms, both)[:SENT]
+    pairs = pairs_of(step)
+    values = [value_ref[0, :, here] for _, here in pairs]
+    states = [jnp.concatenate([state_ref[0, pair], totals], axis=1) for pair, _ in pairs]
+    dnums = [grad_ref[0, :, here] / den_ref[0, :, here] for _, here in pairs]
+    inners = [d * out_ref[0, :, here].astype(f32) for d, (_, here) in zip(dnums, pairs)]
+    ddens = [-jnp.sum(heads_apart(inner), axis=1, keepdims=True) for inner in inners]
+    dnums = [heads_apart(d).astype(low) for d in dnums]
+    both = [
+        jnp.concatenate([dnum, at_head(dden, pair).astype(low)], axis=1)
+        for dnum, dden, (pair, _) in zip(dnums, ddens, pairs)
+    ]
+    own = [features_apart(queries, pair) for pair, _ in pairs]
+    own_small = [o * inv_root for o in own]
+    slopes = [dot_nt(o, keys) + 1.0 for o in own_small]
+    dtaylors = [dot_nt(dnum, v) + dden for dnum, v, dden in zip(dnums, values, ddens)]
+    ones, twos = factors(own, table_ref, base_ref)
+    dterms = [dot_nt(b, s) * scale for b, s in zip(both, states)]
+    weights = [((0.5 * slope * slope + 0.5) * mask).astype(low) for slope in slopes]
+    dscores = [(d * (slope * mask)).astype(low) for d, slope in zip(dtaylors, slopes)]
+    terms = [(one * two * scale).astype(low) for one, two in zip(ones, twos)]
+    by_one = [(d * two).astype(low) for d, two in zip(dterms, twos)]
+    by_two = [(d * one).astype(low) for d, one in zip(dterms, ones)]
+    dvalues = [dot_tn(w, dnum) for w, dnum in zip(weights, dnums)]
+    dkeys = [dot_tn(d, o) for d, o in zip(dscores, own_small)]
+    parts = [dot_tn(t, b)[:SENT] for t, b in zip(terms, both)]
+    through = [
+        dot_nn(d, keys_small) + dot_nt(a, table_ref[0]) + dot_nt(b, table_ref[1])
+        for d, a, b in zip(dscores, by_one, by_two)
+    ]
+    for (pair, here), dvalue, part in zip(pairs, dvalues, parts):
+        dvalue_ref[0, :, here] = dvalue
         dstate_ref[0, pair] = part[:, :128].astype(low)
-        dtotals += part[:, 128:]
-        dterms = dot_nt(both, whole_state) * scale
-        through = dot_nt((dterms * two).astype(low), table_ref[0])
-        through += dot_nt((dterms * one).astype(low), table_ref[1])
-        dquery += features_joined(dot_nn(dscore, keys_small) + through, pair)
+    dtotals += sum(part[:, 128:] for part in parts)
+    dquery = sum(features_joined(value, pair) for value, (pair, _) in zip(through, pairs))
+    dkey = sum(dkeys)
     dstate_ref[0, HEADS // 2] = dtotals.astype(low)
 
     @pl.when(step == 0)
@@ -751,19 +772,24 @@
     keys, last = key_ref[0], last_ref[0]
     last_twice = twice(last[:, :1])
     dtotals = dstate_ref[0, HEADS // 2]
-    dkey = jnp.zeros(keys.shape, f32)
-    for pair, here in pairs_of(step):
-        dstate = dstate_ref[0, pair]
-        whole = jnp.concatenate([dstate, dtotals], axis=1)
-        one, two = factors(features_apart(keys, pair), table_ref, base_ref)
-        terms = (one * two).astype(low)
-        dvalue_ref[0, :, here] = dvalue_in[0, :, here] + heads_joined(dot_nn(terms, dstate)) * last
-        ones = at_head(jnp.ones((terms.shape[0], 1), f32), pair).astype(low)
-        both = jnp.concatenate([heads_apart(value_ref[0, :, here]), ones], axis=1)
-        dterms = dot_nt(both, whole) * last_twice
-        through = dot_nt((dterms * two).astype(low), table_ref[0])
-        through += dot_nt((dterms * one).astype(low), table_ref[1])
-        dkey += features_joined(through, pair)
+    pairs = pairs_of(step)
+    dstates = [dstate_ref[0, pair] for pair, _ in pairs]
+    whole = [jnp.concatenate([dstate, dtotals], axis=1) for dstate in dstates]
+    marks = [at_head(jnp.ones((2 * keys.shape[0], 1), f32), pair).astype(low) for pair, _ in pairs]
+    both = [
+        jnp.concatenate([heads_apart(value_ref[0, :, here]), mark], axis=1)
+        for (_, here), mark in zip(pairs, marks)
+    ]
+    ones, twos = factors([features_apart(keys, pair) for pair, _ in pairs], table_ref, base_ref)
+    dterms = [dot_nt(b, w) * last_twice for b, w in zip(both, whole)]
+    terms = [(one * two).astype(low) for one, two in zip(ones, twos)]
+    by_one = [(d * two).astype(low) for d, two in zip(dterms, twos)]
+    by_two = [(d * one).astype(low) for d, one in zip(dterms, ones)]
+    dvalues = [dot_nn(t, d) for t, d in zip(terms, dstates)]
+    through = [dot_nt(a, table_ref[0]) + dot_nt(b, table_ref[1]) for a, b in zip(by_one, by_two)]
+    for (_, here), dvalue in zip(pairs, dvalues):
+        dvalue_ref[0, :, here] = dvalue_in[0, :, here] + heads_joined(dvalue) * last
+    dkey = sum(features_joined(value, pair) for value, (pair, _) in zip(through, pairs))
 
     @pl.when(step == 0)
     def _():
@@ -1079,7 +1105,7 @@
 
 BAND = 128
 RIM = 64
-WIDE_PER = 4
+WIDE_PER = 8
 
 
 def band_probabilities(queries, keys, bias):

time: 725 us -> 718 us (level)
  Pallas kernels: 490 us -> 481 us
    pallas_call x4, Pallas kernels: 50.9 us -> 43.2 us  [by_pair(): pl.pallas_call(kernel, grid=(ins[0][0].shape[0], HEADS // 2 // PER), in_s...]
where the time goes in v6:
time: 718 us; the launch traced here: 711 us
  Pallas kernels  481 us (67%)
  matrix products  114 us (16%)
  other arithmetic  41.1 us (6%)
  local copies, waits for them, and re-layouts  32 us (4%)
  starting transfers between devices  16.7 us (2%)
  between operations  16 us (2%)
  waiting for transfers between devices  9.8 us (1%)
    pallas_call x2, Pallas kernels, gather_all(): pl.pallas_call(partial(gather_kernel, n_dp, n_ctx, chunks, lag, n, carry)...  218 us
    pallas_call x2, Pallas kernels, scatter_sums(): pl.pallas_call(partial(scatter_kernel, n_dp, n_ctx, plan, lags, pieces, l...  201 us
    dot_general x9, matrix products, matmul_back(): jnp.einsum('mte,de->mtd', operand, weight, preferred_element_type=jnp.flo...  58.7 us
    dot_general x10, matrix products, matmul(): jnp.einsum('mtd,de->mte', operand, weight, preferred_element_type=jnp.flo...  44.3 us
    pallas_call x4, Pallas kernels, by_pair(): pl.pallas_call(kernel, grid=(ins[0][0].shape[0], HEADS // 2 // PER), in_s...  43.2 us
    unnamed x239, local copies, waits for them, and re-layouts  23.6 us
    pallas_call x4, Pallas kernels, by_window(): pl.pallas_call(kernel, grid=(micro, steps), in_specs=[spec(rows, place, a...  17.4 us
    ppermute x4, starting transfers between devices, passed_along(): lax.ppermute(value, axis, [(source, source + steps) for source in range(l...  16.5 us
  transfers between devices with their start and end apart: 7, of which 1 were waited for; matrix products, arithmetic and copies ran while one was open for 18% of the time, Pallas kernels for 68%

profile of v6, /device:TPU:0, one launch (start us, length us, event | category | flops | bytes accessed | tf_op | source)
XLA Modules:
  0.0 710.6 jit_solution(6954227879671684087)
XLA Ops:
  8.8 4.9 collective-permute-start
  15.3 1.5 fusion.48
  20.4 38.6 %gather_weights.2 = (bf16[32,32,128]{2,1,0:T(8,128)(2,1)}, bf16[32,32,512]{2,1,0:T(8,128)(2,1)}, bf16[32,32,1024]{2,1,0:T(8,128)(2,1)}) custom-call(bf16[1,32,128]{2,1,0:T(8,128)(2,1)} %bitcast.256, bf16[1,32,512]{2,1,0:T(8,128)(2,1)} %bitcast.255, bf16[1,32,1024]{2,1,0:T(8,128)(2,1)} %bitcast.254), custom_call_target="tpu_custom_call" | custom-call | tf_op jit(solution)/shard_map/gather_weights/pallas_call | solution.py:206
  59.1 1.2 copy.98
  60.5 2.0 fusion.75
  64.1 1.3 fusion.60
  65.5 1.6 multiply_convert_fusion.5.value_ref
  67.3 4.7 states.1.refs_6_
  73.5 179.8 %gather_weights.3 = (bf16[32,32,1024]{2,1,0:T(8,128)(2,1)}, bf16[32,32,5632]{2,1,0:T(8,128)(2,1)}, bf16[32,88,1024]{2,1,0:T(8,128)(2,1)}, bf16[32,32,3072]{2,1,0...) custom-call(bf16[1,32,1024]{2,1,0:T(8,128)(2,1)} %bitcast.252, ...), custom_call_target="tpu_custom_call" | custom-call | tf_op jit(solution)/shard_map/gather_weights/pallas_call | solution.py:206
  253.5 1.3 copy-done.13
  254.8 8.5 %linear_attend.1 = (bf16[2,256,1024]{2,1,0:T(8,128)(2,1)S(1)}, f32[2,256,1024]{2,1,0:T(8,128)}) custom-call(bf16[2,256,512]{2,1,0:T(8,128)(2,1)S(1)} %convolution_convert_fusion.3.key_ref.query_ref, bf16[2,256,512]{2,1,0:T(8,128)(2,1)S(1)} %convolution_convert_fusion.3.key_ref.query_ref, bf16[2,256,1024]{2,1,0:T(8,128)(2,1)S(1)} %multiply_convert_fusion.5.value_ref, ...), custom_call_target="tpu_custom_call" | custom-call | tf_op jit(solution)/shard_map/linear_attend/pallas_call | solution.py:815
  263.3 1.4 multiply_reduce_fusion.11
  265.0 11.4 %fusion.104 = (bf16[2,256,5632]{2,1,0:T(8,128)(2,1)}, f32[2,256,5632]{2,1,0:T(8,128)S(1)}) fusion(bf16[2,256,1024]{2,1,0:T(8,128)(2,1)S(1)} %multiply_convert_fusion.4, bf16[1024,5632,1]{1,0,2:T(8,128)(2,1)} %bitcast.201), kind=kOutput, calls=%fused_computation.219 | convolution fusion | flops 5908463616 | bytes 29884416 | tf_op jit(solution)/shard_map/mtd,de->mte/dot_general | solution.py:935
  276.3 1.8 fusion.21
  278.2 6.4 multiply_reduce_fusion.10
  284.9 3.7 convolution_convert_fusion.1.query_ref.key_ref.value_ref
  288.6 9.0 %collective-permute-start.1 = (bf16[2,64,2048]{2,1,0:T(8,128)(2,1)S(1)}, bf16[2,64,2048]{2,1,0:T(8,128)(2,1)S(1)}, u32[]{:S(2)}, u32[]{:S(2)}) collective-permute-start(bf16[2,64,2048]{2,1,0:T(8,128)(2,1)S(1)} %slice.232), channel_id=1, source_target_pairs={{0,1},{1,2},{2,3},{4,5},{5,6},{6,7},{8,9},{9,10},{10,11},{12,13},{... | collective-permute-start | bytes 1572872 | tf_op jit(solution)/shard_map/ppermute | solution.py:557
  298.0 2.4 window_later.1
  300.4 9.0 %collective-permute-done.1.rim_key_ref.rim_value_ref = bf16[2,64,2048]{2,1,0:T(8,128)(2,1)S(1)} collective-permute-done((bf16[2,64,2048]{2,1,0:T(8,128)(2,1)S(1)}, bf16[2,64,2048]{2,1,0:T(8,128)(2,1)S(1)}, u32[]{:S(2)}, u32[]{:S(2)}) %collective-permute-start.1) | collective-permute-done | bytes 524320 | tf_op jit(solution)/shard_map/ppermute | solution.py:557
  309.5 2.3 window_first.1
  311.8 1.3 multiply_reduce_fusion.9
  313.2 1.3 copy-done.33
  314.8 9.3 %fusion.105 = (bf16[2,256,5632]{2,1,0:T(8,128)(2,1)S(1)}, f32[2,256,5632]{2,1,0:T(8,128)S(1)}) fusion(bf16[2,256,1024]{2,1,0:T(8,128)(2,1)S(1)} %multiply_convert_fusion.2, bf16[1024,5632]{1,0:T(8,128)(2,1)} %all-gather.2.cloned.1.call-done), kind=kOutput, calls=%fused_computation.220 | convolution fusion | flops 5908463616 | bytes 29884416 | tf_op jit(solution)/shard_map/mtd,de->mte/dot_general | solution.py:935
  324.2 1.8 fusion.20
  326.0 9.2 %fusion.9 = (bf16[2,256,2816]{2,1,0:T(8,128)(2,1)S(1)}, bf16[2,256,2816]{2,1,0:T(8,128)(2,1)}) fusion(bf16[2,256,5632]{2,1,0:T(8,128)(2,1)S(1)} %get-tuple-element.115, bf16[2816,1024,1]{1,0,2:T(8,128)(2,1)} %bitcast.278, bf16[2,1,256,1024]{3,2,1,0:T(8,128)(2,1)S(1)} %copy-done.44, f32[2,256]{1,0:T(2,128)S(1)} %compare_convert_fusion), kind=kOutput, calls=%fused_computation.16 | convolution fusion | flops 2975989760 | bytes 18352128 | tf_op jit(solution)/shard_map/mte,de->mtd/dot_general | solution.py:939
  335.3 1.6 copy-done.108
  336.9 11.1 %convolution_convert_fusion = bf16[1024,5632]{1,0:T(8,128)(2,1)} fusion(bf16[512,1024]{1,0:T(8,128)(2,1)S(1)} %bitcast.208, bf16[512,2816]{1,0:T(8,128)(2,1)} %bitcast.285, bf16[512,2816]{1,0:T(8,128)(2,1)S(1)} %bitcast.284), kind=kOutput, calls=%fused_computation.4 | convolution fusion | flops 5922881536 | bytes 18350080 | tf_op jit(solution)/shard_map/tr,te->re/dot_general | solution.py:1395
  348.1 1.5 bitcast_convert_fusion
  349.6 1.2 fusion.45.refs_12_
  350.8 1.0 copy-done.10
  353.0 1.2 pad_maximum_fusion.2
  354.2 11.9 %fusion = f32[2,256,1024]{2,1,0:T(8,128)S(1)} fusion(bf16[1024,5632]{1,0:T(8,128)(2,1)} %all-gather.2.cloned.1.call-done, bf16[2,256,2816]{2,1,0:T(8,128)(2,1)} %get-tuple-element.234, bf16[2,256,2816]{2,1,0:T(8,128)(2,1)} %copy-done.108), kind=kOutput, calls=%fused_computation | convolution fusion | flops 5917114368 | bytes 19398656 | tf_op jit(solution)/shard_map/mte,de->mtd/dot_general | solution.py:939
  366.7 1.0 copy-done.45
  368.3 1.0 copy-done.50
  370.1 1.3 convolution_convert_fusion.2.grad_ref
  371.4 5.6 window_first_back.1
  377.9 1.3 collective-permute-start.2
  380.0 1.7 copy-done.8
  381.7 7.1 window_later_back.1
  388.7 6.7 fusion.53
  396.0 1.2 copy-done.55
  397.8 1.1 fusion.42
  398.9 6.9 fusion.93
  406.4 1.2 fusion.97
  407.6 9.8 %fusion.17 = (bf16[2,256,2816]{2,1,0:T(8,128)(2,1)}, bf16[2,256,2816]{2,1,0:T(8,128)(2,1)}) fusion(bf16[2,256,5632]{2,1,0:T(8,128)(2,1)S(1)} %bitcast.205, bf16[2,256,1024]{2,1,0:T(8,128)(2,1)S(1)} %get-tuple-element.229, bf16[2816,1024,1]{1,0,2:T(8,128)(2,1)} %bitcast.277), kind=kOutput, calls=%fused_computation.24 | convolution fusion | flops 2974416896 | bytes 18350080 | tf_op jit(solution)/shard_map/mte,de->mtd/dot_general | solution.py:939
  417.5 11.8 %fusion.25 = f32[2,256,1024]{2,1,0:T(8,128)S(1)} fusion(bf16[1024,5632,1]{1,0,2:T(8,128)(2,1)} %bitcast.202, bf16[2,256,2816]{2,1,0:T(8,128)(2,1)} %get-tuple-element.232, bf16[2,256,2816]{2,1,0:T(8,128)(2,1)} %get-tuple-element.231), kind=kOutput, calls=%fused_computation.34 | convolution fusion | flops 5917114368 | bytes 19398656 | tf_op jit(solution)/shard_map/mte,de->mtd/dot_general | solution.py:939
  430.0 1.9 fusion.95
  432.0 2.6 fusion.106.grad_ref
  434.7 18.7 %linear_attend_back.1 = (f32[2,256,256]{2,1,0:T(8,128)S(1)}, f32[2,256,256]{2,1,0:T(8,128)S(1)}, f32[2,256,1024]{2,1,0:T(8,128)}, bf16[2,9,160,128]{3,2,1,0:T(8,128)(2,1)S(1)}) custom-call(bf16[2,256,512]{2,1,0:T(8,128)(2,1)S(1)} %copy-done.4, bf16[2,256,512]{2,1,0:T(8,128)(2,1)S(1)} %copy-done.4, bf16[2,256,1024]{2,1,0:T(8,128)(2,1)S(1)} %copy-done.2, ...), custom_call_target="tpu_custom_call" | custom-call | tf_op jit(solution)/shard_map/linear_attend_back/pallas_call | solution.py:815
  453.3 1.8 pad_maximum_fusion
  455.2 163.9 %scatter_sums.2 = (f32[32,1024]{1,0:T(8,128)}, f32[32,5632]{1,0:T(8,128)}, f32[88,1024]{1,0:T(8,128)}, f32[32,3072]{1,0:T(8,128)}, f32[32,1024]{1,0:T(8,128)}, /...) custom-call(bf16[512,1024]{1,0:T(8,128)(2,1)} %bitcast.199, bf16[512,1024]{1,0:T(8,128)(2,1)} %bitcast.203, ...), custom_call_target="tpu_custom_call" | custom-call | tf_op jit(solution)/shard_map/scatter_sums/pallas_call | solution.py:518
  619.2 1.3 copy-done.29
  620.5 11.3 %states_back.1 = (f32[2,256,256]{2,1,0:T(8,128)S(1)}, f32[2,256,1024]{2,1,0:T(8,128)}) custom-call(bf16[2,256,512]{2,1,0:T(8,128)(2,1)S(1)} %copy-done.4, bf16[2,256,1024]{2,1,0:T(8,128)(2,1)S(1)} %copy-done.2, f32[2,256,128]{2,1,0:T(8,128)S(1)} %copy-done.24, bf16[2,256,256]{2,1,0:T(8,128)(2,1)S(1)} %copy-done.17, f32[8,256]{1,0:T(8,128)S(1)} %copy-done.32, ...), custom_call_target="tpu_custom_call" | custom-call | tf_op jit(solution)/shard_map/states_back/pallas_call | solution.py:815
  631.9 2.9 multiply_reduce_fusion.2
  635.4 1.3 collective-permute-start.3
  637.6 2.3 pad_add_fusion
  639.9 2.1 fusion.63
  642.0 4.1 fusion.38
  648.1 3.0 fusion.51
  651.5 1.3 fusion.44.refs_1_
  652.9 36.7 %scatter_sums.3 = (f32[32,512]{1,0:T(8,128)}, f32[32,512]{1,0:T(8,128)}, f32[32,1024]{1,0:T(8,128)}) custom-call(bf16[512,1024]{1,0:T(8,128)(2,1)} %copy-done.52, bf16[512,1024]{1,0:T(8,128)(2,1)} %fusion.44.refs_1_, bf16[512,512]{1,0:T(8,128)(2,1)} %constant.153.clone.refs_2_, bf16[512,512]{1,0:T(8,128)(2,1)} %pad_maximum_fusion.4.refs_3_, ...), custom_call_target="tpu_custom_call" | custom-call | tf_op jit(solution)/shard_map/scatter_sums/pallas_call | solution.py:518
  691.0 1.7 slice_reduce_fusion
  692.7 3.2 fusion.58
  695.9 2.0 convert_element_type.330
  (322 shorter events, 29.8 us)
Async XLA Ops:
  7.2 12.0 %copy-start.99 = (bf16[32]{0:T(256)(128)(2,1)S(1)}, bf16[32]{0:T(256)(128)(2,1)}, u32[]{:S(2)}) copy-start(bf16[32]{0:T(256)(128)(2,1)} %param.28) | copy-start | bytes 196
  7.2 12.1 %copy-start.100 = (bf16[32]{0:T(256)(128)(2,1)S(1)}, bf16[32]{0:T(256)(128)(2,1)}, u32[]{:S(2)}) copy-start(bf16[32]{0:T(256)(128)(2,1)} %param.33) | copy-start | bytes 196
  7.2 12.2 %copy-start.101 = (bf16[32]{0:T(256)(128)(2,1)S(1)}, bf16[32]{0:T(256)(128)(2,1)}, u32[]{:S(2)}) copy-start(bf16[32]{0:T(256)(128)(2,1)} %param.36) | copy-start | bytes 196
  7.2 12.3 %copy-start.102 = (bf16[32]{0:T(256)(128)(2,1)S(1)}, bf16[32]{0:T(256)(128)(2,1)}, u32[]{:S(2)}) copy-start(bf16[32]{0:T(256)(128)(2,1)} %param.39) | copy-start | bytes 196
  7.2 12.4 %copy-start.98 = (bf16[32,3]{0,1:T(4,128)(2,1)S(1)}, bf16[32,3]{0,1:T(4,128)(2,1)}, u32[]{:S(2)}) copy-start(bf16[32,3]{0,1:T(4,128)(2,1)} %param.31) | copy-start | bytes 580
  7.2 307.6 %all-gather.2.cloned.1.call-start = ((), (), s32[]{:S(2)}) async-start(), calls=%async_computation.2 | async-start | bytes 11894784 | tf_op jit(solution)/shard_map/all_gather | solution.py:1383
  8.0 634.0 %reduce-scatter.3.cloned.1.call-start = ((), (), s32[]{:S(2)}) async-start(), calls=%async_computation.3 | async-start | bytes 12976128 | tf_op jit(solution)/shard_map/reduce_scatter | solution.py:1398
  8.8 50.3 %collective-permute-start = (bf16[2,2,1024]{2,1,0:T(2,128)(2,1)S(1)}, bf16[2,2,1024]{2,1,0:T(2,128)(2,1)S(1)}, u32[]{:S(2)}, u32[]{:S(2)}) collective-permute-start(bf16[2,2,1024]{2,1,0:T(2,128)(2,1)S(1)} %slice_bitcast_fusion), channel_id=1, source_target_pairs={{0,1},{1,2},{2,3},{4,5},{5,6},{6,7},{8,9},{9,10},{10,11},{12,13},{... | collective-permute-start | bytes 24584 | tf_op jit(solution)/shard_map/ppermute | solution.py:557
  14.6 50.8 %copy-start.88 = (f32[256]{0:T(256)}, f32[256]{0:T(256)S(1)}, u32[]{:S(2)}) copy-start(f32[256]{0:T(256)S(1)} %get-tuple-element.274) | copy-start | bytes 3076
  16.8 42.3 %copy-start.90 = (f32[2,256]{1,0:T(2,128)}, f32[2,256]{1,0:T(2,128)S(1)}, u32[]{:S(2)}) copy-start(f32[2,256]{1,0:T(2,128)S(1)} %fusion.48) | copy-start | bytes 6148
  16.8 45.7 %copy-start.41 = (bf16[2,1,256,1024]{3,2,1,0:T(8,128)(2,1)S(1)}, bf16[2,1,256,1024]{3,2,1,0:T(8,128)(2,1)}, u32[]{:S(2)}) copy-start(bf16[2,1,256,1024]{3,2,1,0:T(8,128)(2,1)} %param.26) | copy-start | bytes 3145732
  17.9 45.4 %copy-start.92 = (f32[2,256]{1,0:T(2,128)}, f32[2,256]{1,0:T(2,128)S(1)}, u32[]{:S(2)}) copy-start(f32[2,256]{1,0:T(2,128)S(1)} %fusion.80) | copy-start | bytes 6148
  18.0 47.5 %copy-start.82 = (f32[2,256]{1,0:T(2,128)}, f32[2,256]{1,0:T(2,128)S(1)}, u32[]{:S(2)}) copy-start(f32[2,256]{1,0:T(2,128)S(1)} %get-tuple-element.259) | copy-start | bytes 6148
  18.0 47.5 %copy-start.84 = (f32[2,256]{1,0:T(2,128)}, f32[2,256]{1,0:T(2,128)S(1)}, u32[]{:S(2)}) copy-start(f32[2,256]{1,0:T(2,128)S(1)} %get-tuple-element.260) | copy-start | bytes 6148
  18.5 234.9 %copy-start.14 = (f32[2,256,256]{2,1,0:T(8,128)}, f32[2,256,256]{2,1,0:T(8,128)S(1)}, u32[]{:S(2)}) copy-start(f32[2,256,256]{2,1,0:T(8,128)S(1)} %and_convert_fusion.mask_ref) | copy-start | bytes 1572868
  60.4 5.1 copy-start.71
  60.4 5.1 copy-start.73
  60.5 204.2 %copy-start.79 = (f32[1024,1]{0,1:T(1,128)}, f32[1024,1]{0,1:T(1,128)S(1)}, u32[]{:S(2)}) copy-start(f32[1024,1]{0,1:T(1,128)S(1)} %get-tuple-element.242) | copy-start | bytes 12292
  64.1 189.4 %copy-start.3 = (bf16[2,256,512]{2,1,0:T(8,128)(2,1)}, bf16[2,256,512]{2,1,0:T(8,128)(2,1)S(1)}, u32[]{:S(2)}) copy-start(bf16[2,256,512]{2,1,0:T(8,128)(2,1)S(1)} %convolution_convert_fusion.3.key_ref.query_ref) | copy-start | bytes 1572868
  67.1 186.4 %copy-start.1 = (bf16[2,256,1024]{2,1,0:T(8,128)(2,1)}, bf16[2,256,1024]{2,1,0:T(8,128)(2,1)S(1)}, u32[]{:S(2)}) copy-start(bf16[2,256,1024]{2,1,0:T(8,128)(2,1)S(1)} %multiply_convert_fusion.5.value_ref) | copy-start | bytes 3145732
  67.1 5.7 copy-start.103
  254.8 8.5 %copy-start.21 = (f32[2,256,128]{2,1,0:T(8,128)}, f32[2,256,128]{2,1,0:T(8,128)S(1)}, u32[]{:S(2)}) copy-start(f32[2,256,128]{2,1,0:T(8,128)S(1)} %broadcast_in_dim.86.carried_ref) | copy-start | bytes 786436
  254.8 8.5 %copy-start.104 = (bf16[32,32,1024]{2,1,0:T(8,128)(2,1)S(1)}, bf16[32,32,1024]{2,1,0:T(8,128)(2,1)}, u32[]{:S(2)}) copy-start(bf16[32,32,1024]{2,1,0:T(8,128)(2,1)} %get-tuple-element.105) | copy-start | bytes 6291460
  264.6 11.7 %copy-start.94 = (f32[2,256]{1,0:T(2,128)}, f32[2,256]{1,0:T(2,128)S(1)}, u32[]{:S(2)}) copy-start(f32[2,256]{1,0:T(2,128)S(1)} %get-tuple-element.263) | copy-start | bytes 6148
  264.7 13.5 %copy-start.37 = (f32[2,256,1024]{2,1,0:T(8,128)}, f32[2,256,1024]{2,1,0:T(8,128)S(1)}, u32[]{:S(2)}) copy-start(f32[2,256,1024]{2,1,0:T(8,128)S(1)} %get-tuple-element.264) | copy-start | bytes 6291460
  264.7 11.6 %copy-start.86 = (f32[2,256]{1,0:T(2,128)}, f32[2,256]{1,0:T(2,128)S(1)}, u32[]{:S(2)}) copy-start(f32[2,256]{1,0:T(2,128)S(1)} %fusion.81) | copy-start | bytes 6148
  264.9 11.4 %copy-start.43 = (bf16[2,256,1024]{2,1,0:T(8,128)(2,1)}, bf16[2,256,1024]{2,1,0:T(8,128)(2,1)S(1)}, u32[]{:S(2)}) copy-start(bf16[2,256,1024]{2,1,0:T(8,128)(2,1)S(1)} %multiply_convert_fusion.4) | copy-start | bytes 3145732
  278.2 6.4 copy-start.9
  278.2 6.7 slice-start.2
  278.2 6.7 slice-start.3
  284.6 27.2 %copy-start.39 = (f32[2,256,1024]{2,1,0:T(8,128)}, f32[2,256,1024]{2,1,0:T(8,128)S(1)}, u32[]{:S(2)}) copy-start(f32[2,256,1024]{2,1,0:T(8,128)S(1)} %get-tuple-element.268) | copy-start | bytes 6291460
  284.9 12.8 %copy-start.96 = (s32[2,128]{1,0:T(2,128)S(1)}, s32[2,128]{1,0:T(2,128)}, u32[]{:S(2)}) copy-start(s32[2,128]{1,0:T(2,128)} %get-tuple-element.255) | copy-start | bytes 3076
  284.9 13.0 %copy-start.97 = (s32[2]{0:T(128)S(1)}, s32[2]{0:T(128)}, u32[]{:S(2)}) copy-start(s32[2]{0:T(128)} %slice_reduce_fusion.6) | copy-start | bytes 28
  288.6 20.9 %copy-start = (bf16[2,256,3072]{2,1,0:T(8,128)(2,1)}, bf16[2,256,3072]{2,1,0:T(8,128)(2,1)S(1)}, u32[]{:S(2)}) copy-start(bf16[2,256,3072]{2,1,0:T(8,128)(2,1)S(1)} %convolution_convert_fusion.1.query_ref.key_ref.value_ref) | copy-start | bytes 9437188
  288.6 20.8 %collective-permute-start.1 = (bf16[2,64,2048]{2,1,0:T(8,128)(2,1)S(1)}, bf16[2,64,2048]{2,1,0:T(8,128)(2,1)S(1)}, u32[]{:S(2)}, u32[]{:S(2)}) collective-permute-start(bf16[2,64,2048]{2,1,0:T(8,128)(2,1)S(1)} %slice.232), channel_id=1, source_target_pairs={{0,1},{1,2},{2,3},{4,5},{5,6},{6,7},{8,9},{9,10},{10,11},{12,13},{... | collective-permute-start | bytes 1572872 | tf_op jit(solution)/shard_map/ppermute | solution.py:557
  297.9 11.6 %copy-start.5 = (f32[2,256,256]{2,1,0:T(8,128)}, f32[2,256,256]{2,1,0:T(8,128)S(1)}, u32[]{:S(2)}) copy-start(f32[2,256,256]{2,1,0:T(8,128)S(1)} %add_select_fusion.bias_ref) | copy-start | bytes 1572868
  300.4 11.4 %copy-start.25 = (bf16[2,128,1024]{2,1,0:T(8,128)(2,1)}, bf16[2,128,1024]{2,1,0:T(8,128)(2,1)S(1)}, u32[]{:S(2)}) copy-start(bf16[2,128,1024]{2,1,0:T(8,128)(2,1)S(1)} %window_later.1) | copy-start | bytes 1572868
  300.4 11.4 %copy-start.106 = (bf16[32,32,1024]{2,1,0:T(8,128)(2,1)S(1)}, bf16[32,32,1024]{2,1,0:T(8,128)(2,1)}, u32[]{:S(2)}) copy-start(bf16[32,32,1024]{2,1,0:T(8,128)(2,1)} %get-tuple-element.112) | copy-start | bytes 6291460
  314.8 9.4 %copy-start.48 = (bf16[2,256,1024]{2,1,0:T(8,128)(2,1)}, bf16[2,256,1024]{2,1,0:T(8,128)(2,1)S(1)}, u32[]{:S(2)}) copy-start(bf16[2,256,1024]{2,1,0:T(8,128)(2,1)S(1)} %multiply_convert_fusion.2) | copy-start | bytes 3145732
  326.0 10.9 %copy-start.49 = (bf16[2,256,1024]{2,1,0:T(8,128)(2,1)S(1)}, bf16[2,256,1024]{2,1,0:T(8,128)(2,1)}, u32[]{:S(2)}) copy-start(bf16[2,256,1024]{2,1,0:T(8,128)(2,1)} %copy-done.48) | copy-start | bytes 3145732
  348.0 347.9 %reduce-scatter.5.cloned.1.call-start = ((), (), s32[]{:S(2)}) async-start(), calls=%async_computation.4 | async-start | bytes 1802240 | tf_op jit(solution)/shard_map/reduce_scatter | solution.py:1398
  353.0 13.1 %copy-start.7 = (bf16[3,8,128,512]{3,2,1,0:T(8,128)(2,1)}, bf16[3,8,128,512]{3,2,1,0:T(8,128)(2,1)S(1)}, u32[]{:S(2)}) copy-start(bf16[3,8,128,512]{3,2,1,0:T(8,128)(2,1)S(1)} %turn.2.refs_2_) | copy-start | bytes 9437188
  354.2 11.9 %copy-start.34 = (f32[2,256,1024]{2,1,0:T(8,128)S(1)}, f32[2,256,1024]{2,1,0:T(8,128)}, u32[]{:S(2)}) copy-start(f32[2,256,1024]{2,1,0:T(8,128)} %copy-done.33) | copy-start | bytes 6291460
  377.9 17.6 %collective-permute-start.2 = (bf16[2,64,2048]{2,1,0:T(8,128)(2,1)}, bf16[2,64,2048]{2,1,0:T(8,128)(2,1)S(1)}, u32[]{:S(2)}, u32[]{:S(2)}) collective-permute-start(bf16[2,64,2048]{2,1,0:T(8,128)(2,1)} %pad_maximum_fusion.3), channel_id=1, source_target_pairs={{1,0},{2,1},{3,2},{5,4},{6,5},{7,6},{9,8},{10,9},{11,10},{13,12},{... | collective-permute-start | bytes 1572872 | tf_op jit(solution)/shard_map/ppermute | solution.py:557
  397.8 9.8 %slice-start = ((s8[5767168]{0:T(1024)(128)(4,1)}), s8[4194304]{0:T(1024)(128)(4,1)S(1)}, s32[]{:S(2)}) async-start(s8[5767168]{0:T(1024)(128)(4,1)} %bitcast.204), calls=%async_computation.5 | async-start | bytes 8388608
  398.9 7.0 copy-start.40
  398.9 8.7 %slice-start.1 = ((s8[5767168]{0:T(1024)(128)(4,1)}), s8[1572864]{0:T(1024)(128)(4,1)S(1)}, s32[]{:S(2)}) async-start(s8[5767168]{0:T(1024)(128)(4,1)} %bitcast.204), calls=%async_computation.6 | async-start | bytes 3145728
  407.6 9.9 %copy-start.53 = (bf16[2,256,1024]{2,1,0:T(8,128)(2,1)}, bf16[2,256,1024]{2,1,0:T(8,128)(2,1)S(1)}, u32[]{:S(2)}) copy-start(bf16[2,256,1024]{2,1,0:T(8,128)(2,1)S(1)} %get-tuple-element.229) | copy-start | bytes 3145732
  417.4 11.8 %copy-start.38 = (f32[2,256,1024]{2,1,0:T(8,128)S(1)}, f32[2,256,1024]{2,1,0:T(8,128)}, u32[]{:S(2)}) copy-start(f32[2,256,1024]{2,1,0:T(8,128)} %copy-done.37) | copy-start | bytes 6291460
  417.4 11.8 %copy-start.80 = (f32[1024,1]{0,1:T(1,128)S(1)}, f32[1024,1]{0,1:T(1,128)}, u32[]{:S(2)}) copy-start(f32[1024,1]{0,1:T(1,128)} %copy-done.79) | copy-start | bytes 12292
  417.4 11.8 %copy-start.87 = (f32[2,256]{1,0:T(2,128)S(1)}, f32[2,256]{1,0:T(2,128)}, u32[]{:S(2)}) copy-start(f32[2,256]{1,0:T(2,128)} %copy-done.86) | copy-start | bytes 6148
  455.2 163.9 %copy-start.24 = (f32[2,256,128]{2,1,0:T(8,128)S(1)}, f32[2,256,128]{2,1,0:T(8,128)}, u32[]{:S(2)}) copy-start(f32[2,256,128]{2,1,0:T(8,128)} %copy-done.23) | copy-start | bytes 786436
  620.4 11.4 %copy-start.36 = (f32[2,256,1024]{2,1,0:T(8,128)S(1)}, f32[2,256,1024]{2,1,0:T(8,128)}, u32[]{:S(2)}) copy-start(f32[2,256,1024]{2,1,0:T(8,128)} %copy-done.35) | copy-start | bytes 6291460
  620.4 11.4 %copy-start.67 = (f32[2,2,1024]{2,1,0:T(2,128)S(1)}, f32[2,2,1024]{2,1,0:T(2,128)}, u32[]{:S(2)}) copy-start(f32[2,2,1024]{2,1,0:T(2,128)} %copy-done.66) | copy-start | bytes 49156
  620.4 11.4 %copy-start.83 = (f32[2,256]{1,0:T(2,128)S(1)}, f32[2,256]{1,0:T(2,128)}, u32[]{:S(2)}) copy-start(f32[2,256]{1,0:T(2,128)} %copy-done.82) | copy-start | bytes 6148
  620.4 11.4 %copy-start.85 = (f32[2,256]{1,0:T(2,128)S(1)}, f32[2,256]{1,0:T(2,128)}, u32[]{:S(2)}) copy-start(f32[2,256]{1,0:T(2,128)} %copy-done.84) | copy-start | bytes 6148
  620.4 11.4 %copy-start.89 = (f32[256]{0:T(256)S(1)}, f32[256]{0:T(256)}, u32[]{:S(2)}) copy-start(f32[256]{0:T(256)} %copy-done.88) | copy-start | bytes 3076
  635.4 10.8 %collective-permute-start.3 = (f32[2,2,1024]{2,1,0:T(2,128)S(1)}, f32[2,2,1024]{2,1,0:T(2,128)S(1)}, u32[]{:S(2)}, u32[]{:S(2)}) collective-permute-start(f32[2,2,1024]{2,1,0:T(2,128)S(1)} %pad_add_fusion.1), channel_id=1, source_target_pairs={{1,0},{2,1},{3,2},{5,4},{6,5},{7,6},{9,8},{10,9},{11,10},{13,12},{... | collective-permute-start | bytes 49160 | tf_op jit(solution)/shard_map/ppermute | solution.py:557
  652.9 39.8 %copy-start.46 = (f32[2,256,1024]{2,1,0:T(8,128)S(1)}, f32[2,256,1024]{2,1,0:T(8,128)}, u32[]{:S(2)}) copy-start(f32[2,256,1024]{2,1,0:T(8,128)} %get-tuple-element.228) | copy-start | bytes 6291460
  692.7 5.2 copy-start.81
  692.7 5.9 copy-start.70
  692.7 6.5 copy-start.69
  695.9 5.6 copy-start.63
  695.9 6.3 copy-start.68
  (56 other events, 130.8 us)
Sparse Core Ops, SparseCore 0:
  10.9 129.9 all-gather.1
  348.1 91.1 reduce-scatter.2
  642.1 36.2 reduce-scatter.4
